TPU v7x, 32 devices: a whole 2x2x4 slice. The times are simulated.
32 devices in a mesh: seq: 16 (over z, y, x), tp: 2 (over core).
Axes of the slice: x: 2, y: 2, z: 4, core: 2. Of those that a mesh axis runs over, the one named last changes fastest.
Arguments:
- block_input: bfloat16 [2, 4096, 2048], P(None, 'seq'), may hold values from -6 to 6
- lengths: int32 [2], replicated, may hold values from 1024 to 4096, as said below
- attn_gain: float32 [2048], P('seq'), may hold values from 0.5 to 1.5
- query_weight: float32 [2048, 2048], P('seq', 'tp'), may hold values from -0.125 to 0.125
- key_weight: float32 [2048, 2048], P('seq', 'tp'), may hold values from -0.125 to 0.125
- value_weight: float32 [2048, 2048], P('seq', 'tp'), may hold values from -0.125 to 0.125
- outgate_weight: float32 [2048, 2048], P('seq', 'tp'), may hold values from -0.125 to 0.125
- beta_weight: float32 [2048, 16], P('seq', 'tp'), may hold values from -0.125 to 0.125
- conv_kernel: float32 [16, 3, 4, 128], P('tp', None, None, 'seq'), may hold values from -3 to 3
- head_gain: float32 [128], P('seq'), may hold values from 0.5 to 1.5
- output_weight: float32 [2048, 2048], P('tp', 'seq'), may hold values from -0.125 to 0.125
- mlp_gain: float32 [2048], P('seq'), may hold values from 0.5 to 1.5
- swish_weight: float32 [2048, 5632], P('seq', 'tp'), may hold values from -0.125 to 0.125
- upward_weight: float32 [2048, 5632], P('seq', 'tp'), may hold values from -0.125 to 0.125
- downward_weight: float32 [5632, 2048], P('tp', 'seq'), may hold values from -0.078125 to 0.078125
- out_grad: bfloat16 [2, 4096, 2048], P(None, 'seq'), may hold values from -6 to 6
Outputs:
- block_output: bfloat16 [2, 4096, 2048], P(None, 'seq')
- input_grad: bfloat16 [2, 4096, 2048], P(None, 'seq')
- attn_gain_grad: float32 [2048], P('seq')
- query_grad: float32 [2048, 2048], P('seq', 'tp')
- key_grad: float32 [2048, 2048], P('seq', 'tp')
- value_grad: float32 [2048, 2048], P('seq', 'tp')
- outgate_grad: float32 [2048, 2048], P('seq', 'tp')
- beta_grad: float32 [2048, 16], P('seq', 'tp')
- conv_grad: float32 [16, 3, 4, 128], P('tp', None, None, 'seq')
- head_gain_grad: float32 [128], P('seq')
- output_grad: float32 [2048, 2048], P('tp', 'seq')
- mlp_gain_grad: float32 [2048], P('seq')
- swish_grad: float32 [2048, 5632], P('seq', 'tp')
- upward_grad: float32 [2048, 5632], P('seq', 'tp')
- downward_grad: float32 [5632, 2048], P('tp', 'seq')
Inputs may be any that keep to these rules, and one draw needn't show every extreme that they name: `lengths`: one of the two sequences, chosen by the seed, has 4096 live positions; the other has 1024 or more.
All inputs are finite; a program needn't handle non-finite values.
Results may differ from a plain program's by a relative error of at most 0.02.
The roundings to bfloat16 on the way count: a program that leaves them out, or rounds other values in their place, can miss the bound.
Values may be sent and summed in bfloat16 or wider, within the bound.
A program may use at most 640 MiB of HBM per device.

v0:
```python
import jax
import jax.numpy as jnp
from jax import lax
from jax.sharding import PartitionSpec as P

BLOCK = 64
CONV = 4


PRECISE = lax.Precision.HIGHEST
epsilon = 1e-06


def shifted(value, axis, steps):
    count = lax.axis_size(axis)
    first, last = (max(0, -steps), min(count, count - steps))
    return lax.ppermute(value, axis, [(source, source + steps) for source in range(first, last)])


def entering_2(array, axis, join, neutral):
    place = lax.axis_index(axis)
    gathered = jax.tree.map(
        lambda a, kind: lax.all_gather(a.astype(kind), axis), array, (jnp.bfloat16, jnp.bfloat16)
    )
    state = jax.tree.map(lambda a, e: jnp.zeros_like(a) + jnp.asarray(e, a.dtype), array, neutral)

    def entering_one(hop, state):
        return join(
            state,
            jax.tree.map(
                lambda a, own: lax.dynamic_index_in_dim(a, hop, 0, False).astype(own.dtype),
                gathered,
                array,
            ),
        )

    return lax.fori_loop(0, place, entering_one, state)


def prefix(array, axis, join, neutral):
    count = lax.axis_size(axis)
    place = lax.axis_index(axis)
    ahead = count - 1 - place
    gathered = jax.tree.map(
        lambda a, kind: lax.all_gather(a.astype(kind), axis),
        array,
        jax.tree.map(lambda a: jnp.bfloat16 if a.dtype == jnp.float32 else a.dtype, array),
    )
    state = jax.tree.map(lambda a, e: jnp.zeros_like(a) + jnp.asarray(e, a.dtype), array, neutral)

    def prefix_one(hop, state):
        source = count - 1 - hop
        return join(
            state,
            jax.tree.map(
                lambda a, own: lax.dynamic_index_in_dim(a, source, 0, False).astype(own.dtype),
                gathered,
                array,
            ),
        )

    return lax.fori_loop(0, ahead, prefix_one, state)


def product(form, left, right):
    return jnp.einsum(form, left, right, precision=PRECISE)


def silu_slope(value):
    squash = jax.nn.sigmoid(value)
    return squash * (1.0 + value * (1.0 - squash))


def rms_scale(value):
    return lax.rsqrt(jnp.mean(value * value, axis=-1, keepdims=True) + epsilon)


def norm_back(grad_normed, source, inverse, scale):
    scaled = grad_normed * scale
    gain_grad = jnp.sum(grad_normed * source * inverse, axis=0)
    source_grad = inverse * (
        scaled - source * inverse * inverse * jnp.mean(scaled * source, axis=-1, keepdims=True)
    )
    return (source_grad, gain_grad)


def unit_back(grad_unit, source, inverse, factor):
    return (
        factor
        * inverse
        * (
            grad_unit
            - source * inverse * inverse * jnp.sum(grad_unit * source, axis=-1, keepdims=True)
        )
    )


def compose(earlier, later):
    return (
        product("...ij,...jk->...ik", later[0], earlier[0]),
        product("...ij,...jk->...ik", later[0], earlier[1]) + later[1],
    )


def wy_form(keys, values, betas):
    width = keys.shape[-2]
    head_size = keys.shape[-1]
    gram = product("...id,...jd->...ij", keys, keys)
    strict = jnp.tril(jnp.ones((width, width), jnp.float32), -1)
    system = jnp.eye(width, dtype=jnp.float32) + betas[..., :, None] * gram * strict
    right_side = jnp.concatenate([betas[..., None] * keys, betas[..., None] * values], axis=-1)
    solved = lax.linalg.triangular_solve(
        system, right_side, left_side=True, lower=True, unit_diagonal=True
    )
    return (solved[..., :head_size], solved[..., head_size:])


def delta_maps(keys, wy_keys, wy_values):
    head_size = keys.shape[-1]
    identity = jnp.broadcast_to(
        jnp.eye(head_size, dtype=jnp.float32), keys.shape[:2] + (head_size, head_size)
    )

    def advance(carry, pieces):
        matrix, offset = carry
        key_block, wkey_block, wvalue_block = pieces
        step_map = identity - product("...cd,...ce->...de", key_block, wkey_block)
        new_matrix = product("...ij,...jk->...ik", step_map, matrix)
        new_offset = product("...ij,...jk->...ik", step_map, offset) + product(
            "...cd,...ce->...de", key_block, wvalue_block
        )
        return ((new_matrix, new_offset), None)

    moved = tuple((jnp.moveaxis(array, 2, 0) for array in (keys, wy_keys, wy_values)))
    result, _ = lax.scan(advance, (identity, jnp.zeros_like(identity)), moved)
    return result


def delta_rule(queries, keys, wy_keys, wy_values, start):
    width = queries.shape[-2]
    causal = jnp.tril(jnp.ones((width, width), jnp.float32))

    def advance(state, pieces):
        query_block, key_block, wkey_block, wvalue_block = pieces
        fresh = wvalue_block - product("...cd,...de->...ce", wkey_block, state)
        scores = product("...id,...jd->...ij", query_block, key_block) * causal
        output = product("...cd,...de->...ce", query_block, state) + product(
            "...ij,...je->...ie", scores, fresh
        )
        return (state + product("...cd,...ce->...de", key_block, fresh), output)

    moved = tuple((jnp.moveaxis(array, 2, 0) for array in (queries, keys, wy_keys, wy_values)))
    final, outputs = lax.scan(advance, start, moved)
    return (jnp.moveaxis(outputs, 0, 2), final)


def on_device(
    block_input,
    lengths,
    attn_gain,
    query_weight,
    key_weight,
    value_weight,
    outgate_weight,
    beta_weight,
    conv_kernel,
    head_gain,
    output_weight,
    mlp_gain,
    swish_weight,
    upward_weight,
    downward_weight,
    out_grad,
):
    masters = (
        attn_gain,
        query_weight,
        key_weight,
        value_weight,
        outgate_weight,
        beta_weight,
        conv_kernel,
        head_gain,
        output_weight,
        mlp_gain,
        swish_weight,
        upward_weight,
        downward_weight,
    )
    (
        attn_low,
        query_low,
        key_low,
        value_low,
        outgate_low,
        beta_low,
        conv_low,
        head_low,
        output_low,
        mlp_low,
        swish_low,
        upward_low,
        downward_low,
    ) = tuple((master.astype(jnp.bfloat16) for master in masters))
    params = (
        lax.all_gather(attn_low, "seq", axis=0, tiled=True),
        lax.all_gather(query_low, "seq", axis=0, tiled=True),
        lax.all_gather(key_low, "seq", axis=0, tiled=True),
        lax.all_gather(value_low, "seq", axis=0, tiled=True),
        lax.all_gather(outgate_low, "seq", axis=0, tiled=True),
        lax.all_gather(beta_low, "seq", axis=0, tiled=True),
        lax.all_gather(conv_low, "seq", axis=3, tiled=True),
        lax.all_gather(head_low, "seq", axis=0, tiled=True),
        lax.all_gather(output_low, "seq", axis=1, tiled=True),
        lax.all_gather(mlp_low, "seq", axis=0, tiled=True),
        lax.all_gather(swish_low, "seq", axis=0, tiled=True),
        lax.all_gather(upward_low, "seq", axis=0, tiled=True),
        lax.all_gather(downward_low, "seq", axis=1, tiled=True),
    )
    (
        attn_scale,
        query_full,
        key_full,
        value_full,
        outgate_full,
        beta_full,
        conv_full,
        head_scale,
        output_full,
        mlp_scale,
        swish_full,
        upward_full,
        downward_full,
    ) = params
    seq_count, tokens, model_width = block_input.shape
    heads_local = beta_full.shape[1]
    head_size = head_scale.shape[0]
    local_width = query_full.shape[1]
    row_count = seq_count * tokens
    block_count = tokens // BLOCK
    positions = lax.axis_index("seq") * tokens + jnp.arange(tokens, dtype=jnp.int32)
    validity = (positions[None, :] < lengths[:, None]).astype(jnp.float32)

    def to_blocks(array):
        return array.reshape(seq_count, block_count, BLOCK, heads_local, head_size).transpose(
            0, 3, 1, 2, 4
        )

    def from_blocks(array):
        return array.transpose(0, 2, 3, 1, 4).reshape(seq_count, tokens, heads_local, head_size)

    wide_input = block_input.astype(jnp.float32).reshape(row_count, model_width)
    first_inverse = rms_scale(wide_input)
    flat_normed = (wide_input * first_inverse * attn_scale.astype(jnp.float32)).astype(jnp.bfloat16)
    raw_streams = (
        jnp.stack(
            [
                jnp.dot(flat_normed, weight, preferred_element_type=jnp.float32)
                for weight in (query_full, key_full, value_full)
            ]
        )
        .astype(jnp.bfloat16)
        .reshape(3, seq_count, tokens, local_width)
    )
    gate_values = jnp.dot(flat_normed, outgate_full, preferred_element_type=jnp.float32).astype(
        jnp.bfloat16
    )
    beta_logits = jnp.dot(flat_normed, beta_full, preferred_element_type=jnp.float32).reshape(
        seq_count, tokens, heads_local
    )
    tails = shifted(raw_streams[:, :, tokens - (CONV - 1) :], "seq", 1)
    extended = jnp.concatenate([tails, raw_streams], axis=2).astype(jnp.float32)
    taps = conv_full.astype(jnp.float32).transpose(1, 2, 0, 3).reshape(3, CONV, local_width)
    pre_act = sum(
        (
            taps[:, offset][:, None, None, :] * extended[:, :, offset : offset + tokens]
            for offset in range(CONV)
        )
    )
    activated = jax.nn.silu(pre_act)
    query_raw = activated[0].reshape(seq_count, tokens, heads_local, head_size)
    key_raw = activated[1].reshape(seq_count, tokens, heads_local, head_size)
    query_inverse = lax.rsqrt(jnp.sum(query_raw * query_raw, axis=-1, keepdims=True) + epsilon)
    key_inverse = lax.rsqrt(jnp.sum(key_raw * key_raw, axis=-1, keepdims=True) + epsilon)
    queries = (
        (query_raw * query_inverse * head_size ** (-0.5)).astype(jnp.bfloat16).astype(jnp.float32)
    )
    keys = (key_raw * key_inverse).astype(jnp.bfloat16).astype(jnp.float32)
    values = (
        activated[2]
        .astype(jnp.bfloat16)
        .astype(jnp.float32)
        .reshape(seq_count, tokens, heads_local, head_size)
    )
    beta_squash = jax.nn.sigmoid(beta_logits)
    beta_gate = beta_squash * validity[:, :, None]
    query_blocks = to_blocks(queries)
    key_blocks = to_blocks(keys)
    value_blocks = to_blocks(values)
    beta_blocks = beta_gate.reshape(seq_count, block_count, BLOCK, heads_local).transpose(
        0, 3, 1, 2
    )
    (wy_keys, wy_values), wy_back = jax.vjp(wy_form, key_blocks, value_blocks, beta_blocks)
    map_matrix, map_offset = delta_maps(key_blocks, wy_keys, wy_values)
    identity = jnp.broadcast_to(jnp.eye(head_size, dtype=jnp.float32), map_matrix.shape)
    nothing = jnp.zeros_like(map_matrix)
    entering = entering_2((map_matrix, map_offset), "seq", compose, (identity, nothing))[1]
    (mixed_blocks, leaving), rule_back = jax.vjp(
        delta_rule, query_blocks, key_blocks, wy_keys, wy_values, entering
    )
    mixed = from_blocks(mixed_blocks)
    mix_inverse = rms_scale(mixed)
    head_normed = mixed * mix_inverse * head_scale.astype(jnp.float32)
    gate_wide = gate_values.astype(jnp.float32).reshape(seq_count, tokens, heads_local, head_size)
    silu_gate = jax.nn.silu(gate_wide)
    gated = (head_normed * silu_gate).astype(jnp.bfloat16).reshape(row_count, local_width)
    attn_out = lax.psum(
        jnp.dot(gated, output_full, preferred_element_type=jnp.float32).astype(jnp.bfloat16), "tp"
    ).astype(jnp.float32)
    middle = wide_input + attn_out
    second_inverse = rms_scale(middle)
    mlp_normed = (middle * second_inverse * mlp_scale.astype(jnp.float32)).astype(jnp.bfloat16)
    gate_act = jnp.dot(mlp_normed, swish_full, preferred_element_type=jnp.float32)
    up_act = jnp.dot(mlp_normed, upward_full, preferred_element_type=jnp.float32)
    silu_act = jax.nn.silu(gate_act)
    hidden = (silu_act * up_act).astype(jnp.bfloat16)
    mlp_out = lax.psum(
        jnp.dot(hidden, downward_full, preferred_element_type=jnp.float32).astype(jnp.bfloat16),
        "tp",
    ).astype(jnp.float32)
    block_output = (middle + mlp_out).astype(jnp.bfloat16).reshape(seq_count, tokens, model_width)
    (
        attn_scale,
        query_full,
        key_full,
        value_full,
        outgate_full,
        beta_full,
        conv_full,
        head_scale,
        output_full,
        mlp_scale,
        swish_full,
        upward_full,
        downward_full,
    ) = params
    taps = conv_full.astype(jnp.float32).transpose(1, 2, 0, 3).reshape(3, CONV, local_width)
    grad_low = out_grad.reshape(row_count, model_width)
    grad_wide = grad_low.astype(jnp.float32)
    hidden_grad = jnp.einsum(
        "rd,fd->rf", grad_low, downward_full, preferred_element_type=jnp.float32
    )
    downward_grad = jnp.einsum("rf,rd->fd", hidden, grad_low, preferred_element_type=jnp.float32)
    swish_act_grad = (hidden_grad * up_act * silu_slope(gate_act)).astype(jnp.bfloat16)
    up_act_grad = (hidden_grad * silu_act).astype(jnp.bfloat16)
    swish_grad = jnp.einsum(
        "rd,rf->df", mlp_normed, swish_act_grad, preferred_element_type=jnp.float32
    )
    upward_grad = jnp.einsum(
        "rd,rf->df", mlp_normed, up_act_grad, preferred_element_type=jnp.float32
    )
    normed_two_part = jnp.einsum(
        "rf,df->rd", swish_act_grad, swish_full, preferred_element_type=jnp.float32
    ) + jnp.einsum("rf,df->rd", up_act_grad, upward_full, preferred_element_type=jnp.float32)
    normed_two_grad = lax.psum(normed_two_part.astype(jnp.bfloat16), "tp").astype(jnp.float32)
    middle_part, mlp_gain_grad = norm_back(
        normed_two_grad, middle, second_inverse, mlp_scale.astype(jnp.float32)
    )
    middle_grad = grad_wide + middle_part
    attn_grad_low = middle_grad.astype(jnp.bfloat16)
    output_grad = jnp.einsum("rc,rd->cd", gated, attn_grad_low, preferred_element_type=jnp.float32)
    gated_grad = jnp.einsum(
        "rd,cd->rc", attn_grad_low, output_full, preferred_element_type=jnp.float32
    ).reshape(seq_count, tokens, heads_local, head_size)
    outgate_act_grad = (
        (gated_grad * head_normed * silu_slope(gate_wide))
        .astype(jnp.bfloat16)
        .reshape(row_count, local_width)
    )
    mixed_flat_grad, head_gain_part = norm_back(
        (gated_grad * silu_gate).reshape(-1, head_size),
        mixed.reshape(-1, head_size),
        mix_inverse.reshape(-1, 1),
        head_scale.astype(jnp.float32),
    )
    mixed_grad = mixed_flat_grad.reshape(seq_count, tokens, heads_local, head_size)
    query_bgrad, key_bgrad, wkey_grad, wvalue_grad, local_state = rule_back(
        (to_blocks(mixed_grad), jnp.zeros_like(leaving))
    )
    leaving_grad = prefix(
        (jnp.swapaxes(map_matrix, -1, -2), local_state), "seq", compose, (identity, nothing)
    )[1]
    later_back = rule_back((jnp.zeros_like(mixed_blocks), leaving_grad))
    key_bgrad = key_bgrad + later_back[1]
    wkey_grad = wkey_grad + later_back[2]
    wvalue_grad = wvalue_grad + later_back[3]
    key_cgrad, value_bgrad, beta_bgrad = wy_back((wkey_grad, wvalue_grad))
    query_grad_unit = from_blocks(query_bgrad)
    key_grad_unit = from_blocks(key_bgrad + key_cgrad)
    value_grad_act = from_blocks(value_bgrad)
    beta_token_grad = beta_bgrad.transpose(0, 2, 3, 1).reshape(seq_count, tokens, heads_local)
    beta_logit_grad = (
        (beta_token_grad * validity[:, :, None] * beta_squash * (1.0 - beta_squash))
        .astype(jnp.bfloat16)
        .reshape(row_count, heads_local)
    )
    act_grads = jnp.stack(
        [
            unit_back(query_grad_unit, query_raw, query_inverse, head_size ** (-0.5)).reshape(
                seq_count, tokens, local_width
            ),
            unit_back(key_grad_unit, key_raw, key_inverse, 1.0).reshape(
                seq_count, tokens, local_width
            ),
            value_grad_act.reshape(seq_count, tokens, local_width),
        ]
    )
    pre_grad = act_grads * silu_slope(pre_act)
    padded_grad = jnp.pad(pre_grad, ((0, 0), (0, 0), (CONV - 1, CONV - 1), (0, 0)))
    span = tokens + CONV - 1
    extended_grad = sum(
        (
            taps[:, offset][:, None, None, :]
            * padded_grad[:, :, CONV - 1 - offset : CONV - 1 - offset + span]
            for offset in range(CONV)
        )
    )
    taps_grad = jnp.stack(
        [
            jnp.sum(pre_grad * extended[:, :, offset : offset + tokens], axis=(1, 2))
            for offset in range(CONV)
        ],
        axis=1,
    )
    returned = shifted(extended_grad[:, :, : CONV - 1].astype(jnp.bfloat16), "seq", -1).astype(
        jnp.float32
    )
    raw_grad = extended_grad[:, :, CONV - 1 :].at[:, :, tokens - (CONV - 1) :].add(returned)
    raw_grad_low = raw_grad.astype(jnp.bfloat16).reshape(3, row_count, local_width)
    stream_grads = [
        jnp.einsum(
            "rd,rc->dc", flat_normed, raw_grad_low[index], preferred_element_type=jnp.float32
        )
        for index in range(3)
    ]
    outgate_grad = jnp.einsum(
        "rd,rc->dc", flat_normed, outgate_act_grad, preferred_element_type=jnp.float32
    )
    beta_grad = jnp.einsum(
        "rd,rh->dh", flat_normed, beta_logit_grad, preferred_element_type=jnp.float32
    )
    normed_part = jnp.einsum(
        "rc,dc->rd", outgate_act_grad, outgate_full, preferred_element_type=jnp.float32
    )
    normed_part = normed_part + jnp.einsum(
        "rh,dh->rd", beta_logit_grad, beta_full, preferred_element_type=jnp.float32
    )
    for index, weight in enumerate((query_full, key_full, value_full)):
        normed_part = normed_part + jnp.einsum(
            "rc,dc->rd", raw_grad_low[index], weight, preferred_element_type=jnp.float32
        )
    normed_grad, head_gain_sum = (
        lax.psum(normed_part.astype(jnp.bfloat16), "tp").astype(jnp.float32),
        lax.psum(head_gain_part.astype(jnp.bfloat16), "tp").astype(jnp.float32),
    )
    input_part, attn_gain_grad = norm_back(
        normed_grad, wide_input, first_inverse, attn_scale.astype(jnp.float32)
    )
    input_grad = (
        (middle_grad + input_part).astype(jnp.bfloat16).reshape(seq_count, tokens, model_width)
    )
    conv_grad = taps_grad.reshape(3, CONV, heads_local, head_size).transpose(2, 0, 1, 3)
    summed = (
        lax.psum_scatter(attn_gain_grad, "seq", scatter_dimension=0, tiled=True),
        lax.psum_scatter(stream_grads[0], "seq", scatter_dimension=0, tiled=True),
        lax.psum_scatter(stream_grads[1], "seq", scatter_dimension=0, tiled=True),
        lax.psum_scatter(stream_grads[2], "seq", scatter_dimension=0, tiled=True),
        lax.psum_scatter(outgate_grad, "seq", scatter_dimension=0, tiled=True),
        lax.psum_scatter(beta_grad, "seq", scatter_dimension=0, tiled=True),
        lax.psum_scatter(conv_grad, "seq", scatter_dimension=3, tiled=True),
        lax.psum_scatter(head_gain_sum, "seq", scatter_dimension=0, tiled=True),
        lax.psum_scatter(output_grad, "seq", scatter_dimension=1, tiled=True),
        lax.psum_scatter(mlp_gain_grad, "seq", scatter_dimension=0, tiled=True),
        lax.psum_scatter(swish_grad, "seq", scatter_dimension=0, tiled=True),
        lax.psum_scatter(upward_grad, "seq", scatter_dimension=0, tiled=True),
        lax.psum_scatter(downward_grad, "seq", scatter_dimension=1, tiled=True),
    )
    return (
        block_output,
        input_grad,
        summed[0],
        summed[1],
        summed[2],
        summed[3],
        summed[4],
        summed[5],
        summed[6],
        summed[7],
        summed[8],
        summed[9],
        summed[10],
        summed[11],
        summed[12],
    )


def solution(mesh):
    return jax.shard_map(
        on_device,
        mesh=mesh,
        in_specs=(
            P(None, "seq", None),
            P(),
            P("seq"),
            P("seq", "tp"),
            P("seq", "tp"),
            P("seq", "tp"),
            P("seq", "tp"),
            P("seq", "tp"),
            P("tp", None, None, "seq"),
            P("seq"),
            P("tp", "seq"),
            P("seq"),
            P("seq", "tp"),
            P("seq", "tp"),
            P("tp", "seq"),
            P(None, "seq", None),
        ),
        out_specs=(
            P(None, "seq", None),
            P(None, "seq", None),
            P("seq"),
            P("seq", "tp"),
            P("seq", "tp"),
            P("seq", "tp"),
            P("seq", "tp"),
            P("seq", "tp"),
            P("tp", None, None, "seq"),
            P("seq"),
            P("tp", "seq"),
            P("seq"),
            P("seq", "tp"),
            P("seq", "tp"),
            P("tp", "seq"),
        ),
        check_vma=False,
    )
```

profile of v0, /device:TPU:0, one launch (start us, length us, event | category | flops | bytes accessed | tf_op | source)
XLA Modules:
  0.0 4545.2 jit_solution(1430399439988525048)
XLA Ops:
  11.9 42.3 all-gather.4
  54.3 40.3 all_gather.63
  95.1 38.3 all_gather.68
  142.7 30.3 all-gather.21.cloned.1.call-done
  178.5 72.6 %all-gather.19.cloned.1.call-done = bf16[2048,1024]{1,0:T(8,128)(2,1)} async-done(((bf16[128,1024]{1,0:T(8,128)(2,1)}), bf16[2048,1024]{1,0:T(8,128)(2,1)}) %all-gather.19.cloned.1.call-update) | async-done | bytes 4194320 | tf_op jit(solution)/shard_map/all_gather | solution.py:207
  285.8 315.2 %custom-call.7 = f32[2,8,4,1,64,64]{4,5,3,2,1,0:T(8,128)S(1)} custom-call(f32[2,8,4,1,64,64]{5,4,3,2,1,0:T(8,128)} %add_bitcast_fusion.2), custom_call_target="InvertDiagBlocksLowerTriangular" | custom-call | tf_op jit(solution)/shard_map/jvp()/triangular_solve | solution.py:112
  614.5 44.5 while.107
  671.1 41.1 all-reduce.3
  720.8 54.3 %all-gather.35.cloned.1.call-done = bf16[32,8,128,128]{3,2,1,0:T(8,128)(2,1)} async-done(((bf16[2,8,128,128]{3,2,1,0:T(8,128)(2,1)}), bf16[32,8,128,128]{3,2,1,0:T(8,128)(2,1)}) %all-gather.35.cloned.1.call-update) | async-done | bytes 8388624 | tf_op jit(solution)/shard_map/all_gather | solution.py:23
  775.1 114.2 %all-gather.37.cloned.1.call-done = bf16[32,8,128,128]{3,2,1,0:T(8,128)(2,1)} async-done(((bf16[2,8,128,128]{3,2,1,0:T(8,128)(2,1)}), bf16[32,8,128,128]{3,2,1,0:T(8,128)(2,1)}) %all-gather.37.cloned.1.call-update) | async-done | bytes 8388624 | tf_op jit(solution)/shard_map/all_gather | solution.py:23
  892.7 55.1 %while.105 = (s32[]{:T(128)}, f32[2,8,128,128]{3,2,1,0:T(8,128)S(1)}, f32[4,2,8,64,128]{4,3,2,1,0:T(8,128)}, f32[4,2,8,128,128]{4,3,2,1,0:T(8,128)}, f32[4,2,8,6...) while((s32[]{:T(128)}, ...), condition=%wide.region_8.9_spmd.clone, body=%wide.region_7.8_spmd.clone.sunk | while | flops 805904384 | bytes 24694952 | solution.py:153
  954.3 12.6 all-gather.25.cloned.1.call-done
  968.8 6.7 fusion.189
  975.5 82.4 %all-gather.27.cloned.1.call-done = bf16[1024,2048]{1,0:T(8,128)(2,1)} async-done(((bf16[1024,128]{1,0:T(8,128)(2,1)}), bf16[1024,2048]{1,0:T(8,128)(2,1)}) %all-gather.27.cloned.1.call-update) | async-done | bytes 4194320 | tf_op jit(solution)/shard_map/all_gather | solution.py:214
  1071.0 37.7 all-gather.5
  1114.7 115.2 %all-gather.29.cloned.1.call-done = bf16[2048,2816]{1,0:T(8,128)(2,1)} async-done(((bf16[128,2816]{1,0:T(8,128)(2,1)}), bf16[2048,2816]{1,0:T(8,128)(2,1)}) %all-gather.29.cloned.1.call-update) | async-done | bytes 11534352 | tf_op jit(solution)/shard_map/all_gather | solution.py:216
  1229.9 12.7 fusion.252
  1242.5 130.7 %all-gather.31.cloned.1.call-done = bf16[2048,2816]{1,0:T(8,128)(2,1)} async-done(((bf16[128,2816]{1,0:T(8,128)(2,1)}), bf16[2048,2816]{1,0:T(8,128)(2,1)}) %all-gather.31.cloned.1.call-update) | async-done | bytes 11534352 | tf_op jit(solution)/shard_map/all_gather | solution.py:217
  1373.2 12.5 fusion.253
  1385.7 171.4 %all-gather.33.cloned.1.call-done = bf16[2816,2048]{1,0:T(8,128)(2,1)} async-done(((bf16[2816,128]{1,0:T(8,128)(2,1)}), bf16[2816,2048]{1,0:T(8,128)(2,1)}) %all-gather.33.cloned.1.call-update) | async-done | bytes 11534352 | tf_op jit(solution)/shard_map/all_gather | solution.py:218
  1557.1 15.5 multiply_convert_fusion
  1572.6 11.1 fusion.254
  1583.8 10.3 add_convert_fusion.1
  1601.6 12.0 all-reduce.17.cloned.1.call-done
  1640.8 105.3 %while.108 = (s32[]{:T(128)}, f32[2,8,128,128]{3,2,1,0:T(8,128)S(1)}, f32[4,2,8,64,128]{4,3,2,1,0:T(8,128)}, f32[4,2,8,64,128]{4,3,0,2,1:T(8,128)}, f32[4,2,8,64...) while((s32[]{:T(128)}, ...), condition=%wide.region_17.18_spmd.clone, body=%wide.region_16.17_spmd.clone.sunk | while | flops 1612652544 | bytes 49849636 | solution.py:153
  1761.1 11.0 convolution_convert_fusion.1
  1784.6 6.6 fusion.255
  1791.2 70.1 %all-gather.41.cloned.1.call-done = bf16[32,8,128,128]{3,2,1,0:T(8,128)(2,1)} async-done(((bf16[2,8,128,128]{3,2,1,0:T(8,128)(2,1)}), bf16[32,8,128,128]{3,2,1,0:T(8,128)(2,1)}) %all-gather.41.cloned.1.call-update) | async-done | bytes 8388624 | tf_op jit(solution)/shard_map/all_gather | solution.py:45
  1861.4 30.3 while.104
  1896.5 86.5 %while.106 = (s32[]{:T(128)}, f32[2,8,128,128]{3,2,1,0:T(8,128)S(1)}, f32[4,2,8,64,128]{4,3,0,2,1:T(8,128)}, f32[4,2,8,64,128]{4,3,2,1,0:T(8,128)}, f32[4,2,8,64...) while((s32[]{:T(128)}, ...), condition=%wide.region_21.22_spmd.clone, body=%wide.region_20.21_spmd.clone.sunk | while | flops 1309745152 | bytes 16813212 | solution.py:153
  2026.8 11.5 fusion.181
  2038.3 9.5 multiply_reduce_fusion.3
  2047.9 10.4 multiply_add_fusion
  2080.8 8.7 fusion.235
  2090.7 7.5 fusion.262
  2120.5 12.7 fusion.263
  2133.2 12.8 fusion.264
  2147.5 12.9 fusion.265
  2167.7 78.1 %all-reduce.20 = (f32[2048]{0:T(1024)S(1)}, f32[8,3,4,128]{3,0,1,2:T(8,128)S(1)}, f32[128]{0:T(128)S(1)}, f32[2048]{0:T(1024)S(1)}) all-reduce(f32[2048]{0:T(1024)S(1)} %get-tuple-element.1129, f32[8,3,4,128]{3,0,1,2:T(8,128)S(1)} %maximum_bitcast_fusion, ...), channel_id=6, replica_groups=mesh['seq'=16,'tp'=2] {'seq'}, use_global_device_ids=true, to_apply=%region_30.31.clone | all-reduce | flops 16512 | bytes 131840
  2248.3 6.7 fusion.147
  2255.0 107.6 %reduce-scatter.21.cloned.1.call-done = f32[1024,128]{1,0:T(8,128)} async-done(((f32[1024,2048]{1,0:T(8,128)}), f32[1024,128]{1,0:T(8,128)}) %reduce-scatter.21.cloned.1.call-update) | async-done | bytes 524304 | tf_op jit(solution)/shard_map/reduce_scatter | solution.py:482
  2362.6 182.8 %reduce-scatter.17.cloned.1.call-done = f32[128,1024]{1,0:T(8,128)} async-done(((f32[2048,1024]{1,0:T(8,128)}), f32[128,1024]{1,0:T(8,128)}) %reduce-scatter.17.cloned.1.call-update) | async-done | bytes 524304 | tf_op jit(solution)/shard_map/reduce_scatter | solution.py:478
  2545.4 183.2 %reduce-scatter.11.cloned.1.call-done = f32[128,1024]{1,0:T(8,128)} async-done(((f32[2048,1024]{1,0:T(8,128)}), f32[128,1024]{1,0:T(8,128)}) %reduce-scatter.11.cloned.1.call-update) | async-done | bytes 524304 | tf_op jit(solution)/shard_map/reduce_scatter | solution.py:475
  2728.5 183.0 %reduce-scatter.13.cloned.1.call-done = f32[128,1024]{1,0:T(8,128)} async-done(((f32[2048,1024]{1,0:T(8,128)}), f32[128,1024]{1,0:T(8,128)}) %reduce-scatter.13.cloned.1.call-update) | async-done | bytes 524304 | tf_op jit(solution)/shard_map/reduce_scatter | solution.py:476
  2911.5 183.1 %reduce-scatter.15.cloned.1.call-done = f32[128,1024]{1,0:T(8,128)} async-done(((f32[2048,1024]{1,0:T(8,128)}), f32[128,1024]{1,0:T(8,128)}) %reduce-scatter.15.cloned.1.call-update) | async-done | bytes 524304 | tf_op jit(solution)/shard_map/reduce_scatter | solution.py:477
  3094.6 478.3 %reduce-scatter.23.cloned.1.call-done = f32[128,2816]{1,0:T(8,128)} async-done(((f32[2048,2816]{1,0:T(8,128)}), f32[128,2816]{1,0:T(8,128)}) %reduce-scatter.23.cloned.1.call-update) | async-done | bytes 1441808 | tf_op jit(solution)/shard_map/reduce_scatter | solution.py:484
  3573.0 482.7 %reduce-scatter.25.cloned.1.call-done = f32[128,2816]{1,0:T(8,128)} async-done(((f32[2048,2816]{1,0:T(8,128)}), f32[128,2816]{1,0:T(8,128)}) %reduce-scatter.25.cloned.1.call-update) | async-done | bytes 1441808 | tf_op jit(solution)/shard_map/reduce_scatter | solution.py:485
  4055.6 482.6 %reduce-scatter.27.cloned.1.call-done = f32[2816,128]{1,0:T(8,128)} async-done(((f32[2816,2048]{1,0:T(8,128)}), f32[2816,128]{1,0:T(8,128)}) %reduce-scatter.27.cloned.1.call-update) | async-done | bytes 1441808 | tf_op jit(solution)/shard_map/reduce_scatter | solution.py:486
  (656 shorter events, 602.8 us)
Async XLA Ops:
  7.2 47.0 %copy-start.89 = (f32[8,3,4,8]{3,2,1,0:T(4,128)S(1)}, f32[8,3,4,8]{3,2,1,0:T(4,128)}, u32[]{:S(2)}) copy-start(f32[8,3,4,8]{3,2,1,0:T(4,128)} %param.38) | copy-start | bytes 9220
  7.2 130.2 %all-gather.23.cloned.1.call-start = ((), (), s32[]{:S(2)}) async-start(), calls=%async_computation.11 | async-start | bytes 4456448 | tf_op jit(solution)/shard_map/all_gather | solution.py:209
  9.1 163.9 %all-gather.21.cloned.1.call-start = ((), (), s32[]{:S(2)}) async-start(), calls=%async_computation.10 | async-start | bytes 4456448 | tf_op jit(solution)/shard_map/all_gather | solution.py:208
  10.9 84.1 %copy-start.95 = (f32[128,8]{0,1:T(8,128)S(1)}, f32[128,8]{0,1:T(8,128)}, u32[]{:S(2)}) copy-start(f32[128,8]{0,1:T(8,128)} %param.37) | copy-start | bytes 12292
  10.9 122.5 %copy-start.97 = (s32[2]{0:T(128)S(1)}, s32[2]{0:T(128)}, u32[]{:S(2)}) copy-start(s32[2]{0:T(128)} %param.31) | copy-start | bytes 28
  10.9 122.5 %copy-start.1 = (bf16[2,256,2048]{2,1,0:T(8,128)(2,1)S(1)}, bf16[2,256,2048]{2,1,0:T(8,128)(2,1)}, u32[]{:S(2)}) copy-start(bf16[2,256,2048]{2,1,0:T(8,128)(2,1)} %param.30) | copy-start | bytes 6291460
  11.0 240.1 %all-gather.19.cloned.1.call-start = ((), (), s32[]{:S(2)}) async-start(), calls=%async_computation.9 | async-start | bytes 4456448 | tf_op jit(solution)/shard_map/all_gather | solution.py:207
  11.8 763.3 %all-gather.35.cloned.1.call-start = ((), (), s32[]{:S(2)}) async-start(), calls=%async_computation.28 | async-start | bytes 8912896 | tf_op jit(solution)/shard_map/all_gather | solution.py:23
  54.2 611.8 %copy-start.76 = (f32[16,1,128]{2,1,0:T(1,128)}, f32[16,1,128]{2,1,0:T(1,128)S(1)}, u32[]{:S(2)}) copy-start(f32[16,1,128]{2,1,0:T(1,128)S(1)} %convert_element_type.293) | copy-start | bytes 24580
  134.0 149.7 %copy-start.74 = (f32[64,64]{1,0:T(8,128)}, f32[64,64]{1,0:T(8,128)S(1)}, u32[]{:S(2)}) copy-start(f32[64,64]{1,0:T(8,128)S(1)} %broadcast_select_fusion) | copy-start | bytes 49156
  134.1 149.6 %copy-start.86 = (pred[64,64]{1,0:T(8,128)(4,1)}, pred[64,64]{1,0:T(8,128)(4,1)S(1)}, u32[]{:S(2)}) copy-start(pred[64,64]{1,0:T(8,128)(4,1)S(1)} %get-tuple-element.1294) | copy-start | bytes 12292
  134.2 129.7 %copy-start.78 = (f32[3,1024]{1,0:T(4,128)}, f32[3,1024]{1,0:T(4,128)S(1)}, u32[]{:S(2)}) copy-start(f32[3,1024]{1,0:T(4,128)S(1)} %get-tuple-element.1290) | copy-start | bytes 36868
  134.2 129.7 %copy-start.80 = (f32[3,1024]{1,0:T(4,128)}, f32[3,1024]{1,0:T(4,128)S(1)}, u32[]{:S(2)}) copy-start(f32[3,1024]{1,0:T(4,128)S(1)} %get-tuple-element.1291) | copy-start | bytes 36868
  134.3 129.6 %copy-start.82 = (f32[3,1024]{1,0:T(4,128)}, f32[3,1024]{1,0:T(4,128)S(1)}, u32[]{:S(2)}) copy-start(f32[3,1024]{1,0:T(4,128)S(1)} %get-tuple-element.1292) | copy-start | bytes 36868
  134.3 129.6 %copy-start.84 = (f32[3,1024]{1,0:T(4,128)}, f32[3,1024]{1,0:T(4,128)S(1)}, u32[]{:S(2)}) copy-start(f32[3,1024]{1,0:T(4,128)S(1)} %get-tuple-element.1293) | copy-start | bytes 36868
  137.4 35.6 copy-start.28
  256.7 5.1 collective-permute-start
  260.6 23.2 copy-start.59
  661.2 228.1 %all-gather.37.cloned.1.call-start = ((), (), s32[]{:S(2)}) async-start(), calls=%async_computation.29 | async-start | bytes 8912896 | tf_op jit(solution)/shard_map/all_gather | solution.py:23
  662.2 304.6 %all-gather.25.cloned.1.call-start = ((), (), s32[]{:S(2)}) async-start(), calls=%async_computation.12 | async-start | bytes 4456448 | tf_op jit(solution)/shard_map/all_gather | solution.py:210
  664.1 393.9 %all-gather.27.cloned.1.call-start = ((), (), s32[]{:S(2)}) async-start(), calls=%async_computation.13 | async-start | bytes 4456448 | tf_op jit(solution)/shard_map/all_gather | solution.py:214
  665.9 442.9 %all-reduce.15.cloned.1.call-start = ((), (), s32[]{:S(2)}) async-start(), calls=%async_computation.14 | async-start | bytes 4194304 | tf_op jit(solution)/shard_map/psum | solution.py:317
  975.5 88.2 %copy-start.69 = (bf16[512,1024]{1,0:T(8,128)(2,1)}, bf16[512,1024]{1,0:T(8,128)(2,1)S(1)}, u32[]{:S(2)}) copy-start(bf16[512,1024]{1,0:T(8,128)(2,1)S(1)} %get-tuple-element.1282) | copy-start | bytes 3145732
  1063.8 166.1 %all-gather.29.cloned.1.call-start = ((), (), s32[]{:S(2)}) async-start(), calls=%async_computation.15 | async-start | bytes 12255232 | tf_op jit(solution)/shard_map/all_gather | solution.py:216
  1066.2 307.1 %all-gather.31.cloned.1.call-start = ((), (), s32[]{:S(2)}) async-start(), calls=%async_computation.16 | async-start | bytes 12255232 | tf_op jit(solution)/shard_map/all_gather | solution.py:217
  1068.6 488.5 %all-gather.33.cloned.1.call-start = ((), (), s32[]{:S(2)}) async-start(), calls=%async_computation.17 | async-start | bytes 12255232 | tf_op jit(solution)/shard_map/all_gather | solution.py:218
  1071.0 542.7 %all-reduce.17.cloned.1.call-start = ((), (), s32[]{:S(2)}) async-start(), calls=%async_computation.18 | async-start | bytes 4194304 | tf_op jit(solution)/shard_map/psum | solution.py:365
  1572.6 11.1 copy-start.109
  1572.6 11.1 copy-start.108
  1594.0 197.2 %all-gather.39.cloned.1.call-start = ((), (), s32[]{:S(2)}) async-start(), calls=%async_computation.30 | async-start | bytes 8912896 | tf_op jit(solution)/shard_map/all_gather | solution.py:45
  1598.2 263.1 %all-gather.41.cloned.1.call-start = ((), (), s32[]{:S(2)}) async-start(), calls=%async_computation.31 | async-start | bytes 8912896 | tf_op jit(solution)/shard_map/all_gather | solution.py:45
  1747.0 417.4 %all-reduce.19.cloned.1.call-start = ((), (), s32[]{:S(2)}) async-start(), calls=%async_computation.32 | async-start | bytes 8388608 | tf_op jit(solution)/shard_map/psum | solution.py:327
  1761.1 11.0 copy-start.34
  2026.7 11.6 slice-start
  2026.8 11.5 slice-start.1
  2026.8 11.5 copy-start.44
  2047.9 11.8 copy-start.88
  2047.9 11.8 copy-start.94
  2058.3 6.0 collective-permute-start.1
  2077.8 177.2 %reduce-scatter.19.cloned.1.call-start = ((), (), s32[]{:S(2)}) async-start(), calls=%async_computation.23 | async-start | bytes 69632 | tf_op jit(solution)/shard_map/reduce_scatter | solution.py:479
  2080.4 282.2 %reduce-scatter.21.cloned.1.call-start = ((), (), s32[]{:S(2)}) async-start(), calls=%async_computation.24 | async-start | bytes 8912896 | tf_op jit(solution)/shard_map/reduce_scatter | solution.py:482
  2089.5 455.8 %reduce-scatter.17.cloned.1.call-start = ((), (), s32[]{:S(2)}) async-start(), calls=%async_computation.22 | async-start | bytes 8912896 | tf_op jit(solution)/shard_map/reduce_scatter | solution.py:478
  2098.3 630.3 %reduce-scatter.11.cloned.1.call-start = ((), (), s32[]{:S(2)}) async-start(), calls=%async_computation.19 | async-start | bytes 8912896 | tf_op jit(solution)/shard_map/reduce_scatter | solution.py:475
  2105.2 806.3 %reduce-scatter.13.cloned.1.call-start = ((), (), s32[]{:S(2)}) async-start(), calls=%async_computation.20 | async-start | bytes 8912896 | tf_op jit(solution)/shard_map/reduce_scatter | solution.py:476
  2112.0 982.6 %reduce-scatter.15.cloned.1.call-start = ((), (), s32[]{:S(2)}) async-start(), calls=%async_computation.21 | async-start | bytes 8912896 | tf_op jit(solution)/shard_map/reduce_scatter | solution.py:477
  2118.9 1454.1 %reduce-scatter.23.cloned.1.call-start = ((), (), s32[]{:S(2)}) async-start(), calls=%async_computation.25 | async-start | bytes 24510464 | tf_op jit(solution)/shard_map/reduce_scatter | solution.py:484
  2133.1 1922.5 %reduce-scatter.25.cloned.1.call-start = ((), (), s32[]{:S(2)}) async-start(), calls=%async_computation.26 | async-start | bytes 24510464 | tf_op jit(solution)/shard_map/reduce_scatter | solution.py:485
  2146.0 2392.2 %reduce-scatter.27.cloned.1.call-start = ((), (), s32[]{:S(2)}) async-start(), calls=%async_computation.27 | async-start | bytes 24510464 | tf_op jit(solution)/shard_map/reduce_scatter | solution.py:486
  (111 other events, 409.5 us)
Sparse Core Ops, SparseCore 0:
  11.4 81.7 all-gather.22
  96.5 76.4 all-gather.20
  176.3 74.6 all-gather.18
  661.4 113.6 all-gather.34
  778.3 111.0 all-gather.36
  892.5 74.2 all-gather.24
  970.1 87.7 all-gather.26
  1063.9 19.3 all-reduce.14
  1086.5 143.3 all-gather.28
  1232.8 140.3 all-gather.30
  1376.3 180.7 all-gather.32
  1594.2 19.4 all-reduce.16
  1617.0 114.0 all-gather.38
  1747.2 114.0 all-gather.40
  2077.9 24.4 all-reduce.18
  2105.1 77.1 reduce-scatter.18
  2185.0 177.5 reduce-scatter.20
  2365.3 180.0 reduce-scatter.16
  2548.2 180.2 reduce-scatter.10
  2731.2 180.1 reduce-scatter.12
  2914.4 180.2 reduce-scatter.14
  3097.5 475.4 reduce-scatter.22
  3575.9 479.7 reduce-scatter.24
  4058.4 479.7 reduce-scatter.26
where the time goes:
time: 4560 us; the launch traced here: 4550 us
  waiting for transfers between devices  3150 us (69%)
  matrix products  515 us (11%)
  other arithmetic  432 us (9%)
  blocking collectives  280 us (6%)
  local copies, waits for them, and re-layouts  135 us (3%)
    reduce_scatter x1, waiting for transfers between devices, on_device(): lax.psum_scatter(upward_grad, 'seq', scatter_dimension=0, tiled=True)  483 us
    reduce_scatter x1, waiting for transfers between devices, on_device(): lax.psum_scatter(downward_grad, 'seq', scatter_dimension=1, tiled=True)  483 us
    reduce_scatter x1, waiting for transfers between devices, on_device(): lax.psum_scatter(swish_grad, 'seq', scatter_dimension=0, tiled=True)  478 us
    another operation x5, other arithmetic, wy_form(): lax.linalg.triangular_solve(system, right_side, left_side=True, lower=Tru...  317 us
    dot_general x126, matrix products, product(): return jnp.einsum(form, left, right, precision=PRECISE)  301 us
    reduce_scatter x1, waiting for transfers between devices, on_device(): lax.psum_scatter(stream_grads[0], 'seq', scatter_dimension=0, tiled=True)  183 us
    reduce_scatter x1, waiting for transfers between devices, on_device(): lax.psum_scatter(stream_grads[2], 'seq', scatter_dimension=0, tiled=True)  183 us
    reduce_scatter x1, waiting for transfers between devices, on_device(): lax.psum_scatter(stream_grads[1], 'seq', scatter_dimension=0, tiled=True)  183 us
  transfers between devices with their start and end apart: 26, of which 21 were waited for; matrix products, arithmetic and copies ran while one was open for 9% of the time, Pallas kernels for 0%

commit v1 on v0

v1 whole, which is shorter than its diff:
```python
import jax
import jax.numpy as jnp
from jax import lax
from jax.sharding import PartitionSpec as P

BLOCK = 64
CONV = 4
MATES = 4
SMALL = 8


PRECISE = lax.Precision.HIGHEST
epsilon = 1e-06
low = jnp.bfloat16
wide = jnp.float32


def other_core(value):
    return lax.ppermute(value, "tp", [(0, 1), (1, 0)])


def to_mate(value, flip):
    count = lax.axis_size("seq")
    return lax.ppermute(value, "seq", [(source, source ^ flip) for source in range(count)])


def along(value, step, lines_kept=None):
    count = lax.axis_size("seq")
    lines = count // MATES
    pairs = []
    for source in range(count):
        line = source // MATES
        if 0 <= line + step < lines and (lines_kept is None or line in lines_kept):
            pairs.append((source, source + step * MATES))
    return lax.ppermute(value, "seq", pairs)


def mate_of():
    return lax.axis_index("seq") % MATES


def line_of():
    return lax.axis_index("seq") // MATES


def line_groups():
    lines = lax.axis_size("seq") // MATES
    return [[mate + MATES * line for line in range(lines)] for mate in range(MATES)]


def pick(blocks, index):
    return lax.dynamic_index_in_dim(blocks, index, 0, False)


def in_order(by_flip):
    mate = mate_of()
    out = jnp.zeros((MATES,) + by_flip[0].shape, by_flip[0].dtype)
    for flip, piece in enumerate(by_flip):
        out = lax.dynamic_update_index_in_dim(out, piece, mate ^ flip, 0)
    return out


def swap_blocks(blocks):
    mate = mate_of()
    pieces = [pick(blocks, mate)]
    for flip in range(1, MATES):
        pieces.append(to_mate(pick(blocks, mate ^ flip), flip))
    return in_order(pieces)


def gather_mates(value):
    half = value.shape[-1] // 2
    from_x = to_mate(value, 1)
    from_y = to_mate(value, 2)
    far = jnp.concatenate(
        [to_mate(from_x[..., :half], 2), to_mate(from_y[..., half:], 1)], axis=-1
    )
    return [value, from_x, from_y, far]


def scatter_mates(blocks):
    half = blocks[0].shape[-1] // 2
    far_y = to_mate(blocks[3][..., :half], 2)
    far_x = to_mate(blocks[3][..., half:], 1)
    for_x = jnp.concatenate(
        [(blocks[1][..., :half].astype(wide) + far_y.astype(wide)).astype(low), blocks[1][..., half:]], axis=-1
    )
    for_y = jnp.concatenate(
        [blocks[2][..., :half], (blocks[2][..., half:].astype(wide) + far_x.astype(wide)).astype(low)], axis=-1
    )
    return blocks[0].astype(wide) + to_mate(for_x, 1).astype(wide) + to_mate(for_y, 2).astype(wide)


def gather_lines(block):
    lines = lax.axis_size("seq") // MATES
    if lines > 4:
        return lax.all_gather(block, "seq", axis_index_groups=line_groups())
    line = line_of()
    ups, downs = [block], [block]
    for _ in range(1, lines):
        ups.append(along(ups[-1], 1))
        downs.append(along(downs[-1], -1))
    out = jnp.zeros((lines,) + block.shape, block.dtype)
    out = lax.dynamic_update_index_in_dim(out, block, line, 0)
    for step in range(1, lines):
        out = lax.dynamic_update_index_in_dim(
            out, ups[step] + downs[lines - step], (line - step) % lines, 0
        )
    return out


def scatter_lines(blocks):
    lines = lax.axis_size("seq") // MATES
    if lines > 4:
        return lax.psum_scatter(
            blocks, "seq", scatter_dimension=0, axis_index_groups=line_groups()
        ).astype(wide)
    line = line_of()
    from_below = from_above = None
    for step in range(1, lines):
        up = pick(blocks, (line + lines - step) % lines)
        down = pick(blocks, (line + step) % lines)
        if step > 1:
            up = (up.astype(wide) + from_below.astype(wide)).astype(low)
            down = (down.astype(wide) + from_above.astype(wide)).astype(low)
        from_below = along(up, 1, range(step))
        from_above = along(down, -1, range(lines - step, lines))
    total = pick(blocks, line).astype(wide)
    if lines > 1:
        total = total + from_below.astype(wide) + from_above.astype(wide)
    return total


def hop_states(matrix, offset, step):
    lines = lax.axis_size("seq") // MATES
    state = along(offset, step)
    for _ in range(lines - 2):
        state = along(product("...ij,...jk->...ik", matrix, state) + offset, step)
    return state


def product(form, left, right):
    return jnp.einsum(form, left, right, precision=PRECISE)


def matmul(form, left, right):
    return jnp.einsum(form, left, right, preferred_element_type=wide)


def silu_slope(value):
    squash = jax.nn.sigmoid(value)
    return squash * (1.0 + value * (1.0 - squash))


def rms_scale(value):
    return lax.rsqrt(jnp.mean(value * value, axis=-1, keepdims=True) + epsilon)


def norm_back(grad_normed, source, inverse, scale):
    scaled = grad_normed * scale
    gain_grad = jnp.sum(grad_normed * source * inverse, axis=0)
    source_grad = inverse * (
        scaled - source * inverse * inverse * jnp.mean(scaled * source, axis=-1, keepdims=True)
    )
    return (source_grad, gain_grad)


def unit_back(grad_unit, source, inverse, factor):
    return (
        factor
        * inverse
        * (
            grad_unit
            - source * inverse * inverse * jnp.sum(grad_unit * source, axis=-1, keepdims=True)
        )
    )


def wy_form(keys, values, betas):
    width = keys.shape[-2]
    head_size = keys.shape[-1]
    gram = product("...id,...jd->...ij", keys, keys)
    strict = jnp.tril(jnp.ones((width, width), jnp.float32), -1)
    system = jnp.eye(width, dtype=jnp.float32) + betas[..., :, None] * gram * strict
    right_side = jnp.concatenate([betas[..., None] * keys, betas[..., None] * values], axis=-1)
    solved = lax.linalg.triangular_solve(
        system, right_side, left_side=True, lower=True, unit_diagonal=True
    )
    return (solved[..., :head_size], solved[..., head_size:])


def delta_maps(keys, wy_keys, wy_values):
    head_size = keys.shape[-1]
    identity = jnp.broadcast_to(
        jnp.eye(head_size, dtype=jnp.float32), keys.shape[:2] + (head_size, head_size)
    )

    def advance(carry, pieces):
        matrix, offset = carry
        key_block, wkey_block, wvalue_block = pieces
        step_map = identity - product("...cd,...ce->...de", key_block, wkey_block)
        new_matrix = product("...ij,...jk->...ik", step_map, matrix)
        new_offset = product("...ij,...jk->...ik", step_map, offset) + product(
            "...cd,...ce->...de", key_block, wvalue_block
        )
        return ((new_matrix, new_offset), None)

    moved = tuple((jnp.moveaxis(array, 2, 0) for array in (keys, wy_keys, wy_values)))
    result, _ = lax.scan(advance, (identity, jnp.zeros_like(identity)), moved)
    return result


def delta_rule(queries, keys, wy_keys, wy_values, start):
    width = queries.shape[-2]
    causal = jnp.tril(jnp.ones((width, width), jnp.float32))

    def advance(state, pieces):
        query_block, key_block, wkey_block, wvalue_block = pieces
        fresh = wvalue_block - product("...cd,...de->...ce", wkey_block, state)
        scores = product("...id,...jd->...ij", query_block, key_block) * causal
        output = product("...cd,...de->...ce", query_block, state) + product(
            "...ij,...je->...ie", scores, fresh
        )
        return (state + product("...cd,...ce->...de", key_block, fresh), output)

    moved = tuple((jnp.moveaxis(array, 2, 0) for array in (queries, keys, wy_keys, wy_values)))
    final, outputs = lax.scan(advance, start, moved)
    return (jnp.moveaxis(outputs, 0, 2), final)


def cut_columns(weight):
    depth, columns = weight.shape
    return weight.reshape(depth, MATES, columns // MATES).transpose(1, 0, 2)


def join_columns(blocks):
    return blocks.transpose(1, 0, 2).reshape(blocks.shape[1], -1)


def gather_weights(blocks):
    return gather_lines(swap_blocks(blocks))


def scatter_grads(blocks):
    return swap_blocks(scatter_lines(blocks.astype(low)).astype(low)).astype(wide)


def on_device(
    block_input,
    lengths,
    attn_gain,
    query_weight,
    key_weight,
    value_weight,
    outgate_weight,
    beta_weight,
    conv_kernel,
    head_gain,
    output_weight,
    mlp_gain,
    swish_weight,
    upward_weight,
    downward_weight,
    out_grad,
):
    count = lax.axis_size("seq")
    lines = count // MATES
    core = lax.axis_index("tp")
    seq_count, tokens, model_width = block_input.shape
    depth = attn_gain.shape[0]
    gain_part = head_gain.shape[0]
    head_size = gain_part * count
    heads = beta_weight.shape[1] // MATES
    width = heads * head_size
    units = swish_weight.shape[1] // MATES

    small = jnp.concatenate(
        [
            beta_weight.astype(low).reshape(depth, MATES, heads).transpose(1, 0, 2).reshape(MATES, -1),
            conv_kernel.astype(low).reshape(MATES, -1),
            jnp.broadcast_to(
                jnp.concatenate([attn_gain, mlp_gain, head_gain]).astype(low)[None],
                (MATES, 2 * depth + gain_part),
            ),
        ],
        axis=1,
    )
    small_size = small.shape[1]
    small = jnp.pad(small, ((0, 0), (0, SMALL * 3 * width - small_size))).reshape(
        MATES, SMALL, 3 * width
    )
    streams_cut = jnp.concatenate(
        [cut_columns(w.astype(low)) for w in (query_weight, key_weight, value_weight)], axis=2
    )
    first = gather_weights(jnp.concatenate([streams_cut, small], axis=1))
    streams_full = first[:, :, :depth].reshape(model_width, 3 * width)
    small = first[:, :, depth:].reshape(count, SMALL * 3 * width)[:, :small_size]
    gates_cut = jnp.concatenate(
        [cut_columns(w.astype(low)) for w in (outgate_weight, output_weight.T)], axis=2
    )
    gates_full = gather_weights(gates_cut).reshape(model_width, 2 * width)
    outgate_full, output_full = gates_full[:, :width], gates_full[:, width:]
    ups_cut = jnp.concatenate(
        [cut_columns(w.astype(low)) for w in (swish_weight, upward_weight)], axis=2
    )
    ups_full = gather_weights(ups_cut).reshape(model_width, 2 * units)
    downward_full = gather_weights(cut_columns(downward_weight.astype(low).T)).reshape(
        model_width, units
    )
    sizes = (depth * heads, heads * 3 * CONV * gain_part, depth, depth, gain_part)
    starts = [sum(sizes[:index]) for index in range(len(sizes) + 1)]
    beta_small, conv_small, attn_small, mlp_small, head_small = (
        small[:, starts[index] : starts[index + 1]] for index in range(len(sizes))
    )
    beta_full = beta_small.reshape(model_width, heads)
    taps = (
        conv_small.reshape(count, heads, 3, CONV, gain_part)
        .transpose(2, 3, 1, 0, 4)
        .reshape(3, CONV, width)
        .astype(wide)
    )
    attn_scale = attn_small.reshape(model_width).astype(wide)
    mlp_scale = mlp_small.reshape(model_width).astype(wide)
    head_scale = head_small.reshape(head_size).astype(wide)

    span = MATES * tokens
    rows = seq_count * span

    def ordered_rows(mine):
        gathered = in_order(gather_mates(mine)).reshape(span, model_width)
        return jnp.concatenate([gathered, other_core(gathered)], axis=0)

    def loose_rows(mine):
        gathered = jnp.concatenate(gather_mates(mine), axis=0)
        return jnp.concatenate([gathered, other_core(gathered)], axis=0)

    def sum_cores(partial):
        own = partial[:span]
        return (own.astype(wide) + other_core(partial[span:]).astype(wide)).astype(low)

    def sum_ordered(partial):
        blocks = sum_cores(partial).reshape(MATES, tokens, model_width)
        return scatter_mates([pick(blocks, mate_of() ^ flip) for flip in range(MATES)])

    def sum_loose(partial):
        blocks = sum_cores(partial).reshape(MATES, tokens, model_width)
        return scatter_mates([blocks[flip] for flip in range(MATES)])

    mine_low = pick(block_input, core)
    mine_input = mine_low.astype(wide)
    first_inverse = rms_scale(mine_input)
    grad_mine = pick(out_grad, core)
    grad_rows = loose_rows(grad_mine)
    input_rows = ordered_rows(mine_low).astype(wide)
    flat_normed = (input_rows * rms_scale(input_rows) * attn_scale).astype(low)

    lengths_here = jnp.stack([pick(lengths, core), pick(lengths, 1 - core)])
    positions = line_of() * span + jnp.arange(span, dtype=jnp.int32)
    validity = (positions[None, :] < lengths_here[:, None]).astype(wide)

    block_count = span // BLOCK

    def to_blocks(array):
        return array.reshape(seq_count, block_count, BLOCK, heads, head_size).transpose(
            0, 3, 1, 2, 4
        )

    def from_blocks(array):
        return array.transpose(0, 2, 3, 1, 4).reshape(seq_count, span, heads, head_size)

    raw_streams = (
        matmul("rd,dc->rc", flat_normed, streams_full).astype(low).reshape(seq_count, span, 3, width)
    ).transpose(2, 0, 1, 3)
    gate_values = matmul("rd,dc->rc", flat_normed, outgate_full).astype(low)
    beta_logits = matmul("rd,dh->rh", flat_normed, beta_full).reshape(seq_count, span, heads)
    tails = along(raw_streams[:, :, span - (CONV - 1) :], 1)
    extended = jnp.concatenate([tails, raw_streams], axis=2).astype(wide)
    pre_act = sum(
        (
            taps[:, offset][:, None, None, :] * extended[:, :, offset : offset + span]
            for offset in range(CONV)
        )
    )
    activated = jax.nn.silu(pre_act)
    query_raw = activated[0].reshape(seq_count, span, heads, head_size)
    key_raw = activated[1].reshape(seq_count, span, heads, head_size)
    query_inverse = lax.rsqrt(jnp.sum(query_raw * query_raw, axis=-1, keepdims=True) + epsilon)
    key_inverse = lax.rsqrt(jnp.sum(key_raw * key_raw, axis=-1, keepdims=True) + epsilon)
    queries = (query_raw * query_inverse * head_size ** (-0.5)).astype(low).astype(wide)
    keys = (key_raw * key_inverse).astype(low).astype(wide)
    values = activated[2].astype(low).astype(wide).reshape(seq_count, span, heads, head_size)
    beta_squash = jax.nn.sigmoid(beta_logits)
    beta_gate = beta_squash * validity[:, :, None]
    query_blocks = to_blocks(queries)
    key_blocks = to_blocks(keys)
    value_blocks = to_blocks(values)
    beta_blocks = beta_gate.reshape(seq_count, block_count, BLOCK, heads).transpose(0, 3, 1, 2)
    (wy_keys, wy_values), wy_back = jax.vjp(wy_form, key_blocks, value_blocks, beta_blocks)
    map_matrix, map_offset = delta_maps(key_blocks, wy_keys, wy_values)
    entering = hop_states(map_matrix, map_offset, 1)
    (mixed_blocks, leaving), rule_back = jax.vjp(
        delta_rule, query_blocks, key_blocks, wy_keys, wy_values, entering
    )
    mixed = from_blocks(mixed_blocks)
    mix_inverse = rms_scale(mixed)
    head_normed = mixed * mix_inverse * head_scale
    gate_wide = gate_values.astype(wide).reshape(seq_count, span, heads, head_size)
    silu_gate = jax.nn.silu(gate_wide)
    gated = (head_normed * silu_gate).astype(low).reshape(rows, width)
    attn_out = sum_ordered(matmul("rc,dc->rd", gated, output_full).astype(low))
    middle = mine_input + attn_out
    second_inverse = rms_scale(middle)
    mlp_normed = loose_rows((middle * second_inverse * mlp_scale).astype(low))
    acts = matmul("rd,df->rf", mlp_normed, ups_full)
    gate_act, up_act = acts[:, :units], acts[:, units:]
    silu_act = jax.nn.silu(gate_act)
    hidden = (silu_act * up_act).astype(low)
    mlp_out = sum_loose(matmul("rf,df->rd", hidden, downward_full).astype(low))
    output_mine = (middle + mlp_out).astype(low)

    hidden_grad = matmul("rd,df->rf", grad_rows, downward_full)
    downward_grad = matmul("rd,rf->df", grad_rows, hidden)
    acts_grad = jnp.concatenate(
        [
            (hidden_grad * up_act * silu_slope(gate_act)).astype(low),
            (hidden_grad * silu_act).astype(low),
        ],
        axis=1,
    )
    ups_grad = matmul("rd,rf->df", mlp_normed, acts_grad)
    normed_two_grad = sum_loose(matmul("rf,df->rd", acts_grad, ups_full).astype(low))
    middle_part, mlp_gain_grad = norm_back(normed_two_grad, middle, second_inverse, mlp_scale)
    middle_grad = grad_mine.astype(wide) + middle_part
    attn_grad_rows = ordered_rows(middle_grad.astype(low))
    output_grad = matmul("rd,rc->dc", attn_grad_rows, gated)
    gated_grad = matmul("rd,dc->rc", attn_grad_rows, output_full).reshape(
        seq_count, span, heads, head_size
    )
    outgate_act_grad = (
        (gated_grad * head_normed * silu_slope(gate_wide)).astype(low).reshape(rows, width)
    )
    mixed_flat_grad, head_gain_part = norm_back(
        (gated_grad * silu_gate).reshape(-1, head_size),
        mixed.reshape(-1, head_size),
        mix_inverse.reshape(-1, 1),
        head_scale,
    )
    mixed_grad = mixed_flat_grad.reshape(seq_count, span, heads, head_size)
    query_bgrad, key_bgrad, wkey_grad, wvalue_grad, local_state = rule_back(
        (to_blocks(mixed_grad), jnp.zeros_like(leaving))
    )
    leaving_grad = hop_states(jnp.swapaxes(map_matrix, -1, -2), local_state, -1)
    later_back = rule_back((jnp.zeros_like(mixed_blocks), leaving_grad))
    key_bgrad = key_bgrad + later_back[1]
    wkey_grad = wkey_grad + later_back[2]
    wvalue_grad = wvalue_grad + later_back[3]
    key_cgrad, value_bgrad, beta_bgrad = wy_back((wkey_grad, wvalue_grad))
    query_grad_unit = from_blocks(query_bgrad)
    key_grad_unit = from_blocks(key_bgrad + key_cgrad)
    value_grad_act = from_blocks(value_bgrad)
    beta_token_grad = beta_bgrad.transpose(0, 2, 3, 1).reshape(seq_count, span, heads)
    beta_logit_grad = (
        (beta_token_grad * validity[:, :, None] * beta_squash * (1.0 - beta_squash))
        .astype(low)
        .reshape(rows, heads)
    )
    act_grads = jnp.stack(
        [
            unit_back(query_grad_unit, query_raw, query_inverse, head_size ** (-0.5)).reshape(
                seq_count, span, width
            ),
            unit_back(key_grad_unit, key_raw, key_inverse, 1.0).reshape(seq_count, span, width),
            value_grad_act.reshape(seq_count, span, width),
        ]
    )
    pre_grad = act_grads * silu_slope(pre_act)
    padded_grad = jnp.pad(pre_grad, ((0, 0), (0, 0), (CONV - 1, CONV - 1), (0, 0)))
    reach = span + CONV - 1
    extended_grad = sum(
        (
            taps[:, offset][:, None, None, :]
            * padded_grad[:, :, CONV - 1 - offset : CONV - 1 - offset + reach]
            for offset in range(CONV)
        )
    )
    taps_grad = jnp.stack(
        [
            jnp.sum(pre_grad * extended[:, :, offset : offset + span], axis=(1, 2))
            for offset in range(CONV)
        ],
        axis=1,
    )
    returned = along(extended_grad[:, :, : CONV - 1].astype(low), -1).astype(wide)
    raw_grad = extended_grad[:, :, CONV - 1 :].at[:, :, span - (CONV - 1) :].add(returned)
    raw_grad_low = raw_grad.astype(low).transpose(1, 2, 0, 3).reshape(rows, 3 * width)
    streams_grad = matmul("rd,rc->dc", flat_normed, raw_grad_low)
    outgate_grad = matmul("rd,rc->dc", flat_normed, outgate_act_grad)
    beta_grad = matmul("rd,rh->dh", flat_normed, beta_logit_grad)
    normed_part = (
        matmul("rc,dc->rd", outgate_act_grad, outgate_full)
        + matmul("rh,dh->rd", beta_logit_grad, beta_full)
        + matmul("rc,dc->rd", raw_grad_low, streams_full)
    )
    normed_grad = sum_ordered(normed_part.astype(low))
    input_part, attn_gain_grad = norm_back(normed_grad, mine_input, first_inverse, attn_scale)
    input_grad_mine = (middle_grad + input_part).astype(low)

    def both_sequences(mine):
        other = other_core(mine)
        return jnp.stack([jnp.where(core == 0, mine, other), jnp.where(core == 0, other, mine)])

    def cut_rows(grad):
        return grad.reshape(lines, MATES, depth, grad.shape[1])

    downward_sum = join_columns(scatter_grads(cut_rows(downward_grad))).T
    ups_sum = scatter_grads(cut_rows(ups_grad))
    gates_sum = scatter_grads(cut_rows(jnp.concatenate([outgate_grad, output_grad], axis=1)))
    conv_grad = (
        taps_grad.reshape(3, CONV, heads, count, gain_part)
        .transpose(3, 2, 0, 1, 4)
        .reshape(count, -1)
    )
    small_grad = jnp.concatenate(
        [
            beta_grad.reshape(count, depth * heads),
            conv_grad,
            attn_gain_grad.reshape(count, depth),
            mlp_gain_grad.reshape(count, depth),
            head_gain_part.reshape(count, gain_part),
        ],
        axis=1,
    ).astype(low)
    small_grad = jnp.pad(small_grad, ((0, 0), (0, SMALL * 3 * width - small_size)))
    first_sum = scatter_grads(
        jnp.concatenate(
            [
                cut_rows(streams_grad.astype(low)),
                small_grad.reshape(lines, MATES, SMALL, 3 * width),
            ],
            axis=2,
        )
    )
    streams_sum = first_sum[:, :depth]
    small_sum = first_sum[:, depth:].reshape(MATES, SMALL * 3 * width)
    beta_sum, conv_sum, attn_sum, mlp_sum, head_sum = (
        small_sum[:, starts[index] : starts[index + 1]] for index in range(len(sizes))
    )
    gains_sum = jnp.sum(jnp.concatenate([attn_sum, mlp_sum, head_sum], axis=1), axis=0)
    gains_sum = gains_sum + other_core(gains_sum)
    return (
        both_sequences(output_mine),
        both_sequences(input_grad_mine),
        gains_sum[:depth],
        join_columns(streams_sum[:, :, :width]),
        join_columns(streams_sum[:, :, width : 2 * width]),
        join_columns(streams_sum[:, :, 2 * width :]),
        join_columns(gates_sum[:, :, :width]),
        join_columns(beta_sum.reshape(MATES, depth, heads)),
        conv_sum.reshape(MATES * heads, 3, CONV, gain_part),
        gains_sum[2 * depth :],
        join_columns(gates_sum[:, :, width:]).T,
        gains_sum[depth : 2 * depth],
        join_columns(ups_sum[:, :, :units]),
        join_columns(ups_sum[:, :, units:]),
        downward_sum,
    )


def solution(mesh):
    return jax.shard_map(
        on_device,
        mesh=mesh,
        in_specs=(
            P(None, "seq", None),
            P(),
            P("seq"),
            P("seq", "tp"),
            P("seq", "tp"),
            P("seq", "tp"),
            P("seq", "tp"),
            P("seq", "tp"),
            P("tp", None, None, "seq"),
            P("seq"),
            P("tp", "seq"),
            P("seq"),
            P("seq", "tp"),
            P("seq", "tp"),
            P("tp", "seq"),
            P(None, "seq", None),
        ),
        out_specs=(
            P(None, "seq", None),
            P(None, "seq", None),
            P("seq"),
            P("seq", "tp"),
            P("seq", "tp"),
            P("seq", "tp"),
            P("seq", "tp"),
            P("seq", "tp"),
            P("tp", None, None, "seq"),
            P("seq"),
            P("tp", "seq"),
            P("seq"),
            P("seq", "tp"),
            P("seq", "tp"),
            P("tp", "seq"),
        ),
        check_vma=False,
    )
```

time: 4560 us -> 2440 us (0.54)
  waiting for transfers between devices: 3150 us -> 294 us
  local copies, waits for them, and re-layouts: 135 us -> 467 us
  matrix products: 515 us -> 844 us
  blocking collectives: 280 us -> 0 us
  starting transfers between devices: 6.67 us -> 234 us
  other arithmetic: 432 us -> 579 us
    reduce_scatter x9 -> x0, waiting for transfers between devices: 2280 us -> none  [the longest x1 483 us: on_device(): lax.psum_scatter(upward_grad, 'seq', scatter_dimension=0, tiled=True)]
    all_gather x12 -> x0, waiting for transfers between devices: 854 us -> none  [the longest x1 171 us: on_device(): lax.all_gather(downward_low, 'seq', axis=1, tiled=True)]
    dot_general x126 -> x439, matrix products: 301 us -> 647 us  [product(): return jnp.einsum(form, left, right, precision=PRECISE)]
    ppermute x2 -> x123, waiting for transfers between devices: 4.78 us -> 294 us  [the longest x56 172 us: along(): return lax.ppermute(value, 'seq', pairs)]
    ppermute x2 -> x123, starting transfers between devices: 5.1 us -> 234 us  [the longest x56 171 us: along(): return lax.ppermute(value, 'seq', pairs)]
    all_gather x4 -> x0, blocking collectives: 159 us -> none  [the longest x1 42.3 us: on_device(): lax.all_gather(attn_low, 'seq', axis=0, tiled=True)]
    unnamed x2 -> x0, blocking collectives: 119 us -> none
    dynamic_update_slice x0 -> x41, local copies, waits for them, and re-layouts: none -> 105 us  [the longest x37 98.6 us: in_order(): out = lax.dynamic_update_index_in_dim(out, piece, mate ^ flip, 0)]
  transfers between devices with their start and end apart: 26 -> 123, of which waited for: 21 -> 41; matrix products, arithmetic and copies ran while one was open for 9% -> 67% of each run, Pallas kernels for 0% -> 0%
where the time goes in v1:
time: 2440 us; the launch traced here: 2430 us
  matrix products  844 us (35%)
  other arithmetic  579 us (24%)
  local copies, waits for them, and re-layouts  467 us (19%)
  waiting for transfers between devices  294 us (12%)
  starting transfers between devices  234 us (10%)
    dot_general x439, matrix products, product(): return jnp.einsum(form, left, right, precision=PRECISE)  647 us
    another operation x5, other arithmetic, wy_form(): lax.linalg.triangular_solve(system, right_side, left_side=True, lower=Tru...  329 us
    dot_general x18, matrix products, matmul(): return jnp.einsum(form, left, right, preferred_element_type=wide)  178 us
    ppermute x56, waiting for transfers between devices, along(): return lax.ppermute(value, 'seq', pairs)  172 us
    ppermute x56, starting transfers between devices, along(): return lax.ppermute(value, 'seq', pairs)  171 us
    ppermute x56, waiting for transfers between devices, to_mate(): lax.ppermute(value, 'seq', [(source, source ^ flip) for source in range(c...  122 us
    dynamic_update_slice x37, local copies, waits for them, and re-layouts, in_order(): out = lax.dynamic_update_index_in_dim(out, piece, mate ^ flip, 0)  98.6 us
    unnamed x338, local copies, waits for them, and re-layouts  73.8 us
  transfers between devices with their start and end apart: 123, of which 41 were waited for; matrix products, arithmetic and copies ran while one was open for 67% of the time, Pallas kernels for 0%

profile of v1, /device:TPU:0, one launch (start us, length us, event | category | flops | bytes accessed | tf_op | source)
XLA Modules:
  0.0 2426.3 jit_solution(1999793659413232287)
XLA Ops:
  98.0 21.1 collective-permute-done.21
  164.2 17.4 collective-permute-done.8
  191.6 8.0 fusion.133
  199.6 10.2 convolution_convert_fusion.4
  209.8 9.4 reshape.756
  271.6 326.4 %custom-call.7 = f32[2,2,16,1,64,64]{4,5,3,2,1,0:T(8,128)} custom-call(f32[2,2,16,1,64,64]{5,4,3,2,1,0:T(8,128)} %add_bitcast_fusion.2), custom_call_target="InvertDiagBlocksLowerTriangular" | custom-call | tf_op jit(solution)/shard_map/jvp()/triangular_solve | solution.py:186
  609.8 64.0 %while.79 = (s32[]{:T(128)}, f32[2,2,128,128]{3,2,1,0:T(8,128)S(1)}, f32[2,2,128,128]{3,2,1,0:T(8,128)S(1)}, f32[16,2,2,64,128]{4,3,2,1,0:T(8,128)}, f32[16,2,2,...) while((s32[]{:T(128)}, ...), condition=%wide.region_3.4_spmd.clone, body=%wide.region_2.3_spmd.clone.sunk | while | flops 302186496 | bytes 3475567 | solution.py:209
  712.4 135.9 %while.77 = (s32[]{:T(128)}, f32[2,2,128,128]{3,2,1,0:T(8,128)S(1)}, f32[16,2,2,64,128]{4,3,2,1,0:T(8,128)}, f32[16,2,2,128,128]{4,3,2,1,0:T(8,128)}, f32[16,2,2...) while((s32[]{:T(128)}, ...), condition=%wide.region_6.7_spmd.clone, body=%wide.region_5.6_spmd.clone.sunk | while | flops 201482240 | bytes 3771521 | solution.py:227
  857.1 8.3 multiply_convert_fusion.5
  907.3 10.2 dynamic_update_slice.283
  923.9 9.7 dynamic_update_slice.284
  933.6 9.7 dynamic_update_slice.285
  943.3 9.7 dynamic_update_slice.286
  969.7 22.8 collective-permute-done.39
  1018.2 16.5 collective-permute-done.64
  1047.5 16.6 maximum_maximum_fusion.1
  1075.2 12.5 collective-permute-done.42
  1095.9 15.4 maximum_maximum_fusion
  1128.9 8.7 collective-permute-done.54
  1152.9 13.7 collective-permute-done.45
  1182.7 17.4 fusion.251
  1200.1 15.4 multiply_convert_fusion.1
  1215.5 15.6 convolution_convert_fusion
  1235.0 9.0 convolution_convert_fusion.2
  1283.2 17.4 collective-permute-done.70
  1305.6 16.8 collective-permute-done.59
  1330.0 15.4 convolution_convert_fusion.1
  1373.4 10.6 convolution_convert_fusion.6
  1400.6 9.9 collective-permute-done.114
  1444.2 12.4 collective-permute-done.115
  1469.8 7.9 multiply_convert_fusion.3
  1494.8 259.1 %while.80 = (s32[]{:T(128)}, f32[2,2,128,128]{3,2,1,0:T(8,128)S(1)}, f32[16,2,2,64,128]{4,2,3,0,1:T(2,128)S(1)}, f32[16,2,2,64,128]{4,3,0,2,1:T(8,128)}, f32[16,...) while((s32[]{:T(128)}, ...), condition=%wide.region_13.14_spmd.clone, body=%wide.region_12.13_spmd.clone.sunk | while | flops 403169280 | bytes 5874370 | solution.py:227
  1792.2 208.8 %while.78 = (s32[]{:T(128)}, f32[2,2,128,128]{3,2,1,0:T(8,128)S(1)}, f32[16,2,2,64,128]{4,3,0,2,1:T(8,128)}, f32[16,2,2,64,128]{4,3,2,1,0:T(8,128)}, f32[16,2,2,...) while((s32[]{:T(128)}, ...), condition=%wide.region_15.16_spmd.clone, body=%wide.region_14.15_spmd.clone.sunk | while | flops 327442432 | bytes 4230309 | solution.py:227
  2051.5 9.9 fusion.157
  2061.4 7.8 multiply_reduce_fusion.3
  2076.3 8.2 fusion.252
  2086.7 16.3 collective-permute-done.79
  2113.8 10.3 fusion.253
  2124.1 15.4 add_convert_fusion
  2150.8 7.9 dynamic_update_slice.307
  2161.4 7.7 dynamic_update_slice.308
  2169.0 7.7 dynamic_update_slice.309
  2176.7 7.7 dynamic_update_slice.310
  2254.3 9.3 convolution_convert_fusion.5
  2271.2 11.8 collective-permute-start.96
  2302.2 10.6 collective-permute-done.86
  2330.6 11.2 collective-permute-done.87
  2395.7 7.9 collective-permute-done.91
  (1493 shorter events, 1575.5 us)
Async XLA Ops:
  6.5 60.5 %collective-permute-start.9 = (bf16[256,2048]{0,1:T(8,128)(2,1)S(1)}, bf16[256,2048]{0,1:T(8,128)(2,1)}, u32[]{:S(2)}, u32[]{:S(2)}) collective-permute-start(bf16[256,2048]{0,1:T(8,128)(2,1)S(1)} %bitcast.786), channel_id=1, source_target_pairs={{0,2},{2,0},{4,6},{6,4},{8,10},{10,8},{12,14},{14,12},{16,18},{18,... | collective-permute-start | bytes 3145736 | tf_op jit(solution)/shard_map/ppermute | solution.py:24
  9.5 54.1 %collective-permute-start.10 = (bf16[256,2048]{0,1:T(8,128)(2,1)S(1)}, bf16[256,2048]{0,1:T(8,128)(2,1)}, u32[]{:S(2)}, u32[]{:S(2)}) collective-permute-start(bf16[256,2048]{0,1:T(8,128)(2,1)S(1)} %bitcast.787), channel_id=1, source_target_pairs={{0,4},{2,6},{4,0},{6,2},{8,12},{10,14},{12,8},{14,10},{16,20},{18,... | collective-permute-start | bytes 3145736 | tf_op jit(solution)/shard_map/ppermute | solution.py:24
  22.1 36.9 %collective-permute-start = (bf16[136,768]{1,0:T(8,128)(2,1)}, bf16[136,768]{1,0:T(8,128)(2,1)}, u32[]{:S(2)}, u32[]{:S(2)}) collective-permute-start(bf16[136,768]{1,0:T(8,128)(2,1)} %bitcast.880), channel_id=1, source_target_pairs={{0,2},{2,0},{4,6},{6,4},{8,10},{10,8},{12,14},{14,12},{16,18},{18,... | collective-permute-start | bytes 626696 | tf_op jit(solution)/shard_map/ppermute | solution.py:24
  24.5 37.5 %collective-permute-start.1 = (bf16[136,768]{1,0:T(8,128)(2,1)}, bf16[136,768]{1,0:T(8,128)(2,1)}, u32[]{:S(2)}, u32[]{:S(2)}) collective-permute-start(bf16[136,768]{1,0:T(8,128)(2,1)} %bitcast.879), channel_id=1, source_target_pairs={{0,4},{2,6},{4,0},{6,2},{8,12},{10,14},{12,8},{14,10},{16,20},{18,... | collective-permute-start | bytes 626696 | tf_op jit(solution)/shard_map/ppermute | solution.py:24
  59.0 36.9 %collective-permute-start.22 = (bf16[4,128,512]{2,1,0:T(8,128)(2,1)}, bf16[4,128,512]{2,1,0:T(8,128)(2,1)}, u32[]{:S(2)}, u32[]{:S(2)}) collective-permute-start(bf16[4,128,512]{2,1,0:T(8,128)(2,1)} %bitcast_dynamic-update-slice_fusion.35), channel_id=1, source_target_pairs={{8,0},{10,2},{12,4},{14,6},{16,8},{18,10},{20,12},{22,14},{24,16},... | collective-permute-start | bytes 1572872 | tf_op jit(solution)/shard_map/ppermute | solution.py:35
  83.1 103.6 %collective-permute-start.13 = (bf16[1024,2048]{1,0:T(8,128)(2,1)}, bf16[1024,2048]{1,0:T(8,128)(2,1)}, u32[]{:S(2)}, u32[]{:S(2)}) collective-permute-start(bf16[1024,2048]{1,0:T(8,128)(2,1)} %bitcast.25), channel_id=1, source_target_pairs={{0,1},{1,0},{2,3},{3,2},{4,5},{5,4},{6,7},{7,6},{8,9},{9,8},{10,11... | collective-permute-start | bytes 12582920 | tf_op jit(solution)/shard_map/ppermute | solution.py:19
  84.5 39.7 %collective-permute-start.3 = (bf16[4,136,768]{2,1,0:T(8,128)(2,1)}, bf16[4,136,768]{2,1,0:T(8,128)(2,1)}, u32[]{:S(2)}, u32[]{:S(2)}) collective-permute-start(bf16[4,136,768]{2,1,0:T(8,128)(2,1)} %bitcast_dynamic-update-slice_fusion.29), channel_id=1, source_target_pairs={{0,8},{2,10},{4,12},{6,14},{8,16},{10,18},{12,20},{14,22},{16,24},... | collective-permute-start | bytes 2506760 | tf_op jit(solution)/shard_map/ppermute | solution.py:35
  89.9 40.3 %collective-permute-start.5 = (bf16[4,136,768]{2,1,0:T(8,128)(2,1)}, bf16[4,136,768]{2,1,0:T(8,128)(2,1)}, u32[]{:S(2)}, u32[]{:S(2)}) collective-permute-start(bf16[4,136,768]{2,1,0:T(8,128)(2,1)} %collective-permute-done.4), channel_id=1, source_target_pairs={{8,0},{10,2},{12,4},{14,6},{16,8},{18,10},{20,12},{22,14},{24,16},... | collective-permute-start | bytes 2506760 | tf_op jit(solution)/shard_map/ppermute | solution.py:35
  135.7 542.2 %collective-permute-start.26 = (bf16[4,128,512]{2,1,0:T(8,128)(2,1)}, bf16[4,128,512]{2,1,0:T(8,128)(2,1)}, u32[]{:S(2)}, u32[]{:S(2)}) collective-permute-start(bf16[4,128,512]{2,1,0:T(8,128)(2,1)} %collective-permute-done.25), channel_id=1, source_target_pairs={{0,8},{2,10},{4,12},{6,14},{8,16},{10,18},{12,20},{14,22},{16,24},... | collective-permute-start | bytes 1572872 | tf_op jit(solution)/shard_map/ppermute | solution.py:35
  874.8 42.7 %collective-permute-start.46 = (bf16[128,704]{0,1:T(8,128)(2,1)}, bf16[128,704]{0,1:T(8,128)(2,1)}, u32[]{:S(2)}, u32[]{:S(2)}) collective-permute-start(bf16[128,704]{0,1:T(8,128)(2,1)} %get-tuple-element.1308), channel_id=1, source_target_pairs={{0,2},{2,0},{4,6},{6,4},{8,10},{10,8},{12,14},{14,12},{16,18},{18,... | collective-permute-start | bytes 540680 | tf_op jit(solution)/shard_map/ppermute | solution.py:24
  875.3 44.9 %collective-permute-start.47 = (bf16[128,704]{0,1:T(8,128)(2,1)}, bf16[128,704]{0,1:T(8,128)(2,1)}, u32[]{:S(2)}, u32[]{:S(2)}) collective-permute-start(bf16[128,704]{0,1:T(8,128)(2,1)} %get-tuple-element.1307), channel_id=1, source_target_pairs={{0,4},{2,6},{4,0},{6,2},{8,12},{10,14},{12,8},{14,10},{16,20},{18,... | collective-permute-start | bytes 540680 | tf_op jit(solution)/shard_map/ppermute | solution.py:24
  876.9 45.2 %collective-permute-start.48 = (bf16[128,704]{0,1:T(8,128)(2,1)}, bf16[128,704]{0,1:T(8,128)(2,1)}, u32[]{:S(2)}, u32[]{:S(2)}) collective-permute-start(bf16[128,704]{0,1:T(8,128)(2,1)} %get-tuple-element.1306), channel_id=1, source_target_pairs={{0,6},{2,4},{4,2},{6,0},{8,14},{10,12},{12,10},{14,8},{16,22},{18,... | collective-permute-start | bytes 540680 | tf_op jit(solution)/shard_map/ppermute | solution.py:24
  893.7 61.3 %collective-permute-start.30 = (bf16[256,1024]{0,1:T(8,128)(2,1)}, bf16[256,1024]{0,1:T(8,128)(2,1)}, u32[]{:S(2)}, u32[]{:S(2)}) collective-permute-start(bf16[256,1024]{0,1:T(8,128)(2,1)} %get-tuple-element.1295), channel_id=1, source_target_pairs={{0,2},{2,0},{4,6},{6,4},{8,10},{10,8},{12,14},{14,12},{16,18},{18,... | collective-permute-start | bytes 1572872 | tf_op jit(solution)/shard_map/ppermute | solution.py:24
  898.3 59.6 %collective-permute-start.28 = (bf16[256,1024]{0,1:T(8,128)(2,1)}, bf16[256,1024]{0,1:T(8,128)(2,1)}, u32[]{:S(2)}, u32[]{:S(2)}) collective-permute-start(bf16[256,1024]{0,1:T(8,128)(2,1)} %get-tuple-element.1294), channel_id=1, source_target_pairs={{0,4},{2,6},{4,0},{6,2},{8,12},{10,14},{12,8},{14,10},{16,20},{18,... | collective-permute-start | bytes 1572872 | tf_op jit(solution)/shard_map/ppermute | solution.py:24
  917.5 85.7 %collective-permute-start.61 = (bf16[256,2048]{0,1:T(8,128)(2,1)}, bf16[256,2048]{0,1:T(8,128)(2,1)}, u32[]{:S(2)}, u32[]{:S(2)}) collective-permute-start(bf16[256,2048]{0,1:T(8,128)(2,1)} %bitcast.102), channel_id=1, source_target_pairs={{0,2},{2,0},{4,6},{6,4},{8,10},{10,8},{12,14},{14,12},{16,18},{18,... | collective-permute-start | bytes 3145736 | tf_op jit(solution)/shard_map/ppermute | solution.py:24
  920.3 84.6 %collective-permute-start.62 = (bf16[256,2048]{0,1:T(8,128)(2,1)}, bf16[256,2048]{0,1:T(8,128)(2,1)}, u32[]{:S(2)}, u32[]{:S(2)}) collective-permute-start(bf16[256,2048]{0,1:T(8,128)(2,1)} %bitcast.102), channel_id=1, source_target_pairs={{0,4},{2,6},{4,0},{6,2},{8,12},{10,14},{12,8},{14,10},{16,20},{18,... | collective-permute-start | bytes 3145736 | tf_op jit(solution)/shard_map/ppermute | solution.py:24
  922.0 38.7 %collective-permute-start.37 = (bf16[128,1408]{1,0:T(8,128)(2,1)}, bf16[128,1408]{1,0:T(8,128)(2,1)}, u32[]{:S(2)}, u32[]{:S(2)}) collective-permute-start(bf16[128,1408]{1,0:T(8,128)(2,1)} %bitcast.72), channel_id=1, source_target_pairs={{0,2},{2,0},{4,6},{6,4},{8,10},{10,8},{12,14},{14,12},{16,18},{18,... | collective-permute-start | bytes 1081352 | tf_op jit(solution)/shard_map/ppermute | solution.py:24
  957.9 37.9 %collective-permute-start.31 = (bf16[256,2048]{0,1:T(8,128)(2,1)S(1)}, bf16[256,2048]{0,1:T(8,128)(2,1)}, u32[]{:S(2)}, u32[]{:S(2)}) collective-permute-start(bf16[256,2048]{0,1:T(8,128)(2,1)S(1)} %pad_maximum_fusion.14), channel_id=1, source_target_pairs={{0,4},{2,6},{4,0},{6,2},{8,12},{10,14},{12,8},{14,10},{16,20},{18,... | collective-permute-start | bytes 3145736 | tf_op jit(solution)/shard_map/ppermute | solution.py:24
  995.8 44.4 %collective-permute-start.41 = (bf16[4,128,1408]{2,1,0:T(8,128)(2,1)}, bf16[4,128,1408]{2,1,0:T(8,128)(2,1)S(1)}, u32[]{:S(2)}, u32[]{:S(2)}) collective-permute-start(bf16[4,128,1408]{2,1,0:T(8,128)(2,1)} %bitcast_dynamic-update-slice_fusion.23), channel_id=1, source_target_pairs={{8,0},{10,2},{12,4},{14,6},{16,8},{18,10},{20,12},{22,14},{24,16},... | collective-permute-start | bytes 4325384 | tf_op jit(solution)/shard_map/ppermute | solution.py:35
  1001.7 39.8 %collective-permute-start.32 = (bf16[256,2048]{0,1:T(8,128)(2,1)S(1)}, bf16[256,2048]{0,1:T(8,128)(2,1)S(1)}, u32[]{:S(2)}, u32[]{:S(2)}) collective-permute-start(bf16[256,2048]{0,1:T(8,128)(2,1)S(1)} %get-tuple-element.1212), channel_id=1, source_target_pairs={{0,2},{2,0},{4,6},{6,4},{8,10},{10,8},{12,14},{14,12},{16,18},{18,... | collective-permute-start | bytes 3145736 | tf_op jit(solution)/shard_map/ppermute | solution.py:24
  1013.8 54.8 %collective-permute-start.40 = (bf16[4,128,1408]{2,1,0:T(8,128)(2,1)}, bf16[4,128,1408]{2,1,0:T(8,128)(2,1)S(1)}, u32[]{:S(2)}, u32[]{:S(2)}) collective-permute-start(bf16[4,128,1408]{2,1,0:T(8,128)(2,1)} %bitcast_dynamic-update-slice_fusion.23), channel_id=1, source_target_pairs={{0,8},{2,10},{4,12},{6,14},{8,16},{10,18},{12,20},{14,22},{16,24},... | collective-permute-start | bytes 4325384 | tf_op jit(solution)/shard_map/ppermute | solution.py:35
  1016.4 47.8 %collective-permute-start.33 = (bf16[256,2048]{0,1:T(8,128)(2,1)S(1)}, bf16[256,2048]{0,1:T(8,128)(2,1)S(1)}, u32[]{:S(2)}, u32[]{:S(2)}) collective-permute-start(bf16[256,2048]{0,1:T(8,128)(2,1)S(1)} %get-tuple-element.1212), channel_id=1, source_target_pairs={{0,4},{2,6},{4,0},{6,2},{8,12},{10,14},{12,8},{14,10},{16,20},{18,... | collective-permute-start | bytes 3145736 | tf_op jit(solution)/shard_map/ppermute | solution.py:24
  1041.5 46.1 %collective-permute-start.42 = (bf16[4,128,1408]{2,1,0:T(8,128)(2,1)S(1)}, bf16[4,128,1408]{2,1,0:T(8,128)(2,1)}, u32[]{:S(2)}, u32[]{:S(2)}) collective-permute-start(bf16[4,128,1408]{2,1,0:T(8,128)(2,1)S(1)} %collective-permute-done.41), channel_id=1, source_target_pairs={{8,0},{10,2},{12,4},{14,6},{16,8},{18,10},{20,12},{22,14},{24,16},... | collective-permute-start | bytes 4325384 | tf_op jit(solution)/shard_map/ppermute | solution.py:35
  1064.1 105.2 %collective-permute-start.65 = (bf16[1024,2048]{0,1:T(8,128)(2,1)}, bf16[1024,2048]{0,1:T(8,128)(2,1)}, u32[]{:S(2)}, u32[]{:S(2)}) collective-permute-start(bf16[1024,2048]{0,1:T(8,128)(2,1)} %maximum_maximum_fusion.1), channel_id=1, source_target_pairs={{0,1},{1,0},{2,3},{3,2},{4,5},{5,4},{6,7},{7,6},{8,9},{9,8},{10,11... | collective-permute-start | bytes 12582920 | tf_op jit(solution)/shard_map/ppermute | solution.py:19
  1068.5 42.8 %collective-permute-start.53 = (bf16[4,128,704]{1,0,2:T(4,128)(2,1)S(1)}, bf16[4,128,704]{1,0,2:T(4,128)(2,1)S(1)}, u32[]{:S(2)}, u32[]{:S(2)}) collective-permute-start(bf16[4,128,704]{1,0,2:T(4,128)(2,1)S(1)} %collective-permute-done.49), channel_id=1, source_target_pairs={{0,8},{2,10},{4,12},{6,14},{8,16},{10,18},{12,20},{14,22},{16,24},... | collective-permute-start | bytes 2162696 | tf_op jit(solution)/shard_map/ppermute | solution.py:35
  1094.6 51.6 %collective-permute-start.43 = (bf16[4,128,1408]{2,1,0:T(8,128)(2,1)}, bf16[4,128,1408]{2,1,0:T(8,128)(2,1)}, u32[]{:S(2)}, u32[]{:S(2)}) collective-permute-start(bf16[4,128,1408]{2,1,0:T(8,128)(2,1)} %collective-permute-done.42), channel_id=1, source_target_pairs={{8,0},{10,2},{12,4},{14,6},{16,8},{18,10},{20,12},{22,14},{24,16},... | collective-permute-start | bytes 4325384 | tf_op jit(solution)/shard_map/ppermute | solution.py:35
  1111.4 65.1 %collective-permute-start.36 = (bf16[1024,2048]{0,1:T(8,128)(2,1)}, bf16[1024,2048]{0,1:T(8,128)(2,1)}, u32[]{:S(2)}, u32[]{:S(2)}) collective-permute-start(bf16[1024,2048]{0,1:T(8,128)(2,1)} %maximum_maximum_fusion), channel_id=1, source_target_pairs={{0,1},{1,0},{2,3},{3,2},{4,5},{5,4},{6,7},{7,6},{8,9},{9,8},{10,11... | collective-permute-start | bytes 12582920 | tf_op jit(solution)/shard_map/ppermute | solution.py:19
  1122.2 44.4 %collective-permute-start.45 = (bf16[4,128,1408]{2,1,0:T(8,128)(2,1)}, bf16[4,128,1408]{2,1,0:T(8,128)(2,1)}, u32[]{:S(2)}, u32[]{:S(2)}) collective-permute-start(bf16[4,128,1408]{2,1,0:T(8,128)(2,1)} %collective-permute-done.44), channel_id=1, source_target_pairs={{0,8},{2,10},{4,12},{6,14},{8,16},{10,18},{12,20},{14,22},{16,24},... | collective-permute-start | bytes 4325384 | tf_op jit(solution)/shard_map/ppermute | solution.py:35
  1281.1 41.3 %collective-permute-start.59 = (bf16[256,2048]{0,1:T(8,128)(2,1)}, bf16[256,2048]{0,1:T(8,128)(2,1)}, u32[]{:S(2)}, u32[]{:S(2)}) collective-permute-start(bf16[256,2048]{0,1:T(8,128)(2,1)} %pad_maximum_fusion.16), channel_id=1, source_target_pairs={{0,4},{2,6},{4,0},{6,2},{8,12},{10,14},{12,8},{14,10},{16,20},{18,... | collective-permute-start | bytes 3145736 | tf_op jit(solution)/shard_map/ppermute | solution.py:24
  1282.6 41.0 %collective-permute-start.57 = (bf16[256,2048]{0,1:T(8,128)(2,1)}, bf16[256,2048]{0,1:T(8,128)(2,1)}, u32[]{:S(2)}, u32[]{:S(2)}) collective-permute-start(bf16[256,2048]{0,1:T(8,128)(2,1)} %pad_maximum_fusion.15), channel_id=1, source_target_pairs={{0,2},{2,0},{4,6},{6,4},{8,10},{10,8},{12,14},{14,12},{16,18},{18,... | collective-permute-start | bytes 3145736 | tf_op jit(solution)/shard_map/ppermute | solution.py:24
  1349.1 45.9 %collective-permute-start.105 = (bf16[4,128,1408]{2,1,0:T(8,128)(2,1)}, bf16[4,128,1408]{2,1,0:T(8,128)(2,1)}, u32[]{:S(2)}, u32[]{:S(2)}) collective-permute-start(bf16[4,128,1408]{2,1,0:T(8,128)(2,1)} %dynamic-slice_bitcast_fusion), channel_id=1, source_target_pairs={{0,8},{2,10},{4,12},{6,14},{1,9},{3,11},{5,13},{7,15}} | collective-permute-start | bytes 4325384 | tf_op jit(solution)/shard_map/ppermute | solution.py:35
  1373.4 96.4 %collective-permute-start.75 = (bf16[1024,2048]{1,0:T(8,128)(2,1)}, bf16[1024,2048]{1,0:T(8,128)(2,1)}, u32[]{:S(2)}, u32[]{:S(2)}) collective-permute-start(bf16[1024,2048]{1,0:T(8,128)(2,1)} %bitcast.830), channel_id=1, source_target_pairs={{0,1},{1,0},{2,3},{3,2},{4,5},{5,4},{6,7},{7,6},{8,9},{9,8},{10,11... | collective-permute-start | bytes 12582920 | tf_op jit(solution)/shard_map/ppermute | solution.py:19
  1398.2 66.0 %collective-permute-start.106 = (bf16[4,128,1408]{2,1,0:T(8,128)(2,1)}, bf16[4,128,1408]{2,1,0:T(8,128)(2,1)}, u32[]{:S(2)}, u32[]{:S(2)}) collective-permute-start(bf16[4,128,1408]{2,1,0:T(8,128)(2,1)} %fusion.146), channel_id=1, source_target_pairs={{0,8},{2,10},{4,12},{6,14},{8,16},{10,18},{12,20},{14,22},{1,9},{3... | collective-permute-start | bytes 4325384 | tf_op jit(solution)/shard_map/ppermute | solution.py:35
  1413.5 43.1 %collective-permute-start.115 = (bf16[4,128,704]{1,2,0:T(8,128)(2,1)}, bf16[4,128,704]{1,2,0:T(8,128)(2,1)}, u32[]{:S(2)}, u32[]{:S(2)}) collective-permute-start(bf16[4,128,704]{1,2,0:T(8,128)(2,1)} %get-tuple-element.1304), channel_id=1, source_target_pairs={{0,8},{2,10},{4,12},{6,14},{8,16},{10,18},{12,20},{14,22},{1,9},{3... | collective-permute-start | bytes 2162696 | tf_op jit(solution)/shard_map/ppermute | solution.py:35
  1442.9 312.2 %collective-permute-start.119 = (bf16[4,128,704]{1,2,0:T(8,128)(2,1)}, bf16[4,128,704]{1,2,0:T(8,128)(2,1)}, u32[]{:S(2)}, u32[]{:S(2)}) collective-permute-start(bf16[4,128,704]{1,2,0:T(8,128)(2,1)} %add_convert_fusion.10), channel_id=1, source_target_pairs={{8,0},{10,2},{12,4},{14,6},{16,8},{18,10},{20,12},{22,14},{24,16},... | collective-permute-start | bytes 2162696 | tf_op jit(solution)/shard_map/ppermute | solution.py:35
  1458.9 296.3 %collective-permute-start.116 = (bf16[4,128,704]{1,2,0:T(8,128)(2,1)}, bf16[4,128,704]{1,2,0:T(8,128)(2,1)}, u32[]{:S(2)}, u32[]{:S(2)}) collective-permute-start(bf16[4,128,704]{1,2,0:T(8,128)(2,1)} %add_convert_fusion.11), channel_id=1, source_target_pairs={{0,8},{2,10},{4,12},{6,14},{8,16},{10,18},{12,20},{14,22},{16,24},... | collective-permute-start | bytes 2162696 | tf_op jit(solution)/shard_map/ppermute | solution.py:35
  1468.0 298.8 %collective-permute-start.108 = (bf16[4,128,1408]{2,1,0:T(8,128)(2,1)}, bf16[4,128,1408]{2,1,0:T(8,128)(2,1)}, u32[]{:S(2)}, u32[]{:S(2)}) collective-permute-start(bf16[4,128,1408]{2,1,0:T(8,128)(2,1)} %get-tuple-element.1203), channel_id=1, source_target_pairs={{24,16},{26,18},{28,20},{30,22},{25,17},{27,19},{29,21},{31,23}} | collective-permute-start | bytes 4325384 | tf_op jit(solution)/shard_map/ppermute | solution.py:35
  1757.7 389.2 %collective-permute-start.120 = (bf16[128,704]{0,1:T(8,128)(2,1)}, bf16[128,704]{0,1:T(8,128)(2,1)}, u32[]{:S(2)}, u32[]{:S(2)}) collective-permute-start(bf16[128,704]{0,1:T(8,128)(2,1)} %get-tuple-element.1302), channel_id=1, source_target_pairs={{0,2},{2,0},{4,6},{6,4},{8,10},{10,8},{12,14},{14,12},{16,18},{18,... | collective-permute-start | bytes 540680 | tf_op jit(solution)/shard_map/ppermute | solution.py:24
  1758.2 390.1 %collective-permute-start.121 = (bf16[128,704]{0,1:T(8,128)(2,1)}, bf16[128,704]{0,1:T(8,128)(2,1)}, u32[]{:S(2)}, u32[]{:S(2)}) collective-permute-start(bf16[128,704]{0,1:T(8,128)(2,1)} %get-tuple-element.1301), channel_id=1, source_target_pairs={{0,4},{2,6},{4,0},{6,2},{8,12},{10,14},{12,8},{14,10},{16,20},{18,... | collective-permute-start | bytes 540680 | tf_op jit(solution)/shard_map/ppermute | solution.py:24
  1759.1 430.8 %collective-permute-start.107 = (bf16[4,128,1408]{2,1,0:T(8,128)(2,1)}, bf16[4,128,1408]{2,1,0:T(8,128)(2,1)}, u32[]{:S(2)}, u32[]{:S(2)}) collective-permute-start(bf16[4,128,1408]{2,1,0:T(8,128)(2,1)} %get-tuple-element.1202), channel_id=1, source_target_pairs={{0,8},{2,10},{4,12},{6,14},{8,16},{10,18},{12,20},{14,22},{16,24},... | collective-permute-start | bytes 4325384 | tf_op jit(solution)/shard_map/ppermute | solution.py:35
  1770.0 374.2 %collective-permute-start.109 = (bf16[4,128,1408]{2,1,0:T(8,128)(2,1)}, bf16[4,128,1408]{2,1,0:T(8,128)(2,1)}, u32[]{:S(2)}, u32[]{:S(2)}) collective-permute-start(bf16[4,128,1408]{2,1,0:T(8,128)(2,1)} %fusion.147), channel_id=1, source_target_pairs={{16,8},{18,10},{20,12},{22,14},{24,16},{26,18},{28,20},{30,22},{17... | collective-permute-start | bytes 4325384 | tf_op jit(solution)/shard_map/ppermute | solution.py:35
  2103.0 82.7 %collective-permute-start.60 = (bf16[256,2048]{0,1:T(8,128)(2,1)}, bf16[256,2048]{0,1:T(8,128)(2,1)}, u32[]{:S(2)}, u32[]{:S(2)}) collective-permute-start(bf16[256,2048]{0,1:T(8,128)(2,1)} %get-tuple-element.1271), channel_id=1, source_target_pairs={{0,1},{1,0},{2,3},{3,2},{4,5},{5,4},{6,7},{7,6},{8,9},{9,8},{10,11... | collective-permute-start | bytes 3145736 | tf_op jit(solution)/shard_map/ppermute | solution.py:19
  2144.2 75.6 %collective-permute-start.80 = (bf16[1024,2048]{1,0:T(8,128)(2,1)}, bf16[1024,2048]{1,0:T(8,128)(2,1)}, u32[]{:S(2)}, u32[]{:S(2)}) collective-permute-start(bf16[1024,2048]{1,0:T(8,128)(2,1)} %slice.503), channel_id=1, source_target_pairs={{0,1},{1,0},{2,3},{3,2},{4,5},{5,4},{6,7},{7,6},{8,9},{9,8},{10,11... | collective-permute-start | bytes 12582920 | tf_op jit(solution)/shard_map/ppermute | solution.py:19
  2147.0 43.0 %collective-permute-start.110 = (bf16[4,128,1408]{2,1,0:T(8,128)(2,1)S(1)}, bf16[4,128,1408]{2,1,0:T(8,128)(2,1)}, u32[]{:S(2)}, u32[]{:S(2)}) collective-permute-start(bf16[4,128,1408]{2,1,0:T(8,128)(2,1)S(1)} %add_convert_fusion.5), channel_id=1, source_target_pairs={{8,0},{10,2},{12,4},{14,6},{16,8},{18,10},{20,12},{22,14},{24,16},... | collective-permute-start | bytes 4325384 | tf_op jit(solution)/shard_map/ppermute | solution.py:35
  2195.1 94.0 %collective-permute-start.111 = (bf16[128,1408]{1,0:T(8,128)(2,1)}, bf16[128,1408]{1,0:T(8,128)(2,1)}, u32[]{:S(2)}, u32[]{:S(2)}) collective-permute-start(bf16[128,1408]{1,0:T(8,128)(2,1)} %get-tuple-element.1283), channel_id=1, source_target_pairs={{0,2},{2,0},{4,6},{6,4},{8,10},{10,8},{12,14},{14,12},{16,18},{18,... | collective-permute-start | bytes 1081352 | tf_op jit(solution)/shard_map/ppermute | solution.py:24
  2196.3 97.6 %collective-permute-start.112 = (bf16[128,1408]{1,0:T(8,128)(2,1)}, bf16[128,1408]{1,0:T(8,128)(2,1)}, u32[]{:S(2)}, u32[]{:S(2)}) collective-permute-start(bf16[128,1408]{1,0:T(8,128)(2,1)} %get-tuple-element.1282), channel_id=1, source_target_pairs={{0,4},{2,6},{4,0},{6,2},{8,12},{10,14},{12,8},{14,10},{16,20},{18,... | collective-permute-start | bytes 1081352 | tf_op jit(solution)/shard_map/ppermute | solution.py:24
  2197.4 121.2 %collective-permute-start.113 = (bf16[128,1408]{1,0:T(8,128)(2,1)}, bf16[128,1408]{1,0:T(8,128)(2,1)}, u32[]{:S(2)}, u32[]{:S(2)}) collective-permute-start(bf16[128,1408]{1,0:T(8,128)(2,1)} %get-tuple-element.1281), channel_id=1, source_target_pairs={{0,6},{2,4},{4,2},{6,0},{8,14},{10,12},{12,10},{14,8},{16,22},{18,... | collective-permute-start | bytes 1081352 | tf_op jit(solution)/shard_map/ppermute | solution.py:24
  2322.9 38.0 %collective-permute-start.101 = (bf16[4,128,512]{2,1,0:T(8,128)(2,1)}, bf16[4,128,512]{2,1,0:T(8,128)(2,1)}, u32[]{:S(2)}, u32[]{:S(2)}) collective-permute-start(bf16[4,128,512]{2,1,0:T(8,128)(2,1)} %add_convert_fusion.12), channel_id=1, source_target_pairs={{8,0},{10,2},{12,4},{14,6},{16,8},{18,10},{20,12},{22,14},{24,16},... | collective-permute-start | bytes 1572872 | tf_op jit(solution)/shard_map/ppermute | solution.py:35
  (224 other events, 4789.0 us)

commit v2 on v1

--- a/solution.py
+++ b/solution.py
@@ -1,9 +1,10 @@
 import jax
 import jax.numpy as jnp
 from jax import lax
+from jax.experimental import pallas as pl
+from jax.experimental.pallas import tpu as pltpu
 from jax.sharding import PartitionSpec as P
 
-BLOCK = 64
 CONV = 4
 MATES = 4
 SMALL = 8
@@ -139,6 +140,14 @@
     return state
 
 
+def hop_states_back(matrix, offset):
+    lines = lax.axis_size("seq") // MATES
+    state = along(offset, -1)
+    for _ in range(lines - 2):
+        state = along(product("...ij,...jk->...ik", state, matrix) + offset, -1)
+    return state
+
+
 def product(form, left, right):
     return jnp.einsum(form, left, right, precision=PRECISE)
 
@@ -165,67 +174,575 @@
     return (source_grad, gain_grad)
 
 
-def unit_back(grad_unit, source, inverse, factor):
-    return (
-        factor
-        * inverse
-        * (
-            grad_unit
-            - source * inverse * inverse * jnp.sum(grad_unit * source, axis=-1, keepdims=True)
+CHUNK = 128
+TOGETHER = 4
+VMEM_BYTES = 52 * 1024 * 1024
+NN = (((1,), (0,)), ((), ()))
+NT = (((1,), (1,)), ((), ()))
+
+
+def dot(left, right, dims):
+    return lax.dot_general(left, right, dims, preferred_element_type=wide)
+
+
+def pair(value):
+    high = value.astype(low)
+    return high, (value - high.astype(wide)).astype(low)
+
+
+def side(left, right):
+    return jnp.concatenate([left, right], axis=1)
+
+
+def over(top, bottom):
+    return jnp.concatenate([top, bottom], axis=0)
+
+
+def nn(left, right):
+    width = right[0].shape[1]
+    both = side(*right)
+    out = dot(side(*left), over(both, both), NN)
+    return out[:, :width] + out[:, width:]
+
+
+def nt(left, right):
+    width = right[0].shape[0]
+    out = dot(side(*left), over(side(right[0], right[0]), side(right[1], right[1])), NT)
+    return out[:, :width] + out[:, width:]
+
+
+def nn_wide(left, right):
+    return dot(side(*left), over(right[0], right[0]), NN) + dot(left[0], right[1], NN)
+
+
+def nn_low(left, right):
+    return dot(side(*left), over(right, right), NN)
+
+
+def low_nn(left, right):
+    return dot(side(left, left), over(*right), NN)
+
+
+def low_nt(left, right):
+    return dot(side(left, left), side(*right), NT)
+
+
+def grid_of_rows():
+    rows = lax.broadcasted_iota(jnp.int32, (CHUNK, CHUNK), 0)
+    columns = lax.broadcasted_iota(jnp.int32, (CHUNK, CHUNK), 1)
+    return rows, columns
+
+
+def inverse_of(strict):
+    rows, columns = grid_of_rows()
+    one = jnp.where(rows == columns, 1.0, 0.0).astype(wide)
+
+    def joining(shift):
+        upper = columns >> shift
+        return ((rows >> shift) == upper + 1) & ((upper & 1) == 0)
+
+    solved = [one - jnp.where(joining(0), s, 0.0) for s in strict]
+    shift = 1
+    while (1 << shift) < CHUNK:
+        mask = joining(shift)
+        pairs = [pair(d) for d in solved]
+        crossed = [nn(pair(jnp.where(mask, s, 0.0)), p) for s, p in zip(strict, pairs)]
+        solved = [d - nn(p, pair(c)) for d, p, c in zip(solved, pairs, crossed)]
+        shift += 1
+    return solved
+
+
+def convolved(block, taps, stream):
+    columns = block[:, stream * CHUNK : (stream + 1) * CHUNK]
+    total = None
+    for offset in range(CONV):
+        first = 16 - (CONV - 1) + offset
+        term = taps[stream * CONV + offset][None, :] * columns[first : first + CHUNK]
+        total = term if total is None else total + term
+    return total
+
+
+def silu_parts(value):
+    squash = jax.nn.sigmoid(value)
+    return value * squash, squash * (1.0 + value * (1.0 - squash))
+
+
+def live_rows(limit, start):
+    rows = lax.broadcasted_iota(jnp.int32, (CHUNK, CHUNK), 0)
+    return jnp.where(rows + start < limit, 1.0, 0.0).astype(wide)
+
+
+def write_extended(ext, tail_ref, raw_ref):
+    ext[:16] = tail_ref[0].astype(wide)
+    ext[16:] = raw_ref[...].astype(wide)
+
+
+def prepare_kernel(
+    limit_ref, raw_ref, tail_ref, taps_ref, logit_ref,
+    qkv_ref, solved_ref, wu_ref, map_ref, prefix_ref, local_ref, ends_ref,
+    ext, offsets, maps,
+):
+    seq, head = pl.program_id(0), pl.program_id(1)
+    heads = pl.num_programs(1)
+    chain = seq * heads + head
+    chains, chunks = prefix_ref.shape[0], prefix_ref.shape[1]
+    write_extended(ext, tail_ref, raw_ref)
+    taps = taps_ref[0]
+    limit = limit_ref[seq]
+    rows, columns = grid_of_rows()
+    identity = jnp.where(rows == columns, 1.0, 0.0).astype(wide)
+    head_size = CHUNK
+
+    def group(index, carry):
+        first = index * TOGETHER
+        parts = []
+        for step in range(TOGETHER):
+            start = pl.multiple_of((first + step) * CHUNK, CHUNK)
+            block = ext[pl.ds(start, CHUNK + 16)]
+            query = jax.nn.silu(convolved(block, taps, 0))
+            key = jax.nn.silu(convolved(block, taps, 1))
+            value = jax.nn.silu(convolved(block, taps, 2)).astype(low)
+            query = query * lax.rsqrt(jnp.sum(query * query, axis=1, keepdims=True) + epsilon)
+            query = (query * head_size ** (-0.5)).astype(low)
+            key = key * lax.rsqrt(jnp.sum(key * key, axis=1, keepdims=True) + epsilon)
+            key = key.astype(low)
+            beta = jax.nn.sigmoid(logit_ref[pl.ds(start, CHUNK)]) * live_rows(limit, start)
+            qkv_ref[pl.ds(start, CHUNK)] = jnp.concatenate([query, key, value], axis=1)
+            parts.append((key, value, beta))
+        strict = [
+            jnp.where(rows > columns, beta * dot(key, key, NT), 0.0) for key, _, beta in parts
+        ]
+        solved = inverse_of(strict)
+        for step in range(TOGETHER):
+            key, value, beta = parts[step]
+            solved_ref[0, first + step] = solved[step]
+            weighted = pair(solved[step] * beta.T)
+            both = nn_low(weighted, side(key, value))
+            wu_ref[0, first + step] = both
+            moved = low_nn(key.T, pair(both))
+            step_map = identity - moved[:, :head_size]
+            map_ref[0, first + step] = step_map
+            maps[chain, first + step] = step_map
+            offsets[chain, first + step] = moved[:, head_size:]
+        return carry
+
+    lax.fori_loop(0, chunks // TOGETHER, group, 0)
+
+    @pl.when(chain == chains - 1)
+    def _():
+        start = side(identity, jnp.zeros_like(identity))
+
+        def advance(chunk, states):
+            out = []
+            for index in range(chains):
+                state = states[index]
+                prefix_ref[index, chunk] = state[:, :head_size]
+                local_ref[index, chunk] = state[:, head_size:]
+                moved = nn_wide(pair(maps[index, chunk]), pair(state))
+                out.append(
+                    side(moved[:, :head_size], moved[:, head_size:] + offsets[index, chunk])
+                )
+            return tuple(out)
+
+        ends = lax.fori_loop(0, chunks, advance, (start,) * chains)
+        for index in range(chains):
+            ends_ref[index] = ends[index]
+
+
+def mix_kernel(
+    qkv_ref, wu_ref, prefix_ref, local_ref, enter_ref, gate_ref, scale_ref,
+    state_ref, fresh_ref, mixed_ref, gated_ref,
+):
+    chunks = prefix_ref.shape[1]
+    head_size = CHUNK
+    rows, columns = grid_of_rows()
+    enter = pair(enter_ref[0])
+    scale = scale_ref[...]
+
+    def group(index, carry):
+        for step in range(TOGETHER):
+            chunk = index * TOGETHER + step
+            start = pl.multiple_of(chunk * CHUNK, CHUNK)
+            here = pl.ds(start, CHUNK)
+            state = nn(pair(prefix_ref[0, chunk]), enter) + local_ref[0, chunk]
+            state_ref[0, chunk] = state
+            states = pair(state)
+            both = wu_ref[0, chunk]
+            fresh = both[:, head_size:] - nn(pair(both[:, :head_size]), states)
+            fresh_ref[0, chunk] = fresh
+            query, key = qkv_ref[here, :head_size], qkv_ref[here, head_size : 2 * head_size]
+            scores = jnp.where(rows >= columns, dot(query, key, NT), 0.0)
+            mixed = low_nn(query, states) + nn(pair(scores), pair(fresh))
+            mixed_ref[here] = mixed
+            inverse = lax.rsqrt(jnp.mean(mixed * mixed, axis=1, keepdims=True) + epsilon)
+            normed = mixed * inverse * scale
+            gated_ref[here] = (normed * jax.nn.silu(gate_ref[here].astype(wide))).astype(low)
+        return carry
+
+    lax.fori_loop(0, chunks // TOGETHER, group, 0)
+
+
+def turn_kernel(
+    grad_ref, mixed_ref, gate_ref, scale_ref, qkv_ref, wu_ref, map_ref,
+    out_ref, fresh_ref, gate_grad_ref, gain_ref, source_ref, end_ref,
+    maps, sources,
+):
+    seq, head = pl.program_id(0), pl.program_id(1)
+    heads = pl.num_programs(1)
+    chain = seq * heads + head
+    chains, chunks = maps.shape[0], maps.shape[1]
+    head_size = CHUNK
+    rows, columns = grid_of_rows()
+    scale = scale_ref[...]
+
+    def group(index, gain):
+        for step in range(TOGETHER):
+            chunk = index * TOGETHER + step
+            start = pl.multiple_of(chunk * CHUNK, CHUNK)
+            here = pl.ds(start, CHUNK)
+            grad, mixed = grad_ref[here], mixed_ref[here]
+            silu_gate, slope = silu_parts(gate_ref[here].astype(wide))
+            inverse = lax.rsqrt(jnp.mean(mixed * mixed, axis=1, keepdims=True) + epsilon)
+            unit = mixed * inverse
+            gate_grad_ref[here] = (grad * unit * scale * slope).astype(low)
+            passed = grad * silu_gate
+            gain = gain + jnp.sum(passed * unit, axis=0, keepdims=True)
+            scaled = passed * scale
+            mixed_grad = inverse * (
+                scaled - unit * inverse * jnp.mean(scaled * mixed, axis=1, keepdims=True)
+            )
+            out_ref[0, chunk] = mixed_grad
+            query, key = qkv_ref[here, :head_size], qkv_ref[here, head_size : 2 * head_size]
+            scores = jnp.where(rows >= columns, dot(query, key, NT), 0.0)
+            turned = jnp.where(rows <= columns, dot(key, query, NT), 0.0)
+            grads = pair(mixed_grad)
+            fresh_ref[0, chunk] = nn(pair(turned), grads)
+            reading = query.astype(wide) - nn(pair(scores), pair(wu_ref[0, chunk, :, :head_size]))
+            source = nn(pair(mixed_grad.T), pair(reading))
+            source_ref[0, chunk] = source
+            sources[chain, chunk] = source
+            maps[chain, chunk] = map_ref[0, chunk]
+        return gain
+
+    gain = lax.fori_loop(0, chunks // TOGETHER, group, jnp.zeros((1, head_size), wide))
+    gain_ref[0] = jnp.broadcast_to(gain, (8, head_size))
+
+    @pl.when(chain == chains - 1)
+    def _():
+        def advance(step, states):
+            chunk = chunks - 1 - step
+            return tuple(
+                nn(pair(states[index]), pair(maps[index, chunk])) + sources[index, chunk]
+                for index in range(chains)
+            )
+
+        ends = lax.fori_loop(
+            0, chunks, advance, (jnp.zeros((head_size, head_size), wide),) * chains
         )
-    )
-
-
-def wy_form(keys, values, betas):
-    width = keys.shape[-2]
-    head_size = keys.shape[-1]
-    gram = product("...id,...jd->...ij", keys, keys)
-    strict = jnp.tril(jnp.ones((width, width), jnp.float32), -1)
-    system = jnp.eye(width, dtype=jnp.float32) + betas[..., :, None] * gram * strict
-    right_side = jnp.concatenate([betas[..., None] * keys, betas[..., None] * values], axis=-1)
-    solved = lax.linalg.triangular_solve(
-        system, right_side, left_side=True, lower=True, unit_diagonal=True
-    )
-    return (solved[..., :head_size], solved[..., head_size:])
-
-
-def delta_maps(keys, wy_keys, wy_values):
-    head_size = keys.shape[-1]
-    identity = jnp.broadcast_to(
-        jnp.eye(head_size, dtype=jnp.float32), keys.shape[:2] + (head_size, head_size)
-    )
-
-    def advance(carry, pieces):
-        matrix, offset = carry
-        key_block, wkey_block, wvalue_block = pieces
-        step_map = identity - product("...cd,...ce->...de", key_block, wkey_block)
-        new_matrix = product("...ij,...jk->...ik", step_map, matrix)
-        new_offset = product("...ij,...jk->...ik", step_map, offset) + product(
-            "...cd,...ce->...de", key_block, wvalue_block
+        for index in range(chains):
+            end_ref[index] = ends[index]
+
+
+def unwind_kernel(
+    limit_ref, raw_ref, tail_ref, taps_ref, logit_ref, qkv_ref, solved_ref, wu_ref, state_ref,
+    fresh_in_ref, out_ref, fresh_grad_ref, maps_ref, sources_ref, leave_ref,
+    raw_grad_ref, edge_ref, halo_ref, taps_grad_ref, logit_grad_ref,
+    ext, pre_grads, leaving,
+):
+    seq, head = pl.program_id(0), pl.program_id(1)
+    heads = pl.num_programs(1)
+    chain = seq * heads + head
+    chains, chunks = maps_ref.shape[0], maps_ref.shape[1]
+    head_size = CHUNK
+    span = chunks * CHUNK
+    rows, columns = grid_of_rows()
+    write_extended(ext, tail_ref, raw_ref)
+    taps = taps_ref[0]
+    limit = limit_ref[seq]
+
+    @pl.when(chain == 0)
+    def _():
+        def advance(step, states):
+            chunk = chunks - 1 - step
+            out = []
+            for index in range(chains):
+                leaving[index, chunk] = states[index]
+                out.append(
+                    nn(pair(states[index]), pair(maps_ref[index, chunk]))
+                    + sources_ref[index, chunk]
+                )
+            return tuple(out)
+
+        lax.fori_loop(0, chunks, advance, tuple(leave_ref[index] for index in range(chains)))
+
+    pre_grads[:16] = jnp.zeros((16, 3 * head_size), wide)
+    pre_grads[span + 16 :] = jnp.zeros((16, 3 * head_size), wide)
+
+    def one(chunk):
+        start = pl.multiple_of(chunk * CHUNK, CHUNK)
+        here = pl.ds(start, CHUNK)
+        query = qkv_ref[here, :head_size]
+        key = qkv_ref[here, head_size : 2 * head_size]
+        value = qkv_ref[here, 2 * head_size :]
+        live = live_rows(limit, start)
+        squash = jax.nn.sigmoid(logit_ref[here])
+        beta = squash * live
+        grads = pair(out_ref[0, chunk])
+        fresh = pair(fresh_in_ref[0, chunk])
+        state = pair(state_ref[0, chunk])
+        leave = pair(leaving[chain, chunk])
+        both = wu_ref[0, chunk]
+        fresh_grad = fresh_grad_ref[0, chunk] + low_nt(key, leave)
+        fresh_grads = pair(fresh_grad)
+        score_grad = jnp.where(rows >= columns, nt(grads, fresh), 0.0)
+        turned_grad = jnp.where(rows <= columns, nt(fresh, grads), 0.0)
+        query_grad = nt(grads, state) + nn_low(pair(score_grad), key)
+        key_grad = nn_low(pair(turned_grad), query) + nn(fresh, leave)
+        wkey_grad = -nt(fresh_grads, state)
+        right_grad = nn_wide(pair(solved_ref[0, chunk].T), pair(side(wkey_grad, fresh_grad)))
+        right = pair(right_grad)
+        twos = pair(both)
+        found = dot(right[0], over(*twos), NT)
+        system_grad = found[:, :CHUNK] + found[:, CHUNK:] + dot(right[1], twos[0], NT)
+        system_grad = jnp.where(rows > columns, -system_grad, 0.0)
+        gram = dot(key, key, NT)
+        gram_grad = beta * system_grad
+        key_grad = key_grad + nn_low(pair(gram_grad + gram_grad.T), key)
+        key_right, value_right = right_grad[:, :head_size], right_grad[:, head_size:]
+        key_grad = key_grad + beta * key_right
+        value_grad = beta * value_right
+        beta_grad = jnp.sum(
+            key_right * key.astype(wide) + value_right * value.astype(wide) + system_grad * gram,
+            axis=1,
+            keepdims=True,
         )
-        return ((new_matrix, new_offset), None)
-
-    moved = tuple((jnp.moveaxis(array, 2, 0) for array in (keys, wy_keys, wy_values)))
-    result, _ = lax.scan(advance, (identity, jnp.zeros_like(identity)), moved)
-    return result
-
-
-def delta_rule(queries, keys, wy_keys, wy_values, start):
-    width = queries.shape[-2]
-    causal = jnp.tril(jnp.ones((width, width), jnp.float32))
-
-    def advance(state, pieces):
-        query_block, key_block, wkey_block, wvalue_block = pieces
-        fresh = wvalue_block - product("...cd,...de->...ce", wkey_block, state)
-        scores = product("...id,...jd->...ij", query_block, key_block) * causal
-        output = product("...cd,...de->...ce", query_block, state) + product(
-            "...ij,...je->...ie", scores, fresh
-        )
-        return (state + product("...cd,...ce->...de", key_block, fresh), output)
-
-    moved = tuple((jnp.moveaxis(array, 2, 0) for array in (queries, keys, wy_keys, wy_values)))
-    final, outputs = lax.scan(advance, start, moved)
-    return (jnp.moveaxis(outputs, 0, 2), final)
+        logit_grad_ref[here] = (beta_grad * (live * squash * (1.0 - squash))).astype(low)
+
+        block = ext[pl.ds(start, CHUNK + 16)]
+        grads_pre = []
+        for stream, grad in enumerate((query_grad, key_grad, value_grad)):
+            act, slope = silu_parts(convolved(block, taps, stream))
+            if stream < 2:
+                inverse = lax.rsqrt(jnp.sum(act * act, axis=1, keepdims=True) + epsilon)
+                inner = jnp.sum(act * grad, axis=1, keepdims=True)
+                grad = inverse * (grad - act * (inverse * inverse * inner))
+                if stream == 0:
+                    grad = grad * head_size ** (-0.5)
+            grads_pre.append(grad * slope)
+        pre_grads[pl.ds(start + 16, CHUNK)] = jnp.concatenate(grads_pre, axis=1)
+
+    def group(index, carry):
+        for step in range(2):
+            one(index * 2 + step)
+        return carry
+
+    lax.fori_loop(0, chunks // 2, group, 0)
+
+    def back(block, offset_of_first):
+        streams = []
+        for stream in range(3):
+            part = block[:, stream * head_size : (stream + 1) * head_size]
+            total = None
+            for offset in range(CONV):
+                first = offset_of_first + CONV - 1 - offset
+                term = taps[stream * CONV + offset][None, :] * part[first : first + CHUNK]
+                total = term if total is None else total + term
+            streams.append(total)
+        return jnp.concatenate(streams, axis=1)
+
+    def finish(chunk, totals):
+        start = pl.multiple_of(chunk * CHUNK, CHUNK)
+        block = pre_grads[pl.ds(start + 16, CHUNK + 16)]
+        grad = back(block, 0)
+        raw_grad_ref[pl.ds(start, CHUNK)] = grad.astype(low)
+        edge_ref[0] = grad[CHUNK - 16 :]
+        before = ext[pl.ds(start, CHUNK + 16)]
+        pre = block[:CHUNK]
+        out = []
+        for offset in range(CONV):
+            first = 16 - (CONV - 1) + offset
+            term = jnp.sum(pre * before[first : first + CHUNK], axis=0, keepdims=True)
+            out.append(totals[offset] + term)
+        return tuple(out)
+
+    zero = jnp.zeros((1, 3 * head_size), wide)
+    totals = lax.fori_loop(0, chunks, finish, (zero,) * CONV)
+    for offset in range(CONV):
+        taps_grad_ref[0, offset : offset + 1] = totals[offset]
+    halo = back(pre_grads[: CHUNK + 32], 0)
+    halo_ref[0] = halo[:16]
+
+
+def kernel_call(body, grid, ins, outs, scratch):
+    return pl.pallas_call(
+        body,
+        grid=grid,
+        in_specs=[spec for _, spec in ins],
+        out_specs=[spec for _, _, spec in outs],
+        out_shape=[jax.ShapeDtypeStruct(shape, dtype) for shape, dtype, _ in outs],
+        scratch_shapes=scratch,
+        compiler_params=pltpu.CompilerParams(
+            vmem_limit_bytes=VMEM_BYTES, dimension_semantics=("arbitrary",) * len(grid)
+        ),
+    )(*[array for array, _ in ins])
+
+
+def delta_specs(heads, span):
+    head_size = CHUNK
+    chunks = span // CHUNK
+
+    def chain(s, h):
+        return s * heads + h
+
+    return {
+        "scalar": pl.BlockSpec(memory_space=pltpu.SMEM),
+        "three": pl.BlockSpec((span, 3 * head_size), lambda s, h: (s, h)),
+        "edge": pl.BlockSpec((1, 16, 3 * head_size), lambda s, h: (s, 0, h)),
+        "taps": pl.BlockSpec((1, 3 * CONV, head_size), lambda s, h: (h, 0, 0)),
+        "one": pl.BlockSpec((span, head_size), lambda s, h: (s, h)),
+        "square": pl.BlockSpec((1, chunks, CHUNK, head_size), lambda s, h: (chain(s, h), 0, 0, 0)),
+        "double": pl.BlockSpec(
+            (1, chunks, CHUNK, 2 * head_size), lambda s, h: (chain(s, h), 0, 0, 0)
+        ),
+        "state": pl.BlockSpec((1, head_size, head_size), lambda s, h: (chain(s, h), 0, 0)),
+        "scale": pl.BlockSpec((1, head_size), lambda s, h: (0, 0)),
+        "gain": pl.BlockSpec((1, 8, head_size), lambda s, h: (chain(s, h), 0, 0)),
+        "tapped": pl.BlockSpec((1, 8, 3 * head_size), lambda s, h: (chain(s, h), 0, 0)),
+        "all_squares": lambda chains: pl.BlockSpec(
+            (chains, chunks, CHUNK, head_size), lambda s, h: (0, 0, 0, 0)
+        ),
+        "all_states": lambda chains, columns: pl.BlockSpec(
+            (chains, head_size, columns), lambda s, h: (0, 0, 0)
+        ),
+    }
+
+
+def delta_prepare(limit, raw, tails, taps, logits, seqs, heads, span):
+    specs = delta_specs(heads, span)
+    chains, chunks, size = seqs * heads, span // CHUNK, CHUNK
+    squares = (chains, chunks, CHUNK, size)
+    return kernel_call(
+        prepare_kernel,
+        (seqs, heads),
+        [
+            (limit, specs["scalar"]),
+            (raw, specs["three"]),
+            (tails, specs["edge"]),
+            (taps, specs["taps"]),
+            (logits, specs["one"]),
+        ],
+        [
+            (raw.shape, low, specs["three"]),
+            (squares, wide, specs["square"]),
+            ((chains, chunks, CHUNK, 2 * size), wide, specs["double"]),
+            (squares, wide, specs["square"]),
+            (squares, wide, specs["all_squares"](chains)),
+            (squares, wide, specs["all_squares"](chains)),
+            ((chains, size, 2 * size), wide, specs["all_states"](chains, 2 * size)),
+        ],
+        [
+            pltpu.VMEM((span + 16, 3 * size), wide),
+            pltpu.VMEM(squares, wide),
+            pltpu.VMEM(squares, wide),
+        ],
+    )
+
+
+def delta_mix(qkv, wu, prefix, local, enter, gate, scale, seqs, heads, span):
+    specs = delta_specs(heads, span)
+    chains, chunks, size = seqs * heads, span // CHUNK, CHUNK
+    squares = (chains, chunks, CHUNK, size)
+    return kernel_call(
+        mix_kernel,
+        (seqs, heads),
+        [
+            (qkv, specs["three"]),
+            (wu, specs["double"]),
+            (prefix, specs["square"]),
+            (local, specs["square"]),
+            (enter, specs["state"]),
+            (gate, specs["one"]),
+            (scale, specs["scale"]),
+        ],
+        [
+            (squares, wide, specs["square"]),
+            (squares, wide, specs["square"]),
+            (gate.shape, wide, specs["one"]),
+            (gate.shape, low, specs["one"]),
+        ],
+        [],
+    )
+
+
+def delta_turn(grad, mixed, gate, scale, qkv, wu, maps, seqs, heads, span):
+    specs = delta_specs(heads, span)
+    chains, chunks, size = seqs * heads, span // CHUNK, CHUNK
+    squares = (chains, chunks, CHUNK, size)
+    return kernel_call(
+        turn_kernel,
+        (seqs, heads),
+        [
+            (grad, specs["one"]),
+            (mixed, specs["one"]),
+            (gate, specs["one"]),
+            (scale, specs["scale"]),
+            (qkv, specs["three"]),
+            (wu, specs["double"]),
+            (maps, specs["square"]),
+        ],
+        [
+            (squares, wide, specs["square"]),
+            (squares, wide, specs["square"]),
+            (gate.shape, low, specs["one"]),
+            ((chains, 8, size), wide, specs["gain"]),
+            (squares, wide, specs["square"]),
+            ((chains, size, size), wide, specs["all_states"](chains, size)),
+        ],
+        [pltpu.VMEM(squares, wide), pltpu.VMEM(squares, wide)],
+    )
+
+
+def delta_unwind(
+    limit, raw, tails, taps, logits, qkv, solved, wu, state, fresh, out, fresh_grad, maps,
+    sources, leave, seqs, heads, span,
+):
+    specs = delta_specs(heads, span)
+    chains, chunks, size = seqs * heads, span // CHUNK, CHUNK
+    squares = (chains, chunks, CHUNK, size)
+    edges = (seqs, 16, 3 * heads * size)
+    return kernel_call(
+        unwind_kernel,
+        (seqs, heads),
+        [
+            (limit, specs["scalar"]),
+            (raw, specs["three"]),
+            (tails, specs["edge"]),
+            (taps, specs["taps"]),
+            (logits, specs["one"]),
+            (qkv, specs["three"]),
+            (solved, specs["square"]),
+            (wu, specs["double"]),
+            (state, specs["square"]),
+            (fresh, specs["square"]),
+            (out, specs["square"]),
+            (fresh_grad, specs["square"]),
+            (maps, specs["all_squares"](chains)),
+            (sources, specs["all_squares"](chains)),
+            (leave, specs["all_states"](chains, size)),
+        ],
+        [
+            (raw.shape, low, specs["three"]),
+            (edges, wide, specs["edge"]),
+            (edges, wide, specs["edge"]),
+            ((chains, 8, 3 * size), wide, specs["tapped"]),
+            (logits.shape, low, specs["one"]),
+        ],
+        [
+            pltpu.VMEM((span + 16, 3 * size), wide),
+            pltpu.VMEM((span + 32, 3 * size), wide),
+            pltpu.VMEM(squares, wide),
+        ],
+    )
 
 
 def cut_columns(weight):
@@ -289,9 +806,14 @@
     small = jnp.pad(small, ((0, 0), (0, SMALL * 3 * width - small_size))).reshape(
         MATES, SMALL, 3 * width
     )
-    streams_cut = jnp.concatenate(
-        [cut_columns(w.astype(low)) for w in (query_weight, key_weight, value_weight)], axis=2
-    )
+    streams_cut = jnp.stack(
+        [
+            w.astype(low).reshape(depth, MATES, heads, head_size)
+            for w in (query_weight, key_weight, value_weight)
+        ],
+        axis=3,
+    )
+    streams_cut = streams_cut.transpose(1, 0, 2, 3, 4).reshape(MATES, depth, 3 * width)
     first = gather_weights(jnp.concatenate([streams_cut, small], axis=1))
     streams_full = first[:, :, :depth].reshape(model_width, 3 * width)
     small = first[:, :, depth:].reshape(count, SMALL * 3 * width)[:, :small_size]
@@ -315,8 +837,8 @@
     beta_full = beta_small.reshape(model_width, heads)
     taps = (
         conv_small.reshape(count, heads, 3, CONV, gain_part)
-        .transpose(2, 3, 1, 0, 4)
-        .reshape(3, CONV, width)
+        .transpose(1, 2, 3, 0, 4)
+        .reshape(heads, 3 * CONV, head_size)
         .astype(wide)
     )
     attn_scale = attn_small.reshape(model_width).astype(wide)
@@ -355,58 +877,23 @@
     flat_normed = (input_rows * rms_scale(input_rows) * attn_scale).astype(low)
 
     lengths_here = jnp.stack([pick(lengths, core), pick(lengths, 1 - core)])
-    positions = line_of() * span + jnp.arange(span, dtype=jnp.int32)
-    validity = (positions[None, :] < lengths_here[:, None]).astype(wide)
-
-    block_count = span // BLOCK
-
-    def to_blocks(array):
-        return array.reshape(seq_count, block_count, BLOCK, heads, head_size).transpose(
-            0, 3, 1, 2, 4
-        )
-
-    def from_blocks(array):
-        return array.transpose(0, 2, 3, 1, 4).reshape(seq_count, span, heads, head_size)
-
-    raw_streams = (
-        matmul("rd,dc->rc", flat_normed, streams_full).astype(low).reshape(seq_count, span, 3, width)
-    ).transpose(2, 0, 1, 3)
+    limit = lengths_here - line_of() * span
+    beta_spread = jnp.repeat(beta_full, head_size, axis=1)
+
+    raw = matmul("rd,dc->rc", flat_normed, streams_full).astype(low)
+    tails = along(raw.reshape(seq_count, span, 3 * width)[:, span - 16 :], 1)
+    logits = matmul("rd,dc->rc", flat_normed, beta_spread)
     gate_values = matmul("rd,dc->rc", flat_normed, outgate_full).astype(low)
-    beta_logits = matmul("rd,dh->rh", flat_normed, beta_full).reshape(seq_count, span, heads)
-    tails = along(raw_streams[:, :, span - (CONV - 1) :], 1)
-    extended = jnp.concatenate([tails, raw_streams], axis=2).astype(wide)
-    pre_act = sum(
-        (
-            taps[:, offset][:, None, None, :] * extended[:, :, offset : offset + span]
-            for offset in range(CONV)
-        )
-    )
-    activated = jax.nn.silu(pre_act)
-    query_raw = activated[0].reshape(seq_count, span, heads, head_size)
-    key_raw = activated[1].reshape(seq_count, span, heads, head_size)
-    query_inverse = lax.rsqrt(jnp.sum(query_raw * query_raw, axis=-1, keepdims=True) + epsilon)
-    key_inverse = lax.rsqrt(jnp.sum(key_raw * key_raw, axis=-1, keepdims=True) + epsilon)
-    queries = (query_raw * query_inverse * head_size ** (-0.5)).astype(low).astype(wide)
-    keys = (key_raw * key_inverse).astype(low).astype(wide)
-    values = activated[2].astype(low).astype(wide).reshape(seq_count, span, heads, head_size)
-    beta_squash = jax.nn.sigmoid(beta_logits)
-    beta_gate = beta_squash * validity[:, :, None]
-    query_blocks = to_blocks(queries)
-    key_blocks = to_blocks(keys)
-    value_blocks = to_blocks(values)
-    beta_blocks = beta_gate.reshape(seq_count, block_count, BLOCK, heads).transpose(0, 3, 1, 2)
-    (wy_keys, wy_values), wy_back = jax.vjp(wy_form, key_blocks, value_blocks, beta_blocks)
-    map_matrix, map_offset = delta_maps(key_blocks, wy_keys, wy_values)
+    sizes_of = (seq_count, heads, span)
+    qkv, solved, wu, maps, prefix, local, ends = delta_prepare(
+        limit, raw, tails, taps, logits, *sizes_of
+    )
+    map_matrix, map_offset = ends[:, :, :head_size], ends[:, :, head_size:]
     entering = hop_states(map_matrix, map_offset, 1)
-    (mixed_blocks, leaving), rule_back = jax.vjp(
-        delta_rule, query_blocks, key_blocks, wy_keys, wy_values, entering
-    )
-    mixed = from_blocks(mixed_blocks)
-    mix_inverse = rms_scale(mixed)
-    head_normed = mixed * mix_inverse * head_scale
-    gate_wide = gate_values.astype(wide).reshape(seq_count, span, heads, head_size)
-    silu_gate = jax.nn.silu(gate_wide)
-    gated = (head_normed * silu_gate).astype(low).reshape(rows, width)
+    head_row = head_scale[None]
+    state, fresh, mixed, gated = delta_mix(
+        qkv, wu, prefix, local, entering, gate_values, head_row, *sizes_of
+    )
     attn_out = sum_ordered(matmul("rc,dc->rd", gated, output_full).astype(low))
     middle = mine_input + attn_out
     second_inverse = rms_scale(middle)
@@ -433,73 +920,36 @@
     middle_grad = grad_mine.astype(wide) + middle_part
     attn_grad_rows = ordered_rows(middle_grad.astype(low))
     output_grad = matmul("rd,rc->dc", attn_grad_rows, gated)
-    gated_grad = matmul("rd,dc->rc", attn_grad_rows, output_full).reshape(
-        seq_count, span, heads, head_size
-    )
-    outgate_act_grad = (
-        (gated_grad * head_normed * silu_slope(gate_wide)).astype(low).reshape(rows, width)
-    )
-    mixed_flat_grad, head_gain_part = norm_back(
-        (gated_grad * silu_gate).reshape(-1, head_size),
-        mixed.reshape(-1, head_size),
-        mix_inverse.reshape(-1, 1),
-        head_scale,
-    )
-    mixed_grad = mixed_flat_grad.reshape(seq_count, span, heads, head_size)
-    query_bgrad, key_bgrad, wkey_grad, wvalue_grad, local_state = rule_back(
-        (to_blocks(mixed_grad), jnp.zeros_like(leaving))
-    )
-    leaving_grad = hop_states(jnp.swapaxes(map_matrix, -1, -2), local_state, -1)
-    later_back = rule_back((jnp.zeros_like(mixed_blocks), leaving_grad))
-    key_bgrad = key_bgrad + later_back[1]
-    wkey_grad = wkey_grad + later_back[2]
-    wvalue_grad = wvalue_grad + later_back[3]
-    key_cgrad, value_bgrad, beta_bgrad = wy_back((wkey_grad, wvalue_grad))
-    query_grad_unit = from_blocks(query_bgrad)
-    key_grad_unit = from_blocks(key_bgrad + key_cgrad)
-    value_grad_act = from_blocks(value_bgrad)
-    beta_token_grad = beta_bgrad.transpose(0, 2, 3, 1).reshape(seq_count, span, heads)
-    beta_logit_grad = (
-        (beta_token_grad * validity[:, :, None] * beta_squash * (1.0 - beta_squash))
-        .astype(low)
-        .reshape(rows, heads)
-    )
-    act_grads = jnp.stack(
-        [
-            unit_back(query_grad_unit, query_raw, query_inverse, head_size ** (-0.5)).reshape(
-                seq_count, span, width
-            ),
-            unit_back(key_grad_unit, key_raw, key_inverse, 1.0).reshape(seq_count, span, width),
-            value_grad_act.reshape(seq_count, span, width),
-        ]
-    )
-    pre_grad = act_grads * silu_slope(pre_act)
-    padded_grad = jnp.pad(pre_grad, ((0, 0), (0, 0), (CONV - 1, CONV - 1), (0, 0)))
-    reach = span + CONV - 1
-    extended_grad = sum(
-        (
-            taps[:, offset][:, None, None, :]
-            * padded_grad[:, :, CONV - 1 - offset : CONV - 1 - offset + reach]
-            for offset in range(CONV)
-        )
-    )
-    taps_grad = jnp.stack(
-        [
-            jnp.sum(pre_grad * extended[:, :, offset : offset + span], axis=(1, 2))
-            for offset in range(CONV)
-        ],
-        axis=1,
-    )
-    returned = along(extended_grad[:, :, : CONV - 1].astype(low), -1).astype(wide)
-    raw_grad = extended_grad[:, :, CONV - 1 :].at[:, :, span - (CONV - 1) :].add(returned)
-    raw_grad_low = raw_grad.astype(low).transpose(1, 2, 0, 3).reshape(rows, 3 * width)
-    streams_grad = matmul("rd,rc->dc", flat_normed, raw_grad_low)
+    gated_grad = matmul("rd,dc->rc", attn_grad_rows, output_full)
+    out_grads, fresh_grad, outgate_act_grad, head_gain_parts, sources, local_state = delta_turn(
+        gated_grad, mixed, gate_values, head_row, qkv, wu, maps, *sizes_of
+    )
+    head_gain_part = jnp.sum(head_gain_parts[:, 0], axis=0)
+    leaving_grad = hop_states_back(map_matrix, local_state)
+    raw_grad, edge, halo, taps_grad, logit_grad = delta_unwind(
+        limit, raw, tails, taps, logits, qkv, solved, wu, state, fresh, out_grads, fresh_grad,
+        maps, sources, leaving_grad, *sizes_of,
+    )
+    returned = along(halo.astype(low), -1)
+    edge = (edge + returned.astype(wide)).astype(low)
+    raw_grad_low = (
+        raw_grad.reshape(seq_count, span, 3 * width)
+        .at[:, span - 16 :]
+        .set(edge)
+        .reshape(rows, 3 * width)
+    )
+    beta_logit_grad = logit_grad[:, ::head_size]
+    last_grads = jnp.concatenate(
+        [raw_grad_low, jnp.pad(beta_logit_grad, ((0, 0), (0, head_size - heads)))], axis=1
+    )
+    last_weights = jnp.concatenate(
+        [streams_full, jnp.pad(beta_full, ((0, 0), (0, head_size - heads)))], axis=1
+    )
     outgate_grad = matmul("rd,rc->dc", flat_normed, outgate_act_grad)
-    beta_grad = matmul("rd,rh->dh", flat_normed, beta_logit_grad)
-    normed_part = (
-        matmul("rc,dc->rd", outgate_act_grad, outgate_full)
-        + matmul("rh,dh->rd", beta_logit_grad, beta_full)
-        + matmul("rc,dc->rd", raw_grad_low, streams_full)
+    last_grad = matmul("rd,rc->dc", flat_normed, last_grads)
+    streams_grad, beta_grad = last_grad[:, : 3 * width], last_grad[:, 3 * width : 3 * width + heads]
+    normed_part = matmul("rc,dc->rd", outgate_act_grad, outgate_full) + matmul(
+        "rc,dc->rd", last_grads, last_weights
     )
     normed_grad = sum_ordered(normed_part.astype(low))
     input_part, attn_gain_grad = norm_back(normed_grad, mine_input, first_inverse, attn_scale)
@@ -516,8 +966,10 @@
     ups_sum = scatter_grads(cut_rows(ups_grad))
     gates_sum = scatter_grads(cut_rows(jnp.concatenate([outgate_grad, output_grad], axis=1)))
     conv_grad = (
-        taps_grad.reshape(3, CONV, heads, count, gain_part)
-        .transpose(3, 2, 0, 1, 4)
+        taps_grad[:, :CONV]
+        .reshape(seq_count, heads, CONV, 3, count, gain_part)
+        .sum(axis=0)
+        .transpose(3, 0, 2, 1, 4)
         .reshape(count, -1)
     )
     small_grad = jnp.concatenate(
@@ -540,7 +992,12 @@
             axis=2,
         )
     )
-    streams_sum = first_sum[:, :depth]
+    streams_sum = (
+        first_sum[:, :depth]
+        .reshape(MATES, depth, heads, 3, head_size)
+        .transpose(3, 1, 0, 2, 4)
+        .reshape(3, depth, MATES * width)
+    )
     small_sum = first_sum[:, depth:].reshape(MATES, SMALL * 3 * width)
     beta_sum, conv_sum, attn_sum, mlp_sum, head_sum = (
         small_sum[:, starts[index] : starts[index + 1]] for index in range(len(sizes))
@@ -551,9 +1008,9 @@
         both_sequences(output_mine),
         both_sequences(input_grad_mine),
         gains_sum[:depth],
-        join_columns(streams_sum[:, :, :width]),
-        join_columns(streams_sum[:, :, width : 2 * width]),
-        join_columns(streams_sum[:, :, 2 * width :]),
+        streams_sum[0],
+        streams_sum[1],
+        streams_sum[2],
         join_columns(gates_sum[:, :, :width]),
         join_columns(beta_sum.reshape(MATES, depth, heads)),
         conv_sum.reshape(MATES * heads, 3, CONV, gain_part),

time: 2440 us -> 1310 us (0.54)
  matrix products: 844 us -> 160 us
  other arithmetic: 579 us -> 176 us
  local copies, waits for them, and re-layouts: 467 us -> 317 us
  Pallas kernels: 0 us -> 114 us
    dot_general x439 -> x4, matrix products: 647 us -> 1.6 us  [product(): return jnp.einsum(form, left, right, precision=PRECISE)]
    another operation x12 -> x4, other arithmetic: 340 us -> 1.21 us  [the longest x1 1.19 us: on_device(): jnp.stack([w.astype(low).reshape(depth, MATES, heads, head_size) for w in...]
    pallas_call x0 -> x4, Pallas kernels: none -> 114 us  [kernel_call(): pl.pallas_call(body, grid=grid, in_specs=[spec for _, spec in ins], out_s...]
    mul x16 -> x0, local copies, waits for them, and re-layouts: 43.4 us -> none  [the longest x5 13.9 us: unit_back(): source * inverse * inverse]
    another operation x27 -> x10, local copies, waits for them, and re-layouts: 33.5 us -> 6.94 us
    dynamic_update_slice x64 -> x0, local copies, waits for them, and re-layouts: 25.5 us -> none  [delta_rule(): final, outputs = lax.scan(advance, start, moved)]
    mul x53 -> x0, other arithmetic: 24.9 us -> none  [the longest x2 10.5 us: unit_back(): factor * inverse]
    reshape x9 -> x2, local copies, waits for them, and re-layouts: 25 us -> 0.29 us  [on_device(): conv_grad = taps_grad[:, :CONV].reshape(seq_count, heads, CONV, 3, count,...]
  transfers between devices with their start and end apart: 123 -> 123, of which waited for: 41 -> 42; matrix products, arithmetic and copies ran while one was open for 67% -> 44% of each run, Pallas kernels for 0% -> 7%
where the time goes in v2:
time: 1310 us; the launch traced here: 1290 us
  local copies, waits for them, and re-layouts  317 us (24%)
  waiting for transfers between devices  291 us (22%)
  starting transfers between devices  232 us (18%)
  other arithmetic  176 us (13%)
  matrix products  160 us (12%)
  Pallas kernels  114 us (9%)
    ppermute x56, waiting for transfers between devices, along(): return lax.ppermute(value, 'seq', pairs)  184 us
    ppermute x56, starting transfers between devices, along(): return lax.ppermute(value, 'seq', pairs)  170 us
    dot_general x16, matrix products, matmul(): return jnp.einsum(form, left, right, preferred_element_type=wide)  158 us
    pallas_call x4, Pallas kernels, kernel_call(): pl.pallas_call(body, grid=grid, in_specs=[spec for _, spec in ins], out_s...  114 us
    ppermute x56, waiting for transfers between devices, to_mate(): lax.ppermute(value, 'seq', [(source, source ^ flip) for source in range(c...  107 us
    dynamic_update_slice x37, local copies, waits for them, and re-layouts, in_order(): out = lax.dynamic_update_index_in_dim(out, piece, mate ^ flip, 0)  95.5 us
    ppermute x56, starting transfers between devices, to_mate(): lax.ppermute(value, 'seq', [(source, source ^ flip) for source in range(c...  60.9 us
    unnamed x195, local copies, waits for them, and re-layouts  50.9 us
  transfers between devices with their start and end apart: 123, of which 42 were waited for; matrix products, arithmetic and copies ran while one was open for 44% of the time, Pallas kernels for 7%

profile of v2, /device:TPU:0, one launch (start us, length us, event | category | flops | bytes accessed | tf_op | source)
XLA Modules:
  0.0 1294.3 jit_solution(11015491821434930240)
XLA Ops:
  76.6 6.1 collective-permute-start.8
  82.7 10.1 collective-permute-done.9
  117.4 15.4 %collective-permute-done.23 = bf16[4,128,512]{2,1,0:T(8,128)(2,1)} collective-permute-done((bf16[4,128,512]{2,1,0:T(8,128)(2,1)S(1)}, bf16[4,128,512]{2,1,0:T(8,128)(2,1)}, u32[]{:S(2)}, u32[]{:S(2)}) %collective-permute-start.23) | collective-permute-done | bytes 524320 | tf_op jit(solution)/shard_map/ppermute | solution.py:36
  151.2 15.3 %collective-permute-done.11 = bf16[4,136,768]{2,1,0:T(8,128)(2,1)} collective-permute-done((bf16[4,136,768]{2,1,0:T(8,128)(2,1)}, bf16[4,136,768]{2,1,0:T(8,128)(2,1)}, u32[]{:S(2)}, u32[]{:S(2)}) %collective-permute-start.11) | collective-permute-done | bytes 835616 | tf_op jit(solution)/shard_map/ppermute | solution.py:36
  188.0 6.9 convolution_convert_fusion.5.raw_ref
  209.1 32.6 %shard_map.271 = (bf16[2048,768]{1,0:T(8,128)(2,1)}, f32[4,8,128,128]{3,2,1,0:T(8,128)}, f32[4,8,128,256]{3,2,1,0:T(8,128)}, f32[4,8,128,128]{3,2,1,0:T(8,128)},...) custom-call(s32[2]{0:T(128)S(1)} %add_subtract_fusion.limit_ref, ...), custom_call_target="tpu_custom_call" | custom-call | tf_op jit(solution)/shard_map/pallas_call | solution.py:577
  262.4 7.0 convolution_convert_fusion.8.gate_ref
  269.4 18.2 %shard_map.272 = (f32[4,8,128,128]{3,2,1,0:T(8,128)}, f32[4,8,128,128]{3,2,1,0:T(8,128)}, f32[2048,256]{1,0:T(8,128)}, bf16[2048,256]{1,0:T(8,128)(2,1)S(1)}) custom-call(bf16[2048,768]{1,0:T(8,128)(2,1)} %get-tuple-element.49.qkv_ref, f32[4,8,128,256]{3,2,1,0:T(8,128)} %get-tuple-element.50.wu_ref, f32[4,8,128,128]{3,2,1,0:T(8,128)} %get-tuple-element.51.prefix_ref, ...), custom_call_target="tpu_custom_call" | custom-call | tf_op jit(solution)/shard_map/pallas_call | solution.py:577
  330.0 7.7 dynamic_update_slice.205
  345.7 7.6 dynamic_update_slice.206
  353.4 8.7 dynamic_update_slice.207
  362.1 8.6 dynamic_update_slice.208
  388.0 23.6 %collective-permute-done.39 = bf16[128,1408]{1,0:T(8,128)(2,1)S(1)} collective-permute-done((bf16[128,1408]{1,0:T(8,128)(2,1)S(1)}, bf16[128,1408]{1,0:T(8,128)(2,1)S(1)}, u32[]{:S(2)}, u32[]{:S(2)}) %collective-permute-start.39) | collective-permute-done | bytes 360480 | tf_op jit(solution)/shard_map/ppermute | solution.py:25
  426.3 6.4 collective-permute-done.50
  438.3 15.9 %collective-permute-done.64 = bf16[256,1024]{0,1:T(8,128)(2,1)S(1)} collective-permute-done((bf16[256,1024]{0,1:T(8,128)(2,1)S(1)}, bf16[256,1024]{0,1:T(8,128)(2,1)S(1)}, u32[]{:S(2)}, u32[]{:S(2)}) %collective-permute-start.64) | collective-permute-done | bytes 524320 | tf_op jit(solution)/shard_map/ppermute | solution.py:25
  465.3 16.6 %maximum_maximum_fusion.1 = bf16[1024,2048]{0,1:T(8,128)(2,1)} fusion(bf16[256,1024]{0,1:T(8,128)(2,1)S(1)} %collective-permute-done.64, bf16[256,1024]{0,1:T(8,128)(2,1)S(1)} %collective-permute-done.63, bf16[256,2048]{0,1:T(8,128)(2,1)} %collective-permute-done.62, bf16[256,2048]{0,1:T(8,128)(2,1)} %collective-permute-done.61, bf16[256,2048]{0,1:T(8,128)(2,1)} %bitcast.84), kind=kLoop, calls=%fused_computation.32 | loop fusion | flops 20971520 | bytes 8388608 | tf_op jit(solution)/shard_map/concatenate | solution.py:856
  492.1 14.5 %collective-permute-done.42 = bf16[4,128,1408]{2,1,0:T(8,128)(2,1)} collective-permute-done((bf16[4,128,1408]{2,1,0:T(8,128)(2,1)S(1)}, bf16[4,128,1408]{2,1,0:T(8,128)(2,1)}, u32[]{:S(2)}, u32[]{:S(2)}) %collective-permute-start.42) | collective-permute-done | bytes 1441824 | tf_op jit(solution)/shard_map/ppermute | solution.py:36
  514.9 15.4 %maximum_maximum_fusion = bf16[1024,2048]{0,1:T(8,128)(2,1)} fusion(bf16[256,1024]{0,1:T(8,128)(2,1)S(1)} %collective-permute-done.35, bf16[256,1024]{0,1:T(8,128)(2,1)S(1)} %collective-permute-done.34, bf16[256,2048]{0,1:T(8,128)(2,1)S(1)} %collective-permute-done.33, bf16[256,2048]{0,1:T(8,128)(2,1)S(1)} %collective-permute-done.32, ...), kind=kLoop, calls=%fused_computation.31 | loop fusion | flops 20971520 | bytes 8388608 | tf_op jit(solution)/shard_map/concatenate | solution.py:856
  543.7 9.8 collective-permute-done.54
  556.0 6.2 reshape.359
  568.9 15.2 %collective-permute-done.45 = bf16[4,128,1408]{2,1,0:T(8,128)(2,1)} collective-permute-done((bf16[4,128,1408]{2,1,0:T(8,128)(2,1)}, bf16[4,128,1408]{2,1,0:T(8,128)(2,1)}, u32[]{:S(2)}, u32[]{:S(2)}) %collective-permute-start.45) | collective-permute-done | bytes 1441824 | tf_op jit(solution)/shard_map/ppermute | solution.py:36
  600.6 17.4 %fusion.100 = f32[2048,1408]{0,1:T(8,128)} fusion(bf16[2048,2048]{0,1:T(8,128)(2,1)} %constant_dynamic-update-slice_fusion.11, bf16[2048,1408]{1,0:T(8,128)(2,1)S(1)} %bitcast.406), kind=kOutput, calls=%fused_computation.345 | convolution fusion | flops 11811160064 | bytes 25690112 | tf_op jit(solution)/shard_map/rd,df->rf/dot_general | solution.py:156
  618.0 15.4 %multiply_convert_fusion.1 = (bf16[2048,704]{0,1:T(8,128)(2,1)}, bf16[2048,704]{0,1:T(8,128)(2,1)}, bf16[2048,704]{0,1:T(8,128)(2,1)}) fusion(f32[2048,1408]{0,1:T(8,128)} %fusion.100, bf16[2048,704]{0,1:T(8,128)(2,1)S(1)} %copy-done.39, bf16[2048,2048]{0,1:T(8,128)(2,1)} %constant_dynamic-update-slice_fusion.16), kind=kOutput, calls=%fused_computation.25 | convolution fusion | flops 5927206912 | bytes 31457280 | tf_op jit(solution)/shard_map/rd,df->rf/dot_general | solution.py:156
  633.4 15.6 %convolution_convert_fusion = bf16[2048,2048]{0,1:T(8,128)(2,1)S(1)} fusion(bf16[2048,1408]{1,0:T(8,128)(2,1)S(1)} %bitcast.407, bf16[2048,704]{0,1:T(8,128)(2,1)} %get-tuple-element.163, bf16[2048,704]{0,1:T(8,128)(2,1)} %get-tuple-element.162), kind=kOutput, calls=%fused_computation.12 | convolution fusion | flops 11826888704 | bytes 19922944 | tf_op jit(solution)/shard_map/rf,df->rd/dot_general | solution.py:156
  652.9 9.2 convolution_convert_fusion.2
  678.5 6.4 collective-permute-done.67
  701.5 17.2 %collective-permute-done.70 = bf16[256,2048]{0,1:T(8,128)(2,1)} collective-permute-done((bf16[256,2048]{0,1:T(8,128)(2,1)}, bf16[256,2048]{0,1:T(8,128)(2,1)}, u32[]{:S(2)}, u32[]{:S(2)}) %collective-permute-start.70) | collective-permute-done | bytes 1048608 | tf_op jit(solution)/shard_map/ppermute | solution.py:25
  722.3 18.0 %collective-permute-done.59 = bf16[256,2048]{0,1:T(8,128)(2,1)} collective-permute-done((bf16[256,2048]{0,1:T(8,128)(2,1)}, bf16[256,2048]{0,1:T(8,128)(2,1)}, u32[]{:S(2)}, u32[]{:S(2)}) %collective-permute-start.59) | collective-permute-done | bytes 1048608 | tf_op jit(solution)/shard_map/ppermute | solution.py:25
  748.4 15.3 %convolution_convert_fusion.1 = bf16[2048,1408]{1,0:T(8,128)(2,1)S(1)} fusion(bf16[2048,2048]{0,1:T(8,128)(2,1)S(1)} %bitcast.465, bf16[2048,704]{0,1:T(8,128)(2,1)} %get-tuple-element.163, bf16[2048,704]{0,1:T(8,128)(2,1)S(1)} %copy-done.72), kind=kOutput, calls=%fused_computation.13 | convolution fusion | flops 11825577984 | bytes 19922944 | tf_op jit(solution)/shard_map/rd,rf->df/dot_general | solution.py:156
  791.3 10.6 convolution_convert_fusion.6
  801.9 7.2 convert_element_type.682
  817.4 12.5 collective-permute-done.114
  838.6 22.3 %collective-permute-done.106 = bf16[4,128,1408]{2,1,0:T(8,128)(2,1)S(1)} collective-permute-done((bf16[4,128,1408]{2,1,0:T(8,128)(2,1)S(1)}, bf16[4,128,1408]{2,1,0:T(8,128)(2,1)S(1)}, u32[]{:S(2)}, u32[]{:S(2)}) %collective-permute-start.106) | collective-permute-done | bytes 1441824 | tf_op jit(solution)/shard_map/ppermute | solution.py:36
  869.5 15.9 %shard_map.273 = (f32[4,8,128,128]{3,2,1,0:T(8,128)}, f32[4,8,128,128]{3,2,1,0:T(8,128)}, bf16[2048,256]{1,0:T(8,128)(2,1)S(1)}, f32[4,8,128]{2,1,0:T(8,128)S(1)...) custom-call(f32[2048,256]{1,0:T(8,128)} %fusion.7.grad_ref, f32[2048,256]{1,0:T(8,128)} %get-tuple-element.55.mixed_ref, ...), custom_call_target="tpu_custom_call" | custom-call | tf_op jit(solution)/shard_map/pallas_call | solution.py:577
  898.0 8.1 collective-permute-done.77
  913.1 14.8 %collective-permute-start.107 = (bf16[4,128,1408]{2,1,0:T(8,128)(2,1)}, bf16[4,128,1408]{2,1,0:T(8,128)(2,1)}, u32[]{:S(2)}, u32[]{:S(2)}) collective-permute-start(bf16[4,128,1408]{2,1,0:T(8,128)(2,1)} %get-tuple-element.150), channel_id=1, source_target_pairs={{0,8},{2,10},{4,12},{6,14},{8,16},{10,18},{12,20},{14,22},{16,24},... | collective-permute-start | bytes 4325384 | tf_op jit(solution)/shard_map/ppermute | solution.py:36
  927.9 47.5 %shard_map.274 = (bf16[2048,768]{1,0:T(8,128)(2,1)}, f32[2,16,768]{2,1,0:T(8,128)S(1)}, f32[2,16,768]{2,1,0:T(8,128)S(1)}, f32[4,8,384]{2,1,0:T(8,128)S(1)}, bf16[2048,256]{1,0:T(8,128)(2,1)S(1)}) custom-call(s32[2]{0:T(128)S(1)} %add_subtract_fusion.limit_ref, bf16[2048,768]{1,0:T(8,128)(2,1)} %copy-done.14, bf16[2,16,768]{2,1,0:T(8,128)(2,1)S(1)} %copy-done.7, ...), custom_call_target="tpu_custom_call" | custom-call | tf_op jit(solution)/shard_map/pallas_call | solution.py:577
  986.7 15.1 %fusion.10 = f32[2048,2048]{1,0:T(8,128)} fusion(bf16[2048,2]{1,0:T(8,128)(2,1)} %copy-done.41, bf16[2048,768]{1,0:T(8,128)(2,1)} %bitcast.423, bf16[2048,2]{1,0:T(8,128)(2,1)} %slice.338, bf16[2048,768]{1,0:T(8,128)(2,1)} %bitcast.474), kind=kOutput, calls=%fused_computation.40 | convolution fusion | flops 7538212864 | bytes 23085056 | tf_op jit(solution)/shard_map/rc,dc->rd/dot_general | solution.py:156
  1001.9 11.4 add_convert_fusion
  1024.7 7.8 dynamic_update_slice.229
  1037.6 7.6 dynamic_update_slice.230
  1045.3 8.6 dynamic_update_slice.231
  1053.9 8.6 dynamic_update_slice.232
  1079.2 7.3 fusion.19
  1124.7 11.5 convolution_convert_fusion.4
  1167.8 10.6 collective-permute-done.86
  1196.5 10.9 collective-permute-done.87
  1261.3 7.7 collective-permute-done.91
  (701 shorter events, 662.4 us)
Async XLA Ops:
  6.6 36.0 %collective-permute-start.1 = (bf16[256,2048]{0,1:T(8,128)(2,1)S(1)}, bf16[256,2048]{0,1:T(8,128)(2,1)}, u32[]{:S(2)}, u32[]{:S(2)}) collective-permute-start(bf16[256,2048]{0,1:T(8,128)(2,1)S(1)} %bitcast.381), channel_id=1, source_target_pairs={{0,4},{2,6},{4,0},{6,2},{8,12},{10,14},{12,8},{14,10},{16,20},{18,... | collective-permute-start | bytes 3145736 | tf_op jit(solution)/shard_map/ppermute | solution.py:25
  9.6 35.5 %collective-permute-start = (bf16[256,2048]{0,1:T(8,128)(2,1)S(1)}, bf16[256,2048]{0,1:T(8,128)(2,1)}, u32[]{:S(2)}, u32[]{:S(2)}) collective-permute-start(bf16[256,2048]{0,1:T(8,128)(2,1)S(1)} %bitcast.382), channel_id=1, source_target_pairs={{0,2},{2,0},{4,6},{6,4},{8,10},{10,8},{12,14},{14,12},{16,18},{18,... | collective-permute-start | bytes 3145736 | tf_op jit(solution)/shard_map/ppermute | solution.py:25
  26.3 39.7 %collective-permute-start.6 = (bf16[136,768]{1,0:T(8,128)(2,1)}, bf16[136,768]{1,0:T(8,128)(2,1)}, u32[]{:S(2)}, u32[]{:S(2)}) collective-permute-start(bf16[136,768]{1,0:T(8,128)(2,1)} %bitcast.459), channel_id=1, source_target_pairs={{0,4},{2,6},{4,0},{6,2},{8,12},{10,14},{12,8},{14,10},{16,20},{18,... | collective-permute-start | bytes 626696 | tf_op jit(solution)/shard_map/ppermute | solution.py:25
  28.2 39.4 %collective-permute-start.7 = (bf16[136,768]{1,0:T(8,128)(2,1)}, bf16[136,768]{1,0:T(8,128)(2,1)}, u32[]{:S(2)}, u32[]{:S(2)}) collective-permute-start(bf16[136,768]{1,0:T(8,128)(2,1)} %bitcast.458), channel_id=1, source_target_pairs={{0,6},{2,4},{4,2},{6,0},{8,14},{10,12},{12,10},{14,8},{16,22},{18,... | collective-permute-start | bytes 626696 | tf_op jit(solution)/shard_map/ppermute | solution.py:25
  66.0 111.8 %collective-permute-start.4 = (bf16[1024,2048]{1,0:T(8,128)(2,1)}, bf16[1024,2048]{1,0:T(8,128)(2,1)}, u32[]{:S(2)}, u32[]{:S(2)}) collective-permute-start(bf16[1024,2048]{1,0:T(8,128)(2,1)} %bitcast.4), channel_id=1, source_target_pairs={{0,1},{1,0},{2,3},{3,2},{4,5},{5,4},{6,7},{7,6},{8,9},{9,8},{10,11... | collective-permute-start | bytes 12582920 | tf_op jit(solution)/shard_map/ppermute | solution.py:20
  92.7 41.4 %collective-permute-start.10 = (bf16[4,136,768]{2,1,0:T(8,128)(2,1)S(1)}, bf16[4,136,768]{2,1,0:T(8,128)(2,1)}, u32[]{:S(2)}, u32[]{:S(2)}) collective-permute-start(bf16[4,136,768]{2,1,0:T(8,128)(2,1)S(1)} %collective-permute-done.9), channel_id=1, source_target_pairs={{8,0},{10,2},{12,4},{14,6},{16,8},{18,10},{20,12},{22,14},{24,16},... | collective-permute-start | bytes 2506760 | tf_op jit(solution)/shard_map/ppermute | solution.py:36
  105.3 40.6 %collective-permute-start.12 = (bf16[4,136,768]{2,1,0:T(8,128)(2,1)}, bf16[4,136,768]{2,1,0:T(8,128)(2,1)}, u32[]{:S(2)}, u32[]{:S(2)}) collective-permute-start(bf16[4,136,768]{2,1,0:T(8,128)(2,1)} %collective-permute-done.8), channel_id=1, source_target_pairs={{0,8},{2,10},{4,12},{6,14},{8,16},{10,18},{12,20},{14,22},{16,24},... | collective-permute-start | bytes 2506760 | tf_op jit(solution)/shard_map/ppermute | solution.py:36
  140.7 113.1 %collective-permute-start.26 = (bf16[4,128,512]{2,1,0:T(8,128)(2,1)}, bf16[4,128,512]{2,1,0:T(8,128)(2,1)}, u32[]{:S(2)}, u32[]{:S(2)}) collective-permute-start(bf16[4,128,512]{2,1,0:T(8,128)(2,1)} %collective-permute-done.25), channel_id=1, source_target_pairs={{0,8},{2,10},{4,12},{6,14},{8,16},{10,18},{12,20},{14,22},{16,24},... | collective-permute-start | bytes 1572872 | tf_op jit(solution)/shard_map/ppermute | solution.py:36
  295.4 42.2 %collective-permute-start.46 = (bf16[128,704]{0,1:T(8,128)(2,1)}, bf16[128,704]{0,1:T(8,128)(2,1)}, u32[]{:S(2)}, u32[]{:S(2)}) collective-permute-start(bf16[128,704]{0,1:T(8,128)(2,1)} %get-tuple-element.234), channel_id=1, source_target_pairs={{0,2},{2,0},{4,6},{6,4},{8,10},{10,8},{12,14},{14,12},{16,18},{18,... | collective-permute-start | bytes 540680 | tf_op jit(solution)/shard_map/ppermute | solution.py:25
  297.2 42.1 %collective-permute-start.47 = (bf16[128,704]{0,1:T(8,128)(2,1)}, bf16[128,704]{0,1:T(8,128)(2,1)}, u32[]{:S(2)}, u32[]{:S(2)}) collective-permute-start(bf16[128,704]{0,1:T(8,128)(2,1)} %get-tuple-element.233), channel_id=1, source_target_pairs={{0,4},{2,6},{4,0},{6,2},{8,12},{10,14},{12,8},{14,10},{16,20},{18,... | collective-permute-start | bytes 540680 | tf_op jit(solution)/shard_map/ppermute | solution.py:25
  298.5 43.4 %collective-permute-start.48 = (bf16[128,704]{0,1:T(8,128)(2,1)}, bf16[128,704]{0,1:T(8,128)(2,1)}, u32[]{:S(2)}, u32[]{:S(2)}) collective-permute-start(bf16[128,704]{0,1:T(8,128)(2,1)} %get-tuple-element.232), channel_id=1, source_target_pairs={{0,6},{2,4},{4,2},{6,0},{8,14},{10,12},{12,10},{14,8},{16,22},{18,... | collective-permute-start | bytes 540680 | tf_op jit(solution)/shard_map/ppermute | solution.py:25
  315.1 59.4 %collective-permute-start.30 = (bf16[256,1024]{0,1:T(8,128)(2,1)}, bf16[256,1024]{0,1:T(8,128)(2,1)}, u32[]{:S(2)}, u32[]{:S(2)}) collective-permute-start(bf16[256,1024]{0,1:T(8,128)(2,1)} %get-tuple-element.221), channel_id=1, source_target_pairs={{0,2},{2,0},{4,6},{6,4},{8,10},{10,8},{12,14},{14,12},{16,18},{18,... | collective-permute-start | bytes 1572872 | tf_op jit(solution)/shard_map/ppermute | solution.py:25
  322.2 56.1 %collective-permute-start.28 = (bf16[256,1024]{0,1:T(8,128)(2,1)}, bf16[256,1024]{0,1:T(8,128)(2,1)}, u32[]{:S(2)}, u32[]{:S(2)}) collective-permute-start(bf16[256,1024]{0,1:T(8,128)(2,1)} %get-tuple-element.220), channel_id=1, source_target_pairs={{0,4},{2,6},{4,0},{6,2},{8,12},{10,14},{12,8},{14,10},{16,20},{18,... | collective-permute-start | bytes 1572872 | tf_op jit(solution)/shard_map/ppermute | solution.py:25
  337.6 84.0 %collective-permute-start.61 = (bf16[256,2048]{0,1:T(8,128)(2,1)}, bf16[256,2048]{0,1:T(8,128)(2,1)}, u32[]{:S(2)}, u32[]{:S(2)}) collective-permute-start(bf16[256,2048]{0,1:T(8,128)(2,1)} %bitcast.84), channel_id=1, source_target_pairs={{0,2},{2,0},{4,6},{6,4},{8,10},{10,8},{12,14},{14,12},{16,18},{18,... | collective-permute-start | bytes 3145736 | tf_op jit(solution)/shard_map/ppermute | solution.py:25
  339.4 84.1 %collective-permute-start.62 = (bf16[256,2048]{0,1:T(8,128)(2,1)}, bf16[256,2048]{0,1:T(8,128)(2,1)}, u32[]{:S(2)}, u32[]{:S(2)}) collective-permute-start(bf16[256,2048]{0,1:T(8,128)(2,1)} %bitcast.84), channel_id=1, source_target_pairs={{0,4},{2,6},{4,0},{6,2},{8,12},{10,14},{12,8},{14,10},{16,20},{18,... | collective-permute-start | bytes 3145736 | tf_op jit(solution)/shard_map/ppermute | solution.py:25
  341.9 38.4 %collective-permute-start.37 = (bf16[128,1408]{1,0:T(8,128)(2,1)}, bf16[128,1408]{1,0:T(8,128)(2,1)}, u32[]{:S(2)}, u32[]{:S(2)}) collective-permute-start(bf16[128,1408]{1,0:T(8,128)(2,1)} %bitcast.452), channel_id=1, source_target_pairs={{0,2},{2,0},{4,6},{6,4},{8,10},{10,8},{12,14},{14,12},{16,18},{18,... | collective-permute-start | bytes 1081352 | tf_op jit(solution)/shard_map/ppermute | solution.py:25
  378.3 36.8 %collective-permute-start.31 = (bf16[256,2048]{0,1:T(8,128)(2,1)}, bf16[256,2048]{0,1:T(8,128)(2,1)}, u32[]{:S(2)}, u32[]{:S(2)}) collective-permute-start(bf16[256,2048]{0,1:T(8,128)(2,1)} %pad_maximum_fusion.13), channel_id=1, source_target_pairs={{0,4},{2,6},{4,0},{6,2},{8,12},{10,14},{12,8},{14,10},{16,20},{18,... | collective-permute-start | bytes 3145736 | tf_op jit(solution)/shard_map/ppermute | solution.py:25
  380.3 36.0 %collective-permute-start.29 = (bf16[256,2048]{0,1:T(8,128)(2,1)S(1)}, bf16[256,2048]{0,1:T(8,128)(2,1)}, u32[]{:S(2)}, u32[]{:S(2)}) collective-permute-start(bf16[256,2048]{0,1:T(8,128)(2,1)S(1)} %pad_maximum_fusion.12), channel_id=1, source_target_pairs={{0,2},{2,0},{4,6},{6,4},{8,10},{10,8},{12,14},{14,12},{16,18},{18,... | collective-permute-start | bytes 3145736 | tf_op jit(solution)/shard_map/ppermute | solution.py:25
  415.0 44.2 %collective-permute-start.41 = (bf16[4,128,1408]{2,1,0:T(8,128)(2,1)}, bf16[4,128,1408]{2,1,0:T(8,128)(2,1)S(1)}, u32[]{:S(2)}, u32[]{:S(2)}) collective-permute-start(bf16[4,128,1408]{2,1,0:T(8,128)(2,1)} %bitcast_dynamic-update-slice_fusion.19), channel_id=1, source_target_pairs={{8,0},{10,2},{12,4},{14,6},{16,8},{18,10},{20,12},{22,14},{24,16},... | collective-permute-start | bytes 4325384 | tf_op jit(solution)/shard_map/ppermute | solution.py:36
  421.2 39.3 %collective-permute-start.32 = (bf16[256,2048]{0,1:T(8,128)(2,1)S(1)}, bf16[256,2048]{0,1:T(8,128)(2,1)S(1)}, u32[]{:S(2)}, u32[]{:S(2)}) collective-permute-start(bf16[256,2048]{0,1:T(8,128)(2,1)S(1)} %get-tuple-element.157), channel_id=1, source_target_pairs={{0,2},{2,0},{4,6},{6,4},{8,10},{10,8},{12,14},{14,12},{16,18},{18,... | collective-permute-start | bytes 3145736 | tf_op jit(solution)/shard_map/ppermute | solution.py:25
  432.7 52.9 %collective-permute-start.40 = (bf16[4,128,1408]{2,1,0:T(8,128)(2,1)}, bf16[4,128,1408]{2,1,0:T(8,128)(2,1)S(1)}, u32[]{:S(2)}, u32[]{:S(2)}) collective-permute-start(bf16[4,128,1408]{2,1,0:T(8,128)(2,1)} %bitcast_dynamic-update-slice_fusion.19), channel_id=1, source_target_pairs={{0,8},{2,10},{4,12},{6,14},{8,16},{10,18},{12,20},{14,22},{16,24},... | collective-permute-start | bytes 4325384 | tf_op jit(solution)/shard_map/ppermute | solution.py:36
  436.3 45.7 %collective-permute-start.33 = (bf16[256,2048]{0,1:T(8,128)(2,1)S(1)}, bf16[256,2048]{0,1:T(8,128)(2,1)S(1)}, u32[]{:S(2)}, u32[]{:S(2)}) collective-permute-start(bf16[256,2048]{0,1:T(8,128)(2,1)S(1)} %get-tuple-element.157), channel_id=1, source_target_pairs={{0,4},{2,6},{4,0},{6,2},{8,12},{10,14},{12,8},{14,10},{16,20},{18,... | collective-permute-start | bytes 3145736 | tf_op jit(solution)/shard_map/ppermute | solution.py:25
  460.5 46.1 %collective-permute-start.42 = (bf16[4,128,1408]{2,1,0:T(8,128)(2,1)S(1)}, bf16[4,128,1408]{2,1,0:T(8,128)(2,1)}, u32[]{:S(2)}, u32[]{:S(2)}) collective-permute-start(bf16[4,128,1408]{2,1,0:T(8,128)(2,1)S(1)} %collective-permute-done.41), channel_id=1, source_target_pairs={{8,0},{10,2},{12,4},{14,6},{16,8},{18,10},{20,12},{22,14},{24,16},... | collective-permute-start | bytes 4325384 | tf_op jit(solution)/shard_map/ppermute | solution.py:36
  482.0 104.9 %collective-permute-start.65 = (bf16[1024,2048]{0,1:T(8,128)(2,1)}, bf16[1024,2048]{0,1:T(8,128)(2,1)}, u32[]{:S(2)}, u32[]{:S(2)}) collective-permute-start(bf16[1024,2048]{0,1:T(8,128)(2,1)} %maximum_maximum_fusion.1), channel_id=1, source_target_pairs={{0,1},{1,0},{2,3},{3,2},{4,5},{5,4},{6,7},{7,6},{8,9},{9,8},{10,11... | collective-permute-start | bytes 12582920 | tf_op jit(solution)/shard_map/ppermute | solution.py:20
  485.6 44.8 %collective-permute-start.53 = (bf16[4,128,704]{1,0,2:T(4,128)(2,1)S(1)}, bf16[4,128,704]{1,0,2:T(4,128)(2,1)S(1)}, u32[]{:S(2)}, u32[]{:S(2)}) collective-permute-start(bf16[4,128,704]{1,0,2:T(4,128)(2,1)S(1)} %collective-permute-done.49), channel_id=1, source_target_pairs={{0,8},{2,10},{4,12},{6,14},{8,16},{10,18},{12,20},{14,22},{16,24},... | collective-permute-start | bytes 2162696 | tf_op jit(solution)/shard_map/ppermute | solution.py:36
  513.6 48.6 %collective-permute-start.43 = (bf16[4,128,1408]{2,1,0:T(8,128)(2,1)}, bf16[4,128,1408]{2,1,0:T(8,128)(2,1)}, u32[]{:S(2)}, u32[]{:S(2)}) collective-permute-start(bf16[4,128,1408]{2,1,0:T(8,128)(2,1)} %collective-permute-done.42), channel_id=1, source_target_pairs={{8,0},{10,2},{12,4},{14,6},{16,8},{18,10},{20,12},{22,14},{24,16},... | collective-permute-start | bytes 4325384 | tf_op jit(solution)/shard_map/ppermute | solution.py:36
  530.4 65.5 %collective-permute-start.36 = (bf16[1024,2048]{0,1:T(8,128)(2,1)}, bf16[1024,2048]{0,1:T(8,128)(2,1)}, u32[]{:S(2)}, u32[]{:S(2)}) collective-permute-start(bf16[1024,2048]{0,1:T(8,128)(2,1)} %maximum_maximum_fusion), channel_id=1, source_target_pairs={{0,1},{1,0},{2,3},{3,2},{4,5},{5,4},{6,7},{7,6},{8,9},{9,8},{10,11... | collective-permute-start | bytes 12582920 | tf_op jit(solution)/shard_map/ppermute | solution.py:20
  540.2 43.9 %collective-permute-start.45 = (bf16[4,128,1408]{2,1,0:T(8,128)(2,1)}, bf16[4,128,1408]{2,1,0:T(8,128)(2,1)}, u32[]{:S(2)}, u32[]{:S(2)}) collective-permute-start(bf16[4,128,1408]{2,1,0:T(8,128)(2,1)} %collective-permute-done.44), channel_id=1, source_target_pairs={{0,8},{2,10},{4,12},{6,14},{8,16},{10,18},{12,20},{14,22},{16,24},... | collective-permute-start | bytes 4325384 | tf_op jit(solution)/shard_map/ppermute | solution.py:36
  698.1 42.3 %collective-permute-start.59 = (bf16[256,2048]{0,1:T(8,128)(2,1)}, bf16[256,2048]{0,1:T(8,128)(2,1)}, u32[]{:S(2)}, u32[]{:S(2)}) collective-permute-start(bf16[256,2048]{0,1:T(8,128)(2,1)} %pad_maximum_fusion.15), channel_id=1, source_target_pairs={{0,4},{2,6},{4,0},{6,2},{8,12},{10,14},{12,8},{14,10},{16,20},{18,... | collective-permute-start | bytes 3145736 | tf_op jit(solution)/shard_map/ppermute | solution.py:25
  700.4 40.3 %collective-permute-start.57 = (bf16[256,2048]{0,1:T(8,128)(2,1)}, bf16[256,2048]{0,1:T(8,128)(2,1)}, u32[]{:S(2)}, u32[]{:S(2)}) collective-permute-start(bf16[256,2048]{0,1:T(8,128)(2,1)} %pad_maximum_fusion.14), channel_id=1, source_target_pairs={{0,2},{2,0},{4,6},{6,4},{8,10},{10,8},{12,14},{14,12},{16,18},{18,... | collective-permute-start | bytes 3145736 | tf_op jit(solution)/shard_map/ppermute | solution.py:25
  767.4 46.9 %collective-permute-start.105 = (bf16[4,128,1408]{2,1,0:T(8,128)(2,1)}, bf16[4,128,1408]{2,1,0:T(8,128)(2,1)}, u32[]{:S(2)}, u32[]{:S(2)}) collective-permute-start(bf16[4,128,1408]{2,1,0:T(8,128)(2,1)} %dynamic-slice_bitcast_fusion), channel_id=1, source_target_pairs={{0,8},{2,10},{4,12},{6,14},{1,9},{3,11},{5,13},{7,15}} | collective-permute-start | bytes 4325384 | tf_op jit(solution)/shard_map/ppermute | solution.py:36
  791.3 72.3 %collective-permute-start.75 = (bf16[1024,2048]{1,0:T(8,128)(2,1)}, bf16[1024,2048]{1,0:T(8,128)(2,1)}, u32[]{:S(2)}, u32[]{:S(2)}) collective-permute-start(bf16[1024,2048]{1,0:T(8,128)(2,1)} %bitcast.418), channel_id=1, source_target_pairs={{0,1},{1,0},{2,3},{3,2},{4,5},{5,4},{6,7},{7,6},{8,9},{9,8},{10,11... | collective-permute-start | bytes 12582920 | tf_op jit(solution)/shard_map/ppermute | solution.py:20
  816.0 44.8 %collective-permute-start.106 = (bf16[4,128,1408]{2,1,0:T(8,128)(2,1)S(1)}, bf16[4,128,1408]{2,1,0:T(8,128)(2,1)S(1)}, u32[]{:S(2)}, u32[]{:S(2)}) collective-permute-start(bf16[4,128,1408]{2,1,0:T(8,128)(2,1)S(1)} %fusion.15), channel_id=1, source_target_pairs={{0,8},{2,10},{4,12},{6,14},{8,16},{10,18},{12,20},{14,22},{1,9},{3... | collective-permute-start | bytes 4325384 | tf_op jit(solution)/shard_map/ppermute | solution.py:36
  831.0 55.8 %collective-permute-start.115 = (bf16[4,128,704]{1,2,0:T(8,128)(2,1)S(1)}, bf16[4,128,704]{1,2,0:T(8,128)(2,1)}, u32[]{:S(2)}, u32[]{:S(2)}) collective-permute-start(bf16[4,128,704]{1,2,0:T(8,128)(2,1)S(1)} %get-tuple-element.230), channel_id=1, source_target_pairs={{0,8},{2,10},{4,12},{6,14},{8,16},{10,18},{12,20},{14,22},{1,9},{3... | collective-permute-start | bytes 2162696 | tf_op jit(solution)/shard_map/ppermute | solution.py:36
  837.0 70.8 %collective-permute-start.119 = (bf16[4,128,704]{1,2,0:T(8,128)(2,1)S(1)}, bf16[4,128,704]{1,2,0:T(8,128)(2,1)}, u32[]{:S(2)}, u32[]{:S(2)}) collective-permute-start(bf16[4,128,704]{1,2,0:T(8,128)(2,1)S(1)} %add_convert_fusion.10), channel_id=1, source_target_pairs={{8,0},{10,2},{12,4},{14,6},{16,8},{18,10},{20,12},{22,14},{24,16},... | collective-permute-start | bytes 2162696 | tf_op jit(solution)/shard_map/ppermute | solution.py:36
  862.8 114.0 %collective-permute-start.108 = (bf16[4,128,1408]{2,1,0:T(8,128)(2,1)}, bf16[4,128,1408]{2,1,0:T(8,128)(2,1)S(1)}, u32[]{:S(2)}, u32[]{:S(2)}) collective-permute-start(bf16[4,128,1408]{2,1,0:T(8,128)(2,1)} %get-tuple-element.151), channel_id=1, source_target_pairs={{24,16},{26,18},{28,20},{30,22},{25,17},{27,19},{29,21},{31,23}} | collective-permute-start | bytes 4325384 | tf_op jit(solution)/shard_map/ppermute | solution.py:36
  910.7 111.2 %collective-permute-start.120 = (bf16[128,704]{0,1:T(8,128)(2,1)}, bf16[128,704]{0,1:T(8,128)(2,1)}, u32[]{:S(2)}, u32[]{:S(2)}) collective-permute-start(bf16[128,704]{0,1:T(8,128)(2,1)} %get-tuple-element.228), channel_id=1, source_target_pairs={{0,2},{2,0},{4,6},{6,4},{8,10},{10,8},{12,14},{14,12},{16,18},{18,... | collective-permute-start | bytes 540680 | tf_op jit(solution)/shard_map/ppermute | solution.py:25
  911.9 111.2 %collective-permute-start.121 = (bf16[128,704]{0,1:T(8,128)(2,1)}, bf16[128,704]{0,1:T(8,128)(2,1)}, u32[]{:S(2)}, u32[]{:S(2)}) collective-permute-start(bf16[128,704]{0,1:T(8,128)(2,1)} %get-tuple-element.227), channel_id=1, source_target_pairs={{0,4},{2,6},{4,0},{6,2},{8,12},{10,14},{12,8},{14,10},{16,20},{18,... | collective-permute-start | bytes 540680 | tf_op jit(solution)/shard_map/ppermute | solution.py:25
  913.1 157.6 %collective-permute-start.107 = (bf16[4,128,1408]{2,1,0:T(8,128)(2,1)}, bf16[4,128,1408]{2,1,0:T(8,128)(2,1)}, u32[]{:S(2)}, u32[]{:S(2)}) collective-permute-start(bf16[4,128,1408]{2,1,0:T(8,128)(2,1)} %get-tuple-element.150), channel_id=1, source_target_pairs={{0,8},{2,10},{4,12},{6,14},{8,16},{10,18},{12,20},{14,22},{16,24},... | collective-permute-start | bytes 4325384 | tf_op jit(solution)/shard_map/ppermute | solution.py:36
  979.7 38.3 %collective-permute-start.109 = (bf16[4,128,1408]{2,1,0:T(8,128)(2,1)}, bf16[4,128,1408]{2,1,0:T(8,128)(2,1)}, u32[]{:S(2)}, u32[]{:S(2)}) collective-permute-start(bf16[4,128,1408]{2,1,0:T(8,128)(2,1)} %fusion.16), channel_id=1, source_target_pairs={{16,8},{18,10},{20,12},{22,14},{24,16},{26,18},{28,20},{30,22},{17... | collective-permute-start | bytes 4325384 | tf_op jit(solution)/shard_map/ppermute | solution.py:36
  986.1 77.7 %collective-permute-start.60 = (bf16[256,2048]{0,1:T(8,128)(2,1)S(1)}, bf16[256,2048]{0,1:T(8,128)(2,1)}, u32[]{:S(2)}, u32[]{:S(2)}) collective-permute-start(bf16[256,2048]{0,1:T(8,128)(2,1)S(1)} %copy-done.28), channel_id=1, source_target_pairs={{0,1},{1,0},{2,3},{3,2},{4,5},{5,4},{6,7},{7,6},{8,9},{9,8},{10,11... | collective-permute-start | bytes 3145736 | tf_op jit(solution)/shard_map/ppermute | solution.py:20
  1018.0 72.0 %collective-permute-start.80 = (bf16[1024,2048]{1,0:T(8,128)(2,1)}, bf16[1024,2048]{1,0:T(8,128)(2,1)}, u32[]{:S(2)}, u32[]{:S(2)}) collective-permute-start(bf16[1024,2048]{1,0:T(8,128)(2,1)} %slice.413), channel_id=1, source_target_pairs={{0,1},{1,0},{2,3},{3,2},{4,5},{5,4},{6,7},{7,6},{8,9},{9,8},{10,11... | collective-permute-start | bytes 12582920 | tf_op jit(solution)/shard_map/ppermute | solution.py:20
  1021.8 48.8 %collective-permute-start.110 = (bf16[4,128,1408]{2,1,0:T(8,128)(2,1)}, bf16[4,128,1408]{2,1,0:T(8,128)(2,1)}, u32[]{:S(2)}, u32[]{:S(2)}) collective-permute-start(bf16[4,128,1408]{2,1,0:T(8,128)(2,1)} %add_convert_fusion.5), channel_id=1, source_target_pairs={{8,0},{10,2},{12,4},{14,6},{16,8},{18,10},{20,12},{22,14},{24,16},... | collective-permute-start | bytes 4325384 | tf_op jit(solution)/shard_map/ppermute | solution.py:36
  1075.7 78.6 %collective-permute-start.111 = (bf16[128,1408]{1,0:T(8,128)(2,1)}, bf16[128,1408]{1,0:T(8,128)(2,1)}, u32[]{:S(2)}, u32[]{:S(2)}) collective-permute-start(bf16[128,1408]{1,0:T(8,128)(2,1)} %get-tuple-element.209), channel_id=1, source_target_pairs={{0,2},{2,0},{4,6},{6,4},{8,10},{10,8},{12,14},{14,12},{16,18},{18,... | collective-permute-start | bytes 1081352 | tf_op jit(solution)/shard_map/ppermute | solution.py:25
  1077.3 81.8 %collective-permute-start.112 = (bf16[128,1408]{1,0:T(8,128)(2,1)}, bf16[128,1408]{1,0:T(8,128)(2,1)}, u32[]{:S(2)}, u32[]{:S(2)}) collective-permute-start(bf16[128,1408]{1,0:T(8,128)(2,1)} %get-tuple-element.208), channel_id=1, source_target_pairs={{0,4},{2,6},{4,0},{6,2},{8,12},{10,14},{12,8},{14,10},{16,20},{18,... | collective-permute-start | bytes 1081352 | tf_op jit(solution)/shard_map/ppermute | solution.py:25
  1078.2 106.1 %collective-permute-start.113 = (bf16[128,1408]{1,0:T(8,128)(2,1)}, bf16[128,1408]{1,0:T(8,128)(2,1)}, u32[]{:S(2)}, u32[]{:S(2)}) collective-permute-start(bf16[128,1408]{1,0:T(8,128)(2,1)} %get-tuple-element.207), channel_id=1, source_target_pairs={{0,6},{2,4},{4,2},{6,0},{8,14},{10,12},{12,10},{14,8},{16,22},{18,... | collective-permute-start | bytes 1081352 | tf_op jit(solution)/shard_map/ppermute | solution.py:25
  1188.6 38.0 %collective-permute-start.101 = (bf16[4,128,512]{2,1,0:T(8,128)(2,1)}, bf16[4,128,512]{2,1,0:T(8,128)(2,1)}, u32[]{:S(2)}, u32[]{:S(2)}) collective-permute-start(bf16[4,128,512]{2,1,0:T(8,128)(2,1)} %add_convert_fusion.12), channel_id=1, source_target_pairs={{8,0},{10,2},{12,4},{14,6},{16,8},{18,10},{20,12},{22,14},{24,16},... | collective-permute-start | bytes 1572872 | tf_op jit(solution)/shard_map/ppermute | solution.py:36
  1191.1 35.5 %collective-permute-start.98 = (bf16[4,128,512]{2,1,0:T(8,128)(2,1)}, bf16[4,128,512]{2,1,0:T(8,128)(2,1)}, u32[]{:S(2)}, u32[]{:S(2)}) collective-permute-start(bf16[4,128,512]{2,1,0:T(8,128)(2,1)} %add_convert_fusion.13), channel_id=1, source_target_pairs={{0,8},{2,10},{4,12},{6,14},{8,16},{10,18},{12,20},{14,22},{16,24},... | collective-permute-start | bytes 1572872 | tf_op jit(solution)/shard_map/ppermute | solution.py:36
  (158 other events, 2993.5 us)

commit v3 on v2

--- a/solution.py
+++ b/solution.py
@@ -1,13 +1,16 @@
+import functools
+
 import jax
 import jax.numpy as jnp
 from jax import lax
 from jax.experimental import pallas as pl
+from jax.experimental.layout import Layout, with_layout_constraint
 from jax.experimental.pallas import tpu as pltpu
 from jax.sharding import PartitionSpec as P
 
 CONV = 4
 MATES = 4
-SMALL = 8
+SMALL = 16
 
 
 PRECISE = lax.Precision.HIGHEST
@@ -36,6 +39,10 @@
     return lax.ppermute(value, "seq", pairs)
 
 
+def row_major(value):
+    return with_layout_constraint(value, Layout(major_to_minor=tuple(range(value.ndim))))
+
+
 def mate_of():
     return lax.axis_index("seq") % MATES
 
@@ -55,7 +62,7 @@
 
 def in_order(by_flip):
     mate = mate_of()
-    out = jnp.zeros((MATES,) + by_flip[0].shape, by_flip[0].dtype)
+    out = row_major(jnp.zeros((MATES,) + by_flip[0].shape, by_flip[0].dtype))
     for flip, piece in enumerate(by_flip):
         out = lax.dynamic_update_index_in_dim(out, piece, mate ^ flip, 0)
     return out
@@ -67,29 +74,6 @@
     for flip in range(1, MATES):
         pieces.append(to_mate(pick(blocks, mate ^ flip), flip))
     return in_order(pieces)
-
-
-def gather_mates(value):
-    half = value.shape[-1] // 2
-    from_x = to_mate(value, 1)
-    from_y = to_mate(value, 2)
-    far = jnp.concatenate(
-        [to_mate(from_x[..., :half], 2), to_mate(from_y[..., half:], 1)], axis=-1
-    )
-    return [value, from_x, from_y, far]
-
-
-def scatter_mates(blocks):
-    half = blocks[0].shape[-1] // 2
-    far_y = to_mate(blocks[3][..., :half], 2)
-    far_x = to_mate(blocks[3][..., half:], 1)
-    for_x = jnp.concatenate(
-        [(blocks[1][..., :half].astype(wide) + far_y.astype(wide)).astype(low), blocks[1][..., half:]], axis=-1
-    )
-    for_y = jnp.concatenate(
-        [blocks[2][..., :half], (blocks[2][..., half:].astype(wide) + far_x.astype(wide)).astype(low)], axis=-1
-    )
-    return blocks[0].astype(wide) + to_mate(for_x, 1).astype(wide) + to_mate(for_y, 2).astype(wide)
 
 
 def gather_lines(block):
@@ -165,15 +149,6 @@
     return lax.rsqrt(jnp.mean(value * value, axis=-1, keepdims=True) + epsilon)
 
 
-def norm_back(grad_normed, source, inverse, scale):
-    scaled = grad_normed * scale
-    gain_grad = jnp.sum(grad_normed * source * inverse, axis=0)
-    source_grad = inverse * (
-        scaled - source * inverse * inverse * jnp.mean(scaled * source, axis=-1, keepdims=True)
-    )
-    return (source_grad, gain_grad)
-
-
 CHUNK = 128
 TOGETHER = 4
 VMEM_BYTES = 52 * 1024 * 1024
@@ -270,6 +245,12 @@
 def live_rows(limit, start):
     rows = lax.broadcasted_iota(jnp.int32, (CHUNK, CHUNK), 0)
     return jnp.where(rows + start < limit, 1.0, 0.0).astype(wide)
+
+
+def head_squash(logits, head):
+    lanes = lax.broadcasted_iota(jnp.int32, logits.shape, 1)
+    column = jnp.sum(jnp.where(lanes == head, logits, 0.0), axis=1, keepdims=True)
+    return jax.nn.sigmoid(jnp.broadcast_to(column, logits.shape))
 
 
 def write_extended(ext, tail_ref, raw_ref):
@@ -306,7 +287,7 @@
             query = (query * head_size ** (-0.5)).astype(low)
             key = key * lax.rsqrt(jnp.sum(key * key, axis=1, keepdims=True) + epsilon)
             key = key.astype(low)
-            beta = jax.nn.sigmoid(logit_ref[pl.ds(start, CHUNK)]) * live_rows(limit, start)
+            beta = head_squash(logit_ref[pl.ds(start, CHUNK)], head) * live_rows(limit, start)
             qkv_ref[pl.ds(start, CHUNK)] = jnp.concatenate([query, key, value], axis=1)
             parts.append((key, value, beta))
         strict = [
@@ -445,7 +426,7 @@
 
 def unwind_kernel(
     limit_ref, raw_ref, tail_ref, taps_ref, logit_ref, qkv_ref, solved_ref, wu_ref, state_ref,
-    fresh_in_ref, out_ref, fresh_grad_ref, maps_ref, sources_ref, leave_ref,
+    fresh_in_ref, out_ref, fresh_grad_ref, maps_ref, sources_ref, leave_ref, all_grads_ref,
     raw_grad_ref, edge_ref, halo_ref, taps_grad_ref, logit_grad_ref,
     ext, pre_grads, leaving,
 ):
@@ -485,7 +466,7 @@
         key = qkv_ref[here, head_size : 2 * head_size]
         value = qkv_ref[here, 2 * head_size :]
         live = live_rows(limit, start)
-        squash = jax.nn.sigmoid(logit_ref[here])
+        squash = head_squash(logit_ref[here], head)
         beta = squash * live
         grads = pair(out_ref[0, chunk])
         fresh = pair(fresh_in_ref[0, chunk])
@@ -516,7 +497,19 @@
             axis=1,
             keepdims=True,
         )
-        logit_grad_ref[here] = (beta_grad * (live * squash * (1.0 - squash))).astype(low)
+        lanes = lax.broadcasted_iota(jnp.int32, (CHUNK, head_size), 1)
+        logit_grad = jnp.where(
+            lanes == head, beta_grad * (live * squash * (1.0 - squash)), 0.0
+        ).astype(low)
+
+        @pl.when(head == 0)
+        def _():
+            logit_grad_ref[here] = logit_grad
+
+        @pl.when(head > 0)
+        def _():
+            logit_grad_ref[here] = logit_grad_ref[here] + logit_grad
+
 
         block = ext[pl.ds(start, CHUNK + 16)]
         grads_pre = []
@@ -573,7 +566,7 @@
     halo_ref[0] = halo[:16]
 
 
-def kernel_call(body, grid, ins, outs, scratch):
+def kernel_call(body, grid, ins, outs, scratch, aliases=None):
     return pl.pallas_call(
         body,
         grid=grid,
@@ -581,6 +574,7 @@
         out_specs=[spec for _, _, spec in outs],
         out_shape=[jax.ShapeDtypeStruct(shape, dtype) for shape, dtype, _ in outs],
         scratch_shapes=scratch,
+        input_output_aliases=aliases or {},
         compiler_params=pltpu.CompilerParams(
             vmem_limit_bytes=VMEM_BYTES, dimension_semantics=("arbitrary",) * len(grid)
         ),
@@ -600,6 +594,8 @@
         "edge": pl.BlockSpec((1, 16, 3 * head_size), lambda s, h: (s, 0, h)),
         "taps": pl.BlockSpec((1, 3 * CONV, head_size), lambda s, h: (h, 0, 0)),
         "one": pl.BlockSpec((span, head_size), lambda s, h: (s, h)),
+        "gate": pl.BlockSpec((span, head_size), lambda s, h: (s, 3 * heads + h)),
+        "logit": pl.BlockSpec((span, head_size), lambda s, h: (s, 0)),
         "square": pl.BlockSpec((1, chunks, CHUNK, head_size), lambda s, h: (chain(s, h), 0, 0, 0)),
         "double": pl.BlockSpec(
             (1, chunks, CHUNK, 2 * head_size), lambda s, h: (chain(s, h), 0, 0, 0)
@@ -629,10 +625,10 @@
             (raw, specs["three"]),
             (tails, specs["edge"]),
             (taps, specs["taps"]),
-            (logits, specs["one"]),
+            (logits, specs["logit"]),
         ],
         [
-            (raw.shape, low, specs["three"]),
+            ((seqs * span, 3 * heads * size), low, specs["three"]),
             (squares, wide, specs["square"]),
             ((chains, chunks, CHUNK, 2 * size), wide, specs["double"]),
             (squares, wide, specs["square"]),
@@ -661,14 +657,14 @@
             (prefix, specs["square"]),
             (local, specs["square"]),
             (enter, specs["state"]),
-            (gate, specs["one"]),
+            (gate, specs["gate"]),
             (scale, specs["scale"]),
         ],
         [
             (squares, wide, specs["square"]),
             (squares, wide, specs["square"]),
-            (gate.shape, wide, specs["one"]),
-            (gate.shape, low, specs["one"]),
+            ((seqs * span, heads * size), wide, specs["one"]),
+            ((seqs * span, heads * size), low, specs["one"]),
         ],
         [],
     )
@@ -684,7 +680,7 @@
         [
             (grad, specs["one"]),
             (mixed, specs["one"]),
-            (gate, specs["one"]),
+            (gate, specs["gate"]),
             (scale, specs["scale"]),
             (qkv, specs["three"]),
             (wu, specs["double"]),
@@ -693,7 +689,7 @@
         [
             (squares, wide, specs["square"]),
             (squares, wide, specs["square"]),
-            (gate.shape, low, specs["one"]),
+            ((seqs * span, (4 * heads + 1) * size), low, specs["gate"]),
             ((chains, 8, size), wide, specs["gain"]),
             (squares, wide, specs["square"]),
             ((chains, size, size), wide, specs["all_states"](chains, size)),
@@ -704,7 +700,7 @@
 
 def delta_unwind(
     limit, raw, tails, taps, logits, qkv, solved, wu, state, fresh, out, fresh_grad, maps,
-    sources, leave, seqs, heads, span,
+    sources, leave, all_grads, seqs, heads, span,
 ):
     specs = delta_specs(heads, span)
     chains, chunks, size = seqs * heads, span // CHUNK, CHUNK
@@ -718,7 +714,7 @@
             (raw, specs["three"]),
             (tails, specs["edge"]),
             (taps, specs["taps"]),
-            (logits, specs["one"]),
+            (logits, specs["logit"]),
             (qkv, specs["three"]),
             (solved, specs["square"]),
             (wu, specs["double"]),
@@ -729,19 +725,762 @@
             (maps, specs["all_squares"](chains)),
             (sources, specs["all_squares"](chains)),
             (leave, specs["all_states"](chains, size)),
+            (all_grads, pl.BlockSpec(memory_space=pl.ANY)),
         ],
         [
-            (raw.shape, low, specs["three"]),
+            (all_grads.shape, low, specs["three"]),
             (edges, wide, specs["edge"]),
             (edges, wide, specs["edge"]),
             ((chains, 8, 3 * size), wide, specs["tapped"]),
-            (logits.shape, low, specs["one"]),
+            (logits.shape, low, specs["logit"]),
         ],
         [
             pltpu.VMEM((span + 16, 3 * size), wide),
             pltpu.VMEM((span + 32, 3 * size), wide),
             pltpu.VMEM(squares, wide),
         ],
+        {15: 0},
+    )
+
+
+MESH = pl.DeviceIdType.MESH
+STEP = 16
+
+
+class Place:
+    def __init__(self):
+        self.seq = lax.axis_index("seq")
+        self.core = lax.axis_index("tp")
+        self.mate = self.seq % MATES
+        self.line = self.seq // MATES
+        x, y = self.mate % 2, self.mate // 2
+        self.x = 2 * y + (1 - x)
+        self.y = 2 * (1 - y) + x
+        self.far = 2 * (1 - y) + (1 - x)
+        self.base = self.seq - self.mate
+
+    def of(self, mate):
+        return (self.base + mate, self.core)
+
+    @property
+    def sibling(self):
+        return (self.seq, 1 - self.core)
+
+    def lines_away(self, step):
+        return (self.seq + step * MATES, self.core)
+
+
+def meet(place, far=False, lines=0):
+    barrier = pltpu.get_barrier_semaphore()
+    partners = [place.of(place.x), place.of(place.y), place.sibling]
+    if far:
+        partners.append(place.of(place.far))
+    for partner in partners:
+        pl.semaphore_signal(barrier, inc=1, device_id=partner, device_id_type=MESH)
+    count = len(partners)
+    if lines > 1:
+        below, above = place.line > 0, place.line < lines - 1
+
+        @pl.when(below)
+        def _():
+            pl.semaphore_signal(
+                barrier, inc=1, device_id=place.lines_away(-1), device_id_type=MESH
+            )
+
+        @pl.when(above)
+        def _():
+            pl.semaphore_signal(barrier, inc=1, device_id=place.lines_away(1), device_id_type=MESH)
+
+        count = count + jnp.where(below, 1, 0) + jnp.where(above, 1, 0)
+    pl.semaphore_wait(barrier, count)
+
+
+def sender(sems):
+    send, receive = sems
+
+    def make(index, source, target, device):
+        return pltpu.make_async_remote_copy(
+            src_ref=source,
+            dst_ref=target,
+            send_sem=send.at[index],
+            recv_sem=receive.at[index],
+            device_id=device,
+            device_id_type=MESH,
+        )
+
+    return make
+
+
+def row_steps(first, last, body):
+    def one(step, carry):
+        body(pl.ds(pl.multiple_of(first + step * STEP, STEP), STEP))
+        return carry
+
+    lax.fori_loop(0, (last - first) // STEP, one, 0)
+
+
+class SumRows:
+    SCRATCH = 4
+
+    @staticmethod
+    def scratch(rows, columns):
+        return [
+            pltpu.VMEM((MATES, rows, columns), low),
+            pltpu.VMEM((MATES, rows, columns), low),
+            pltpu.VMEM((2, rows // 2, columns), low),
+            pltpu.VMEM((2, rows, columns), low),
+            pltpu.SemaphoreType.DMA((MATES,)),
+            pltpu.SemaphoreType.DMA((10,)),
+            pltpu.SemaphoreType.DMA((10,)),
+        ]
+
+    def __init__(self, place, partial, scratch):
+        self.place, self.partial = place, partial
+        self.own, self.swapped, self.relay, self.arrived, self.local_sems, send, receive = scratch
+        self.make = sender((send, receive))
+        self.rows = self.own.shape[1]
+        self.order = [place.far, place.x, place.y, place.mate]
+
+    def begin(self):
+        self.swaps, self.loads = [], []
+        for slot, mate in enumerate(self.order):
+            copy = self.make(
+                slot, self.partial.at[1, mate], self.swapped.at[slot], self.place.sibling
+            )
+            copy.start()
+            self.swaps.append(copy)
+            load = pltpu.make_async_copy(
+                self.partial.at[0, mate], self.own.at[slot], self.local_sems.at[slot]
+            )
+            load.start()
+            self.loads.append(load)
+
+    def add(self, target, target_slot, source, source_slot, first, last, shift=0):
+        def body(here):
+            there = pl.ds(pl.multiple_of(here.start - shift, STEP), STEP) if shift else here
+            target[target_slot, here] = (
+                target[target_slot, here].astype(wide) + source[source_slot, there].astype(wide)
+            ).astype(low)
+
+        row_steps(first, last, body)
+
+    def sum_cores(self, slot):
+        self.loads[slot].wait()
+        self.swaps[slot].wait_recv()
+        self.add(self.own, slot, self.swapped, slot, 0, self.rows)
+
+    def send_far(self):
+        half = self.rows // 2
+        self.sum_cores(0)
+        self.far_low = self.make(
+            4, self.own.at[0, :half], self.relay.at[0], self.place.of(self.place.y)
+        )
+        self.far_high = self.make(
+            5, self.own.at[0, half:], self.relay.at[1], self.place.of(self.place.x)
+        )
+        self.far_low.start()
+        self.far_high.start()
+
+    def send_near(self):
+        half, place = self.rows // 2, self.place
+        self.sum_cores(1)
+        self.x_high = self.make(
+            6, self.own.at[1, half:], self.arrived.at[0, half:], place.of(place.x)
+        )
+        self.x_high.start()
+        self.sum_cores(2)
+        self.y_low = self.make(
+            7, self.own.at[2, :half], self.arrived.at[1, :half], place.of(place.y)
+        )
+        self.y_low.start()
+
+    def send_relayed(self):
+        half, place = self.rows // 2, self.place
+        self.far_low.wait_recv()
+        self.add(self.own, 1, self.relay, 0, 0, half)
+        self.x_low = self.make(
+            8, self.own.at[1, :half], self.arrived.at[0, :half], place.of(place.x)
+        )
+        self.x_low.start()
+        self.far_high.wait_recv()
+        self.add(self.own, 2, self.relay, 1, half, self.rows, shift=half)
+        self.y_high = self.make(
+            9, self.own.at[2, half:], self.arrived.at[1, half:], place.of(place.y)
+        )
+        self.y_high.start()
+        self.sum_cores(3)
+
+    def wait_half(self, upper):
+        if upper:
+            self.x_high.wait_recv()
+            self.y_high.wait_recv()
+        else:
+            self.x_low.wait_recv()
+            self.y_low.wait_recv()
+
+    def total(self, here):
+        return (
+            self.own[3, here].astype(wide)
+            + self.arrived[0, here].astype(wide)
+            + self.arrived[1, here].astype(wide)
+        )
+
+    def finish(self):
+        for copy in self.swaps + [
+            self.far_low, self.far_high, self.x_high, self.y_low, self.x_low, self.y_high,
+        ]:
+            copy.wait_send()
+
+
+class ShareRows:
+    @staticmethod
+    def scratch():
+        return [
+            pltpu.SemaphoreType.DMA((1,)),
+            pltpu.SemaphoreType.DMA((11,)),
+            pltpu.SemaphoreType.DMA((11,)),
+        ]
+
+    def __init__(self, place, source, target, scratch):
+        self.place, self.source, self.target = place, source, target
+        self.local_sem, send, receive = scratch
+        self.make = sender((send, receive))
+        self.rows = target.shape[2]
+        self.copies = {}
+
+    def put(self, index, source, target, device):
+        copy = self.make(index, source, target, device)
+        copy.start()
+        self.copies[index] = copy
+
+    def begin_half(self, upper):
+        place, half = self.place, self.rows // 2
+        rows = pl.ds(half, half) if upper else pl.ds(0, half)
+        source, target = self.source.at[rows], self.target.at[0, place.mate, rows]
+        if upper:
+            self.put(0, source, target, place.of(place.y))
+            self.put(1, source, target, place.of(place.x))
+        else:
+            self.put(2, source, target, place.of(place.x))
+            self.put(3, source, target, place.of(place.y))
+
+    def begin_rest(self):
+        place = self.place
+        self.local = pltpu.make_async_copy(
+            self.source, self.target.at[0, place.mate], self.local_sem.at[0]
+        )
+        self.local.start()
+        self.put(6, self.source, self.target.at[1, place.mate], place.sibling)
+
+    def forward(self):
+        place, half = self.place, self.rows // 2
+        self.copies[2].wait_recv()
+        piece = self.target.at[0, place.x, :half]
+        self.put(4, piece, piece, place.of(place.y))
+        self.copies[0].wait_recv()
+        piece = self.target.at[0, place.y, half:]
+        self.put(5, piece, piece, place.of(place.x))
+        self.copies[1].wait_recv()
+        self.put(7, self.target.at[0, place.x], self.target.at[1, place.x], place.sibling)
+        self.copies[3].wait_recv()
+        self.put(8, self.target.at[0, place.y], self.target.at[1, place.y], place.sibling)
+
+    def forward_far(self):
+        place, half = self.place, self.rows // 2
+        self.copies[4].wait_recv()
+        piece = self.target.at[0, place.far, :half]
+        self.put(9, piece, self.target.at[1, place.far, :half], place.sibling)
+        self.copies[5].wait_recv()
+        piece = self.target.at[0, place.far, half:]
+        self.put(10, piece, self.target.at[1, place.far, half:], place.sibling)
+
+    def finish(self):
+        self.local.wait()
+        for index in range(6, 11):
+            self.copies[index].wait_recv()
+        for copy in self.copies.values():
+            copy.wait_send()
+
+
+class GatherLines:
+    @staticmethod
+    def scratch(lines):
+        return [
+            pltpu.SemaphoreType.DMA((1,)),
+            pltpu.SemaphoreType.DMA((3,)),
+            pltpu.SemaphoreType.DMA((3,)),
+            pltpu.SemaphoreType.DMA((lines, MATES)),
+            pltpu.SemaphoreType.DMA((lines, MATES)),
+            pltpu.SemaphoreType.DMA((lines, MATES)),
+        ]
+
+    def __init__(self, place, blocks, target, scratch):
+        self.place, self.blocks, self.target = place, blocks, target
+        self.lines = target.shape[0]
+        self.local_sem, send, receive, self.up_sem, self.down_sem, self.got = scratch
+        self.make = sender((send, receive))
+        self.order = [place.mate, place.x, place.y, place.far]
+
+    def begin(self):
+        place = self.place
+        here = self.target.at[place.line, place.mate]
+        self.copies = [
+            pltpu.make_async_copy(self.blocks.at[place.mate], here, self.local_sem.at[0])
+        ]
+        for index, mate in enumerate(self.order[1:]):
+            self.copies.append(self.make(index, self.blocks.at[mate], here, place.of(mate)))
+        for copy in self.copies:
+            copy.start()
+
+    def hop(self, step, mate, direction):
+        place = self.place
+        line = place.line - step * direction
+        piece = self.target.at[line, mate]
+        sems = self.up_sem if direction > 0 else self.down_sem
+        copy = pltpu.make_async_remote_copy(
+            src_ref=piece,
+            dst_ref=piece,
+            send_sem=sems.at[step, mate],
+            recv_sem=self.got.at[line, mate],
+            device_id=place.lines_away(direction),
+            device_id_type=MESH,
+        )
+        came = (line >= 0) & (line < self.lines)
+        goes = (place.line < self.lines - 1) if direction > 0 else (place.line > 0)
+        return copy, came, goes
+
+    def leave(self):
+        for slot, mate in enumerate(self.order):
+            if slot == 0:
+                self.copies[0].wait()
+            else:
+                self.copies[slot].wait_recv()
+            for direction in (1, -1):
+                copy, _, goes = self.hop(0, mate, direction)
+                pl.when(goes)(copy.start)
+
+    def onwards(self, step):
+        for mate in self.order:
+            for direction in (1, -1):
+                copy, came, goes = self.hop(step, mate, direction)
+                pl.when(came)(copy.wait_recv)
+                if step < self.lines - 1:
+                    pl.when(came & goes)(copy.start)
+
+    def finish(self):
+        for copy in self.copies[1:]:
+            copy.wait_send()
+        for step in range(self.lines - 1):
+            for mate in self.order:
+                for direction in (1, -1):
+                    copy, came, goes = self.hop(step, mate, direction)
+                    pl.when(came & goes)(copy.wait_send)
+
+
+class SumLines:
+    @staticmethod
+    def scratch(lines, shape):
+        return [
+            pltpu.VMEM((lines,) + shape, low),
+            pltpu.VMEM((2, max(lines - 1, 1)) + shape, low),
+            pltpu.SemaphoreType.DMA((lines + 1,)),
+            pltpu.SemaphoreType.DMA((2, lines)),
+            pltpu.SemaphoreType.DMA((2, lines)),
+            pltpu.SemaphoreType.DMA((3,)),
+            pltpu.SemaphoreType.DMA((3,)),
+        ]
+
+    def __init__(self, place, blocks, result, scratch):
+        self.place, self.blocks, self.result = place, blocks, result
+        self.held, self.came, self.local_sems, self.send, self.got, send, receive = scratch
+        self.lines = self.held.shape[0]
+        self.make = sender((send, receive))
+
+    def begin(self):
+        self.loads = [
+            pltpu.make_async_copy(self.blocks.at[line], self.held.at[line], self.local_sems.at[line])
+            for line in range(self.lines)
+        ]
+        for load in self.loads:
+            load.start()
+
+    def wait_loads(self):
+        for load in self.loads:
+            load.wait()
+
+    def put_gains(self, gains):
+        lines, mates, height, lanes = self.held.shape
+        top = lax.broadcasted_iota(jnp.int32, (height, lanes), 0) == 0
+        for line in range(lines):
+            for mate in range(mates):
+                first = (line * mates + mate) * lanes
+                part = jnp.broadcast_to(gains[:, first : first + lanes], (height, lanes))
+                self.held[line, mate] = jnp.where(
+                    top, part, self.held[line, mate].astype(wide)
+                ).astype(low)
+
+    def copy(self, turn, way):
+        direction = 1 - 2 * way
+        line = self.place.line + direction * (self.lines - turn)
+        return line, pltpu.make_async_remote_copy(
+            src_ref=self.held.at[line],
+            dst_ref=self.came.at[way, turn - 1],
+            send_sem=self.send.at[way, turn],
+            recv_sem=self.got.at[way, turn],
+            device_id=self.place.lines_away(direction),
+            device_id_type=MESH,
+        )
+
+    def arrival(self, turn, way):
+        slot = self.came.at[way, turn - 1]
+        return pltpu.make_async_remote_copy(
+            src_ref=slot,
+            dst_ref=slot,
+            send_sem=self.send.at[way, turn],
+            recv_sem=self.got.at[way, turn],
+            device_id=self.place.sibling,
+            device_id_type=MESH,
+        )
+
+    def sends(self, turn, way):
+        line = self.place.line
+        return line <= turn - 1 if way == 0 else line >= self.lines - turn
+
+    def inner(self, way):
+        return self.place.line >= 1 if way == 0 else self.place.line <= self.lines - 2
+
+    def add(self, line, way, turn):
+        for mate in range(self.held.shape[1]):
+
+            def body(here, mate=mate):
+                self.held[line, mate, here] = (
+                    self.held[line, mate, here].astype(wide)
+                    + self.came[way, turn - 1, mate, here].astype(wide)
+                ).astype(low)
+
+            row_steps(0, self.held.shape[2], body)
+
+    def round(self, turn):
+        for way in (0, 1):
+            line, copy = self.copy(turn, way)
+
+            @pl.when(self.sends(turn, way))
+            def _(line=line, copy=copy, way=way):
+                if turn > 1:
+                    before = self.arrival(turn - 1, way)
+
+                    @pl.when(self.inner(way))
+                    def _():
+                        before.wait_recv()
+                        self.add(line, way, turn - 1)
+
+                copy.start()
+
+    def exchange(self):
+        place, line = self.place, self.place.line
+        for way in (0, 1):
+            if self.lines > 1:
+                last = self.arrival(self.lines - 1, way)
+
+                @pl.when(self.inner(way))
+                def _(way=way, last=last):
+                    last.wait_recv()
+                    self.add(line, way, self.lines - 1)
+
+        self.copies = []
+        for index, mate in enumerate((place.x, place.y, place.far)):
+            copy = self.make(
+                index, self.held.at[line, mate], self.result.at[place.mate], place.of(mate)
+            )
+            copy.start()
+            self.copies.append(copy)
+        self.local = pltpu.make_async_copy(
+            self.held.at[line, place.mate],
+            self.result.at[place.mate],
+            self.local_sems.at[self.lines],
+        )
+        self.local.start()
+
+    def finish(self):
+        self.local.wait()
+        for copy in self.copies:
+            copy.wait()
+        for turn in range(1, self.lines):
+            for way in (0, 1):
+                _, copy = self.copy(turn, way)
+                pl.when(self.sends(turn, way))(copy.wait_send)
+
+
+def remote_call(body, identity, ins, outs, scratch):
+    anywhere = pl.BlockSpec(memory_space=pl.ANY)
+    held = pl.BlockSpec(memory_space=pltpu.VMEM)
+    return pl.pallas_call(
+        body,
+        in_specs=[anywhere if kind == "any" else held for _, kind in ins],
+        out_specs=[anywhere if kind == "any" else held for _, _, kind in outs],
+        out_shape=[jax.ShapeDtypeStruct(shape, dtype) for shape, dtype, _ in outs],
+        scratch_shapes=scratch,
+        compiler_params=pltpu.CompilerParams(
+            vmem_limit_bytes=VMEM_BYTES, collective_id=identity, has_side_effects=True
+        ),
+    )(*[array for array, _ in ins])
+
+
+def inverse_rms(value):
+    return lax.rsqrt(jnp.mean(value * value, axis=1, keepdims=True) + epsilon)
+
+
+def middle_kernel(partial, input_ref, scale_ref, middle_ref, shared, normed, *scratch):
+    place = Place()
+    meet(place)
+    rows = SumRows(place, partial, scratch[:7])
+    share = ShareRows(place, normed, shared, scratch[7:])
+    half = normed.shape[0] // 2
+    rows.begin()
+    rows.send_far()
+    rows.send_near()
+    rows.send_relayed()
+
+    def body(here):
+        middle = input_ref[here].astype(wide) + rows.total(here)
+        middle_ref[here] = middle
+        normed[here] = (middle * inverse_rms(middle) * scale_ref[...]).astype(low)
+
+    rows.wait_half(False)
+    row_steps(0, half, body)
+    share.begin_half(False)
+    rows.wait_half(True)
+    row_steps(half, 2 * half, body)
+    share.begin_half(True)
+    share.begin_rest()
+    rows.finish()
+    share.forward()
+    share.forward_far()
+    share.finish()
+
+
+def norm_back_rows(grad, source, scale):
+    inverse = inverse_rms(source)
+    scaled = grad * scale
+    unit = source * inverse
+    inner = jnp.mean(scaled * source, axis=1, keepdims=True)
+    return inverse * (scaled - unit * (inverse * inner)), grad * unit
+
+
+def turn_rows_kernel(
+    partial, middle_ref, grad_ref, scale_ref, middle_grad_ref, gain_ref, shared, low_grad, *scratch
+):
+    place = Place()
+    meet(place)
+    rows = SumRows(place, partial, scratch[:7])
+    share = ShareRows(place, low_grad, shared, scratch[7:])
+    half = low_grad.shape[0] // 2
+    rows.begin()
+    gain_ref[...] = jnp.zeros_like(gain_ref)
+    rows.send_far()
+    rows.send_near()
+    rows.send_relayed()
+
+    def body(here):
+        part, gains = norm_back_rows(rows.total(here), middle_ref[here], scale_ref[...])
+        total = grad_ref[here].astype(wide) + part
+        middle_grad_ref[here] = total
+        low_grad[here] = total.astype(low)
+        gain_ref[...] += jnp.sum(gains, axis=0, keepdims=True)
+
+    rows.wait_half(False)
+    row_steps(0, half, body)
+    share.begin_half(False)
+    rows.wait_half(True)
+    row_steps(half, 2 * half, body)
+    share.begin_half(True)
+    share.begin_rest()
+    rows.finish()
+    share.forward()
+    share.forward_far()
+    share.finish()
+
+
+def last_rows_kernel(
+    lines, pieces, partial, mlp_partial, input_ref, middle_ref, middle_grad_ref, scale_ref, *rest
+):
+    place = Place()
+    blocks, rest = rest[:pieces], rest[pieces:]
+    input_grad, block_output, gain_ref = rest[:3]
+    results, scratch = rest[3 : 3 + pieces], rest[3 + pieces :]
+    low_grad, low_output = scratch[:2]
+    meet(place, far=bool(pieces), lines=lines if pieces else 0)
+    rows = SumRows(place, partial, scratch[2:9])
+    outs = SumRows(place, mlp_partial, scratch[9:16])
+    make = sender(scratch[16:18])
+    local_sems = scratch[18]
+    sums = [
+        SumLines(place, blocks[index], results[index], scratch[19 + 7 * index : 26 + 7 * index])
+        for index in range(pieces)
+    ]
+    whole = low_grad.shape[0]
+    for each in sums:
+        each.begin()
+    rows.begin()
+    outs.begin()
+    for each in sums:
+        each.wait_loads()
+    for each in sums[1:]:
+        if lines > 1:
+            each.round(1)
+    gain_ref[...] = jnp.zeros_like(gain_ref)
+    rows.send_far()
+    rows.send_near()
+    outs.send_far()
+    rows.send_relayed()
+    outs.send_near()
+    for each in sums[1:]:
+        if lines > 2:
+            each.round(2)
+    outs.send_relayed()
+    rows.wait_half(False)
+    rows.wait_half(True)
+
+    def body(here):
+        part, gains = norm_back_rows(
+            rows.total(here), input_ref[here].astype(wide), scale_ref[...]
+        )
+        low_grad[here] = (middle_grad_ref[here] + part).astype(low)
+        gain_ref[...] += jnp.sum(gains, axis=0, keepdims=True)
+
+    row_steps(0, whole, body)
+    if sums:
+        sums[0].put_gains(gain_ref)
+        for turn in range(1, lines):
+            sums[0].round(turn)
+    first = make(0, low_grad, input_grad.at[place.core], place.sibling)
+    first.start()
+    first_local = pltpu.make_async_copy(low_grad, input_grad.at[place.core], local_sems.at[0])
+    first_local.start()
+    for turn in range(3, lines):
+        for each in sums[1:]:
+            each.round(turn)
+    outs.wait_half(False)
+    outs.wait_half(True)
+
+    def out_body(here):
+        low_output[here] = (middle_ref[here] + outs.total(here)).astype(low)
+
+    row_steps(0, whole, out_body)
+    second = make(1, low_output, block_output.at[place.core], place.sibling)
+    second.start()
+    second_local = pltpu.make_async_copy(low_output, block_output.at[place.core], local_sems.at[1])
+    second_local.start()
+    for each in sums:
+        each.exchange()
+    rows.finish()
+    outs.finish()
+    first_local.wait()
+    second_local.wait()
+    first.wait()
+    second.wait()
+    for each in sums:
+        each.finish()
+
+
+def first_rows_kernel(lines, pieces, input_ref, grad_ref, *rest):
+    place = Place()
+    ins, rest = rest[:pieces], rest[pieces:]
+    inputs, grads = rest[:2]
+    outs, scratch = rest[2 : 2 + pieces], rest[2 + pieces :]
+    meet(place, far=bool(pieces), lines=lines if pieces else 0)
+    share = ShareRows(place, input_ref.at[place.core], inputs, scratch[:3])
+    other = ShareRows(place, grad_ref.at[place.core], grads, scratch[3:6])
+    gathers = [
+        GatherLines(place, ins[index], outs[index], scratch[6 + 6 * index : 12 + 6 * index])
+        for index in range(pieces)
+    ]
+    for gather in gathers:
+        gather.begin()
+    for each in (share, other):
+        each.begin_half(False)
+        each.begin_half(True)
+        each.begin_rest()
+    for gather in gathers:
+        gather.leave()
+    share.forward()
+    for gather in gathers:
+        if lines > 1:
+            gather.onwards(1)
+    share.forward_far()
+    other.forward()
+    for step in range(2, lines):
+        for gather in gathers:
+            gather.onwards(step)
+    other.forward_far()
+    share.finish()
+    other.finish()
+    for gather in gathers:
+        gather.finish()
+
+
+def first_rows(block_input, out_grad, blocks, lines):
+    seqs, rows, columns = block_input.shape
+    shape = (seqs, MATES, rows, columns)
+    return remote_call(
+        functools.partial(first_rows_kernel, lines, len(blocks)),
+        0,
+        [(array, "any") for array in (block_input, out_grad, *blocks)],
+        [(shape, low, "any"), (shape, low, "any")]
+        + [((lines,) + block.shape, low, "any") for block in blocks],
+        ShareRows.scratch() + ShareRows.scratch() + GatherLines.scratch(lines) * len(blocks),
+    )
+
+
+def middle_rows(partial, mine, scale):
+    seqs, _, rows, columns = partial.shape
+    return remote_call(
+        middle_kernel,
+        1,
+        [(partial, "any"), (mine, "held"), (scale, "held")],
+        [((rows, columns), wide, "held"), (partial.shape, low, "any")],
+        [pltpu.VMEM((rows, columns), low)] + SumRows.scratch(rows, columns) + ShareRows.scratch(),
+    )
+
+
+def turn_rows(partial, middle, grad, scale):
+    seqs, _, rows, columns = partial.shape
+    return remote_call(
+        turn_rows_kernel,
+        2,
+        [(partial, "any"), (middle, "held"), (grad, "held"), (scale, "held")],
+        [
+            ((rows, columns), wide, "held"),
+            ((1, columns), wide, "held"),
+            (partial.shape, low, "any"),
+        ],
+        [pltpu.VMEM((rows, columns), low)] + SumRows.scratch(rows, columns) + ShareRows.scratch(),
+    )
+
+
+def last_rows(partial, mlp_partial, mine, middle, middle_grad, scale, blocks, lines):
+    seqs, _, rows, columns = partial.shape
+    scratch = (
+        [pltpu.VMEM((rows, columns), low), pltpu.VMEM((rows, columns), low)]
+        + SumRows.scratch(rows, columns)
+        + SumRows.scratch(rows, columns)
+        + [pltpu.SemaphoreType.DMA((2,))] * 3
+    )
+    for block in blocks:
+        scratch += SumLines.scratch(lines, block.shape[1:])
+    return remote_call(
+        functools.partial(last_rows_kernel, lines, len(blocks)),
+        3,
+        [(partial, "any"), (mlp_partial, "any")]
+        + [(array, "held") for array in (mine, middle, middle_grad, scale)]
+        + [(block, "any") for block in blocks],
+        [
+            ((seqs, rows, columns), low, "any"),
+            ((seqs, rows, columns), low, "any"),
+            ((1, columns), wide, "held"),
+        ]
+        + [(block.shape[1:], low, "any") for block in blocks],
+        scratch,
     )
 
 
@@ -791,21 +1530,24 @@
     width = heads * head_size
     units = swish_weight.shape[1] // MATES
 
-    small = jnp.concatenate(
+    near = lines <= 4 and depth % 128 == 0
+    rows = seq_count * MATES * tokens
+    span = MATES * tokens
+
+    small_cut = jnp.concatenate(
         [
-            beta_weight.astype(low).reshape(depth, MATES, heads).transpose(1, 0, 2).reshape(MATES, -1),
-            conv_kernel.astype(low).reshape(MATES, -1),
             jnp.broadcast_to(
                 jnp.concatenate([attn_gain, mlp_gain, head_gain]).astype(low)[None],
                 (MATES, 2 * depth + gain_part),
             ),
+            conv_kernel.astype(low).reshape(MATES, -1),
         ],
         axis=1,
     )
-    small_size = small.shape[1]
-    small = jnp.pad(small, ((0, 0), (0, SMALL * 3 * width - small_size))).reshape(
-        MATES, SMALL, 3 * width
-    )
+    sizes = (depth, depth, gain_part, heads * 3 * CONV * gain_part)
+    starts = [sum(sizes[:index]) for index in range(len(sizes) + 1)]
+    small_cut = jnp.pad(small_cut, ((0, 0), (0, SMALL * 128 - starts[-1])))
+    small_cut = small_cut.reshape(MATES, SMALL, 128)
     streams_cut = jnp.stack(
         [
             w.astype(low).reshape(depth, MATES, heads, head_size)
@@ -814,99 +1556,76 @@
         axis=3,
     )
     streams_cut = streams_cut.transpose(1, 0, 2, 3, 4).reshape(MATES, depth, 3 * width)
-    first = gather_weights(jnp.concatenate([streams_cut, small], axis=1))
-    streams_full = first[:, :, :depth].reshape(model_width, 3 * width)
-    small = first[:, :, depth:].reshape(count, SMALL * 3 * width)[:, :small_size]
-    gates_cut = jnp.concatenate(
-        [cut_columns(w.astype(low)) for w in (outgate_weight, output_weight.T)], axis=2
-    )
-    gates_full = gather_weights(gates_cut).reshape(model_width, 2 * width)
-    outgate_full, output_full = gates_full[:, :width], gates_full[:, width:]
-    ups_cut = jnp.concatenate(
-        [cut_columns(w.astype(low)) for w in (swish_weight, upward_weight)], axis=2
-    )
-    ups_full = gather_weights(ups_cut).reshape(model_width, 2 * units)
-    downward_full = gather_weights(cut_columns(downward_weight.astype(low).T)).reshape(
-        model_width, units
-    )
-    sizes = (depth * heads, heads * 3 * CONV * gain_part, depth, depth, gain_part)
-    starts = [sum(sizes[:index]) for index in range(len(sizes) + 1)]
-    beta_small, conv_small, attn_small, mlp_small, head_small = (
+    beta_cut = jnp.pad(
+        cut_columns(beta_weight.astype(low)), ((0, 0), (0, 0), (0, head_size - heads))
+    )
+    attn_cut = jnp.concatenate(
+        [streams_cut, cut_columns(outgate_weight.astype(low)), beta_cut], axis=2
+    )
+    output_cut = cut_columns(output_weight.astype(low).T)
+    cuts = (small_cut, attn_cut, output_cut)
+    if near:
+        input_rows, grad_rows, *gathered = first_rows(block_input, out_grad, cuts, lines)
+    else:
+        input_rows, grad_rows = first_rows(block_input, out_grad, (), lines)
+        gathered = [gather_weights(cut) for cut in cuts]
+    small, attn_full, output_full = gathered
+    attn_full = attn_full.reshape(model_width, (4 * heads + 1) * head_size)
+    output_full = output_full.reshape(model_width, width)
+    input_rows = input_rows.reshape(rows, model_width)
+    grad_rows = grad_rows.reshape(rows, model_width)
+    mlp_cut = jnp.concatenate(
+        [cut_columns(w.astype(low)) for w in (swish_weight, upward_weight, downward_weight.T)],
+        axis=2,
+    )
+    mlp_full = gather_weights(row_major(mlp_cut)).reshape(model_width, 3 * units)
+    ups_full, downward_full = mlp_full[:, : 2 * units], mlp_full[:, 2 * units :]
+    small = small.reshape(count, SMALL * 128)
+    attn_small, mlp_small, head_small, conv_small = (
         small[:, starts[index] : starts[index + 1]] for index in range(len(sizes))
     )
-    beta_full = beta_small.reshape(model_width, heads)
     taps = (
         conv_small.reshape(count, heads, 3, CONV, gain_part)
         .transpose(1, 2, 3, 0, 4)
         .reshape(heads, 3 * CONV, head_size)
         .astype(wide)
     )
-    attn_scale = attn_small.reshape(model_width).astype(wide)
-    mlp_scale = mlp_small.reshape(model_width).astype(wide)
-    head_scale = head_small.reshape(head_size).astype(wide)
-
-    span = MATES * tokens
-    rows = seq_count * span
-
-    def ordered_rows(mine):
-        gathered = in_order(gather_mates(mine)).reshape(span, model_width)
-        return jnp.concatenate([gathered, other_core(gathered)], axis=0)
-
-    def loose_rows(mine):
-        gathered = jnp.concatenate(gather_mates(mine), axis=0)
-        return jnp.concatenate([gathered, other_core(gathered)], axis=0)
-
-    def sum_cores(partial):
-        own = partial[:span]
-        return (own.astype(wide) + other_core(partial[span:]).astype(wide)).astype(low)
-
-    def sum_ordered(partial):
-        blocks = sum_cores(partial).reshape(MATES, tokens, model_width)
-        return scatter_mates([pick(blocks, mate_of() ^ flip) for flip in range(MATES)])
-
-    def sum_loose(partial):
-        blocks = sum_cores(partial).reshape(MATES, tokens, model_width)
-        return scatter_mates([blocks[flip] for flip in range(MATES)])
+    attn_scale = attn_small.reshape(1, model_width).astype(wide)
+    mlp_scale = mlp_small.reshape(1, model_width).astype(wide)
+    head_scale = head_small.reshape(1, head_size).astype(wide)
 
     mine_low = pick(block_input, core)
-    mine_input = mine_low.astype(wide)
-    first_inverse = rms_scale(mine_input)
     grad_mine = pick(out_grad, core)
-    grad_rows = loose_rows(grad_mine)
-    input_rows = ordered_rows(mine_low).astype(wide)
-    flat_normed = (input_rows * rms_scale(input_rows) * attn_scale).astype(low)
-
+    blocked = (seq_count, MATES, tokens, model_width)
+    input_wide = input_rows.astype(wide)
+    flat_normed = (input_wide * rms_scale(input_wide) * attn_scale).astype(low)
     lengths_here = jnp.stack([pick(lengths, core), pick(lengths, 1 - core)])
     limit = lengths_here - line_of() * span
-    beta_spread = jnp.repeat(beta_full, head_size, axis=1)
-
-    raw = matmul("rd,dc->rc", flat_normed, streams_full).astype(low)
-    tails = along(raw.reshape(seq_count, span, 3 * width)[:, span - 16 :], 1)
-    logits = matmul("rd,dc->rc", flat_normed, beta_spread)
-    gate_values = matmul("rd,dc->rc", flat_normed, outgate_full).astype(low)
+
+    streams_end, gates_end = 3 * width, 4 * width
+    raw = matmul("rd,dc->rc", flat_normed, attn_full[:, :gates_end]).astype(low)
+    tails = along(raw.reshape(seq_count, span, gates_end)[:, span - 16 :, :streams_end], 1)
+    logits = matmul("rd,dc->rc", flat_normed, attn_full[:, gates_end:])
     sizes_of = (seq_count, heads, span)
     qkv, solved, wu, maps, prefix, local, ends = delta_prepare(
         limit, raw, tails, taps, logits, *sizes_of
     )
     map_matrix, map_offset = ends[:, :, :head_size], ends[:, :, head_size:]
     entering = hop_states(map_matrix, map_offset, 1)
-    head_row = head_scale[None]
     state, fresh, mixed, gated = delta_mix(
-        qkv, wu, prefix, local, entering, gate_values, head_row, *sizes_of
-    )
-    attn_out = sum_ordered(matmul("rc,dc->rd", gated, output_full).astype(low))
-    middle = mine_input + attn_out
-    second_inverse = rms_scale(middle)
-    mlp_normed = loose_rows((middle * second_inverse * mlp_scale).astype(low))
+        qkv, wu, prefix, local, entering, raw, head_scale, *sizes_of
+    )
+    attn_part = matmul("rc,dc->rd", gated, output_full).astype(low)
+    middle, mlp_normed = middle_rows(attn_part.reshape(blocked), mine_low, mlp_scale)
+    mlp_normed = mlp_normed.reshape(rows, model_width)
     acts = matmul("rd,df->rf", mlp_normed, ups_full)
     gate_act, up_act = acts[:, :units], acts[:, units:]
     silu_act = jax.nn.silu(gate_act)
     hidden = (silu_act * up_act).astype(low)
-    mlp_out = sum_loose(matmul("rf,df->rd", hidden, downward_full).astype(low))
-    output_mine = (middle + mlp_out).astype(low)
+    mlp_part = matmul("rf,df->rd", hidden, downward_full).astype(low)
 
     hidden_grad = matmul("rd,df->rf", grad_rows, downward_full)
-    downward_grad = matmul("rd,rf->df", grad_rows, hidden)
+    downward_grad = matmul("rd,rf->df", grad_rows, hidden).astype(low)
     acts_grad = jnp.concatenate(
         [
             (hidden_grad * up_act * silu_slope(gate_act)).astype(low),
@@ -914,57 +1633,35 @@
         ],
         axis=1,
     )
-    ups_grad = matmul("rd,rf->df", mlp_normed, acts_grad)
-    normed_two_grad = sum_loose(matmul("rf,df->rd", acts_grad, ups_full).astype(low))
-    middle_part, mlp_gain_grad = norm_back(normed_two_grad, middle, second_inverse, mlp_scale)
-    middle_grad = grad_mine.astype(wide) + middle_part
-    attn_grad_rows = ordered_rows(middle_grad.astype(low))
-    output_grad = matmul("rd,rc->dc", attn_grad_rows, gated)
+    ups_grad = matmul("rd,rf->df", mlp_normed, acts_grad).astype(low)
+    normed_two_part = matmul("rf,df->rd", acts_grad, ups_full).astype(low)
+    middle_grad, mlp_gain_grad, attn_grad_rows = turn_rows(
+        normed_two_part.reshape(blocked), middle, grad_mine, mlp_scale
+    )
+    attn_grad_rows = attn_grad_rows.reshape(rows, model_width)
+    output_grad = matmul("rd,rc->dc", attn_grad_rows, gated).astype(low)
     gated_grad = matmul("rd,dc->rc", attn_grad_rows, output_full)
-    out_grads, fresh_grad, outgate_act_grad, head_gain_parts, sources, local_state = delta_turn(
-        gated_grad, mixed, gate_values, head_row, qkv, wu, maps, *sizes_of
-    )
-    head_gain_part = jnp.sum(head_gain_parts[:, 0], axis=0)
+    out_grads, fresh_grad, all_grads, head_gain_parts, sources, local_state = delta_turn(
+        gated_grad, mixed, raw, head_scale, qkv, wu, maps, *sizes_of
+    )
     leaving_grad = hop_states_back(map_matrix, local_state)
-    raw_grad, edge, halo, taps_grad, logit_grad = delta_unwind(
+    all_grads, edge, halo, taps_grad, logit_grad = delta_unwind(
         limit, raw, tails, taps, logits, qkv, solved, wu, state, fresh, out_grads, fresh_grad,
-        maps, sources, leaving_grad, *sizes_of,
+        maps, sources, leaving_grad, all_grads, *sizes_of,
     )
     returned = along(halo.astype(low), -1)
     edge = (edge + returned.astype(wide)).astype(low)
-    raw_grad_low = (
-        raw_grad.reshape(seq_count, span, 3 * width)
-        .at[:, span - 16 :]
-        .set(edge)
-        .reshape(rows, 3 * width)
-    )
-    beta_logit_grad = logit_grad[:, ::head_size]
-    last_grads = jnp.concatenate(
-        [raw_grad_low, jnp.pad(beta_logit_grad, ((0, 0), (0, head_size - heads)))], axis=1
-    )
-    last_weights = jnp.concatenate(
-        [streams_full, jnp.pad(beta_full, ((0, 0), (0, head_size - heads)))], axis=1
-    )
-    outgate_grad = matmul("rd,rc->dc", flat_normed, outgate_act_grad)
-    last_grad = matmul("rd,rc->dc", flat_normed, last_grads)
-    streams_grad, beta_grad = last_grad[:, : 3 * width], last_grad[:, 3 * width : 3 * width + heads]
-    normed_part = matmul("rc,dc->rd", outgate_act_grad, outgate_full) + matmul(
-        "rc,dc->rd", last_grads, last_weights
-    )
-    normed_grad = sum_ordered(normed_part.astype(low))
-    input_part, attn_gain_grad = norm_back(normed_grad, mine_input, first_inverse, attn_scale)
-    input_grad_mine = (middle_grad + input_part).astype(low)
-
-    def both_sequences(mine):
-        other = other_core(mine)
-        return jnp.stack([jnp.where(core == 0, mine, other), jnp.where(core == 0, other, mine)])
+    all_grads = all_grads.at[:, gates_end:].set(logit_grad)
+    for seq in range(seq_count):
+        first = (seq + 1) * span
+        all_grads = all_grads.at[first - 16 : first, :streams_end].set(edge[seq])
+    normed_part = matmul("rc,dc->rd", all_grads, attn_full).astype(low)
+    attn_grads = matmul("rd,rc->dc", flat_normed, all_grads).astype(low)
 
     def cut_rows(grad):
         return grad.reshape(lines, MATES, depth, grad.shape[1])
 
-    downward_sum = join_columns(scatter_grads(cut_rows(downward_grad))).T
-    ups_sum = scatter_grads(cut_rows(ups_grad))
-    gates_sum = scatter_grads(cut_rows(jnp.concatenate([outgate_grad, output_grad], axis=1)))
+    mlp_sum = scatter_grads(row_major(cut_rows(jnp.concatenate([ups_grad, downward_grad], axis=1))))
     conv_grad = (
         taps_grad[:, :CONV]
         .reshape(seq_count, heads, CONV, 3, count, gain_part)
@@ -972,54 +1669,72 @@
         .transpose(3, 0, 2, 1, 4)
         .reshape(count, -1)
     )
-    small_grad = jnp.concatenate(
-        [
-            beta_grad.reshape(count, depth * heads),
-            conv_grad,
+
+    def small_blocks(attn_gain_grad):
+        parts = [
             attn_gain_grad.reshape(count, depth),
             mlp_gain_grad.reshape(count, depth),
-            head_gain_part.reshape(count, gain_part),
-        ],
-        axis=1,
-    ).astype(low)
-    small_grad = jnp.pad(small_grad, ((0, 0), (0, SMALL * 3 * width - small_size)))
-    first_sum = scatter_grads(
-        jnp.concatenate(
-            [
-                cut_rows(streams_grad.astype(low)),
-                small_grad.reshape(lines, MATES, SMALL, 3 * width),
-            ],
-            axis=2,
-        )
-    )
+            jnp.sum(head_gain_parts[:, 0], axis=0).reshape(count, gain_part),
+            conv_grad,
+        ]
+        flat = jnp.concatenate(parts, axis=1).astype(low)
+        flat = jnp.pad(flat, ((0, 0), (0, SMALL * 128 - starts[-1])))
+        return flat.reshape(lines, MATES, SMALL, 128)
+
+    last_ins = (
+        normed_part.reshape(blocked),
+        mlp_part.reshape(blocked),
+        mine_low,
+        middle,
+        middle_grad,
+        attn_scale,
+    )
+    if near:
+        blocks = (
+            small_blocks(jnp.zeros((1, model_width), wide)),
+            cut_rows(attn_grads),
+            cut_rows(output_grad),
+        )
+        input_grad, block_output, _, small_sum, attn_sum, output_sum = last_rows(
+            *last_ins, blocks, lines
+        )
+        attn_sum, output_sum, small_sum = (
+            v.astype(wide) for v in (attn_sum, output_sum, small_sum)
+        )
+    else:
+        input_grad, block_output, attn_gain_grad = last_rows(*last_ins, (), lines)
+        small_sum, attn_sum, output_sum = (
+            scatter_grads(block)
+            for block in (
+                small_blocks(attn_gain_grad), cut_rows(attn_grads), cut_rows(output_grad)
+            )
+        )
+    small_sum = small_sum.reshape(MATES, SMALL * 128)
+    gains_sum = jnp.sum(small_sum[:, : starts[3]], axis=0)
+    gains_sum = gains_sum + other_core(gains_sum)
+    conv_sum = small_sum[:, starts[3] : starts[4]]
     streams_sum = (
-        first_sum[:, :depth]
+        attn_sum[:, :, :streams_end]
         .reshape(MATES, depth, heads, 3, head_size)
         .transpose(3, 1, 0, 2, 4)
         .reshape(3, depth, MATES * width)
     )
-    small_sum = first_sum[:, depth:].reshape(MATES, SMALL * 3 * width)
-    beta_sum, conv_sum, attn_sum, mlp_sum, head_sum = (
-        small_sum[:, starts[index] : starts[index + 1]] for index in range(len(sizes))
-    )
-    gains_sum = jnp.sum(jnp.concatenate([attn_sum, mlp_sum, head_sum], axis=1), axis=0)
-    gains_sum = gains_sum + other_core(gains_sum)
     return (
-        both_sequences(output_mine),
-        both_sequences(input_grad_mine),
+        block_output,
+        input_grad,
         gains_sum[:depth],
         streams_sum[0],
         streams_sum[1],
         streams_sum[2],
-        join_columns(gates_sum[:, :, :width]),
-        join_columns(beta_sum.reshape(MATES, depth, heads)),
+        join_columns(attn_sum[:, :, streams_end:gates_end]),
+        join_columns(attn_sum[:, :, gates_end : gates_end + heads]),
         conv_sum.reshape(MATES * heads, 3, CONV, gain_part),
         gains_sum[2 * depth :],
-        join_columns(gates_sum[:, :, width:]).T,
+        join_columns(output_sum).T,
         gains_sum[depth : 2 * depth],
-        join_columns(ups_sum[:, :, :units]),
-        join_columns(ups_sum[:, :, units:]),
-        downward_sum,
+        join_columns(mlp_sum[:, :, :units]),
+        join_columns(mlp_sum[:, :, units : 2 * units]),
+        join_columns(mlp_sum[:, :, 2 * units :]).T,
     )
 
 

time: 1310 us -> 1140 us (0.87)
  Pallas kernels: 114 us -> 544 us
  waiting for transfers between devices: 291 us -> 94 us
  local copies, waits for them, and re-layouts: 317 us -> 159 us
  starting transfers between devices: 232 us -> 112 us
  other arithmetic: 176 us -> 57.3 us
    pallas_call x0 -> x4, Pallas kernels: none -> 425 us  [remote_call(): pl.pallas_call(body, in_specs=[anywhere if kind == 'any' else held for _,...]
    ppermute x56 -> x20, waiting for transfers between devices: 184 us -> 72.6 us  [along(): return lax.ppermute(value, 'seq', pairs)]
    dynamic_update_slice x37 -> x7, local copies, waits for them, and re-layouts: 95.5 us -> 6.84 us  [in_order(): out = lax.dynamic_update_index_in_dim(out, piece, mate ^ flip, 0)]
    ppermute x56 -> x6, waiting for transfers between devices: 107 us -> 21.4 us  [to_mate(): lax.ppermute(value, 'seq', [(source, source ^ flip) for source in range(c...]
    ppermute x56 -> x20, starting transfers between devices: 170 us -> 104 us  [along(): return lax.ppermute(value, 'seq', pairs)]
    ppermute x56 -> x6, starting transfers between devices: 60.9 us -> 8 us  [to_mate(): lax.ppermute(value, 'seq', [(source, source ^ flip) for source in range(c...]
    concatenate x15 -> x4, other arithmetic: 48 us -> 7.29 us  [the longest x1 6 us: on_device(): jnp.concatenate([ups_grad, downward_grad], axis=1)]
    slice x31 -> x4, local copies, waits for them, and re-layouts: 32.2 us -> 1.8 us  [the longest x2 1.72 us: on_device(): attn_sum[:, :, :streams_end].reshape(MATES, depth, heads, 3, head_size)]
  transfers between devices with their start and end apart: 123 -> 27, of which waited for: 42 -> 7; matrix products, arithmetic and copies ran while one was open for 44% -> 18% of each run, Pallas kernels for 7% -> 39%
where the time goes in v3:
time: 1140 us; the launch traced here: 1130 us
  Pallas kernels  544 us (48%)
  matrix products  165 us (14%)
  local copies, waits for them, and re-layouts  159 us (14%)
  starting transfers between devices  112 us (10%)
  waiting for transfers between devices  94 us (8%)
  other arithmetic  57.3 us (5%)
    pallas_call x4, Pallas kernels, remote_call(): pl.pallas_call(body, in_specs=[anywhere if kind == 'any' else held for _,...  425 us
    dot_general x13, matrix products, matmul(): return jnp.einsum(form, left, right, preferred_element_type=wide)  163 us
    pallas_call x4, Pallas kernels, kernel_call(): pl.pallas_call(body, grid=grid, in_specs=[spec for _, spec in ins], out_s...  119 us
    ppermute x20, starting transfers between devices, along(): return lax.ppermute(value, 'seq', pairs)  104 us
    ppermute x20, waiting for transfers between devices, along(): return lax.ppermute(value, 'seq', pairs)  72.6 us
    dynamic_slice x12, local copies, waits for them, and re-layouts, pick(): return lax.dynamic_index_in_dim(blocks, index, 0, False)  24.8 us
    unnamed x77, local copies, waits for them, and re-layouts  24.2 us
  transfers between devices with their start and end apart: 27, of which 7 were waited for; matrix products, arithmetic and copies ran while one was open for 18% of the time, Pallas kernels for 39%

profile of v3, /device:TPU:0, one launch (start us, length us, event | category | flops | bytes accessed | tf_op | source)
XLA Modules:
  0.0 1133.8 jit_solution(14397807654238817044)
XLA Ops:
  28.0 126.1 %shard_map.271 = (bf16[2,4,256,2048]{3,2,1,0:T(8,128)(2,1)}, bf16[2,4,256,2048]{3,2,1,0:T(8,128)(2,1)}, bf16[4,4,16,128]{3,2,1,0:T(8,128)(2,1)S(1)}, bf16[4,4,12...) custom-call(bf16[2,256,2048]{2,1,0:T(8,128)(2,1)} %input_ref.1, bf16[2,256,2048]{2,1,0:T(8,128)(2,1)} %grad_ref.1, ...), custom_call_target="tpu_custom_call" | custom-call | tf_op jit(solution)/shard_map/pallas_call | solution.py:1217
  159.8 4.1 copy.204
  165.1 5.1 multiply_reduce_fusion
  170.3 8.7 fusion.1
  178.9 5.9 collective-permute-start.7
  184.9 30.5 %collective-permute-done.8 = bf16[4,128,2112]{1,2,0:T(8,128)(2,1)} collective-permute-done((bf16[4,128,2112]{1,2,0:T(8,128)(2,1)}, bf16[4,128,2112]{1,2,0:T(8,128)(2,1)}, u32[]{:S(2)}, u32[]{:S(2)}) %collective-permute-start.8) | collective-permute-done | bytes 2162720 | tf_op jit(solution)/shard_map/ppermute | solution.py:39
  216.9 12.5 %fusion.12.raw_ref.gate_ref = bf16[2048,1024]{1,0:T(8,128)(2,1)S(1)} fusion(bf16[2048,2048]{1,0:T(8,128)(2,1)} %fusion.1, bf16[2048,1152]{1,0:T(8,128)(2,1)} %bitcast.248), kind=kOutput, calls=%fused_computation.31 | convolution fusion | flops 8592031744 | bytes 16777216 | tf_op jit(solution)/shard_map/rd,dc->rc/dot_general | solution.py:140
  231.3 4.5 collective-permute-start
  236.7 5.9 fusion.20.logit_ref
  247.5 32.8 %shard_map.272 = (bf16[2048,768]{1,0:T(8,128)(2,1)}, f32[4,8,128,128]{3,2,1,0:T(8,128)}, f32[4,8,128,256]{3,2,1,0:T(8,128)}, f32[4,8,128,128]{3,2,1,0:T(8,128)},...) custom-call(s32[2]{0:T(128)S(1)} %add_subtract_fusion.limit_ref, ...), custom_call_target="tpu_custom_call" | custom-call | tf_op jit(solution)/shard_map/pallas_call | solution.py:570
  284.3 11.8 %collective-permute-done.1 = f32[4,128,128]{2,1,0:T(8,128)S(1)} collective-permute-done((f32[4,128,128]{2,1,0:T(8,128)S(1)}, f32[4,128,128]{2,1,0:T(8,128)S(1)}, u32[]{:S(2)}, u32[]{:S(2)}) %collective-permute-start.1) | collective-permute-done | bytes 262176 | tf_op jit(solution)/shard_map/ppermute | solution.py:39
  296.5 4.4 collective-permute-start.2
  305.5 4.4 collective-permute-start.3
  311.2 4.6 broadcast_in_dim.45
  319.0 17.7 %shard_map.273 = (f32[4,8,128,128]{3,2,1,0:T(8,128)}, f32[4,8,128,128]{3,2,1,0:T(8,128)}, f32[2048,256]{1,0:T(8,128)}, bf16[2048,256]{1,0:T(8,128)(2,1)S(1)}) custom-call(bf16[2048,768]{1,0:T(8,128)(2,1)} %get-tuple-element.91.qkv_ref, f32[4,8,128,256]{3,2,1,0:T(8,128)} %get-tuple-element.93.wu_ref, f32[4,8,128,128]{3,2,1,0:T(8,128)} %get-tuple-element.94.prefix_ref, ...), custom_call_target="tpu_custom_call" | custom-call | tf_op jit(solution)/shard_map/pallas_call | solution.py:570
  336.7 6.4 collective-permute-start.12
  343.1 5.7 convolution_convert_fusion.5
  348.8 81.7 %shard_map.274 = (f32[256,2048]{1,0:T(8,128)}, bf16[2,4,256,2048]{3,2,1,0:T(8,128)(2,1)}) custom-call(bf16[2,4,256,2048]{3,2,1,0:T(8,128)(2,1)} %bitcast.188, bf16[256,2048]{1,0:T(8,128)(2,1)S(1)} %get-tuple-element.214.input_ref, f32[1,2048]{1,0:T(1,128)S(1)} %bitcast.182), custom_call_target="tpu_custom_call" | custom-call | tf_op jit(solution)/shard_map/pallas_call | solution.py:1217
  434.4 4.1 copy.207
  460.9 18.8 %fusion.4 = f32[2048,1408]{0,1:T(8,128)} fusion(bf16[2048,2048]{1,0:T(8,128)(2,1)} %bitcast.246, bf16[2048,2112]{1,0:T(8,128)(2,1)} %bitcast.192), kind=kOutput, calls=%fused_computation.20 | convolution fusion | flops 11811160064 | bytes 25690112 | tf_op jit(solution)/shard_map/rd,df->rf/dot_general | solution.py:140
  479.7 16.9 %multiply_convert_fusion.2 = (bf16[2048,704]{0,1:T(8,128)(2,1)}, bf16[2048,704]{0,1:T(8,128)(2,1)}, bf16[2048,704]{0,1:T(8,128)(2,1)}) fusion(f32[2048,1408]{0,1:T(8,128)} %fusion.4, bf16[2048,2048]{1,0:T(8,128)(2,1)} %bitcast.242, bf16[2048,2112]{1,0:T(8,128)(2,1)} %bitcast.193), kind=kOutput, calls=%fused_computation.14 | convolution fusion | flops 5927206912 | bytes 31719424 | tf_op jit(solution)/shard_map/rd,df->rf/dot_general | solution.py:140
  496.7 16.8 %convolution_convert_fusion = bf16[2048,1408]{0,1:T(8,128)(2,1)S(1)} fusion(bf16[2048,2048]{1,0:T(8,128)(2,1)} %bitcast.247, bf16[2048,704]{0,1:T(8,128)(2,1)} %get-tuple-element.186, bf16[2048,704]{0,1:T(8,128)(2,1)} %get-tuple-element.185), kind=kOutput, calls=%fused_computation.5 | convolution fusion | flops 11825577984 | bytes 19922944 | tf_op jit(solution)/shard_map/rd,rf->df/dot_general | solution.py:140
  513.5 19.2 %convolution_convert_fusion.4 = bf16[2048,2048]{1,0:T(8,128)(2,1)} fusion(bf16[2048,2112]{1,0:T(8,128)(2,1)} %bitcast.194, bf16[2048,704]{0,1:T(8,128)(2,1)} %get-tuple-element.186, bf16[2048,704]{0,1:T(8,128)(2,1)} %get-tuple-element.185), kind=kOutput, calls=%fused_computation.9 | convolution fusion | flops 11826888704 | bytes 19922944 | tf_op jit(solution)/shard_map/rf,df->rd/dot_general | solution.py:140
  532.6 10.7 convolution_convert_fusion.6
  543.3 10.9 convolution_convert_fusion.2
  554.3 83.5 %shard_map.275 = (f32[256,2048]{1,0:T(8,128)}, f32[1,2048]{1,0:T(1,128)S(1)}, bf16[2,4,256,2048]{3,2,1,0:T(8,128)(2,1)}) custom-call(bf16[2,4,256,2048]{3,2,1,0:T(8,128)(2,1)} %bitcast.198, f32[256,2048]{1,0:T(8,128)} %get-tuple-element.103.middle_ref, bf16[256,2048]{1,0:T(8,128)(2,1)S(1)} %get-tuple-element.213.grad_ref, f32[1,2048]{1,0:T(1,128)S(1)} %bitcast.183), custom_call_target="tpu_custom_call" | custom-call | tf_op jit(solution)/shard_map/pallas_call | solution.py:1217
  637.8 7.1 fusion.34.grad_ref
  644.9 15.6 %shard_map.276 = (f32[4,8,128,128]{3,2,1,0:T(8,128)}, f32[4,8,128,128]{3,2,1,0:T(8,128)}, bf16[2048,1152]{1,0:T(8,128)(2,1)}, f32[4,8,128]{2,1,0:T(8,128)S(1)}, ...) custom-call(f32[2048,256]{1,0:T(8,128)} %fusion.34.grad_ref, f32[2048,256]{1,0:T(8,128)} %get-tuple-element.105.mixed_ref, ...), custom_call_target="tpu_custom_call" | custom-call | tf_op jit(solution)/shard_map/pallas_call | solution.py:570
  661.8 6.0 pad_maximum_fusion
  667.8 11.8 %copy.216 = bf16[2048,2112]{1,0:T(8,128)(2,1)} copy(bf16[2048,2112]{0,1:T(8,128)(2,1)} %pad_maximum_fusion) | data formatting | bytes 17301504 | tf_op jit(solution)/shard_map/concatenate | solution.py:1664
  681.3 4.9 constant_dynamic-slice_fusion.3
  686.2 4.2 copy.218
  690.4 6.6 collective-permute-start.18
  696.9 4.1 copy.217
  704.8 6.9 convolution_convert_fusion.7
  713.5 52.9 %shard_map.277 = (bf16[2048,1152]{1,0:T(8,128)(2,1)}, f32[2,16,768]{2,1,0:T(8,128)S(1)}, f32[2,16,768]{2,1,0:T(8,128)S(1)}, f32[4,8,384]{2,1,0:T(8,128)S(1)}, bf16[2048,128]{1,0:T(8,128)(2,1)S(1)}) custom-call(s32[2]{0:T(128)S(1)} %copy-done.10, bf16[2048,1024]{1,0:T(8,128)(2,1)} %copy-done.11, ...), custom_call_target="tpu_custom_call", output_to_operand_aliasing={{0}: (15, {})} | custom-call | tf_op jit(solution)/shard_map/pallas_call | solution.py:570
  773.0 4.7 copy.219
  777.7 4.3 copy.222
  782.0 6.5 fusion.6
  788.5 4.1 copy.220
  792.6 46.2 %collective-permute-start.19 = (bf16[4,128,2112]{1,2,0:T(8,128)(2,1)}, bf16[4,128,2112]{1,2,0:T(8,128)(2,1)}, u32[]{:S(2)}, u32[]{:S(2)}) collective-permute-start(bf16[4,128,2112]{1,2,0:T(8,128)(2,1)} %copy.220), channel_id=1, source_target_pairs={{0,8},{2,10},{4,12},{6,14},{8,16},{10,18},{12,20},{14,22},{1,9},{3... | collective-permute-start | bytes 6488072 | tf_op jit(solution)/shard_map/ppermute | solution.py:39
  842.8 16.4 %convolution_convert_fusion.3 = bf16[2048,2048]{1,0:T(8,128)(2,1)} fusion(bf16[2048,1152]{1,0:T(8,128)(2,1)} %fusion.26, bf16[2048,1152]{1,0:T(8,128)(2,1)} %bitcast.250), kind=kOutput, calls=%fused_computation.8 | convolution fusion | flops 9667870720 | bytes 17825792 | tf_op jit(solution)/shard_map/rc,dc->rd/dot_general | solution.py:140
  859.2 23.1 %collective-permute-done.19 = bf16[4,128,2112]{1,2,0:T(8,128)(2,1)} collective-permute-done((bf16[4,128,2112]{1,2,0:T(8,128)(2,1)}, bf16[4,128,2112]{1,2,0:T(8,128)(2,1)}, u32[]{:S(2)}, u32[]{:S(2)}) %collective-permute-start.19) | collective-permute-done | bytes 2162720 | tf_op jit(solution)/shard_map/ppermute | solution.py:39
  885.8 6.1 collective-permute-start.20
  895.3 15.4 %convolution_convert_fusion.1 = bf16[2048,1152]{1,0:T(8,128)(2,1)} fusion(bf16[2048,2048]{1,0:T(8,128)(2,1)} %fusion.1, bf16[2048,1152]{1,0:T(8,128)(2,1)S(1)} %copy-done.16), kind=kOutput, calls=%fused_computation.6 | convolution fusion | flops 9666035712 | bytes 17825792 | tf_op jit(solution)/shard_map/rd,rc->dc/dot_general | solution.py:140
  910.7 133.8 %shard_map.278 = (bf16[2,256,2048]{2,1,0:T(8,128)(2,1)}, bf16[2,256,2048]{2,1,0:T(8,128)(2,1)}, f32[1,2048]{1,0:T(1,128)}, bf16[4,16,128]{2,1,0:T(8,128)(2,1)S(1...) custom-call(bf16[2,4,256,2048]{3,2,1,0:T(8,128)(2,1)} %bitcast.200, ...), custom_call_target="tpu_custom_call" | custom-call | tf_op jit(solution)/shard_map/pallas_call | solution.py:1217
  1055.2 4.1 copy.224
  1090.7 21.4 %collective-permute-done.25 = bf16[128,2112]{0,1:T(8,128)(2,1)} collective-permute-done((bf16[128,2112]{0,1:T(8,128)(2,1)}, bf16[128,2112]{0,1:T(8,128)(2,1)}, u32[]{:S(2)}, u32[]{:S(2)}) %collective-permute-start.25) | collective-permute-done | bytes 540704 | tf_op jit(solution)/shard_map/ppermute | solution.py:28
  (236 shorter events, 171.8 us)
Async XLA Ops:
  13.6 9.3 copy-start.19
  13.6 9.6 copy-start.20
  15.8 138.4 %collective-permute-start.4 = (bf16[128,2112]{0,1:T(8,128)(2,1)}, bf16[128,2112]{0,1:T(8,128)(2,1)}, u32[]{:S(2)}, u32[]{:S(2)}) collective-permute-start(bf16[128,2112]{0,1:T(8,128)(2,1)} %bitcast.26), channel_id=1, source_target_pairs={{0,2},{2,0},{4,6},{6,4},{8,10},{10,8},{12,14},{14,12},{16,18},{18,... | collective-permute-start | bytes 1622024 | tf_op jit(solution)/shard_map/ppermute | solution.py:28
  19.7 136.7 %collective-permute-start.5 = (bf16[128,2112]{0,1:T(8,128)(2,1)}, bf16[128,2112]{0,1:T(8,128)(2,1)}, u32[]{:S(2)}, u32[]{:S(2)}) collective-permute-start(bf16[128,2112]{0,1:T(8,128)(2,1)} %bitcast.28), channel_id=1, source_target_pairs={{0,4},{2,6},{4,0},{6,2},{8,12},{10,14},{12,8},{14,10},{16,20},{18,... | collective-permute-start | bytes 1622024 | tf_op jit(solution)/shard_map/ppermute | solution.py:28
  21.6 137.0 %collective-permute-start.6 = (bf16[128,2112]{0,1:T(8,128)(2,1)S(1)}, bf16[128,2112]{0,1:T(8,128)(2,1)S(1)}, u32[]{:S(2)}, u32[]{:S(2)}) collective-permute-start(bf16[128,2112]{0,1:T(8,128)(2,1)S(1)} %bitcast.224), channel_id=1, source_target_pairs={{0,6},{2,4},{4,2},{6,0},{8,14},{10,12},{12,10},{14,8},{16,22},{18,... | collective-permute-start | bytes 1622024 | tf_op jit(solution)/shard_map/ppermute | solution.py:28
  22.9 3.8 copy-start.27
  163.9 51.6 %collective-permute-start.8 = (bf16[4,128,2112]{1,2,0:T(8,128)(2,1)}, bf16[4,128,2112]{1,2,0:T(8,128)(2,1)}, u32[]{:S(2)}, u32[]{:S(2)}) collective-permute-start(bf16[4,128,2112]{1,2,0:T(8,128)(2,1)} %copy.204), channel_id=1, source_target_pairs={{8,0},{10,2},{12,4},{14,6},{16,8},{18,10},{20,12},{22,14},{24,16},... | collective-permute-start | bytes 6488072 | tf_op jit(solution)/shard_map/ppermute | solution.py:39
  178.9 63.6 %collective-permute-start.7 = (bf16[4,128,2112]{1,2,0:T(8,128)(2,1)}, bf16[4,128,2112]{1,2,0:T(8,128)(2,1)}, u32[]{:S(2)}, u32[]{:S(2)}) collective-permute-start(bf16[4,128,2112]{1,2,0:T(8,128)(2,1)} %copy.204), channel_id=1, source_target_pairs={{0,8},{2,10},{4,12},{6,14},{8,16},{10,18},{12,20},{14,22},{16,24},... | collective-permute-start | bytes 6488072 | tf_op jit(solution)/shard_map/ppermute | solution.py:39
  215.4 94.5 %collective-permute-start.9 = (bf16[4,128,2112]{1,2,0:T(8,128)(2,1)}, bf16[4,128,2112]{1,2,0:T(8,128)(2,1)}, u32[]{:S(2)}, u32[]{:S(2)}) collective-permute-start(bf16[4,128,2112]{1,2,0:T(8,128)(2,1)} %collective-permute-done.8), channel_id=1, source_target_pairs={{8,0},{10,2},{12,4},{14,6},{16,8},{18,10},{20,12},{22,14},{24,16},... | collective-permute-start | bytes 6488072 | tf_op jit(solution)/shard_map/ppermute | solution.py:39
  216.9 19.2 %copy-start.24 = (s32[2]{0:T(128)S(1)}, s32[2]{0:T(128)}, u32[]{:S(2)}) copy-start(s32[2]{0:T(128)} %param.23) | copy-start | bytes 28
  231.3 16.1 %collective-permute-start = (bf16[2,16,768]{2,1,0:T(8,128)(2,1)S(1)}, bf16[2,16,768]{2,1,0:T(8,128)(2,1)S(1)}, u32[]{:S(2)}, u32[]{:S(2)}) collective-permute-start(bf16[2,16,768]{2,1,0:T(8,128)(2,1)S(1)} %slice.192), channel_id=1, source_target_pairs={{0,8},{2,10},{4,12},{6,14},{8,16},{10,18},{12,20},{14,22},{16,24},... | collective-permute-start | bytes 147464 | tf_op jit(solution)/shard_map/ppermute | solution.py:39
  242.6 54.0 %copy-start.2 = (f32[2048,128]{1,0:T(8,128)}, f32[2048,128]{1,0:T(8,128)S(1)}, u32[]{:S(2)}) copy-start(f32[2048,128]{1,0:T(8,128)S(1)} %fusion.20.logit_ref) | copy-start | bytes 3145732
  242.6 94.1 %collective-permute-start.11 = (bf16[4,128,2112]{1,2,0:T(8,128)(2,1)}, bf16[4,128,2112]{1,2,0:T(8,128)(2,1)}, u32[]{:S(2)}, u32[]{:S(2)}) collective-permute-start(bf16[4,128,2112]{1,2,0:T(8,128)(2,1)} %collective-permute-done.7), channel_id=1, source_target_pairs={{0,8},{2,10},{4,12},{6,14},{8,16},{10,18},{12,20},{14,22},{16,24},... | collective-permute-start | bytes 6488072 | tf_op jit(solution)/shard_map/ppermute | solution.py:39
  247.2 36.4 %copy-start.9 = (s32[2]{0:T(128)}, s32[2]{0:T(128)S(1)}, u32[]{:S(2)}) copy-start(s32[2]{0:T(128)S(1)} %add_subtract_fusion.limit_ref) | copy-start | bytes 28
  280.3 35.5 %copy-start.3 = (f32[4,128,256]{2,1,0:T(8,128)}, f32[4,128,256]{2,1,0:T(8,128)S(1)}, u32[]{:S(2)}) copy-start(f32[4,128,256]{2,1,0:T(8,128)S(1)} %get-tuple-element.96) | copy-start | bytes 1572868
  280.4 15.8 %collective-permute-start.1 = (f32[4,128,128]{2,1,0:T(8,128)S(1)}, f32[4,128,128]{2,1,0:T(8,128)S(1)}, u32[]{:S(2)}, u32[]{:S(2)}) collective-permute-start(f32[4,128,128]{2,1,0:T(8,128)S(1)} %slice.165), channel_id=1, source_target_pairs={{0,8},{2,10},{4,12},{6,14},{8,16},{10,18},{12,20},{14,22},{16,24},... | collective-permute-start | bytes 786440 | tf_op jit(solution)/shard_map/ppermute | solution.py:39
  283.7 35.3 %copy-start.7 = (f32[1,128]{1,0:T(1,128)}, f32[1,128]{1,0:T(1,128)S(1)}, u32[]{:S(2)}) copy-start(f32[1,128]{1,0:T(1,128)S(1)} %reshape.397.scale_ref) | copy-start | bytes 1540
  296.5 8.5 collective-permute-start.2
  302.7 46.1 %copy-start = (bf16[256,2048]{1,0:T(8,128)(2,1)}, bf16[256,2048]{1,0:T(8,128)(2,1)S(1)}, u32[]{:S(2)}) copy-start(bf16[256,2048]{1,0:T(8,128)(2,1)S(1)} %get-tuple-element.214.input_ref) | copy-start | bytes 3145732
  305.5 13.5 %collective-permute-start.3 = (f32[4,128,128]{2,1,0:T(8,128)S(1)}, f32[4,128,128]{2,1,0:T(8,128)S(1)}, u32[]{:S(2)}, u32[]{:S(2)}) collective-permute-start(f32[4,128,128]{2,1,0:T(8,128)S(1)} %convolution_add_fusion.2), channel_id=1, source_target_pairs={{0,8},{2,10},{4,12},{6,14},{8,16},{10,18},{12,20},{14,22},{16,24},... | collective-permute-start | bytes 786440 | tf_op jit(solution)/shard_map/ppermute | solution.py:39
  309.9 128.6 %collective-permute-start.10 = (bf16[4,128,2112]{1,2,0:T(8,128)(2,1)}, bf16[4,128,2112]{1,2,0:T(8,128)(2,1)}, u32[]{:S(2)}, u32[]{:S(2)}) collective-permute-start(bf16[4,128,2112]{1,2,0:T(8,128)(2,1)} %collective-permute-done.9), channel_id=1, source_target_pairs={{8,0},{10,2},{12,4},{14,6},{16,8},{18,10},{20,12},{22,14},{24,16},... | collective-permute-start | bytes 6488072 | tf_op jit(solution)/shard_map/ppermute | solution.py:39
  336.7 12.1 %copy-start.5 = (bf16[2048,256]{1,0:T(8,128)(2,1)}, bf16[2048,256]{1,0:T(8,128)(2,1)S(1)}, u32[]{:S(2)}) copy-start(bf16[2048,256]{1,0:T(8,128)(2,1)S(1)} %get-tuple-element.100) | copy-start | bytes 3145732
  336.7 109.8 %collective-permute-start.12 = (bf16[4,128,2112]{1,2,0:T(8,128)(2,1)}, bf16[4,128,2112]{1,2,0:T(8,128)(2,1)}, u32[]{:S(2)}, u32[]{:S(2)}) collective-permute-start(bf16[4,128,2112]{1,2,0:T(8,128)(2,1)} %collective-permute-done.11), channel_id=1, source_target_pairs={{0,8},{2,10},{4,12},{6,14},{8,16},{10,18},{12,20},{14,22},{16,24},... | collective-permute-start | bytes 6488072 | tf_op jit(solution)/shard_map/ppermute | solution.py:39
  454.4 4.9 copy-start.13
  532.6 10.7 copy-start.28
  637.8 7.1 copy-start.8
  660.5 19.1 %collective-permute-start.13 = (f32[4,128,128]{2,1,0:T(8,128)S(1)}, f32[4,128,128]{2,1,0:T(8,128)S(1)}, u32[]{:S(2)}, u32[]{:S(2)}) collective-permute-start(f32[4,128,128]{2,1,0:T(8,128)S(1)} %get-tuple-element.110), channel_id=1, source_target_pairs={{8,0},{10,2},{12,4},{14,6},{16,8},{18,10},{20,12},{22,14},{24,16},... | collective-permute-start | bytes 786440 | tf_op jit(solution)/shard_map/ppermute | solution.py:39
  667.8 11.8 %copy-start.4 = (f32[4,128,256]{2,1,0:T(8,128)S(1)}, f32[4,128,256]{2,1,0:T(8,128)}, u32[]{:S(2)}) copy-start(f32[4,128,256]{2,1,0:T(8,128)} %copy-done.3) | copy-start | bytes 1572868
  680.0 23.1 %collective-permute-start.14 = (f32[4,128,128]{2,1,0:T(8,128)S(1)}, f32[4,128,128]{2,1,0:T(8,128)S(1)}, u32[]{:S(2)}, u32[]{:S(2)}) collective-permute-start(f32[4,128,128]{2,1,0:T(8,128)S(1)} %convolution_add_fusion.1), channel_id=1, source_target_pairs={{8,0},{10,2},{12,4},{14,6},{16,8},{18,10},{20,12},{22,14},{24,16},... | collective-permute-start | bytes 786440 | tf_op jit(solution)/shard_map/ppermute | solution.py:39
  686.2 18.6 %copy-start.6 = (bf16[2048,256]{1,0:T(8,128)(2,1)S(1)}, bf16[2048,256]{1,0:T(8,128)(2,1)}, u32[]{:S(2)}) copy-start(bf16[2048,256]{1,0:T(8,128)(2,1)} %copy-done.5) | copy-start | bytes 3145732
  690.4 82.6 %collective-permute-start.18 = (bf16[4,128,2112]{1,2,0:T(8,128)(2,1)}, bf16[4,128,2112]{1,2,0:T(8,128)(2,1)}, u32[]{:S(2)}, u32[]{:S(2)}) collective-permute-start(bf16[4,128,2112]{1,2,0:T(8,128)(2,1)} %bitcast.196), channel_id=1, source_target_pairs={{0,8},{2,10},{4,12},{6,14},{1,9},{3,11},{5,13},{7,15}} | collective-permute-start | bytes 6488072 | tf_op jit(solution)/shard_map/ppermute | solution.py:39
  701.1 76.6 %collective-permute-start.21 = (bf16[4,128,2112]{1,2,0:T(8,128)(2,1)}, bf16[4,128,2112]{1,2,0:T(8,128)(2,1)}, u32[]{:S(2)}, u32[]{:S(2)}) collective-permute-start(bf16[4,128,2112]{1,2,0:T(8,128)(2,1)} %bitcast.197), channel_id=1, source_target_pairs={{24,16},{26,18},{28,20},{30,22},{25,17},{27,19},{29,21},{31,23}} | collective-permute-start | bytes 6488072 | tf_op jit(solution)/shard_map/ppermute | solution.py:39
  703.5 10.0 copy-start.10
  703.5 10.0 collective-permute-start.15
  713.5 54.7 %copy-start.22 = (bf16[456]{0:T(512)(128)(2,1)S(1)}, bf16[456]{0:T(512)(128)(2,1)}, u32[]{:S(2)}) copy-start(bf16[456]{0:T(512)(128)(2,1)} %pad.27.clone) | copy-start | bytes 2740
  766.4 6.0 collective-permute-start.16
  792.6 89.6 %collective-permute-start.19 = (bf16[4,128,2112]{1,2,0:T(8,128)(2,1)}, bf16[4,128,2112]{1,2,0:T(8,128)(2,1)}, u32[]{:S(2)}, u32[]{:S(2)}) collective-permute-start(bf16[4,128,2112]{1,2,0:T(8,128)(2,1)} %copy.220), channel_id=1, source_target_pairs={{0,8},{2,10},{4,12},{6,14},{8,16},{10,18},{12,20},{14,22},{1,9},{3... | collective-permute-start | bytes 6488072 | tf_op jit(solution)/shard_map/ppermute | solution.py:39
  841.9 40.4 %copy-start.15 = (bf16[1,4,128,2112]{2,3,1,0:T(8,128)(2,1)S(1)}, bf16[1,4,128,2112]{2,3,1,0:T(8,128)(2,1)}, u32[]{:S(2)}) copy-start(bf16[1,4,128,2112]{2,3,1,0:T(8,128)(2,1)} %copy.217) | copy-start | bytes 6488068
  841.9 50.0 %collective-permute-start.22 = (bf16[4,128,2112]{1,2,0:T(8,128)(2,1)}, bf16[4,128,2112]{1,2,0:T(8,128)(2,1)S(1)}, u32[]{:S(2)}, u32[]{:S(2)}) collective-permute-start(bf16[4,128,2112]{1,2,0:T(8,128)(2,1)} %copy.223), channel_id=1, source_target_pairs={{16,8},{18,10},{20,12},{22,14},{24,16},{26,18},{28,20},{30,22},{17... | collective-permute-start | bytes 6488072 | tf_op jit(solution)/shard_map/ppermute | solution.py:39
  859.2 32.7 %copy-start.14 = (bf16[1,4,128,2112]{2,3,1,0:T(8,128)(2,1)S(1)}, bf16[1,4,128,2112]{2,3,1,0:T(8,128)(2,1)}, u32[]{:S(2)}) copy-start(bf16[1,4,128,2112]{2,3,1,0:T(8,128)(2,1)} %copy.218) | copy-start | bytes 6488068
  885.8 9.4 copy-start.16
  885.8 166.4 %collective-permute-start.20 = (bf16[4,128,2112]{1,2,0:T(8,128)(2,1)}, bf16[4,128,2112]{1,2,0:T(8,128)(2,1)}, u32[]{:S(2)}, u32[]{:S(2)}) collective-permute-start(bf16[4,128,2112]{1,2,0:T(8,128)(2,1)} %add_convert_fusion.1), channel_id=1, source_target_pairs={{0,8},{2,10},{4,12},{6,14},{8,16},{10,18},{12,20},{14,22},{16,24},... | collective-permute-start | bytes 6488072 | tf_op jit(solution)/shard_map/ppermute | solution.py:39
  893.8 16.8 %copy-start.1 = (bf16[256,2048]{1,0:T(8,128)(2,1)S(1)}, bf16[256,2048]{1,0:T(8,128)(2,1)}, u32[]{:S(2)}) copy-start(bf16[256,2048]{1,0:T(8,128)(2,1)} %copy-done) | copy-start | bytes 3145732
  893.8 161.4 %collective-permute-start.23 = (bf16[4,128,2112]{1,2,0:T(8,128)(2,1)}, bf16[4,128,2112]{1,2,0:T(8,128)(2,1)}, u32[]{:S(2)}, u32[]{:S(2)}) collective-permute-start(bf16[4,128,2112]{1,2,0:T(8,128)(2,1)} %add_convert_fusion), channel_id=1, source_target_pairs={{8,0},{10,2},{12,4},{14,6},{16,8},{18,10},{20,12},{22,14},{24,16},... | collective-permute-start | bytes 6488072 | tf_op jit(solution)/shard_map/ppermute | solution.py:39
  1049.1 33.5 %collective-permute-start.17 = (f32[264]{0:T(512)S(1)}, f32[264]{0:T(512)S(1)}, u32[]{:S(2)}, u32[]{:S(2)}) collective-permute-start(f32[264]{0:T(512)S(1)} %slice_reduce_fusion), channel_id=1, source_target_pairs={{0,1},{1,0},{2,3},{3,2},{4,5},{5,4},{6,7},{7,6},{8,9},{9,8},{10,11... | collective-permute-start | bytes 3176 | tf_op jit(solution)/shard_map/ppermute | solution.py:23
  1066.1 23.2 %collective-permute-start.24 = (bf16[128,2112]{0,1:T(8,128)(2,1)}, bf16[128,2112]{0,1:T(8,128)(2,1)}, u32[]{:S(2)}, u32[]{:S(2)}) collective-permute-start(bf16[128,2112]{0,1:T(8,128)(2,1)} %bitcast.225), channel_id=1, source_target_pairs={{0,2},{2,0},{4,6},{6,4},{8,10},{10,8},{12,14},{14,12},{16,18},{18,... | collective-permute-start | bytes 1622024 | tf_op jit(solution)/shard_map/ppermute | solution.py:28
  1085.7 26.3 %collective-permute-start.25 = (bf16[128,2112]{0,1:T(8,128)(2,1)}, bf16[128,2112]{0,1:T(8,128)(2,1)}, u32[]{:S(2)}, u32[]{:S(2)}) collective-permute-start(bf16[128,2112]{0,1:T(8,128)(2,1)} %bitcast.227), channel_id=1, source_target_pairs={{0,4},{2,6},{4,0},{6,2},{8,12},{10,14},{12,8},{14,10},{16,20},{18,... | collective-permute-start | bytes 1622024 | tf_op jit(solution)/shard_map/ppermute | solution.py:28
  1088.0 25.5 %collective-permute-start.26 = (bf16[128,2112]{0,1:T(8,128)(2,1)}, bf16[128,2112]{0,1:T(8,128)(2,1)}, u32[]{:S(2)}, u32[]{:S(2)}) collective-permute-start(bf16[128,2112]{0,1:T(8,128)(2,1)} %bitcast.226), channel_id=1, source_target_pairs={{0,6},{2,4},{4,2},{6,0},{8,14},{10,12},{12,10},{14,8},{16,22},{18,... | collective-permute-start | bytes 1622024 | tf_op jit(solution)/shard_map/ppermute | solution.py:28
  (8 other events, 25.7 us)

commit v4 on v3

v4 whole, which is shorter than its diff:
```python
import functools

import jax
import jax.numpy as jnp
from jax import lax
from jax.experimental import pallas as pl
from jax.experimental.pallas import tpu as pltpu
from jax.sharding import PartitionSpec as P

CONV = 4
MATES = 4
SMALL = 16


epsilon = 1e-06
low = jnp.bfloat16
wide = jnp.float32


def other_core(value):
    return lax.ppermute(value, "tp", [(0, 1), (1, 0)])


def to_mate(value, flip):
    count = lax.axis_size("seq")
    return lax.ppermute(value, "seq", [(source, source ^ flip) for source in range(count)])


def mate_of():
    return lax.axis_index("seq") % MATES


def line_of():
    return lax.axis_index("seq") // MATES


def line_groups():
    lines = lax.axis_size("seq") // MATES
    return [[mate + MATES * line for line in range(lines)] for mate in range(MATES)]


def pick(blocks, index):
    return lax.dynamic_index_in_dim(blocks, index, 0, False)


def in_order(by_flip):
    mate = mate_of()
    out = jnp.zeros((MATES,) + by_flip[0].shape, by_flip[0].dtype)
    for flip, piece in enumerate(by_flip):
        out = lax.dynamic_update_index_in_dim(out, piece, mate ^ flip, 0)
    return out


def swap_blocks(blocks):
    mate = mate_of()
    pieces = [pick(blocks, mate)]
    for flip in range(1, MATES):
        pieces.append(to_mate(pick(blocks, mate ^ flip), flip))
    return in_order(pieces)


def gather_lines(block):
    return lax.all_gather(block, "seq", axis_index_groups=line_groups())


def scatter_lines(blocks):
    return lax.psum_scatter(blocks, "seq", scatter_dimension=0, axis_index_groups=line_groups())


def matmul(form, left, right):
    return jnp.einsum(form, left, right, preferred_element_type=wide)


def silu_slope(value):
    squash = jax.nn.sigmoid(value)
    return squash * (1.0 + value * (1.0 - squash))


CHUNK = 128
TOGETHER = 4
VMEM_BYTES = 58 * 1024 * 1024
NN = (((1,), (0,)), ((), ()))
NT = (((1,), (1,)), ((), ()))


def dot(left, right, dims):
    return lax.dot_general(left, right, dims, preferred_element_type=wide)


def pair(value):
    high = value.astype(low)
    return high, (value - high.astype(wide)).astype(low)


def side(left, right):
    return jnp.concatenate([left, right], axis=1)


def over(top, bottom):
    return jnp.concatenate([top, bottom], axis=0)


def nn(left, right):
    width = right[0].shape[1]
    both = side(*right)
    out = dot(side(*left), over(both, both), NN)
    return out[:, :width] + out[:, width:]


def nt(left, right):
    width = right[0].shape[0]
    out = dot(side(*left), over(side(right[0], right[0]), side(right[1], right[1])), NT)
    return out[:, :width] + out[:, width:]


def nn_wide(left, right):
    return dot(side(*left), over(right[0], right[0]), NN) + dot(left[0], right[1], NN)


def nn_low(left, right):
    return dot(side(*left), over(right, right), NN)


def low_nn(left, right):
    return dot(side(left, left), over(*right), NN)


def low_nt(left, right):
    return dot(side(left, left), side(*right), NT)


def grid_of_rows():
    rows = lax.broadcasted_iota(jnp.int32, (CHUNK, CHUNK), 0)
    columns = lax.broadcasted_iota(jnp.int32, (CHUNK, CHUNK), 1)
    return rows, columns


def inverse_of(strict):
    rows, columns = grid_of_rows()
    one = jnp.where(rows == columns, 1.0, 0.0).astype(wide)

    def joining(shift):
        upper = columns >> shift
        return ((rows >> shift) == upper + 1) & ((upper & 1) == 0)

    solved = [one - jnp.where(joining(0), s, 0.0) for s in strict]
    shift = 1
    while (1 << shift) < CHUNK:
        mask = joining(shift)
        pairs = [pair(d) for d in solved]
        crossed = [nn(pair(jnp.where(mask, s, 0.0)), p) for s, p in zip(strict, pairs)]
        solved = [d - nn(p, pair(c)) for d, p, c in zip(solved, pairs, crossed)]
        shift += 1
    return solved


def convolved(block, taps, stream):
    columns = block[:, stream * CHUNK : (stream + 1) * CHUNK]
    total = None
    for offset in range(CONV):
        first = 16 - (CONV - 1) + offset
        term = taps[stream * CONV + offset][None, :] * columns[first : first + CHUNK]
        total = term if total is None else total + term
    return total


def silu_parts(value):
    squash = jax.nn.sigmoid(value)
    return value * squash, squash * (1.0 + value * (1.0 - squash))


def live_rows(limit, start):
    rows = lax.broadcasted_iota(jnp.int32, (CHUNK, CHUNK), 0)
    return jnp.where(rows + start < limit, 1.0, 0.0).astype(wide)


def head_squash(logits, head):
    lanes = lax.broadcasted_iota(jnp.int32, logits.shape, 1)
    column = jnp.sum(jnp.where(lanes == head, logits, 0.0), axis=1, keepdims=True)
    return jax.nn.sigmoid(jnp.broadcast_to(column, logits.shape))


def front_kernel(
    lines, heads, moves, limit_ref, raw_any, raw_ref, taps_ref, logit_ref, gate_ref, scale_ref, grad_any,
    *rest,
):
    count = len(moves)
    outs = rest[count:]
    qkv_ref, solved_ref, wu_ref, map_ref, total_ref, tails_ref = outs[:6]
    state_ref, fresh_ref, mixed_ref, gated_ref, grads = outs[6:11]
    targets, scratch = outs[11 : 11 + count], outs[11 + count :]
    ext, offsets, maps, prefixes, locals_, wus, qkvs, enters, leaves, tails = scratch[:10]
    tail_sems, state_sems = scratch[10:12]
    scratch = scratch[12:]
    step = pl.program_id(0)
    chains, chunks = maps.shape[0], maps.shape[1]
    span = chunks * CHUNK
    head_size = CHUNK
    streams = 3 * heads * head_size
    place = Place()
    share = ShareRows(place, grad_any.at[place.core], grads, scratch[:3])
    gathers = [
        GatherLines(place, None, target, scratch[3 + 6 * index : 9 + 6 * index], moves[index])
        for index, target in enumerate(targets)
    ]
    below, above = place.line > 0, place.line < lines - 1
    rows, columns = grid_of_rows()
    identity = jnp.where(rows == columns, 1.0, 0.0).astype(wide)

    def tail(seq):
        return pltpu.make_async_remote_copy(
            src_ref=raw_any.at[pl.ds((seq + 1) * span - 16, 16), pl.ds(0, streams)],
            dst_ref=tails.at[seq],
            send_sem=tail_sems.at[0, seq],
            recv_sem=tail_sems.at[1, seq],
            device_id=place.lines_away(1),
            device_id_type=MESH,
        )

    state_copy = pltpu.make_async_remote_copy(
        src_ref=leaves,
        dst_ref=enters,
        send_sem=state_sems.at[0],
        recv_sem=state_sems.at[1],
        device_id=place.lines_away(1),
        device_id_type=MESH,
    )
    seqs = chains // heads

    @pl.when(step == 0)
    def _():
        meet(place, lines=lines)
        for seq in range(seqs):
            pl.when(above)(tail(seq).start)
        for gather in gathers:
            gather.leave(False)
        share.begin_half(False)
        share.begin_half(True)
        share.begin_rest()
        for seq in range(seqs):

            @pl.when(below)
            def _(seq=seq):
                tail(seq).wait_recv()

            @pl.when(place.line == 0)
            def _(seq=seq):
                tails[seq] = jnp.zeros(tails.shape[1:], low)

        tails_ref[...] = tails[...]

    def form(chain):
        seq, head = chain // heads, chain % heads
        ext[:16] = tails[seq, :, pl.ds(pl.multiple_of(head * 3 * head_size, 128), 3 * head_size)].astype(wide)
        ext[16:] = raw_ref[...].astype(wide)
        taps = taps_ref[0]
        limit = limit_ref[seq]

        def group(index, carry):
            first = index * TOGETHER
            parts = []
            for number in range(TOGETHER):
                start = pl.multiple_of((first + number) * CHUNK, CHUNK)
                block = ext[pl.ds(start, CHUNK + 16)]
                query = jax.nn.silu(convolved(block, taps, 0))
                key = jax.nn.silu(convolved(block, taps, 1))
                value = jax.nn.silu(convolved(block, taps, 2)).astype(low)
                query = query * lax.rsqrt(jnp.sum(query * query, axis=1, keepdims=True) + epsilon)
                query = (query * head_size ** (-0.5)).astype(low)
                key = key * lax.rsqrt(jnp.sum(key * key, axis=1, keepdims=True) + epsilon)
                key = key.astype(low)
                beta = head_squash(logit_ref[pl.ds(start, CHUNK)], head) * live_rows(limit, start)
                together = jnp.concatenate([query, key, value], axis=1)
                qkv_ref[pl.ds(start, CHUNK)] = together
                qkvs[chain, pl.ds(start, CHUNK)] = together
                parts.append((key, value, beta))
            strict = [
                jnp.where(rows > columns, beta * dot(key, key, NT), 0.0) for key, _, beta in parts
            ]
            solved = inverse_of(strict)
            for number in range(TOGETHER):
                key, value, beta = parts[number]
                solved_ref[0, first + number] = solved[number]
                weighted = pair(solved[number] * beta.T)
                both = nn_low(weighted, side(key, value))
                wu_ref[0, first + number] = both
                wus[chain, first + number] = both
                moved = low_nn(key.T, pair(both))
                step_map = identity - moved[:, :head_size]
                map_ref[0, first + number] = step_map
                maps[chain, first + number] = step_map
                offsets[chain, first + number] = moved[:, head_size:]
            return carry

        lax.fori_loop(0, chunks // TOGETHER, group, 0)

    @pl.when(step < chains)
    def _():
        form(step)

    @pl.when(step == chains - 2)
    def _():
        share.forward()

    @pl.when(step == chains - 1)
    def _():
        start = side(identity, jnp.zeros_like(identity))

        def advance(chunk, states):
            out = []
            for index in range(chains):
                state = states[index]
                prefixes[index, chunk] = state[:, :head_size]
                locals_[index, chunk] = state[:, head_size:]
                moved = nn_wide(pair(maps[index, chunk]), pair(state))
                out.append(
                    side(moved[:, :head_size], moved[:, head_size:] + offsets[index, chunk])
                )
            return tuple(out)

        ends = lax.fori_loop(0, chunks, advance, (start,) * chains)

        @pl.when(below)
        def _():
            state_copy.wait_recv()

        @pl.when(place.line == 0)
        def _():
            enters[...] = jnp.zeros_like(enters)

        for index in range(chains):
            total_ref[index] = ends[index][:, :head_size]
            leaving = nn_low(pair(ends[index][:, :head_size]), enters[index])
            leaves[index] = (leaving + ends[index][:, head_size:]).astype(low)
        pl.when(above)(state_copy.start)
        for gather in gathers:
            gather.onwards(1)
        share.forward_far()

    def outputs(chain):
        enter = enters[chain]
        scale = scale_ref[...]

        def group(index, carry):
            for number in range(TOGETHER):
                chunk = index * TOGETHER + number
                start = pl.multiple_of(chunk * CHUNK, CHUNK)
                here = pl.ds(start, CHUNK)
                state = nn_low(pair(prefixes[chain, chunk]), enter) + locals_[chain, chunk]
                state_ref[0, chunk] = state
                states = pair(state)
                both = wus[chain, chunk]
                fresh = both[:, head_size:] - nn(pair(both[:, :head_size]), states)
                fresh_ref[0, chunk] = fresh
                query = qkvs[chain, here, :head_size]
                key = qkvs[chain, here, head_size : 2 * head_size]
                scores = jnp.where(rows >= columns, dot(query, key, NT), 0.0)
                mixed = low_nn(query, states) + nn(pair(scores), pair(fresh))
                mixed_ref[here] = mixed
                inverse = lax.rsqrt(jnp.mean(mixed * mixed, axis=1, keepdims=True) + epsilon)
                normed = mixed * inverse * scale
                gated_ref[here] = (normed * jax.nn.silu(gate_ref[here].astype(wide))).astype(low)
            return carry

        lax.fori_loop(0, chunks // TOGETHER, group, 0)

    @pl.when(step >= chains)
    def _():
        outputs(step - chains)

    @pl.when(step == 2 * chains - 2)
    def _():
        for gather in gathers:
            gather.onwards(2)

    @pl.when(step == 2 * chains - 1)
    def _():
        for number in range(3, lines):
            for gather in gathers:
                gather.onwards(number)
        for gather in gathers:
            gather.finish_lines()
        share.finish()
        for seq in range(seqs):
            pl.when(above)(tail(seq).wait_send)
        pl.when(above)(state_copy.wait_send)


def back_kernel(
    lines, heads, parts, limit_ref, raw_ref, tails_ref, taps_ref, logit_ref, gate_ref, scale_ref, qkv_ref,
    wu_ref, map_ref, total_ref, grad_ref, mixed_ref, solved_ref, state_ref, fresh_in_ref, *rest,
):
    count = len(parts)
    blocks, rest = rest[:count], rest[count:]
    all_ref, gain_ref, taps_grad_ref = rest[:3]
    results, scratch = rest[3 : 3 + count], rest[3 + count :]
    ext, pre_grads, maps, sources, out_grads, fresh_grads, leaving, leaves, enters = scratch[:9]
    halos, edges, returned, halo_sems, state_sems = scratch[9:14]
    scratch = scratch[14:]
    step = pl.program_id(0)
    chains, chunks = maps.shape[0], maps.shape[1]
    span = chunks * CHUNK
    head_size = CHUNK
    streams = 3 * heads * head_size
    place = Place()
    sums = [
        SumLines(place, blocks[index], results[index], scratch[7 * index : 7 * index + 7], first)
        for index, (first, _) in enumerate(parts)
    ]
    below, above = place.line > 0, place.line < lines - 1
    rows, columns = grid_of_rows()

    def halo(chain):
        return pltpu.make_async_remote_copy(
            src_ref=halos.at[chain],
            dst_ref=returned.at[chain],
            send_sem=halo_sems.at[0, chain],
            recv_sem=halo_sems.at[1, chain],
            device_id=place.lines_away(-1),
            device_id_type=MESH,
        )

    state_copy = pltpu.make_async_remote_copy(
        src_ref=enters,
        dst_ref=leaves,
        send_sem=state_sems.at[0],
        recv_sem=state_sems.at[1],
        device_id=place.lines_away(-1),
        device_id_type=MESH,
    )

    @pl.when(step == 0)
    def _():
        meet(place, far=bool(parts), lines=lines)
        for each in sums:
            each.begin()
        for each in sums:
            each.wait_loads()
            each.round(1)

    def turn(chain):
        scale = scale_ref[...]

        def group(index, gain):
            for number in range(TOGETHER):
                chunk = index * TOGETHER + number
                start = pl.multiple_of(chunk * CHUNK, CHUNK)
                here = pl.ds(start, CHUNK)
                grad, mixed = grad_ref[here], mixed_ref[here]
                silu_gate, slope = silu_parts(gate_ref[here].astype(wide))
                inverse = lax.rsqrt(jnp.mean(mixed * mixed, axis=1, keepdims=True) + epsilon)
                unit = mixed * inverse
                gate_grad = (grad * unit * scale * slope).astype(low)
                there = pl.ds(pl.multiple_of(chain // heads * span + start, CHUNK), CHUNK)
                lanes = pl.ds(pl.multiple_of(streams + chain % heads * head_size, 128), head_size)
                all_ref[there, lanes] = gate_grad
                passed = grad * silu_gate
                gain = gain + jnp.sum(passed * unit, axis=0, keepdims=True)
                scaled = passed * scale
                mixed_grad = inverse * (
                    scaled - unit * inverse * jnp.mean(scaled * mixed, axis=1, keepdims=True)
                )
                out_grads[chain, chunk] = mixed_grad
                query, key = qkv_ref[here, :head_size], qkv_ref[here, head_size : 2 * head_size]
                scores = jnp.where(rows >= columns, dot(query, key, NT), 0.0)
                turned = jnp.where(rows <= columns, dot(key, query, NT), 0.0)
                grads = pair(mixed_grad)
                fresh_grads[chain, chunk] = nn(pair(turned), grads)
                reading = query.astype(wide) - nn(
                    pair(scores), pair(wu_ref[0, chunk, :, :head_size])
                )
                sources[chain, chunk] = nn(pair(mixed_grad.T), pair(reading))
                maps[chain, chunk] = map_ref[0, chunk]
            return gain

        gain = lax.fori_loop(0, chunks // TOGETHER, group, jnp.zeros((1, head_size), wide))
        gain_ref[0] = jnp.broadcast_to(gain, (8, head_size))

    @pl.when(step < chains)
    def _():
        turn(step)

    @pl.when(step == chains - 1)
    def _():
        def advance(number, states):
            chunk = chunks - 1 - number
            return tuple(
                nn(pair(states[index]), pair(maps[index, chunk])) + sources[index, chunk]
                for index in range(chains)
            )

        ends = lax.fori_loop(
            0, chunks, advance, (jnp.zeros((head_size, head_size), wide),) * chains
        )

        @pl.when(above)
        def _():
            state_copy.wait_recv()

        @pl.when(place.line == lines - 1)
        def _():
            leaves[...] = jnp.zeros_like(leaves)

        for index in range(chains):
            entering = low_nn(leaves[index], pair(total_ref[index]))
            enters[index] = (entering + ends[index]).astype(low)
        pl.when(below)(state_copy.start)

        def again(number, states):
            chunk = chunks - 1 - number
            out = []
            for index in range(chains):
                leaving[index, chunk] = states[index]
                out.append(
                    nn(pair(states[index]), pair(maps[index, chunk])) + sources[index, chunk]
                )
            return tuple(out)

        lax.fori_loop(
            0, chunks, again, tuple(leaves[index].astype(wide) for index in range(chains))
        )
        for each in sums:
            each.round(2)

    def unwind(chain):
        seq, head = chain // heads, chain % heads
        ext[:16] = tails_ref[seq, :, pl.ds(pl.multiple_of(head * 3 * head_size, 128), 3 * head_size)].astype(wide)
        ext[16:] = raw_ref[...].astype(wide)
        taps = taps_ref[0]
        limit = limit_ref[seq]
        pre_grads[:16] = jnp.zeros((16, 3 * head_size), wide)
        pre_grads[span + 16 :] = jnp.zeros((16, 3 * head_size), wide)

        def one(chunk):
            start = pl.multiple_of(chunk * CHUNK, CHUNK)
            here = pl.ds(start, CHUNK)
            query = qkv_ref[here, :head_size]
            key = qkv_ref[here, head_size : 2 * head_size]
            value = qkv_ref[here, 2 * head_size :]
            live = live_rows(limit, start)
            squash = head_squash(logit_ref[here], head)
            beta = squash * live
            grads = pair(out_grads[chain, chunk])
            fresh = pair(fresh_in_ref[0, chunk])
            state = pair(state_ref[0, chunk])
            leave = pair(leaving[chain, chunk])
            both = wu_ref[0, chunk]
            fresh_grad = fresh_grads[chain, chunk] + low_nt(key, leave)
            fresh_pair = pair(fresh_grad)
            score_grad = jnp.where(rows >= columns, nt(grads, fresh), 0.0)
            turned_grad = jnp.where(rows <= columns, nt(fresh, grads), 0.0)
            query_grad = nt(grads, state) + nn_low(pair(score_grad), key)
            key_grad = nn_low(pair(turned_grad), query) + nn(fresh, leave)
            wkey_grad = -nt(fresh_pair, state)
            right_grad = nn_wide(pair(solved_ref[0, chunk].T), pair(side(wkey_grad, fresh_grad)))
            right = pair(right_grad)
            twos = pair(both)
            found = dot(right[0], over(*twos), NT)
            system_grad = found[:, :CHUNK] + found[:, CHUNK:] + dot(right[1], twos[0], NT)
            system_grad = jnp.where(rows > columns, -system_grad, 0.0)
            gram = dot(key, key, NT)
            gram_grad = beta * system_grad
            key_grad = key_grad + nn_low(pair(gram_grad + gram_grad.T), key)
            key_right, value_right = right_grad[:, :head_size], right_grad[:, head_size:]
            key_grad = key_grad + beta * key_right
            value_grad = beta * value_right
            beta_grad = jnp.sum(
                key_right * key.astype(wide) + value_right * value.astype(wide) + system_grad * gram,
                axis=1,
                keepdims=True,
            )
            lanes = lax.broadcasted_iota(jnp.int32, (CHUNK, head_size), 1)
            logit_grad = jnp.where(
                lanes == head, beta_grad * (live * squash * (1.0 - squash)), 0.0
            ).astype(low)

            there = pl.ds(pl.multiple_of(seq * span + start, CHUNK), CHUNK)
            last_lanes = pl.ds(streams + heads * head_size, head_size)

            @pl.when(head == 0)
            def _():
                all_ref[there, last_lanes] = logit_grad

            @pl.when(head > 0)
            def _():
                all_ref[there, last_lanes] = all_ref[there, last_lanes] + logit_grad

            block = ext[pl.ds(start, CHUNK + 16)]
            grads_pre = []
            for stream, grad in enumerate((query_grad, key_grad, value_grad)):
                act, slope = silu_parts(convolved(block, taps, stream))
                if stream < 2:
                    inverse = lax.rsqrt(jnp.sum(act * act, axis=1, keepdims=True) + epsilon)
                    inner = jnp.sum(act * grad, axis=1, keepdims=True)
                    grad = inverse * (grad - act * (inverse * inverse * inner))
                    if stream == 0:
                        grad = grad * head_size ** (-0.5)
                grads_pre.append(grad * slope)
            pre_grads[pl.ds(start + 16, CHUNK)] = jnp.concatenate(grads_pre, axis=1)

        def group(index, carry):
            for number in range(2):
                one(index * 2 + number)
            return carry

        lax.fori_loop(0, chunks // 2, group, 0)

        def back(block):
            parts = []
            for stream in range(3):
                part = block[:, stream * head_size : (stream + 1) * head_size]
                total = None
                for offset in range(CONV):
                    first = CONV - 1 - offset
                    term = taps[stream * CONV + offset][None, :] * part[first : first + CHUNK]
                    total = term if total is None else total + term
                parts.append(total)
            return jnp.concatenate(parts, axis=1)

        lanes = pl.ds(pl.multiple_of(head * 3 * head_size, 128), 3 * head_size)

        def finish(chunk, totals):
            start = pl.multiple_of(chunk * CHUNK, CHUNK)
            block = pre_grads[pl.ds(start + 16, CHUNK + 16)]
            grad = back(block)
            there = pl.ds(pl.multiple_of(seq * span + start, CHUNK), CHUNK)
            all_ref[there, lanes] = grad.astype(low)
            edges[chain] = grad[CHUNK - 16 :]
            before = ext[pl.ds(start, CHUNK + 16)]
            pre = block[:CHUNK]
            out = []
            for offset in range(CONV):
                first = 16 - (CONV - 1) + offset
                term = jnp.sum(pre * before[first : first + CHUNK], axis=0, keepdims=True)
                out.append(totals[offset] + term)
            return tuple(out)

        zero = jnp.zeros((1, 3 * head_size), wide)
        totals = lax.fori_loop(0, chunks, finish, (zero,) * CONV)
        for offset in range(CONV):
            taps_grad_ref[0, offset : offset + 1] = totals[offset]
        halos[chain] = back(pre_grads[: CHUNK + 32])[:16].astype(low)
        pl.when(below)(halo(chain).start)

    @pl.when(step >= chains)
    def _():
        unwind(step - chains)

    @pl.when(step == 2 * chains - 3)
    def _():
        for each in sums:
            each.round(3)

    @pl.when(step == 2 * chains - 1)
    def _():
        for each in sums:
            for number in range(4, lines):
                each.round(number)
            each.exchange()
        for chain in range(chains):
            seq, head = chain // heads, chain % heads
            last = pl.ds((seq + 1) * span - 16, 16)
            lanes = pl.ds(head * 3 * head_size, 3 * head_size)

            @pl.when(above)
            def _(chain=chain, last=last, lanes=lanes):
                halo(chain).wait_recv()
                all_ref[last, lanes] = (edges[chain] + returned[chain].astype(wide)).astype(low)

        for chain in range(chains):
            pl.when(below)(halo(chain).wait_send)
        pl.when(below)(state_copy.wait_send)
        for each in sums:
            each.finish()


def project_kernel(input_ref, scale_ref, weight_ref, normed_ref, raw_ref, logit_ref):
    value = input_ref[...].astype(wide)
    normed = (value * inverse_rms(value) * scale_ref[...]).astype(low)
    normed_ref[...] = normed
    out = dot(normed, weight_ref[...], NN)
    width = raw_ref.shape[1]
    raw_ref[...] = out[:, :width].astype(low)
    logit_ref[...] = out[:, width:]


MESH = pl.DeviceIdType.MESH
STEP = 16


class Place:
    def __init__(self):
        self.seq = lax.axis_index("seq")
        self.core = lax.axis_index("tp")
        self.mate = self.seq % MATES
        self.line = self.seq // MATES
        x, y = self.mate % 2, self.mate // 2
        self.x = 2 * y + (1 - x)
        self.y = 2 * (1 - y) + x
        self.far = 2 * (1 - y) + (1 - x)
        self.base = self.seq - self.mate

    def of(self, mate):
        return (self.base + mate, self.core)

    @property
    def sibling(self):
        return (self.seq, 1 - self.core)

    def lines_away(self, step):
        return (self.seq + step * MATES, self.core)


def meet(place, far=False, lines=0):
    barrier = pltpu.get_barrier_semaphore()
    partners = [place.of(place.x), place.of(place.y), place.sibling]
    if far:
        partners.append(place.of(place.far))
    for partner in partners:
        pl.semaphore_signal(barrier, inc=1, device_id=partner, device_id_type=MESH)
    count = len(partners)
    if lines > 1:
        below, above = place.line > 0, place.line < lines - 1

        @pl.when(below)
        def _():
            pl.semaphore_signal(
                barrier, inc=1, device_id=place.lines_away(-1), device_id_type=MESH
            )

        @pl.when(above)
        def _():
            pl.semaphore_signal(barrier, inc=1, device_id=place.lines_away(1), device_id_type=MESH)

        count = count + jnp.where(below, 1, 0) + jnp.where(above, 1, 0)
    pl.semaphore_wait(barrier, count)


def sender(sems):
    send, receive = sems

    def make(index, source, target, device):
        return pltpu.make_async_remote_copy(
            src_ref=source,
            dst_ref=target,
            send_sem=send.at[index],
            recv_sem=receive.at[index],
            device_id=device,
            device_id_type=MESH,
        )

    return make


def row_steps(first, last, body):
    def one(step, carry):
        body(pl.ds(pl.multiple_of(first + step * STEP, STEP), STEP))
        return carry

    lax.fori_loop(0, (last - first) // STEP, one, 0)


class SumRows:
    SCRATCH = 4

    @staticmethod
    def scratch(rows, columns):
        return [
            pltpu.VMEM((MATES, rows, columns), low),
            pltpu.VMEM((MATES, rows, columns), low),
            pltpu.VMEM((2, rows // 2, columns), low),
            pltpu.VMEM((2, rows, columns), low),
            pltpu.SemaphoreType.DMA((MATES,)),
            pltpu.SemaphoreType.DMA((10,)),
            pltpu.SemaphoreType.DMA((10,)),
        ]

    def __init__(self, place, partial, scratch):
        self.place, self.partial = place, partial
        self.own, self.swapped, self.relay, self.arrived, self.local_sems, send, receive = scratch
        self.make = sender((send, receive))
        self.rows = self.own.shape[1]
        self.order = [place.far, place.x, place.y, place.mate]

    def begin(self):
        self.swaps, self.loads = [], []
        for slot, mate in enumerate(self.order):
            copy = self.make(
                slot, self.partial.at[1, mate], self.swapped.at[slot], self.place.sibling
            )
            copy.start()
            self.swaps.append(copy)
            load = pltpu.make_async_copy(
                self.partial.at[0, mate], self.own.at[slot], self.local_sems.at[slot]
            )
            load.start()
            self.loads.append(load)

    def add(self, target, target_slot, source, source_slot, first, last, shift=0):
        def body(here):
            there = pl.ds(pl.multiple_of(here.start - shift, STEP), STEP) if shift else here
            target[target_slot, here] = (
                target[target_slot, here].astype(wide) + source[source_slot, there].astype(wide)
            ).astype(low)

        row_steps(first, last, body)

    def sum_cores(self, slot):
        self.loads[slot].wait()
        self.swaps[slot].wait_recv()
        self.add(self.own, slot, self.swapped, slot, 0, self.rows)

    def send_far(self):
        half = self.rows // 2
        self.sum_cores(0)
        self.far_low = self.make(
            4, self.own.at[0, :half], self.relay.at[0], self.place.of(self.place.y)
        )
        self.far_high = self.make(
            5, self.own.at[0, half:], self.relay.at[1], self.place.of(self.place.x)
        )
        self.far_low.start()
        self.far_high.start()

    def send_near(self):
        half, place = self.rows // 2, self.place
        self.sum_cores(1)
        self.x_high = self.make(
            6, self.own.at[1, half:], self.arrived.at[0, half:], place.of(place.x)
        )
        self.x_high.start()
        self.sum_cores(2)
        self.y_low = self.make(
            7, self.own.at[2, :half], self.arrived.at[1, :half], place.of(place.y)
        )
        self.y_low.start()

    def send_relayed(self):
        half, place = self.rows // 2, self.place
        self.far_low.wait_recv()
        self.add(self.own, 1, self.relay, 0, 0, half)
        self.x_low = self.make(
            8, self.own.at[1, :half], self.arrived.at[0, :half], place.of(place.x)
        )
        self.x_low.start()
        self.far_high.wait_recv()
        self.add(self.own, 2, self.relay, 1, half, self.rows, shift=half)
        self.y_high = self.make(
            9, self.own.at[2, half:], self.arrived.at[1, half:], place.of(place.y)
        )
        self.y_high.start()
        self.sum_cores(3)

    def wait_half(self, upper):
        if upper:
            self.x_high.wait_recv()
            self.y_high.wait_recv()
        else:
            self.x_low.wait_recv()
            self.y_low.wait_recv()

    def total(self, here):
        return (
            self.own[3, here].astype(wide)
            + self.arrived[0, here].astype(wide)
            + self.arrived[1, here].astype(wide)
        )

    def finish(self):
        for copy in self.swaps + [
            self.far_low, self.far_high, self.x_high, self.y_low, self.x_low, self.y_high,
        ]:
            copy.wait_send()


class ShareRows:
    @staticmethod
    def scratch():
        return [
            pltpu.SemaphoreType.DMA((1,)),
            pltpu.SemaphoreType.DMA((11,)),
            pltpu.SemaphoreType.DMA((11,)),
        ]

    def __init__(self, place, source, target, scratch):
        self.place, self.source, self.target = place, source, target
        self.local_sem, send, receive = scratch
        self.make = sender((send, receive))
        self.rows = target.shape[2]

    def copy(self, index):
        place, half = self.place, self.rows // 2
        lower, upper, whole = pl.ds(0, half), pl.ds(half, half), pl.ds(0, self.rows)
        x, y, sibling = place.of(place.x), place.of(place.y), place.sibling

        def own(rows, device, side=0):
            return self.source.at[rows], self.target.at[side, place.mate, rows], device

        def passed(mate, rows, device, side=0):
            return self.target.at[0, mate, rows], self.target.at[side, mate, rows], device

        return self.make(
            index,
            *(
                lambda: own(upper, y),
                lambda: own(upper, x),
                lambda: own(lower, x),
                lambda: own(lower, y),
                lambda: passed(place.x, lower, y),
                lambda: passed(place.y, upper, x),
                lambda: own(whole, sibling, 1),
                lambda: passed(place.x, whole, sibling, 1),
                lambda: passed(place.y, whole, sibling, 1),
                lambda: passed(place.far, lower, sibling, 1),
                lambda: passed(place.far, upper, sibling, 1),
            )[index](),
        )

    def local(self):
        return pltpu.make_async_copy(
            self.source, self.target.at[0, self.place.mate], self.local_sem.at[0]
        )

    def begin_half(self, upper):
        for index in (0, 1) if upper else (2, 3):
            self.copy(index).start()

    def begin_rest(self):
        self.local().start()
        self.copy(6).start()

    def forward(self):
        for came, then in ((2, 4), (0, 5), (1, 7), (3, 8)):
            self.copy(came).wait_recv()
            self.copy(then).start()

    def forward_far(self):
        for came, then in ((4, 9), (5, 10)):
            self.copy(came).wait_recv()
            self.copy(then).start()

    def finish(self):
        self.local().wait()
        for index in range(6, 11):
            self.copy(index).wait_recv()
        for index in range(11):
            self.copy(index).wait_send()


class GatherLines:
    @staticmethod
    def scratch(lines):
        return [
            pltpu.SemaphoreType.DMA((1,)),
            pltpu.SemaphoreType.DMA((3,)),
            pltpu.SemaphoreType.DMA((3,)),
            pltpu.SemaphoreType.DMA((lines, MATES)),
            pltpu.SemaphoreType.DMA((lines, MATES)),
            pltpu.SemaphoreType.DMA((lines, MATES)),
        ]

    def __init__(self, place, blocks, target, scratch, rows=None):
        self.place, self.blocks, self.target = place, blocks, target
        self.lines = target.shape[0]
        self.part = pl.ds(*(rows or (0, target.shape[2])))
        self.local_sem, send, receive, self.up_sem, self.down_sem, self.got = scratch
        self.make = sender((send, receive))
        self.order = [place.mate, place.x, place.y, place.far]

    def plane(self, slot):
        place, mate = self.place, self.order[slot]
        here = self.target.at[place.line, place.mate]
        if slot == 0:
            return pltpu.make_async_copy(self.blocks.at[mate], here, self.local_sem.at[0])
        return self.make(slot - 1, self.blocks.at[mate], here, place.of(mate))

    def begin(self):
        for slot in range(MATES):
            self.plane(slot).start()

    def arrive(self, slot):
        copy = self.plane(slot)
        copy.wait_recv() if slot else copy.wait()

    def hop(self, step, mate, direction):
        place = self.place
        line = place.line - step * direction
        piece = self.target.at[line, mate, self.part]
        sems = self.up_sem if direction > 0 else self.down_sem
        copy = pltpu.make_async_remote_copy(
            src_ref=piece,
            dst_ref=piece,
            send_sem=sems.at[step, mate],
            recv_sem=self.got.at[line, mate],
            device_id=place.lines_away(direction),
            device_id_type=MESH,
        )
        came = (line >= 0) & (line < self.lines)
        goes = (place.line < self.lines - 1) if direction > 0 else (place.line > 0)
        return copy, came, goes

    def leave(self, arriving=True):
        for slot, mate in enumerate(self.order):
            if arriving:
                self.arrive(slot)
            for direction in (1, -1):
                copy, _, goes = self.hop(0, mate, direction)
                pl.when(goes)(copy.start)

    def onwards(self, step):
        if step >= self.lines:
            return
        for mate in self.order:
            for direction in (1, -1):
                copy, came, goes = self.hop(step, mate, direction)
                pl.when(came)(copy.wait_recv)
                if step < self.lines - 1:
                    pl.when(came & goes)(copy.start)

    def finish_plane(self):
        for slot in range(1, MATES):
            self.plane(slot).wait_send()

    def finish_lines(self):
        for step in range(self.lines - 1):
            for mate in self.order:
                for direction in (1, -1):
                    copy, came, goes = self.hop(step, mate, direction)
                    pl.when(came & goes)(copy.wait_send)


class SumLines:
    @staticmethod
    def scratch(lines, shape):
        return [
            pltpu.VMEM((lines,) + shape, low),
            pltpu.VMEM((2, max(lines - 1, 1)) + shape, low),
            pltpu.SemaphoreType.DMA((lines + 1,)),
            pltpu.SemaphoreType.DMA((2, lines)),
            pltpu.SemaphoreType.DMA((2, lines)),
            pltpu.SemaphoreType.DMA((3,)),
            pltpu.SemaphoreType.DMA((3,)),
        ]

    def __init__(self, place, blocks, result, scratch, first=0):
        self.place, self.blocks, self.result, self.first = place, blocks, result, first
        self.held, self.came, self.local_sems, self.send, self.got, send, receive = scratch
        self.lines = self.held.shape[0]
        self.make = sender((send, receive))

    def load(self, line):
        return pltpu.make_async_copy(
            self.blocks.at[line, :, pl.ds(self.first, self.held.shape[2])],
            self.held.at[line],
            self.local_sems.at[line],
        )

    def begin(self):
        for line in range(self.lines):
            self.load(line).start()

    def wait_loads(self):
        for line in range(self.lines):
            self.load(line).wait()

    def put_gains(self, gains):
        lines, mates, height, lanes = self.held.shape
        top = lax.broadcasted_iota(jnp.int32, (height, lanes), 0) == 0
        for line in range(lines):
            for mate in range(mates):
                first = (line * mates + mate) * lanes
                part = jnp.broadcast_to(gains[:, first : first + lanes], (height, lanes))
                self.held[line, mate] = jnp.where(
                    top, part, self.held[line, mate].astype(wide)
                ).astype(low)

    def add_top(self, other, count):
        lines, mates, height, lanes = self.held.shape
        top = lax.broadcasted_iota(jnp.int32, (height, lanes), 0) < count
        for line in range(lines):
            for mate in range(mates):
                own = self.held[line, mate].astype(wide)
                both = own + other[line, mate].astype(wide)
                self.held[line, mate] = jnp.where(top, both, own).astype(low)

    def copy(self, turn, way):
        direction = 1 - 2 * way
        line = self.place.line + direction * (self.lines - turn)
        return line, pltpu.make_async_remote_copy(
            src_ref=self.held.at[line],
            dst_ref=self.came.at[way, turn - 1],
            send_sem=self.send.at[way, turn],
            recv_sem=self.got.at[way, turn],
            device_id=self.place.lines_away(direction),
            device_id_type=MESH,
        )

    def arrival(self, turn, way):
        slot = self.came.at[way, turn - 1]
        return pltpu.make_async_remote_copy(
            src_ref=slot,
            dst_ref=slot,
            send_sem=self.send.at[way, turn],
            recv_sem=self.got.at[way, turn],
            device_id=self.place.sibling,
            device_id_type=MESH,
        )

    def sends(self, turn, way):
        line = self.place.line
        return line <= turn - 1 if way == 0 else line >= self.lines - turn

    def inner(self, way):
        return self.place.line >= 1 if way == 0 else self.place.line <= self.lines - 2

    def add(self, line, way, turn):
        def mates(mate, carry):
            def body(here):
                self.held[line, mate, here] = (
                    self.held[line, mate, here].astype(wide)
                    + self.came[way, turn - 1, mate, here].astype(wide)
                ).astype(low)

            row_steps(0, self.held.shape[2], body)
            return carry

        lax.fori_loop(0, self.held.shape[1], mates, 0)

    def round(self, turn):
        if turn >= self.lines:
            return
        for way in (0, 1):
            line, copy = self.copy(turn, way)

            @pl.when(self.sends(turn, way))
            def _(line=line, copy=copy, way=way):
                if turn > 1:

                    @pl.when(self.inner(way))
                    def _():
                        self.arrival(turn - 1, way).wait_recv()
                        self.add(line, way, turn - 1)

                copy.start()

    def plane(self, index):
        place = self.place
        mate = (place.x, place.y, place.far)[index]
        return self.make(
            index, self.held.at[place.line, mate], self.result.at[place.mate], place.of(mate)
        )

    def local(self):
        place = self.place
        return pltpu.make_async_copy(
            self.held.at[place.line, place.mate],
            self.result.at[place.mate],
            self.local_sems.at[self.lines],
        )

    def exchange(self):
        for way in (0, 1):
            if self.lines > 1:

                @pl.when(self.inner(way))
                def _(way=way):
                    self.arrival(self.lines - 1, way).wait_recv()
                    self.add(self.place.line, way, self.lines - 1)

        for index in range(3):
            self.plane(index).start()
        self.local().start()

    def finish(self):
        self.local().wait()
        for index in range(3):
            self.plane(index).wait()
        for turn in range(1, self.lines):
            for way in (0, 1):
                _, copy = self.copy(turn, way)
                pl.when(self.sends(turn, way))(copy.wait_send)


def remote_call(body, identity, ins, outs, scratch, aliases=None):
    anywhere = pl.BlockSpec(memory_space=pl.ANY)
    held = pl.BlockSpec(memory_space=pltpu.VMEM)
    return pl.pallas_call(
        body,
        in_specs=[anywhere if kind == "any" else held for _, kind in ins],
        out_specs=[anywhere if kind == "any" else held for _, _, kind in outs],
        out_shape=[jax.ShapeDtypeStruct(shape, dtype) for shape, dtype, _ in outs],
        scratch_shapes=scratch,
        input_output_aliases=aliases or {},
        compiler_params=pltpu.CompilerParams(
            vmem_limit_bytes=VMEM_BYTES, collective_id=identity, has_side_effects=True
        ),
    )(*[array for array, _ in ins])


def inverse_rms(value):
    return lax.rsqrt(jnp.mean(value * value, axis=1, keepdims=True) + epsilon)


def norm_back_rows(grad, source, scale):
    inverse = inverse_rms(source)
    scaled = grad * scale
    unit = source * inverse
    inner = jnp.mean(scaled * source, axis=1, keepdims=True)
    return inverse * (scaled - unit * (inverse * inner)), grad * unit


def sum_and_share(rows, share, body, half, during):
    begin, *steps = during
    rows.begin()
    begin()
    rows.send_far()
    rows.send_near()
    rows.send_relayed()
    rows.wait_half(False)
    row_steps(0, half, body)
    share.begin_half(False)
    rows.wait_half(True)
    row_steps(half, 2 * half, body)
    share.begin_half(True)
    share.begin_rest()
    steps[0]()
    rows.finish()
    share.forward()
    steps[1]()
    share.forward_far()
    steps[2]()
    share.finish()


def middle_kernel(lines, moves, partial, input_ref, scale_ref, *rest):
    place = Place()
    count = len(moves)
    middle_ref, shared = rest[count : count + 2]
    targets, scratch = rest[count + 2 : 2 * count + 2], rest[2 * count + 2 :]
    normed, scratch = scratch[0], scratch[1:]
    meet(place, lines=lines if moves else 0)
    rows = SumRows(place, partial, scratch[:7])
    share = ShareRows(place, normed, shared, scratch[7:10])
    gathers = [
        GatherLines(place, None, target, scratch[10 + 6 * index : 16 + 6 * index], moves[index])
        for index, target in enumerate(targets)
    ]

    def body(here):
        middle = input_ref[here].astype(wide) + rows.total(here)
        middle_ref[here] = middle
        normed[here] = (middle * inverse_rms(middle) * scale_ref[...]).astype(low)

    def leave():
        for gather in gathers:
            gather.leave(False)

    def step(number):
        def go():
            for gather in gathers:
                gather.onwards(number)

        return go

    def last():
        for number in range(3, lines):
            for gather in gathers:
                gather.onwards(number)
        for gather in gathers:
            gather.finish_lines()

    sum_and_share(rows, share, body, normed.shape[0] // 2, (leave, step(1), step(2), last))


def turn_rows_kernel(lines, parts, partial, middle_ref, grad_ref, scale_ref, *rest):
    place = Place()
    count = len(parts)
    blocks, rest = rest[:count], rest[count:]
    middle_grad_ref, gain_ref, shared = rest[:3]
    results, scratch = rest[3 : 3 + count], rest[3 + count :]
    low_grad, scratch = scratch[0], scratch[1:]
    meet(place, far=bool(parts), lines=lines if parts else 0)
    rows = SumRows(place, partial, scratch[:7])
    share = ShareRows(place, low_grad, shared, scratch[7:10])
    sums = [
        SumLines(place, blocks[index], results[index], scratch[10 + 7 * index : 17 + 7 * index], first)
        for index, (first, _) in enumerate(parts)
    ]
    for each in sums:
        each.begin()
    gain_ref[...] = jnp.zeros_like(gain_ref)

    def body(here):
        part, gains = norm_back_rows(rows.total(here), middle_ref[here], scale_ref[...])
        total = grad_ref[here].astype(wide) + part
        middle_grad_ref[here] = total
        low_grad[here] = total.astype(low)
        gain_ref[...] += jnp.sum(gains, axis=0, keepdims=True)

    def begin():
        for each in sums:
            each.wait_loads()
            each.round(1)

    def step(number):
        def go():
            for each in sums:
                each.round(number)

        return go

    def last():
        for each in sums:
            for number in range(4, lines):
                each.round(number)
            each.exchange()
        for each in sums:
            each.finish()

    sum_and_share(rows, share, body, low_grad.shape[0] // 2, (begin, step(2), step(3), last))


def last_rows_kernel(
    lines, pieces, partial, mlp_partial, input_ref, middle_ref, middle_grad_ref, scale_ref, *rest
):
    place = Place()
    blocks, rest = rest[:pieces], rest[pieces:]
    input_grad, block_output, gain_ref = rest[:3]
    results, scratch = rest[3 : 3 + pieces], rest[3 + pieces :]
    low_grad, low_output = scratch[:2]
    meet(place, far=bool(pieces), lines=lines if pieces else 0)
    rows = SumRows(place, partial, scratch[2:9])
    outs = SumRows(place, mlp_partial, scratch[9:16])
    make = sender(scratch[16:18])
    local_sems = scratch[18]
    sums = [
        SumLines(place, blocks[index], results[index], scratch[19 + 7 * index : 26 + 7 * index])
        for index in range(pieces)
    ]
    whole = low_grad.shape[0]
    for each in sums:
        each.begin()
    rows.begin()
    outs.begin()
    for each in sums:
        each.wait_loads()
    for each in sums[1:]:
        each.round(1)
    gain_ref[...] = jnp.zeros_like(gain_ref)
    rows.send_far()
    rows.send_near()
    outs.send_far()
    rows.send_relayed()
    outs.send_near()
    for each in sums[1:]:
        each.round(2)
    outs.send_relayed()
    rows.wait_half(False)
    rows.wait_half(True)

    def body(here):
        part, gains = norm_back_rows(
            rows.total(here), input_ref[here].astype(wide), scale_ref[...]
        )
        low_grad[here] = (middle_grad_ref[here] + part).astype(low)
        gain_ref[...] += jnp.sum(gains, axis=0, keepdims=True)

    row_steps(0, whole, body)
    first = make(0, low_grad, input_grad.at[place.core], place.sibling)
    first.start()
    first_local = pltpu.make_async_copy(low_grad, input_grad.at[place.core], local_sems.at[0])
    first_local.start()
    if sums:
        mine, theirs = scratch[19 + 7 * pieces :]
        small = sums[0]
        small.put_gains(gain_ref)
        mine[...] = small.held[...]
        swap = make(2, mine, theirs, place.sibling)
        swap.start()
        swap.wait_recv()
        small.add_top(theirs, 3)
        small.round(1)
        small.round(2)
    outs.wait_half(False)
    outs.wait_half(True)

    def out_body(here):
        low_output[here] = (middle_ref[here] + outs.total(here)).astype(low)

    row_steps(0, whole, out_body)
    second = make(1, low_output, block_output.at[place.core], place.sibling)
    second.start()
    second_local = pltpu.make_async_copy(low_output, block_output.at[place.core], local_sems.at[1])
    second_local.start()
    for turn in range(3, lines):
        for each in sums:
            each.round(turn)
    for each in sums:
        each.exchange()
    rows.finish()
    outs.finish()
    first_local.wait()
    second_local.wait()
    first.wait()
    second.wait()
    if sums:
        swap.wait_send()
    for each in sums:
        each.finish()


def first_rows_kernel(lines, whole, pieces, input_ref, *rest):
    place = Place()
    ins, rest = rest[:pieces], rest[pieces:]
    inputs, outs, scratch = rest[0], rest[1 : 1 + pieces], rest[1 + pieces :]
    meet(place, far=bool(pieces), lines=lines if pieces else 0)
    share = ShareRows(place, input_ref.at[place.core], inputs, scratch[:3])
    gathers = [
        GatherLines(place, ins[index], outs[index], scratch[3 + 6 * index : 9 + 6 * index])
        for index in range(pieces)
    ]
    for gather in gathers[:whole]:
        gather.begin()
    share.begin_half(False)
    share.begin_half(True)
    share.begin_rest()
    for gather in gathers[whole:]:
        gather.begin()
    for gather in gathers[:whole]:
        gather.leave()
    share.forward()
    for gather in gathers[:whole]:
        gather.onwards(1)
    share.forward_far()
    for step in range(2, lines):
        for gather in gathers[:whole]:
            gather.onwards(step)
    share.finish()
    for gather in gathers[whole:]:
        for slot in range(MATES):
            gather.arrive(slot)
    for gather in gathers:
        gather.finish_plane()
    for gather in gathers[:whole]:
        gather.finish_lines()


def first_rows(block_input, blocks, whole, lines):
    seqs, rows, columns = block_input.shape
    shape = (seqs, MATES, rows, columns)
    return remote_call(
        functools.partial(first_rows_kernel, lines, whole, len(blocks)),
        0,
        [(array, "any") for array in (block_input, *blocks)],
        [(shape, low, "any")] + [((lines,) + block.shape, low, "any") for block in blocks],
        ShareRows.scratch() + GatherLines.scratch(lines) * len(blocks),
    )


def middle_rows(partial, mine, scale, moving, lines):
    seqs, _, rows, columns = partial.shape
    arrays = [array for array, _ in moving]
    return remote_call(
        functools.partial(middle_kernel, lines, tuple(part for _, part in moving)),
        1,
        [(partial, "any"), (mine, "held"), (scale, "held")] + [(array, "any") for array in arrays],
        [((rows, columns), wide, "held"), (partial.shape, low, "any")]
        + [(array.shape, low, "any") for array in arrays],
        [pltpu.VMEM((rows, columns), low)]
        + SumRows.scratch(rows, columns)
        + ShareRows.scratch()
        + GatherLines.scratch(lines) * len(arrays),
        {3 + index: 2 + index for index in range(len(arrays))},
    )


def turn_rows(partial, middle, grad, scale, summing, lines):
    seqs, _, rows, columns = partial.shape
    scratch = (
        [pltpu.VMEM((rows, columns), low)] + SumRows.scratch(rows, columns) + ShareRows.scratch()
    )
    outs = []
    for array, (_, height) in summing:
        shape = (MATES, height, array.shape[3])
        scratch += SumLines.scratch(lines, shape)
        outs.append((shape, low, "any"))
    return remote_call(
        functools.partial(turn_rows_kernel, lines, tuple(part for _, part in summing)),
        2,
        [(partial, "any"), (middle, "held"), (grad, "held"), (scale, "held")]
        + [(array, "any") for array, _ in summing],
        [
            ((rows, columns), wide, "held"),
            ((1, columns), wide, "held"),
            (partial.shape, low, "any"),
        ]
        + outs,
        scratch,
    )


def last_rows(partial, mlp_partial, mine, middle, middle_grad, scale, blocks, lines):
    seqs, _, rows, columns = partial.shape
    scratch = (
        [pltpu.VMEM((rows, columns), low), pltpu.VMEM((rows, columns), low)]
        + SumRows.scratch(rows, columns)
        + SumRows.scratch(rows, columns)
        + [pltpu.SemaphoreType.DMA((3,))] * 3
    )
    for block in blocks:
        scratch += SumLines.scratch(lines, block.shape[1:])
    if blocks:
        scratch += [pltpu.VMEM(blocks[0].shape, low)] * 2
    return remote_call(
        functools.partial(last_rows_kernel, lines, len(blocks)),
        3,
        [(partial, "any"), (mlp_partial, "any")]
        + [(array, "held") for array in (mine, middle, middle_grad, scale)]
        + [(block, "any") for block in blocks],
        [
            ((seqs, rows, columns), low, "any"),
            ((seqs, rows, columns), low, "any"),
            ((1, columns), wide, "held"),
        ]
        + [(block.shape[1:], low, "any") for block in blocks],
        scratch,
    )


class Steps:
    def __init__(self, seqs, heads, span):
        self.seqs, self.heads, self.span = seqs, heads, span
        self.chains, self.chunks = seqs * heads, span // CHUNK

    def chain(self, step, when):
        if when == "first":
            return jnp.minimum(step, self.chains - 1)
        if when == "second":
            return jnp.maximum(step - self.chains, 0)
        return step % self.chains

    def rows(self, when, columns, place):
        def index(step):
            chain = self.chain(step, when)
            return chain // self.heads, place(chain % self.heads)

        return pl.BlockSpec((self.span, columns), index)

    def streams(self, when):
        return self.rows(when, 3 * CHUNK, lambda head: head)

    def head(self, when):
        return self.rows(when, CHUNK, lambda head: head)

    def gate(self, when):
        return self.rows(when, CHUNK, lambda head: 3 * self.heads + head)

    def logit(self, when):
        return self.rows(when, CHUNK, lambda head: 0)

    def taps(self, when):
        return pl.BlockSpec(
            (1, 3 * CONV, CHUNK), lambda step: (self.chain(step, when) % self.heads, 0, 0)
        )

    def blocks(self, when, columns=CHUNK):
        return pl.BlockSpec(
            (1, self.chunks, CHUNK, columns), lambda step: (self.chain(step, when), 0, 0, 0)
        )

    def few(self, when, columns):
        return pl.BlockSpec((1, 8, columns), lambda step: (self.chain(step, when), 0, 0))

    def whole(self, shape):
        return pl.BlockSpec(shape, lambda step: (0,) * len(shape), pipeline_mode=pl.Buffered(1))

    def call(self, body, identity, ins, outs, scratch, aliases=None):
        return pl.pallas_call(
            body,
            grid=(2 * self.chains,),
            in_specs=[spec for _, spec in ins],
            out_specs=[spec for _, _, spec in outs],
            out_shape=[jax.ShapeDtypeStruct(shape, dtype) for shape, dtype, _ in outs],
            scratch_shapes=scratch,
            input_output_aliases=aliases or {},
            compiler_params=pltpu.CompilerParams(
                vmem_limit_bytes=VMEM_BYTES,
                dimension_semantics=("arbitrary",),
                collective_id=identity,
                has_side_effects=True,
            ),
        )(*[array for array, _ in ins])


def delta_front(limit, raw, taps, logits, scale, out_grad, moving, lines, seqs, heads, span):
    steps = Steps(seqs, heads, span)
    chains, chunks, size = steps.chains, steps.chunks, CHUNK
    squares, doubles = (chains, chunks, CHUNK, size), (chains, chunks, CHUNK, 2 * size)
    states, tails = (chains, size, size), (seqs, 16, 3 * heads * size)
    tokens, model_width = out_grad.shape[1:]
    anywhere = pl.BlockSpec(memory_space=pl.ANY)
    arrays = [array for array, _ in moving]
    ins = [
        (limit, pl.BlockSpec(memory_space=pltpu.SMEM)),
        (raw, anywhere),
        (raw, steps.streams("first")),
        (taps, steps.taps("first")),
        (logits, steps.logit("first")),
        (raw, steps.gate("second")),
        (scale, steps.whole((1, size))),
        (out_grad, anywhere),
    ] + [(array, anywhere) for array in arrays]
    outs = [
        ((seqs * span, 3 * heads * size), low, steps.streams("first")),
        (squares, wide, steps.blocks("first")),
        (doubles, wide, steps.blocks("first", 2 * size)),
        (squares, wide, steps.blocks("first")),
        (states, wide, steps.whole(states)),
        (tails, low, steps.whole(tails)),
        (squares, wide, steps.blocks("second")),
        (squares, wide, steps.blocks("second")),
        ((seqs * span, heads * size), wide, steps.head("second")),
        ((seqs * span, heads * size), low, steps.head("second")),
        ((seqs, MATES, tokens, model_width), low, anywhere),
    ] + [(array.shape, low, anywhere) for array in arrays]
    scratch = [
        pltpu.VMEM((span + 16, 3 * size), wide),
        pltpu.VMEM(squares, wide),
        pltpu.VMEM(squares, wide),
        pltpu.VMEM(squares, wide),
        pltpu.VMEM(squares, wide),
        pltpu.VMEM(doubles, wide),
        pltpu.VMEM((chains, span, 3 * size), low),
        pltpu.VMEM(states, low),
        pltpu.VMEM(states, low),
        pltpu.VMEM(tails, low),
        pltpu.SemaphoreType.DMA((2, seqs)),
        pltpu.SemaphoreType.DMA((2,)),
    ]
    scratch += ShareRows.scratch() + GatherLines.scratch(lines) * len(arrays)
    moves = tuple(part for _, part in moving)
    return steps.call(
        functools.partial(front_kernel, lines, heads, moves),
        4,
        ins,
        outs,
        scratch,
        {8 + index: 11 + index for index in range(len(arrays))},
    )


def delta_back(
    limit, raw, tails, taps, logits, scale, qkv, wu, maps, total, grad, mixed, solved, state, fresh,
    summing, lines, seqs, heads, span,
):
    steps = Steps(seqs, heads, span)
    chains, chunks, size = steps.chains, steps.chunks, CHUNK
    squares, states = (chains, chunks, CHUNK, size), (chains, size, size)
    all_shape = (seqs * span, (4 * heads + 1) * size)
    anywhere = pl.BlockSpec(memory_space=pl.ANY)
    ins = [
        (limit, pl.BlockSpec(memory_space=pltpu.SMEM)),
        (raw, steps.streams("second")),
        (tails, steps.whole(tails.shape)),
        (taps, steps.taps("second")),
        (logits, steps.logit("second")),
        (raw, steps.gate("first")),
        (scale, steps.whole((1, size))),
        (qkv, steps.streams("both")),
        (wu, steps.blocks("both", 2 * size)),
        (maps, steps.blocks("first")),
        (total, steps.whole(states)),
        (grad, steps.head("first")),
        (mixed, steps.head("first")),
        (solved, steps.blocks("second")),
        (state, steps.blocks("second")),
        (fresh, steps.blocks("second")),
    ] + [(array, anywhere) for array, _ in summing]
    outs = [
        (all_shape, low, steps.whole(all_shape)),
        ((chains, 8, size), wide, steps.few("first", size)),
        ((chains, 8, 3 * size), wide, steps.few("second", 3 * size)),
    ]
    edges = (chains, 16, 3 * size)
    scratch = [
        pltpu.VMEM((span + 16, 3 * size), wide),
        pltpu.VMEM((span + 32, 3 * size), wide),
        pltpu.VMEM(squares, wide),
        pltpu.VMEM(squares, wide),
        pltpu.VMEM(squares, wide),
        pltpu.VMEM(squares, wide),
        pltpu.VMEM(squares, wide),
        pltpu.VMEM(states, low),
        pltpu.VMEM(states, low),
        pltpu.VMEM(edges, low),
        pltpu.VMEM(edges, wide),
        pltpu.VMEM(edges, low),
        pltpu.SemaphoreType.DMA((2, chains)),
        pltpu.SemaphoreType.DMA((2,)),
    ]
    for array, (_, height) in summing:
        shape = (MATES, height, array.shape[3])
        scratch += SumLines.scratch(lines, shape)
        outs.append((shape, low, anywhere))
    return steps.call(
        functools.partial(back_kernel, lines, heads, tuple(part for _, part in summing)),
        5,
        ins,
        outs,
        scratch,
    )


def project(inputs, scale, weight, raw_width):
    rows, model_width = inputs.shape
    columns = weight.shape[1]
    tile = 256

    def tall(width):
        return pl.BlockSpec((tile, width), lambda step: (step, 0))

    def whole(array):
        return pl.BlockSpec(array.shape, lambda step: (0, 0), pipeline_mode=pl.Buffered(1))

    return pl.pallas_call(
        project_kernel,
        grid=(rows // tile,),
        in_specs=[tall(model_width), whole(scale), whole(weight)],
        out_specs=[tall(model_width), tall(raw_width), tall(columns - raw_width)],
        out_shape=[
            jax.ShapeDtypeStruct((rows, model_width), low),
            jax.ShapeDtypeStruct((rows, raw_width), low),
            jax.ShapeDtypeStruct((rows, columns - raw_width), wide),
        ],
        compiler_params=pltpu.CompilerParams(vmem_limit_bytes=VMEM_BYTES),
    )(inputs, scale, weight)


def held_call(body, ins, outs):
    held = pl.BlockSpec(memory_space=pltpu.VMEM)
    return pl.pallas_call(
        body,
        in_specs=[held] * len(ins),
        out_specs=[held] * len(outs),
        out_shape=[jax.ShapeDtypeStruct(shape, dtype) for shape, dtype in outs],
        compiler_params=pltpu.CompilerParams(vmem_limit_bytes=VMEM_BYTES),
    )(*ins)


def pack_kernel(
    heads, query, key, value, outgate, beta, output, swish, upward, downward,
    attn_ref, output_ref, ups_ref, downs_ref,
):
    size = CHUNK
    width = heads * size
    units = downs_ref.shape[2]
    beta_low = beta[...].astype(low)
    for mate in range(MATES):
        first = mate * width
        for head in range(heads):
            for stream, weight in enumerate((query, key, value)):
                lanes = (3 * head + stream) * size
                attn_ref[mate, :, lanes : lanes + size] = weight[
                    :, first + head * size : first + (head + 1) * size
                ].astype(low)
        attn_ref[mate, :, 3 * width : 4 * width] = outgate[:, first : first + width].astype(low)
        shape = (beta.shape[1], size)
        rows = lax.broadcasted_iota(jnp.int32, shape, 0)
        columns = lax.broadcasted_iota(jnp.int32, shape, 1)
        chosen = (rows == columns + mate * heads) & (columns < heads)
        attn_ref[mate, :, 4 * width :] = dot(
            beta_low, jnp.where(chosen, 1.0, 0.0).astype(low), NN
        ).astype(low)
        output_ref[mate] = output[first : first + width, :].T.astype(low)
        here = mate * units
        ups_ref[mate, :, :units] = swish[:, here : here + units].astype(low)
        ups_ref[mate, :, units:] = upward[:, here : here + units].astype(low)
        downs_ref[mate] = downward[here : here + units, :].T.astype(low)


def unpack_kernel(
    heads, attn, outs, ups_low, ups_high, downs,
    query, key, value, outgate, beta, output, swish, upward, downward,
):
    size = CHUNK
    width = heads * size
    units = downs.shape[2]
    split = ups_low.shape[1]
    beta_all = None
    for mate in range(MATES):
        first = mate * width
        for head in range(heads):
            for stream, grad in enumerate((query, key, value)):
                lanes = (3 * head + stream) * size
                grad[:, first + head * size : first + (head + 1) * size] = attn[
                    mate, :, lanes : lanes + size
                ].astype(wide)
        outgate[:, first : first + width] = attn[mate, :, 3 * width : 4 * width].astype(wide)
        shape = (size, beta.shape[1])
        rows = lax.broadcasted_iota(jnp.int32, shape, 0)
        columns = lax.broadcasted_iota(jnp.int32, shape, 1)
        chosen = (columns == rows + mate * heads) & (rows < heads)
        part = dot(attn[mate, :, 4 * width :], jnp.where(chosen, 1.0, 0.0).astype(low), NN)
        beta_all = part if beta_all is None else beta_all + part
        output[first : first + width, :] = outs[mate].astype(wide).T
        here = mate * units
        for rows_here, part in ((pl.ds(0, split), ups_low), (pl.ds(split, swish.shape[0] - split), ups_high)):
            swish[rows_here, here : here + units] = part[mate, :, :units].astype(wide)
            upward[rows_here, here : here + units] = part[mate, :, units:].astype(wide)
        downward[here : here + units, :] = downs[mate].astype(wide).T
    beta[...] = beta_all


def cut_columns(weight):
    depth, columns = weight.shape
    return weight.reshape(depth, MATES, columns // MATES).transpose(1, 0, 2)


def join_columns(blocks):
    return blocks.transpose(1, 0, 2).reshape(blocks.shape[1], -1)


def gather_weights(blocks):
    return gather_lines(swap_blocks(blocks))


def scatter_grads(blocks):
    return swap_blocks(scatter_lines(blocks.astype(low))).astype(wide)


def on_device(
    block_input,
    lengths,
    attn_gain,
    query_weight,
    key_weight,
    value_weight,
    outgate_weight,
    beta_weight,
    conv_kernel,
    head_gain,
    output_weight,
    mlp_gain,
    swish_weight,
    upward_weight,
    downward_weight,
    out_grad,
):
    count = lax.axis_size("seq")
    lines = count // MATES
    core = lax.axis_index("tp")
    seq_count, tokens, model_width = block_input.shape
    depth = attn_gain.shape[0]
    gain_part = head_gain.shape[0]
    head_size = gain_part * count
    heads = beta_weight.shape[1] // MATES
    width = heads * head_size
    units = swish_weight.shape[1] // MATES

    near = lines <= 4 and depth % 128 == 0
    rows = seq_count * MATES * tokens
    span = MATES * tokens

    small_cut = jnp.concatenate(
        [
            jnp.broadcast_to(
                jnp.concatenate([attn_gain, mlp_gain, head_gain]).astype(low)[None],
                (MATES, 2 * depth + gain_part),
            ),
            jnp.zeros((MATES, -gain_part % 128), low),
            conv_kernel.astype(low).reshape(MATES, -1),
        ],
        axis=1,
    )
    sizes = (depth, depth, gain_part, -gain_part % 128, heads * 3 * CONV * gain_part)
    starts = [sum(sizes[:index]) for index in range(len(sizes) + 1)]
    small_cut = jnp.pad(small_cut, ((0, 0), (0, SMALL * 128 - starts[-1])))
    small_cut = small_cut.reshape(MATES, SMALL, 128)
    streams_end, gates_end = 3 * width, 4 * width
    attn_width = gates_end + head_size
    if near:
        cuts = held_call(
            functools.partial(pack_kernel, heads),
            (
                query_weight, key_weight, value_weight, outgate_weight, beta_weight, output_weight,
                swish_weight, upward_weight, downward_weight,
            ),
            [
                ((MATES, depth, columns), low)
                for columns in (attn_width, width, 2 * units, units)
            ],
        )
        input_rows, small, attn_full, output_full, ups_full, downward_full = first_rows(
            block_input, (small_cut, *cuts), 2, lines
        )
        ups_split = depth // 128 * 80
        front_moves = ((output_full, (0, depth)), (ups_full, (0, ups_split)))
    else:
        streams_cut = jnp.stack(
            [
                w.astype(low).reshape(depth, MATES, heads, head_size)
                for w in (query_weight, key_weight, value_weight)
            ],
            axis=3,
        )
        streams_cut = streams_cut.transpose(1, 0, 2, 3, 4).reshape(MATES, depth, streams_end)
        beta_cut = jnp.pad(
            cut_columns(beta_weight.astype(low)), ((0, 0), (0, 0), (0, head_size - heads))
        )
        cuts = (
            small_cut,
            jnp.concatenate([streams_cut, cut_columns(outgate_weight.astype(low)), beta_cut], axis=2),
            cut_columns(output_weight.astype(low).T),
            jnp.concatenate([cut_columns(w.astype(low)) for w in (swish_weight, upward_weight)], axis=2),
            cut_columns(downward_weight.astype(low).T),
        )
        input_rows, = first_rows(block_input, (), 0, lines)
        small, attn_full, output_full, ups_full, downward_full = (gather_weights(cut) for cut in cuts)
        front_moves = ()
    attn_full = attn_full.reshape(model_width, attn_width)
    input_rows = input_rows.reshape(rows, model_width)
    small = small.reshape(count, SMALL * 128)
    attn_small, mlp_small, head_small, _, conv_small = (
        small[:, starts[index] : starts[index + 1]] for index in range(len(sizes))
    )
    taps = (
        conv_small.reshape(count, heads, 3, CONV, gain_part)
        .transpose(1, 2, 3, 0, 4)
        .reshape(heads, 3 * CONV, head_size)
        .astype(wide)
    )
    attn_scale = attn_small.reshape(1, model_width).astype(wide)
    mlp_scale = mlp_small.reshape(1, model_width).astype(wide)
    head_scale = head_small.reshape(1, head_size).astype(wide)

    mine_low = pick(block_input, core)
    grad_mine = pick(out_grad, core)
    blocked = (seq_count, MATES, tokens, model_width)
    lengths_here = jnp.stack([pick(lengths, core), pick(lengths, 1 - core)])
    limit = lengths_here - line_of() * span

    flat_normed, raw, logits = project(input_rows, attn_scale, attn_full, gates_end)
    sizes_of = (lines, seq_count, heads, span)
    qkv, solved, wu, maps, total, tails, state, fresh, mixed, gated, grad_rows, *moved = delta_front(
        limit, raw, taps, logits, head_scale, out_grad, front_moves, *sizes_of
    )
    grad_rows = grad_rows.reshape(rows, model_width)
    middle_moves = ()
    if near:
        output_full, ups_full = moved
        middle_moves = (
            (ups_full, (ups_split, depth - ups_split)), (downward_full, (0, depth))
        )
    output_full = output_full.reshape(model_width, width)
    attn_part = matmul("rc,dc->rd", gated, output_full).astype(low)
    middle, mlp_normed, *moved = middle_rows(
        attn_part.reshape(blocked), mine_low, mlp_scale, middle_moves, lines
    )
    if near:
        ups_full, downward_full = moved
    ups_full = ups_full.reshape(model_width, 2 * units)
    downward_full = downward_full.reshape(model_width, units)
    mlp_normed = mlp_normed.reshape(rows, model_width)
    acts = matmul("rd,df->rf", mlp_normed, ups_full)
    gate_act, up_act = acts[:, :units], acts[:, units:]
    silu_act = jax.nn.silu(gate_act)
    hidden = (silu_act * up_act).astype(low)
    mlp_part = matmul("rf,df->rd", hidden, downward_full).astype(low)

    hidden_grad = matmul("rd,df->rf", grad_rows, downward_full)
    downward_grad = matmul("rd,rf->df", grad_rows, hidden).astype(low)
    acts_grad = jnp.concatenate(
        [
            (hidden_grad * up_act * silu_slope(gate_act)).astype(low),
            (hidden_grad * silu_act).astype(low),
        ],
        axis=1,
    )
    ups_grad = matmul("rd,rf->df", mlp_normed, acts_grad).astype(low)
    normed_two_part = matmul("rf,df->rd", acts_grad, ups_full).astype(low)

    def cut_rows(grad):
        return grad.reshape(lines, MATES, depth, grad.shape[1])

    ups_blocks, downward_blocks = cut_rows(ups_grad), cut_rows(downward_grad)
    turn_sums = back_sums = ()
    if near:
        sums_split = depth // 128 * 96
        turn_sums = ((ups_blocks, (0, sums_split)),)
    middle_grad, mlp_gain_grad, attn_grad_rows, *summed = turn_rows(
        normed_two_part.reshape(blocked), middle, grad_mine, mlp_scale, turn_sums, lines
    )
    attn_grad_rows = attn_grad_rows.reshape(rows, model_width)
    output_grad = cut_rows(matmul("rd,rc->dc", attn_grad_rows, gated).astype(low))
    gated_grad = matmul("rd,dc->rc", attn_grad_rows, output_full)
    if near:
        ups_low, = summed
        back_sums = (
            (ups_blocks, (sums_split, depth - sums_split)),
            (downward_blocks, (0, depth)),
            (output_grad, (0, depth)),
        )
    all_grads, head_gain_parts, taps_grad, *summed = delta_back(
        limit, raw, tails, taps, logits, head_scale, qkv, wu, maps, total, gated_grad, mixed, solved,
        state, fresh, back_sums, *sizes_of,
    )
    normed_part = matmul("rc,dc->rd", all_grads, attn_full).astype(low)
    attn_grads = cut_rows(matmul("rd,rc->dc", flat_normed, all_grads).astype(low))

    conv_grad = (
        taps_grad[:, :CONV]
        .reshape(seq_count, heads, CONV, 3, count, gain_part)
        .sum(axis=0)
        .transpose(3, 0, 2, 1, 4)
        .reshape(count, -1)
    )

    def small_blocks(attn_gain_grad):
        parts = [
            attn_gain_grad.reshape(count, depth),
            mlp_gain_grad.reshape(count, depth),
            jnp.sum(head_gain_parts[:, 0], axis=0).reshape(count, gain_part),
            jnp.zeros((count, -gain_part % 128), wide),
            conv_grad,
        ]
        flat = jnp.concatenate(parts, axis=1).astype(low)
        flat = jnp.pad(flat, ((0, 0), (0, SMALL * 128 - starts[-1])))
        return flat.reshape(lines, MATES, SMALL, 128)

    last_ins = (
        normed_part.reshape(blocked),
        mlp_part.reshape(blocked),
        mine_low,
        middle,
        middle_grad,
        attn_scale,
    )
    if near:
        ups_high, downward_sum, output_sum = summed
        blocks = (small_blocks(jnp.zeros((1, model_width), wide)), attn_grads)
        input_grad, block_output, _, small_sum, attn_sum = last_rows(*last_ins, blocks, lines)
        grads = held_call(
            functools.partial(unpack_kernel, heads),
            (attn_sum, output_sum, ups_low, ups_high, downward_sum),
            [
                (w.shape, wide)
                for w in (
                    query_weight, key_weight, value_weight, outgate_weight, beta_weight, output_weight,
                    swish_weight, upward_weight, downward_weight,
                )
            ],
        )
        small_sum = small_sum.reshape(MATES, SMALL * 128).astype(wide)
        gains_sum = jnp.sum(small_sum[:, : starts[3]], axis=0)
    else:
        input_grad, block_output, attn_gain_grad = last_rows(*last_ins, (), lines)
        small_sum, attn_sum, output_sum, ups_sum, downward_sum = (
            scatter_grads(block)
            for block in (
                small_blocks(attn_gain_grad), attn_grads, output_grad, ups_blocks, downward_blocks
            )
        )
        small_sum = small_sum.reshape(MATES, SMALL * 128)
        gains_sum = jnp.sum(small_sum[:, : starts[3]], axis=0)
        gains_sum = gains_sum + other_core(gains_sum)
        streams_sum = (
            attn_sum[:, :, :streams_end]
            .reshape(MATES, depth, heads, 3, head_size)
            .transpose(3, 1, 0, 2, 4)
            .reshape(3, depth, MATES * width)
        )
        grads = (
            streams_sum[0],
            streams_sum[1],
            streams_sum[2],
            join_columns(attn_sum[:, :, streams_end:gates_end]),
            join_columns(attn_sum[:, :, gates_end : gates_end + heads]),
            join_columns(output_sum).T,
            join_columns(ups_sum[:, :, :units]),
            join_columns(ups_sum[:, :, units:]),
            join_columns(downward_sum).T,
        )
    conv_sum = small_sum[:, starts[4] : starts[5]]
    return (
        block_output,
        input_grad,
        gains_sum[:depth],
        *grads[:5],
        conv_sum.reshape(MATES * heads, 3, CONV, gain_part),
        gains_sum[2 * depth :],
        grads[5],
        gains_sum[depth : 2 * depth],
        *grads[6:],
    )


def solution(mesh):
    return jax.shard_map(
        on_device,
        mesh=mesh,
        in_specs=(
            P(None, "seq", None),
            P(),
            P("seq"),
            P("seq", "tp"),
            P("seq", "tp"),
            P("seq", "tp"),
            P("seq", "tp"),
            P("seq", "tp"),
            P("tp", None, None, "seq"),
            P("seq"),
            P("tp", "seq"),
            P("seq"),
            P("seq", "tp"),
            P("seq", "tp"),
            P("tp", "seq"),
            P(None, "seq", None),
        ),
        out_specs=(
            P(None, "seq", None),
            P(None, "seq", None),
            P("seq"),
            P("seq", "tp"),
            P("seq", "tp"),
            P("seq", "tp"),
            P("seq", "tp"),
            P("seq", "tp"),
            P("tp", None, None, "seq"),
            P("seq"),
            P("tp", "seq"),
            P("seq"),
            P("seq", "tp"),
            P("seq", "tp"),
            P("tp", "seq"),
        ),
        check_vma=False,
    )
```

time: 1140 us -> 880 us (0.77)
  Pallas kernels: 544 us -> 697 us
  local copies, waits for them, and re-layouts: 159 us -> 21.3 us
  starting transfers between devices: 112 us -> 0 us
  waiting for transfers between devices: 94 us -> 0 us
  other arithmetic: 57.3 us -> 4.18 us
  matrix products: 165 us -> 147 us
    pallas_call x4 -> x5, Pallas kernels: 119 us -> 239 us  [the longest x2 210 us: call(): pl.pallas_call(body, grid=(2 * self.chains,), in_specs=[spec for _, spec...]
    ppermute x27 -> x0, starting transfers between devices: 112 us -> none  [the longest x20 104 us: along(): return lax.ppermute(value, 'seq', pairs)]
    ppermute x27 -> x0, waiting for transfers between devices: 94 us -> none  [the longest x20 72.6 us: along(): return lax.ppermute(value, 'seq', pairs)]
    pallas_call x4, Pallas kernels: 425 us -> 457 us  [remote_call(): pl.pallas_call(body, in_specs=[anywhere if kind == 'any' else held for _,...]
    convert_element_type x16 -> x1, other arithmetic: 30.8 us -> 0.61 us  [on_device(): mlp_scale = mlp_small.reshape(1, model_width).astype(wide)]
    dynamic_slice x12 -> x1, local copies, waits for them, and re-layouts: 24.8 us -> 1.33 us  [pick(): return lax.dynamic_index_in_dim(blocks, index, 0, False)]
    broadcast_in_dim x4 -> x2, local copies, waits for them, and re-layouts: 16.9 us -> 0.01 us  [the longest x1 0.01 us: on_device(): jnp.zeros((MATES, -gain_part % 128), low)]
    dynamic_update_slice x11 -> x0, local copies, waits for them, and re-layouts: 16.5 us -> none  [the longest x7 6.84 us: in_order(): out = lax.dynamic_update_index_in_dim(out, piece, mate ^ flip, 0)]
  transfers between devices with their start and end apart: 27 -> 0, of which waited for: 7 -> 0; matrix products, arithmetic and copies ran while one was open for 18% -> 0% of each run, Pallas kernels for 39% -> 0%
where the time goes in v4:
time: 880 us; the launch traced here: 871 us
  Pallas kernels  697 us (79%)
  matrix products  147 us (17%)
  local copies, waits for them, and re-layouts  21.3 us (2%)
    pallas_call x4, Pallas kernels, remote_call(): pl.pallas_call(body, in_specs=[anywhere if kind == 'any' else held for _,...  457 us
    pallas_call x2, Pallas kernels, call(): pl.pallas_call(body, grid=(2 * self.chains,), in_specs=[spec for _, spec...  210 us
    dot_general x11, matrix products, matmul(): return jnp.einsum(form, left, right, preferred_element_type=wide)  147 us
    pallas_call x1, Pallas kernels, project(): pl.pallas_call(project_kernel, grid=(rows // tile,), in_specs=[tall(model...  17.9 us

profile of v4, /device:TPU:0, one launch (start us, length us, event | category | flops | bytes accessed | tf_op | source)
XLA Modules:
  0.0 870.6 jit_solution(4989848686198692776)
XLA Ops:
  0.7 1.3 fusion.5
  2.0 1.9 add_subtract_fusion.limit_ref
  3.9 1.4 copy.49.beta
  5.3 5.4 shard_map.271
  10.8 0.1 reshape.187
  11.0 0.1 fusion.1
  11.1 0.6 copy.70
  11.7 108.7 %shard_map.272 = (bf16[2,4,256,2048]{3,2,1,0:T(8,128)(2,1)}, bf16[4,4,16,128]{3,2,1,0:T(8,128)(2,1)}, bf16[4,4,128,1152]{3,2,1,0:T(8,128)(2,1)}, bf16[4,4,128,25...) custom-call(bf16[2,256,2048]{2,1,0:T(8,128)(2,1)} %input_ref.1, ...), custom_call_target="tpu_custom_call" | custom-call | tf_op jit(solution)/shard_map/pallas_call | solution.py:1187
  120.4 0.9 copy.68
  121.2 0.6 slice_convert_fusion
  121.8 17.9 %shard_map.273 = (bf16[2048,2048]{1,0:T(8,128)(2,1)}, bf16[2048,1024]{1,0:T(8,128)(2,1)}, f32[2048,128]{1,0:T(8,128)}) custom-call(bf16[2048,2048]{1,0:T(8,128)(2,1)} %bitcast.80, f32[1,2048]{1,0:T(1,128)} %bitcast.103, bf16[2048,1152]{1,0:T(8,128)(2,1)} %bitcast.84), custom_call_target="tpu_custom_call" | custom-call | tf_op jit(solution)/shard_map/pallas_call | solution.py:1725
  139.8 0.1 copy.60
  139.9 0.1 copy.58
  140.0 0.7 reshape.219.taps_ref
  140.8 0.6 reshape.215.scale_ref
  141.4 95.3 %shard_map.274 = (bf16[2048,768]{1,0:T(8,128)(2,1)}, f32[4,8,128,128]{3,2,1,0:T(8,128)}, f32[4,8,128,256]{3,2,1,0:T(8,128)}, f32[4,8,128,128]{3,2,1,0:T(8,128)},...) custom-call(s32[2]{0:T(128)} %add_subtract_fusion.limit_ref, ...), custom_call_target="tpu_custom_call", output_to_operand_aliasing={{11}: (8, {}), {12}: (9, {})} | custom-call | tf_op jit(solution)/shard_map/pallas_call | solution.py:1578
  236.7 7.3 convolution_convert_fusion.4
  244.0 1.6 dynamic-slice_bitcast_fusion
  245.6 106.5 %shard_map.275 = (f32[256,2048]{1,0:T(8,128)}, bf16[2,4,256,2048]{3,2,1,0:T(8,128)(2,1)}, bf16[4,4,128,1408]{3,2,1,0:T(8,128)(2,1)}, bf16[4,4,128,704]{3,2,1,0:T(8,128)(2,1)}) custom-call(bf16[2,4,256,2048]{3,2,1,0:T(8,128)(2,1)} %bitcast.72, bf16[256,2048]{1,0:T(8,128)(2,1)} %get-tuple-element.176.input_ref, ...), custom_call_target="tpu_custom_call", output_to_operand_aliasing={{2}: (3, {}), {3}: (4, {})} | custom-call | tf_op jit(solution)/shard_map/pallas_call | solution.py:1187
  352.1 18.9 %fusion.6 = f32[2048,1408]{0,1:T(8,128)} fusion(bf16[2048,2048]{1,0:T(8,128)(2,1)} %bitcast.114, bf16[2048,1408]{1,0:T(8,128)(2,1)} %bitcast.75), kind=kOutput, calls=%fused_computation.39 | convolution fusion | flops 11811160064 | bytes 25690112 | tf_op jit(solution)/shard_map/rd,df->rf/dot_general | solution.py:71
  371.1 15.1 %multiply_convert_fusion.2 = (bf16[2048,704]{0,1:T(8,128)(2,1)}, bf16[2048,704]{0,1:T(8,128)(2,1)}, bf16[2048,704]{0,1:T(8,128)(2,1)}) fusion(f32[2048,1408]{0,1:T(8,128)} %fusion.6, bf16[2048,2048]{1,0:T(8,128)(2,1)} %bitcast.110, bf16[2048,704]{1,0:T(8,128)(2,1)S(1)} %bitcast.92), kind=kOutput, calls=%fused_computation.9 | convolution fusion | flops 5927206912 | bytes 31457280 | tf_op jit(solution)/shard_map/rd,df->rf/dot_general | solution.py:71
  386.1 19.6 %convolution_convert_fusion.5 = bf16[2048,1408]{1,0:T(8,128)(2,1)} fusion(bf16[2048,2048]{1,0:T(8,128)(2,1)} %bitcast.115, bf16[2048,704]{0,1:T(8,128)(2,1)} %get-tuple-element.167, bf16[2048,704]{0,1:T(8,128)(2,1)} %get-tuple-element.166), kind=kOutput, calls=%fused_computation.5 | convolution fusion | flops 11825577984 | bytes 19922944 | tf_op jit(solution)/shard_map/rd,rf->df/dot_general | solution.py:71
  405.7 17.5 %convolution_convert_fusion.3 = bf16[2048,2048]{1,0:T(8,128)(2,1)} fusion(bf16[2048,1408]{1,0:T(8,128)(2,1)S(1)} %bitcast.78, bf16[2048,704]{0,1:T(8,128)(2,1)} %get-tuple-element.167, bf16[2048,704]{0,1:T(8,128)(2,1)S(1)} %copy-done.13), kind=kOutput, calls=%fused_computation.3 | convolution fusion | flops 11826888704 | bytes 19922944 | tf_op jit(solution)/shard_map/rf,df->rd/dot_general | solution.py:71
  423.2 112.5 %shard_map.276 = (f32[256,2048]{1,0:T(8,128)}, f32[1,2048]{1,0:T(1,128)}, bf16[2,4,256,2048]{3,2,1,0:T(8,128)(2,1)}, bf16[4,96,1408]{2,1,0:T(8,128)(2,1)}) custom-call(bf16[2,4,256,2048]{3,2,1,0:T(8,128)(2,1)} %bitcast.83, f32[256,2048]{1,0:T(8,128)} %get-tuple-element.92.middle_ref, bf16[256,2048]{1,0:T(8,128)(2,1)} %get-tuple-element.175.grad_ref, ...), custom_call_target="tpu_custom_call" | custom-call | tf_op jit(solution)/shard_map/pallas_call | solution.py:1187
  535.7 7.0 convolution_convert_fusion.7
  542.7 10.8 %convolution_convert_fusion.6 = bf16[2048,704]{0,1:T(8,128)(2,1)} fusion(bf16[2048,704]{0,1:T(8,128)(2,1)S(1)} %copy-done.12, bf16[2048,2048]{1,0:T(8,128)(2,1)} %bitcast.111), kind=kOutput, calls=%fused_computation.12 | convolution fusion | flops 5907021824 | bytes 14155776 | tf_op jit(solution)/shard_map/rd,rf->df/dot_general | solution.py:71
  553.5 4.8 copy.53
  558.3 7.1 fusion.7.grad_ref
  565.3 114.9 %shard_map.277 = (bf16[2048,1152]{1,0:T(8,128)(2,1)}, f32[4,8,128]{2,1,0:T(8,128)}, f32[4,8,384]{2,1,0:T(8,128)}, bf16[4,32,1408]{2,1,0:T(8,128)(2,1)}, bf16[4,1...) custom-call(s32[2]{0:T(128)} %add_subtract_fusion.limit_ref, ...), custom_call_target="tpu_custom_call" | custom-call | tf_op jit(solution)/shard_map/pallas_call | solution.py:1578
  680.3 16.6 %convolution_convert_fusion = bf16[2048,1152]{1,0:T(8,128)(2,1)} fusion(bf16[2048,2048]{1,0:T(8,128)(2,1)} %get-tuple-element.103, bf16[2048,1152]{1,0:T(8,128)(2,1)} %get-tuple-element.98), kind=kOutput, calls=%fused_computation | convolution fusion | flops 9666035712 | bytes 17825792 | tf_op jit(solution)/shard_map/rd,rc->dc/dot_general | solution.py:71
  696.9 0.2 reshape.208
  697.2 0.1 copy.55
  697.3 0.1 copy.56
  697.4 0.8 slice_reduce_fusion.1
  698.2 0.1 reshape.207
  698.3 0.1 concatenate.21
  698.4 0.6 copy.63
  699.1 11.6 %convolution_convert_fusion.1 = bf16[2048,2048]{1,0:T(8,128)(2,1)} fusion(bf16[2048,704]{0,1:T(8,128)(2,1)} %get-tuple-element.168, bf16[2048,704]{1,0:T(8,128)(2,1)} %bitcast.91), kind=kOutput, calls=%fused_computation.1 | convolution fusion | flops 5909774336 | bytes 14155776 | tf_op jit(solution)/shard_map/rf,df->rd/dot_general | solution.py:71
  710.7 15.7 %convolution_convert_fusion.2 = bf16[2048,2048]{1,0:T(8,128)(2,1)} fusion(bf16[2048,1152]{1,0:T(8,128)(2,1)} %get-tuple-element.98, bf16[2048,1152]{1,0:T(8,128)(2,1)S(1)} %bitcast.87), kind=kOutput, calls=%fused_computation.2 | convolution fusion | flops 9667870720 | bytes 17825792 | tf_op jit(solution)/shard_map/rc,dc->rd/dot_general | solution.py:71
  726.4 129.7 %shard_map.278 = (bf16[2,256,2048]{2,1,0:T(8,128)(2,1)}, bf16[2,256,2048]{2,1,0:T(8,128)(2,1)}, f32[1,2048]{1,0:T(1,128)}, bf16[4,16,128]{2,1,0:T(8,128)(2,1)}, bf16[4,128,1152]{2,1,0:T(8,128)(2,1)}) custom-call(bf16[2,4,256,2048]{3,2,1,0:T(8,128)(2,1)} %bitcast.82, bf16[2,4,256,2048]{3,2,1,0:T(8,128)(2,1)} %bitcast.81, ...), custom_call_target="tpu_custom_call" | custom-call | tf_op jit(solution)/shard_map/pallas_call | solution.py:1187
  856.1 5.6 shard_map.279
  861.7 1.5 copy.57
  863.2 0.7 convert_bitcast_fusion.2
  863.9 0.7 reshape.212
  864.7 0.5 fusion.4
  865.2 0.5 slice.50
  865.7 3.2 copy.77
  868.9 1.3 copy.78
  (57 shorter events, 0.3 us)
Async XLA Ops:
  0.6 10.1 %copy-start.6 = (f32[8,3,4,8]{3,2,1,0:T(4,128)S(1)}, f32[8,3,4,8]{3,2,1,0:T(4,128)}, u32[]{:S(2)}) copy-start(f32[8,3,4,8]{3,2,1,0:T(4,128)} %param.24) | copy-start | bytes 9220
  0.7 10.2 %copy-start.9 = (f32[128]{0:T(128)S(1)}, f32[128]{0:T(128)}, u32[]{:S(2)}) copy-start(f32[128]{0:T(128)} %param.18) | copy-start | bytes 1540
  0.7 10.2 %copy-start.10 = (f32[128]{0:T(128)S(1)}, f32[128]{0:T(128)}, u32[]{:S(2)}) copy-start(f32[128]{0:T(128)} %param.27) | copy-start | bytes 1540
  0.7 10.3 %copy-start.11 = (f32[8]{0:T(128)S(1)}, f32[8]{0:T(128)}, u32[]{:S(2)}) copy-start(f32[8]{0:T(128)} %param.25) | copy-start | bytes 100
  236.7 7.3 copy-start
  236.7 7.3 copy-start.1
  352.1 18.9 %copy-start.3 = (bf16[4,4,128,704]{3,2,1,0:T(8,128)(2,1)S(1)}, bf16[4,4,128,704]{3,2,1,0:T(8,128)(2,1)}, u32[]{:S(2)}) copy-start(bf16[4,4,128,704]{3,2,1,0:T(8,128)(2,1)} %get-tuple-element.89) | copy-start | bytes 8650756
  371.1 34.6 %slice-start = ((s8[5767168]{0:T(1024)(128)(4,1)}), s8[1572864]{0:T(1024)(128)(4,1)S(1)}, s32[]{:S(2)}) async-start(s8[5767168]{0:T(1024)(128)(4,1)} %bitcast.76), calls=%async_computation | async-start | bytes 3145728
  386.1 19.6 %slice-start.1 = ((s8[5767168]{0:T(1024)(128)(4,1)}), s8[4194304]{0:T(1024)(128)(4,1)S(1)}, s32[]{:S(2)}) async-start(s8[5767168]{0:T(1024)(128)(4,1)} %bitcast.76), calls=%async_computation.1 | async-start | bytes 8388608
  386.1 19.6 %copy-start.13 = (bf16[2048,704]{0,1:T(8,128)(2,1)S(1)}, bf16[2048,704]{0,1:T(8,128)(2,1)}, u32[]{:S(2)}) copy-start(bf16[2048,704]{0,1:T(8,128)(2,1)} %get-tuple-element.166) | copy-start | bytes 8650756
  423.2 112.5 %copy-start.5 = (bf16[2048,256]{1,0:T(8,128)(2,1)S(1)}, bf16[2048,256]{1,0:T(8,128)(2,1)}, u32[]{:S(2)}) copy-start(bf16[2048,256]{1,0:T(8,128)(2,1)} %get-tuple-element.85) | copy-start | bytes 3145732
  535.7 7.0 copy-start.12
  553.5 4.8 copy-start.2
  680.3 16.7 %copy-start.7 = (f32[4,8,384]{2,1,0:T(8,128)S(1)}, f32[4,8,384]{2,1,0:T(8,128)}, u32[]{:S(2)}) copy-start(f32[4,8,384]{2,1,0:T(8,128)} %get-tuple-element.102) | copy-start | bytes 147460
  680.3 18.0 %copy-start.8 = (f32[1,2048]{1,0:T(1,128)S(1)}, f32[1,2048]{1,0:T(1,128)}, u32[]{:S(2)}) copy-start(f32[1,2048]{1,0:T(1,128)} %get-tuple-element.100) | copy-start | bytes 24580
  680.3 30.4 %slice-start.2 = ((s8[4718592]{0:T(1024)(128)(4,1)}), s8[524288]{0:T(1024)(128)(4,1)S(1)}, s32[]{:S(2)}) async-start(s8[4718592]{0:T(1024)(128)(4,1)} %bitcast.85), calls=%async_computation.2 | async-start | bytes 1048576
  699.1 11.6 %slice-start.3 = ((s8[4718592]{0:T(1024)(128)(4,1)}), s8[4194304]{0:T(1024)(128)(4,1)S(1)}, s32[]{:S(2)}) async-start(s8[4718592]{0:T(1024)(128)(4,1)} %bitcast.85), calls=%async_computation.3 | async-start | bytes 8388608
  856.1 12.8 %copy-start.4 = (bf16[2,256,2048]{2,1,0:T(8,128)(2,1)S(1)}, bf16[2,256,2048]{2,1,0:T(8,128)(2,1)}, u32[]{:S(2)}) copy-start(bf16[2,256,2048]{2,1,0:T(8,128)(2,1)} %get-tuple-element.193) | copy-start | bytes 6291460

commit v5 on v4

--- a/solution.py
+++ b/solution.py
@@ -181,27 +181,34 @@
 
 
 def front_kernel(
-    lines, heads, moves, limit_ref, raw_any, raw_ref, taps_ref, logit_ref, gate_ref, scale_ref, grad_any,
-    *rest,
+    lines, heads, moves, limit_ref, raw_any, raw_ref, taps_ref, logit_ref, gate_ref, scale_ref, *rest,
 ):
     count = len(moves)
     outs = rest[count:]
     qkv_ref, solved_ref, wu_ref, map_ref, total_ref, tails_ref = outs[:6]
-    state_ref, fresh_ref, mixed_ref, gated_ref, grads = outs[6:11]
-    targets, scratch = outs[11 : 11 + count], outs[11 + count :]
+    state_ref, fresh_ref, mixed_ref, gated_ref, gathered, weights = outs[6:12]
+    targets, scratch = outs[12 : 12 + count], outs[12 + count :]
     ext, offsets, maps, prefixes, locals_, wus, qkvs, enters, leaves, tails = scratch[:10]
-    tail_sems, state_sems = scratch[10:12]
-    scratch = scratch[12:]
+    tail_sems, state_sems, gateds = scratch[10:13]
+    scratch = scratch[13:]
     step = pl.program_id(0)
     chains, chunks = maps.shape[0], maps.shape[1]
     span = chunks * CHUNK
     head_size = CHUNK
     streams = 3 * heads * head_size
     place = Place()
-    share = ShareRows(place, grad_any.at[place.core], grads, scratch[:3])
+    tokens = gathered.shape[2]
+    share = ShareRows(place, targets[0], weights, scratch[:3])
+    swap = SwapBlocks(
+        place,
+        lambda slot, mate: gateds.at[slot, pl.ds(pl.multiple_of(mate * tokens, 16), tokens)],
+        gathered,
+        scratch[3:6],
+    )
     gathers = [
-        GatherLines(place, None, target, scratch[3 + 6 * index : 9 + 6 * index], moves[index])
+        GatherLines(place, None, target, scratch[6 + 6 * index : 12 + 6 * index], moves[index])
         for index, target in enumerate(targets)
+        if moves[index]
     ]
     below, above = place.line > 0, place.line < lines - 1
     rows, columns = grid_of_rows()
@@ -229,14 +236,11 @@
 
     @pl.when(step == 0)
     def _():
-        meet(place, lines=lines)
+        meet(place, lines=lines, cores=True)
         for seq in range(seqs):
             pl.when(above)(tail(seq).start)
         for gather in gathers:
             gather.leave(False)
-        share.begin_half(False)
-        share.begin_half(True)
-        share.begin_rest()
         for seq in range(seqs):
 
             @pl.when(below)
@@ -294,13 +298,30 @@
 
         lax.fori_loop(0, chunks // TOGETHER, group, 0)
 
+    @pl.when((step == 1) & (step < chains))
+    def _():
+        for gather in gathers[:1]:
+            gather.onwards(1)
+
+    @pl.when((step == 2) & (step < chains))
+    def _():
+        for gather in gathers[:1]:
+            gather.onwards(2)
+
     @pl.when(step < chains)
     def _():
         form(step)
 
     @pl.when(step == chains - 2)
     def _():
-        share.forward()
+        for gather in gathers[:1]:
+            for number in range(3, lines):
+                gather.onwards(number)
+        share.begin_half(False)
+        share.begin_half(True)
+        share.begin_rest()
+        for gather in gathers[1:]:
+            gather.onwards(1)
 
     @pl.when(step == chains - 1)
     def _():
@@ -333,9 +354,6 @@
             leaving = nn_low(pair(ends[index][:, :head_size]), enters[index])
             leaves[index] = (leaving + ends[index][:, head_size:]).astype(low)
         pl.when(above)(state_copy.start)
-        for gather in gathers:
-            gather.onwards(1)
-        share.forward_far()
 
     def outputs(chain):
         enter = enters[chain]
@@ -359,7 +377,10 @@
                 mixed_ref[here] = mixed
                 inverse = lax.rsqrt(jnp.mean(mixed * mixed, axis=1, keepdims=True) + epsilon)
                 normed = mixed * inverse * scale
-                gated_ref[here] = (normed * jax.nn.silu(gate_ref[here].astype(wide))).astype(low)
+                gated = (normed * jax.nn.silu(gate_ref[here].astype(wide))).astype(low)
+                gated_ref[here] = gated
+                lanes = pl.ds(pl.multiple_of(chain % heads * head_size, 128), head_size)
+                gateds[chain // heads, here, lanes] = gated
             return carry
 
         lax.fori_loop(0, chunks // TOGETHER, group, 0)
@@ -368,19 +389,27 @@
     def _():
         outputs(step - chains)
 
+    @pl.when(step == chains + heads - 1)
+    def _():
+        swap.begin(0)
+        share.forward()
+
     @pl.when(step == 2 * chains - 2)
     def _():
-        for gather in gathers:
+        for gather in gathers[1:]:
             gather.onwards(2)
 
     @pl.when(step == 2 * chains - 1)
     def _():
-        for number in range(3, lines):
-            for gather in gathers:
+        swap.begin(1)
+        share.forward_far()
+        for gather in gathers[1:]:
+            for number in range(3, lines):
                 gather.onwards(number)
         for gather in gathers:
             gather.finish_lines()
         share.finish()
+        swap.finish()
         for seq in range(seqs):
             pl.when(above)(tail(seq).wait_send)
         pl.when(above)(state_copy.wait_send)
@@ -388,15 +417,15 @@
 
 def back_kernel(
     lines, heads, parts, limit_ref, raw_ref, tails_ref, taps_ref, logit_ref, gate_ref, scale_ref, qkv_ref,
-    wu_ref, map_ref, total_ref, grad_ref, mixed_ref, solved_ref, state_ref, fresh_in_ref, *rest,
+    wu_ref, map_ref, total_ref, grad_ref, mixed_ref, solved_ref, state_ref, fresh_in_ref, row_grad, *rest,
 ):
     count = len(parts)
     blocks, rest = rest[:count], rest[count:]
-    all_ref, gain_ref, taps_grad_ref = rest[:3]
-    results, scratch = rest[3 : 3 + count], rest[3 + count :]
+    all_ref, gain_ref, taps_grad_ref, row_grads = rest[:4]
+    results, scratch = rest[4 : 4 + count], rest[4 + count :]
     ext, pre_grads, maps, sources, out_grads, fresh_grads, leaving, leaves, enters = scratch[:9]
     halos, edges, returned, halo_sems, state_sems = scratch[9:14]
-    scratch = scratch[14:]
+    share_scratch, scratch = scratch[14:17], scratch[17:]
     step = pl.program_id(0)
     chains, chunks = maps.shape[0], maps.shape[1]
     span = chunks * CHUNK
@@ -407,6 +436,7 @@
         SumLines(place, blocks[index], results[index], scratch[7 * index : 7 * index + 7], first)
         for index, (first, _) in enumerate(parts)
     ]
+    share = ShareRows(place, row_grad, row_grads, share_scratch)
     below, above = place.line > 0, place.line < lines - 1
     rows, columns = grid_of_rows()
 
@@ -432,6 +462,9 @@
     @pl.when(step == 0)
     def _():
         meet(place, far=bool(parts), lines=lines)
+        share.begin_half(False)
+        share.begin_half(True)
+        share.begin_rest()
         for each in sums:
             each.begin()
         for each in sums:
@@ -446,7 +479,7 @@
                 chunk = index * TOGETHER + number
                 start = pl.multiple_of(chunk * CHUNK, CHUNK)
                 here = pl.ds(start, CHUNK)
-                grad, mixed = grad_ref[here], mixed_ref[here]
+                grad, mixed = grad_ref[here].astype(wide), mixed_ref[here]
                 silu_gate, slope = silu_parts(gate_ref[here].astype(wide))
                 inverse = lax.rsqrt(jnp.mean(mixed * mixed, axis=1, keepdims=True) + epsilon)
                 unit = mixed * inverse
@@ -646,8 +679,13 @@
     def _():
         unwind(step - chains)
 
+    @pl.when(step == chains)
+    def _():
+        share.forward()
+
     @pl.when(step == 2 * chains - 3)
     def _():
+        share.forward_far()
         for each in sums:
             each.round(3)
 
@@ -670,6 +708,7 @@
         for chain in range(chains):
             pl.when(below)(halo(chain).wait_send)
         pl.when(below)(state_copy.wait_send)
+        share.finish()
         for each in sums:
             each.finish()
 
@@ -700,8 +739,8 @@
         self.far = 2 * (1 - y) + (1 - x)
         self.base = self.seq - self.mate
 
-    def of(self, mate):
-        return (self.base + mate, self.core)
+    def of(self, mate, other=0):
+        return (self.base + mate, 1 - self.core if other else self.core)
 
     @property
     def sibling(self):
@@ -711,15 +750,27 @@
         return (self.seq + step * MATES, self.core)
 
 
-def meet(place, far=False, lines=0):
+def meet(place, far=False, lines=0, cores=False, straight=False):
     barrier = pltpu.get_barrier_semaphore()
     partners = [place.of(place.x), place.of(place.y), place.sibling]
-    if far:
+    if far or cores:
         partners.append(place.of(place.far))
+    if cores:
+        partners += [place.of(mate, 1) for mate in (place.x, place.y, place.far)]
     for partner in partners:
         pl.semaphore_signal(barrier, inc=1, device_id=partner, device_id_type=MESH)
     count = len(partners)
-    if lines > 1:
+    if straight:
+        for step in range(1, lines):
+            line = (place.line + step) % lines
+            pl.semaphore_signal(
+                barrier,
+                inc=1,
+                device_id=(line * MATES + place.mate, place.core),
+                device_id_type=MESH,
+            )
+        count = count + max(lines - 1, 0)
+    elif lines > 1:
         below, above = place.line > 0, place.line < lines - 1
 
         @pl.when(below)
@@ -1029,6 +1080,38 @@
                     pl.when(came & goes)(copy.wait_send)
 
 
+class SwapBlocks:
+    @staticmethod
+    def scratch():
+        return [
+            pltpu.SemaphoreType.DMA((1,)),
+            pltpu.SemaphoreType.DMA((2 * MATES,)),
+            pltpu.SemaphoreType.DMA((2 * MATES,)),
+        ]
+
+    def __init__(self, place, piece, target, scratch):
+        self.place, self.piece, self.target = place, piece, target
+        self.local_sem, send, receive = scratch
+        self.make = sender((send, receive))
+        self.order = [place.far, place.x, place.y, place.mate]
+
+    def copy(self, slot, index):
+        place, mate = self.place, self.order[index]
+        source, target = self.piece(slot, mate), self.target.at[slot, place.mate]
+        if slot == 0 and index == MATES - 1:
+            return pltpu.make_async_copy(source, target, self.local_sem.at[0]), True
+        return self.make(slot * MATES + index, source, target, place.of(mate, slot)), False
+
+    def begin(self, slot, index=None):
+        for each in range(MATES) if index is None else (index,):
+            self.copy(slot, each)[0].start()
+
+    def finish(self):
+        for slot in range(2):
+            for index in range(MATES):
+                self.copy(slot, index)[0].wait()
+
+
 class SumLines:
     @staticmethod
     def scratch(lines, shape):
@@ -1171,10 +1254,37 @@
             self.plane(index).start()
         self.local().start()
 
-    def finish(self):
+    def straight(self, step):
+        line = (self.place.line + step) % self.lines
+        return pltpu.make_async_remote_copy(
+            src_ref=self.held.at[line],
+            dst_ref=self.came.at[0, step - 1],
+            send_sem=self.send.at[0, step],
+            recv_sem=self.got.at[0, step],
+            device_id=(line * MATES + self.place.mate, self.place.core),
+            device_id_type=MESH,
+        )
+
+    def direct(self):
+        for step in range(1, self.lines):
+            self.straight(step).start()
+
+    def exchange_direct(self):
+        for step in range(1, self.lines):
+            self.straight(step).wait_recv()
+            self.add(self.place.line, 0, step)
+        for index in range(3):
+            self.plane(index).start()
+        self.local().start()
+
+    def finish(self, direct=False):
         self.local().wait()
         for index in range(3):
             self.plane(index).wait()
+        if direct:
+            for step in range(1, self.lines):
+                self.straight(step).wait_send()
+            return
         for turn in range(1, self.lines):
             for way in (0, 1):
                 _, copy = self.copy(turn, way)
@@ -1209,86 +1319,121 @@
     return inverse * (scaled - unit * (inverse * inner)), grad * unit
 
 
-def sum_and_share(rows, share, body, half, during):
-    begin, *steps = during
-    rows.begin()
-    begin()
-    rows.send_far()
-    rows.send_near()
-    rows.send_relayed()
-    rows.wait_half(False)
+def load_weights(weights, held, sems):
+    return [
+        pltpu.make_async_copy(weights.at[slot, mate], held.at[slot, mate], sems.at[slot, mate])
+        for slot in range(2)
+        for mate in range(MATES)
+    ]
+
+
+def middle_kernel(lines, moves, gathered, weights, input_ref, scale_ref, grad_any, *rest):
+    place = Place()
+    count = len(moves)
+    middle_ref, shared, grads = rest[count : count + 3]
+    targets, scratch = rest[count + 3 : 2 * count + 3], rest[2 * count + 3 :]
+    normed, held, weight_sems = scratch[:3]
+    share = ShareRows(place, normed, shared, scratch[3:6])
+    other = ShareRows(place, grad_any.at[place.core], grads, scratch[6:9])
+    gathers = [
+        GatherLines(place, None, target, scratch[9 + 6 * index : 15 + 6 * index], moves[index])
+        for index, target in enumerate(targets)
+    ]
+    meet(place, lines=lines if moves else 0)
+    loads = load_weights(weights, held, weight_sems)
+    for load in loads:
+        load.start()
+    for gather in gathers:
+        gather.leave(False)
+    for load in loads:
+        load.wait()
+    rows = normed.shape[0]
+    half = rows // 2
+    _, _, all_lines, _, depth, width = held.shape
+
+    height = MATES * depth
+    some = max(1, 512 // height)
+
+    def product(step, carry):
+        columns = pl.ds(pl.multiple_of(step * some * height, 128), some * height)
+        part = pl.ds(step * some, some)
+        for first in (0, half):
+            total = None
+            for slot in range(2):
+                for mate in range(MATES):
+                    term = dot(
+                        gathered[slot, mate, first : first + half],
+                        held[slot, mate, part].reshape(some * height, width),
+                        NT,
+                    )
+                    total = term if total is None else total + term
+            here = pl.ds(first, half)
+            middle_ref[here, columns] = input_ref[here, columns].astype(wide) + total
+        return carry
+
+    def body(here):
+        middle = middle_ref[here]
+        normed[here] = (middle * inverse_rms(middle) * scale_ref[...]).astype(low)
+
+    lax.fori_loop(0, all_lines // some, product, 0)
     row_steps(0, half, body)
     share.begin_half(False)
-    rows.wait_half(True)
-    row_steps(half, 2 * half, body)
+    row_steps(half, rows, body)
     share.begin_half(True)
     share.begin_rest()
-    steps[0]()
-    rows.finish()
+    for gather in gathers:
+        gather.onwards(1)
     share.forward()
-    steps[1]()
+    other.begin_half(False)
+    other.begin_half(True)
+    other.begin_rest()
     share.forward_far()
-    steps[2]()
+    for gather in gathers:
+        gather.onwards(2)
+    other.forward()
+    other.forward_far()
+    for number in range(3, lines):
+        for gather in gathers:
+            gather.onwards(number)
+    for gather in gathers:
+        gather.finish_lines()
     share.finish()
-
-
-def middle_kernel(lines, moves, partial, input_ref, scale_ref, *rest):
-    place = Place()
-    count = len(moves)
-    middle_ref, shared = rest[count : count + 2]
-    targets, scratch = rest[count + 2 : 2 * count + 2], rest[2 * count + 2 :]
-    normed, scratch = scratch[0], scratch[1:]
-    meet(place, lines=lines if moves else 0)
-    rows = SumRows(place, partial, scratch[:7])
-    share = ShareRows(place, normed, shared, scratch[7:10])
-    gathers = [
-        GatherLines(place, None, target, scratch[10 + 6 * index : 16 + 6 * index], moves[index])
-        for index, target in enumerate(targets)
-    ]
-
-    def body(here):
-        middle = input_ref[here].astype(wide) + rows.total(here)
-        middle_ref[here] = middle
-        normed[here] = (middle * inverse_rms(middle) * scale_ref[...]).astype(low)
-
-    def leave():
-        for gather in gathers:
-            gather.leave(False)
-
-    def step(number):
-        def go():
-            for gather in gathers:
-                gather.onwards(number)
-
-        return go
-
-    def last():
-        for number in range(3, lines):
-            for gather in gathers:
-                gather.onwards(number)
-        for gather in gathers:
-            gather.finish_lines()
-
-    sum_and_share(rows, share, body, normed.shape[0] // 2, (leave, step(1), step(2), last))
-
-
-def turn_rows_kernel(lines, parts, partial, middle_ref, grad_ref, scale_ref, *rest):
+    other.finish()
+
+
+def turn_rows_kernel(
+    lines, parts, partial, weights, middle_ref, grad_ref, scale_ref, *rest
+):
     place = Place()
     count = len(parts)
     blocks, rest = rest[:count], rest[count:]
-    middle_grad_ref, gain_ref, shared = rest[:3]
-    results, scratch = rest[3 : 3 + count], rest[3 + count :]
-    low_grad, scratch = scratch[0], scratch[1:]
-    meet(place, far=bool(parts), lines=lines if parts else 0)
-    rows = SumRows(place, partial, scratch[:7])
-    share = ShareRows(place, low_grad, shared, scratch[7:10])
+    middle_grad_ref, gain_ref, low_grad, gated_grads = rest[:4]
+    results, scratch = rest[4 : 4 + count], rest[4 + count :]
+    held, weight_sems, sent = scratch[:3]
+    rows = SumRows(place, partial, scratch[3:10])
+    swap = SwapBlocks(place, lambda slot, mate: sent.at[slot, mate], gated_grads, scratch[10:13])
     sums = [
-        SumLines(place, blocks[index], results[index], scratch[10 + 7 * index : 17 + 7 * index], first)
+        SumLines(place, blocks[index], results[index], scratch[13 + 7 * index : 20 + 7 * index], first)
         for index, (first, _) in enumerate(parts)
     ]
+    meet(place, lines=lines if parts else 0, cores=True)
+    rows.begin()
     for each in sums:
         each.begin()
+    loads = load_weights(weights, held, weight_sems)
+    for load in loads:
+        load.start()
     gain_ref[...] = jnp.zeros_like(gain_ref)
+    rows.send_far()
+    for each in sums:
+        each.wait_loads()
+        each.round(1)
+    rows.send_near()
+    rows.send_relayed()
+    for load in loads:
+        load.wait()
+    rows.wait_half(False)
+    rows.wait_half(True)
 
     def body(here):
         part, gains = norm_back_rows(rows.total(here), middle_ref[here], scale_ref[...])
@@ -1297,27 +1442,24 @@
         low_grad[here] = total.astype(low)
         gain_ref[...] += jnp.sum(gains, axis=0, keepdims=True)
 
-    def begin():
-        for each in sums:
-            each.wait_loads()
-            each.round(1)
-
-    def step(number):
-        def go():
-            for each in sums:
-                each.round(number)
-
-        return go
-
-    def last():
-        for each in sums:
-            for number in range(4, lines):
-                each.round(number)
-            each.exchange()
-        for each in sums:
-            each.finish()
-
-    sum_and_share(rows, share, body, low_grad.shape[0] // 2, (begin, step(2), step(3), last))
+    row_steps(0, low_grad.shape[0], body)
+    _, _, all_lines, _, depth, width = held.shape
+    for slot in range(2):
+        for index, mate in enumerate(swap.order):
+            weight = held[slot, mate].reshape(all_lines * MATES * depth, width)
+            sent[slot, mate] = dot(low_grad[...], weight, NN).astype(low)
+            swap.begin(slot, index)
+    rows.finish()
+    for each in sums:
+        each.round(2)
+        each.round(3)
+    swap.finish()
+    for each in sums:
+        for number in range(4, lines):
+            each.round(number)
+        each.exchange()
+    for each in sums:
+        each.finish()
 
 
 def last_rows_kernel(
@@ -1328,7 +1470,7 @@
     input_grad, block_output, gain_ref = rest[:3]
     results, scratch = rest[3 : 3 + pieces], rest[3 + pieces :]
     low_grad, low_output = scratch[:2]
-    meet(place, far=bool(pieces), lines=lines if pieces else 0)
+    meet(place, far=bool(pieces), lines=lines if pieces else 0, straight=True)
     rows = SumRows(place, partial, scratch[2:9])
     outs = SumRows(place, mlp_partial, scratch[9:16])
     make = sender(scratch[16:18])
@@ -1379,8 +1521,7 @@
         swap.start()
         swap.wait_recv()
         small.add_top(theirs, 3)
-        small.round(1)
-        small.round(2)
+        small.direct()
     outs.wait_half(False)
     outs.wait_half(True)
 
@@ -1393,9 +1534,11 @@
     second_local = pltpu.make_async_copy(low_output, block_output.at[place.core], local_sems.at[1])
     second_local.start()
     for turn in range(3, lines):
-        for each in sums:
+        for each in sums[1:]:
             each.round(turn)
-    for each in sums:
+    for each in sums[:1]:
+        each.exchange_direct()
+    for each in sums[1:]:
         each.exchange()
     rows.finish()
     outs.finish()
@@ -1406,7 +1549,7 @@
     if sums:
         swap.wait_send()
     for each in sums:
-        each.finish()
+        each.finish(direct=each is sums[0])
 
 
 def first_rows_kernel(lines, whole, pieces, input_ref, *rest):
@@ -1421,13 +1564,13 @@
     ]
     for gather in gathers[:whole]:
         gather.begin()
+    for gather in gathers[:whole]:
+        gather.leave()
     share.begin_half(False)
     share.begin_half(True)
     share.begin_rest()
     for gather in gathers[whole:]:
         gather.begin()
-    for gather in gathers[:whole]:
-        gather.leave()
     share.forward()
     for gather in gathers[:whole]:
         gather.onwards(1)
@@ -1457,28 +1600,38 @@
     )
 
 
-def middle_rows(partial, mine, scale, moving, lines):
-    seqs, _, rows, columns = partial.shape
+def middle_rows(gathered, weights, mine, scale, out_grad, moving, lines):
+    rows, columns = mine.shape
+    shared = (2, MATES, rows, columns)
     arrays = [array for array, _ in moving]
     return remote_call(
         functools.partial(middle_kernel, lines, tuple(part for _, part in moving)),
         1,
-        [(partial, "any"), (mine, "held"), (scale, "held")] + [(array, "any") for array in arrays],
-        [((rows, columns), wide, "held"), (partial.shape, low, "any")]
+        [(gathered, "held"), (weights, "any"), (mine, "held"), (scale, "held"), (out_grad, "any")]
+        + [(array, "any") for array in arrays],
+        [((rows, columns), wide, "held"), (shared, low, "any"), (shared, low, "any")]
         + [(array.shape, low, "any") for array in arrays],
-        [pltpu.VMEM((rows, columns), low)]
-        + SumRows.scratch(rows, columns)
-        + ShareRows.scratch()
+        [
+            pltpu.VMEM((rows, columns), low),
+            pltpu.VMEM(weights.shape, low),
+            pltpu.SemaphoreType.DMA((2, MATES)),
+        ]
+        + ShareRows.scratch() * 2
         + GatherLines.scratch(lines) * len(arrays),
-        {3 + index: 2 + index for index in range(len(arrays))},
+        {5 + index: 3 + index for index in range(len(arrays))},
     )
 
 
-def turn_rows(partial, middle, grad, scale, summing, lines):
+def turn_rows(partial, weights, middle, grad, scale, summing, lines):
     seqs, _, rows, columns = partial.shape
-    scratch = (
-        [pltpu.VMEM((rows, columns), low)] + SumRows.scratch(rows, columns) + ShareRows.scratch()
-    )
+    width = weights.shape[-1]
+    blocks = (2, MATES, rows, width)
+    scratch = [
+        pltpu.VMEM(weights.shape, low),
+        pltpu.SemaphoreType.DMA((2, MATES)),
+        pltpu.VMEM(blocks, low),
+    ]
+    scratch += SumRows.scratch(rows, columns) + SwapBlocks.scratch()
     outs = []
     for array, (_, height) in summing:
         shape = (MATES, height, array.shape[3])
@@ -1487,12 +1640,13 @@
     return remote_call(
         functools.partial(turn_rows_kernel, lines, tuple(part for _, part in summing)),
         2,
-        [(partial, "any"), (middle, "held"), (grad, "held"), (scale, "held")]
+        [(partial, "any"), (weights, "any"), (middle, "held"), (grad, "held"), (scale, "held")]
         + [(array, "any") for array, _ in summing],
         [
             ((rows, columns), wide, "held"),
             ((1, columns), wide, "held"),
-            (partial.shape, low, "any"),
+            ((rows, columns), low, "held"),
+            (blocks, low, "any"),
         ]
         + outs,
         scratch,
@@ -1592,12 +1746,12 @@
         )(*[array for array, _ in ins])
 
 
-def delta_front(limit, raw, taps, logits, scale, out_grad, moving, lines, seqs, heads, span):
+def delta_front(limit, raw, taps, logits, scale, moving, lines, seqs, heads, span):
     steps = Steps(seqs, heads, span)
     chains, chunks, size = steps.chains, steps.chunks, CHUNK
     squares, doubles = (chains, chunks, CHUNK, size), (chains, chunks, CHUNK, 2 * size)
     states, tails = (chains, size, size), (seqs, 16, 3 * heads * size)
-    tokens, model_width = out_grad.shape[1:]
+    tokens = span // MATES
     anywhere = pl.BlockSpec(memory_space=pl.ANY)
     arrays = [array for array, _ in moving]
     ins = [
@@ -1608,7 +1762,6 @@
         (logits, steps.logit("first")),
         (raw, steps.gate("second")),
         (scale, steps.whole((1, size))),
-        (out_grad, anywhere),
     ] + [(array, anywhere) for array in arrays]
     outs = [
         ((seqs * span, 3 * heads * size), low, steps.streams("first")),
@@ -1621,7 +1774,8 @@
         (squares, wide, steps.blocks("second")),
         ((seqs * span, heads * size), wide, steps.head("second")),
         ((seqs * span, heads * size), low, steps.head("second")),
-        ((seqs, MATES, tokens, model_width), low, anywhere),
+        ((seqs, MATES, tokens, heads * size), low, anywhere),
+        ((seqs, MATES) + arrays[0].shape, low, anywhere),
     ] + [(array.shape, low, anywhere) for array in arrays]
     scratch = [
         pltpu.VMEM((span + 16, 3 * size), wide),
@@ -1636,8 +1790,10 @@
         pltpu.VMEM(tails, low),
         pltpu.SemaphoreType.DMA((2, seqs)),
         pltpu.SemaphoreType.DMA((2,)),
+        pltpu.VMEM((seqs, span, heads * size), low),
     ]
-    scratch += ShareRows.scratch() + GatherLines.scratch(lines) * len(arrays)
+    scratch += ShareRows.scratch() + SwapBlocks.scratch()
+    scratch += GatherLines.scratch(lines) * len(arrays)
     moves = tuple(part for _, part in moving)
     return steps.call(
         functools.partial(front_kernel, lines, heads, moves),
@@ -1645,13 +1801,13 @@
         ins,
         outs,
         scratch,
-        {8 + index: 11 + index for index in range(len(arrays))},
+        {7 + index: 12 + index for index in range(len(arrays))},
     )
 
 
 def delta_back(
     limit, raw, tails, taps, logits, scale, qkv, wu, maps, total, grad, mixed, solved, state, fresh,
-    summing, lines, seqs, heads, span,
+    row_grad, summing, lines, seqs, heads, span,
 ):
     steps = Steps(seqs, heads, span)
     chains, chunks, size = steps.chains, steps.chunks, CHUNK
@@ -1675,11 +1831,13 @@
         (solved, steps.blocks("second")),
         (state, steps.blocks("second")),
         (fresh, steps.blocks("second")),
+        (row_grad, anywhere),
     ] + [(array, anywhere) for array, _ in summing]
     outs = [
         (all_shape, low, steps.whole(all_shape)),
         ((chains, 8, size), wide, steps.few("first", size)),
         ((chains, 8, 3 * size), wide, steps.few("second", 3 * size)),
+        ((seqs, MATES) + row_grad.shape, low, anywhere),
     ]
     edges = (chains, 16, 3 * size)
     scratch = [
@@ -1697,7 +1855,7 @@
         pltpu.VMEM(edges, low),
         pltpu.SemaphoreType.DMA((2, chains)),
         pltpu.SemaphoreType.DMA((2,)),
-    ]
+    ] + ShareRows.scratch()
     for array, (_, height) in summing:
         shape = (MATES, height, array.shape[3])
         scratch += SumLines.scratch(lines, shape)
@@ -1916,7 +2074,7 @@
         )
         input_rows, = first_rows(block_input, (), 0, lines)
         small, attn_full, output_full, ups_full, downward_full = (gather_weights(cut) for cut in cuts)
-        front_moves = ()
+        front_moves = ((output_full, None),)
     attn_full = attn_full.reshape(model_width, attn_width)
     input_rows = input_rows.reshape(rows, model_width)
     small = small.reshape(count, SMALL * 128)
@@ -1941,21 +2099,19 @@
 
     flat_normed, raw, logits = project(input_rows, attn_scale, attn_full, gates_end)
     sizes_of = (lines, seq_count, heads, span)
-    qkv, solved, wu, maps, total, tails, state, fresh, mixed, gated, grad_rows, *moved = delta_front(
-        limit, raw, taps, logits, head_scale, out_grad, front_moves, *sizes_of
+    (
+        qkv, solved, wu, maps, total, tails, state, fresh, mixed, gated, gathered, output_all, *moved
+    ) = delta_front(limit, raw, taps, logits, head_scale, front_moves, *sizes_of)
+    middle_moves = ()
+    if near:
+        ups_full = moved[1]
+        middle_moves = (
+            (ups_full, (ups_split, depth - ups_split)), (downward_full, (0, depth))
+        )
+    middle, mlp_normed, grad_rows, *moved = middle_rows(
+        gathered, output_all, mine_low, mlp_scale, out_grad, middle_moves, lines
     )
     grad_rows = grad_rows.reshape(rows, model_width)
-    middle_moves = ()
-    if near:
-        output_full, ups_full = moved
-        middle_moves = (
-            (ups_full, (ups_split, depth - ups_split)), (downward_full, (0, depth))
-        )
-    output_full = output_full.reshape(model_width, width)
-    attn_part = matmul("rc,dc->rd", gated, output_full).astype(low)
-    middle, mlp_normed, *moved = middle_rows(
-        attn_part.reshape(blocked), mine_low, mlp_scale, middle_moves, lines
-    )
     if near:
         ups_full, downward_full = moved
     ups_full = ups_full.reshape(model_width, 2 * units)
@@ -1985,25 +2141,24 @@
     ups_blocks, downward_blocks = cut_rows(ups_grad), cut_rows(downward_grad)
     turn_sums = back_sums = ()
     if near:
-        sums_split = depth // 128 * 96
+        sums_split = depth // 128 * 80
         turn_sums = ((ups_blocks, (0, sums_split)),)
-    middle_grad, mlp_gain_grad, attn_grad_rows, *summed = turn_rows(
-        normed_two_part.reshape(blocked), middle, grad_mine, mlp_scale, turn_sums, lines
+    middle_grad, mlp_gain_grad, attn_grad_mine, gated_grad, *summed = turn_rows(
+        normed_two_part.reshape(blocked), output_all, middle, grad_mine, mlp_scale, turn_sums, lines
     )
-    attn_grad_rows = attn_grad_rows.reshape(rows, model_width)
-    output_grad = cut_rows(matmul("rd,rc->dc", attn_grad_rows, gated).astype(low))
-    gated_grad = matmul("rd,dc->rc", attn_grad_rows, output_full)
     if near:
         ups_low, = summed
         back_sums = (
             (ups_blocks, (sums_split, depth - sums_split)),
             (downward_blocks, (0, depth)),
-            (output_grad, (0, depth)),
-        )
-    all_grads, head_gain_parts, taps_grad, *summed = delta_back(
-        limit, raw, tails, taps, logits, head_scale, qkv, wu, maps, total, gated_grad, mixed, solved,
-        state, fresh, back_sums, *sizes_of,
+        )
+    all_grads, head_gain_parts, taps_grad, attn_grad_rows, *summed = delta_back(
+        limit, raw, tails, taps, logits, head_scale, qkv, wu, maps, total,
+        gated_grad.reshape(rows, width), mixed, solved, state, fresh, attn_grad_mine, back_sums,
+        *sizes_of,
     )
+    attn_grad_rows = attn_grad_rows.reshape(rows, model_width)
+    output_grad = cut_rows(matmul("rd,rc->dc", attn_grad_rows, gated).astype(low))
     normed_part = matmul("rc,dc->rd", all_grads, attn_full).astype(low)
     attn_grads = cut_rows(matmul("rd,rc->dc", flat_normed, all_grads).astype(low))
 
@@ -2036,9 +2191,11 @@
         attn_scale,
     )
     if near:
-        ups_high, downward_sum, output_sum = summed
-        blocks = (small_blocks(jnp.zeros((1, model_width), wide)), attn_grads)
-        input_grad, block_output, _, small_sum, attn_sum = last_rows(*last_ins, blocks, lines)
+        ups_high, downward_sum = summed
+        blocks = (small_blocks(jnp.zeros((1, model_width), wide)), attn_grads, output_grad)
+        input_grad, block_output, _, small_sum, attn_sum, output_sum = last_rows(
+            *last_ins, blocks, lines
+        )
         grads = held_call(
             functools.partial(unpack_kernel, heads),
             (attn_sum, output_sum, ups_low, ups_high, downward_sum),

time: 880 us -> 847 us (0.963)
  Pallas kernels: 697 us -> 680 us
  matrix products: 147 us -> 131 us
    dot_general x11 -> x9, matrix products: 147 us -> 131 us  [matmul(): return jnp.einsum(form, left, right, preferred_element_type=wide)]
    pallas_call x4, Pallas kernels: 457 us -> 447 us  [remote_call(): pl.pallas_call(body, in_specs=[anywhere if kind == 'any' else held for _,...]
where the time goes in v5:
time: 847 us; the launch traced here: 839 us
  Pallas kernels  680 us (80%)
  matrix products  131 us (15%)
  local copies, waits for them, and re-layouts  23 us (3%)
    pallas_call x4, Pallas kernels, remote_call(): pl.pallas_call(body, in_specs=[anywhere if kind == 'any' else held for _,...  447 us
    pallas_call x2, Pallas kernels, call(): pl.pallas_call(body, grid=(2 * self.chains,), in_specs=[spec for _, spec...  203 us
    dot_general x9, matrix products, matmul(): return jnp.einsum(form, left, right, preferred_element_type=wide)  131 us
    pallas_call x1, Pallas kernels, project(): pl.pallas_call(project_kernel, grid=(rows // tile,), in_specs=[tall(model...  17.9 us

profile of v5, /device:TPU:0, one launch (start us, length us, event | category | flops | bytes accessed | tf_op | source)
XLA Modules:
  0.0 839.1 jit_solution(5192232900091543013)
XLA Ops:
  0.7 1.3 fusion.5
  2.0 1.9 add_subtract_fusion.limit_ref
  3.9 1.4 copy.49.beta
  5.3 5.4 shard_map.271
  10.8 0.0 copy-done.4
  10.8 0.1 reshape.184
  11.0 0.1 fusion.1
  11.1 0.6 copy.70
  11.7 109.5 %shard_map.272 = (bf16[2,4,256,2048]{3,2,1,0:T(8,128)(2,1)}, bf16[4,4,16,128]{3,2,1,0:T(8,128)(2,1)}, bf16[4,4,128,1152]{3,2,1,0:T(8,128)(2,1)}, bf16[4,4,128,25...) custom-call(bf16[2,256,2048]{2,1,0:T(8,128)(2,1)} %input_ref.1, ...), custom_call_target="tpu_custom_call" | custom-call | tf_op jit(solution)/shard_map/pallas_call | solution.py:1297
  121.2 0.9 copy.68
  122.1 0.6 slice_convert_fusion
  122.7 17.9 %shard_map.273 = (bf16[2048,2048]{1,0:T(8,128)(2,1)}, bf16[2048,1024]{1,0:T(8,128)(2,1)}, f32[2048,128]{1,0:T(8,128)}) custom-call(bf16[2048,2048]{1,0:T(8,128)(2,1)} %bitcast.74, f32[1,2048]{1,0:T(1,128)} %bitcast.96, bf16[2048,1152]{1,0:T(8,128)(2,1)} %bitcast.79), custom_call_target="tpu_custom_call" | custom-call | tf_op jit(solution)/shard_map/pallas_call | solution.py:1883
  140.6 0.1 copy.60
  140.7 0.1 copy.58
  140.9 0.7 reshape.215.taps_ref
  141.6 0.6 reshape.211.scale_ref
  142.2 91.5 %shard_map.274 = (bf16[2048,768]{1,0:T(8,128)(2,1)}, f32[4,8,128,128]{3,2,1,0:T(8,128)}, f32[4,8,128,256]{3,2,1,0:T(8,128)}, f32[4,8,128,128]{3,2,1,0:T(8,128)},...) custom-call(s32[2]{0:T(128)} %add_subtract_fusion.limit_ref, ...), custom_call_target="tpu_custom_call", output_to_operand_aliasing={{12}: (7, {}), {13}: (8, {})} | custom-call | tf_op jit(solution)/shard_map/pallas_call | solution.py:1732
  233.7 1.6 dynamic-slice_bitcast_fusion
  235.3 99.4 %shard_map.275 = (f32[256,2048]{1,0:T(8,128)}, bf16[2,4,256,2048]{3,2,1,0:T(8,128)(2,1)}, bf16[2,4,256,2048]{3,2,1,0:T(8,128)(2,1)}, bf16[4,4,128,1408]{3,2,1,0:T(8,128)(2,1)}, bf16[4,4,128,704]{3,2,1,0:T(8,128)(2,1)}) custom-call(bf16[2,4,256,256]{3,2,1,0:T(8,128)(2,1)} %get-tuple-element.87.gathered, ...), custom_call_target="tpu_custom_call", output_to_operand_aliasing={{3}: (5, {}), {4}: (6, {})} | custom-call | tf_op jit(solution)/shard_map/pallas_call | solution.py:1297
  334.7 18.9 %fusion.6 = f32[2048,1408]{0,1:T(8,128)} fusion(bf16[2048,2048]{1,0:T(8,128)(2,1)} %bitcast.104, bf16[2048,1408]{1,0:T(8,128)(2,1)} %bitcast.67), kind=kOutput, calls=%fused_computation.38 | convolution fusion | flops 11811160064 | bytes 25690112 | tf_op jit(solution)/shard_map/rd,df->rf/dot_general | solution.py:71
  353.6 14.7 %multiply_convert_fusion.2 = (bf16[2048,704]{0,1:T(8,128)(2,1)}, bf16[2048,704]{0,1:T(8,128)(2,1)}, bf16[2048,704]{0,1:T(8,128)(2,1)S(1)}) fusion(f32[2048,1408]{0,1:T(8,128)} %fusion.6, bf16[2048,2048]{1,0:T(8,128)(2,1)} %bitcast.106, bf16[2048,704]{1,0:T(8,128)(2,1)S(1)} %bitcast.84), kind=kOutput, calls=%fused_computation.8 | convolution fusion | flops 5927206912 | bytes 31457280 | tf_op jit(solution)/shard_map/rd,df->rf/dot_general | solution.py:71
  368.3 1.6 copy-done.12
  369.9 10.8 %convolution_convert_fusion.5 = bf16[2048,704]{0,1:T(8,128)(2,1)} fusion(bf16[2048,704]{0,1:T(8,128)(2,1)S(1)} %get-tuple-element.174, bf16[2048,2048]{1,0:T(8,128)(2,1)} %bitcast.107), kind=kOutput, calls=%fused_computation.11 | convolution fusion | flops 5907021824 | bytes 14155776 | tf_op jit(solution)/shard_map/rd,rf->df/dot_general | solution.py:71
  380.8 4.8 copy.53
  385.6 19.5 %convolution_convert_fusion.4 = bf16[2048,1408]{1,0:T(8,128)(2,1)} fusion(bf16[2048,2048]{1,0:T(8,128)(2,1)} %bitcast.105, bf16[2048,704]{0,1:T(8,128)(2,1)} %get-tuple-element.173, bf16[2048,704]{0,1:T(8,128)(2,1)} %get-tuple-element.172), kind=kOutput, calls=%fused_computation.4 | convolution fusion | flops 11825577984 | bytes 19922944 | tf_op jit(solution)/shard_map/rd,rf->df/dot_general | solution.py:71
  405.2 17.4 %convolution_convert_fusion.3 = bf16[2048,2048]{1,0:T(8,128)(2,1)} fusion(bf16[2048,1408]{1,0:T(8,128)(2,1)S(1)} %bitcast.70, bf16[2048,704]{0,1:T(8,128)(2,1)} %get-tuple-element.173, bf16[2048,704]{0,1:T(8,128)(2,1)S(1)} %copy-done.13), kind=kOutput, calls=%fused_computation.3 | convolution fusion | flops 11826888704 | bytes 19922944 | tf_op jit(solution)/shard_map/rf,df->rd/dot_general | solution.py:71
  422.6 108.7 %shard_map.276 = (f32[256,2048]{1,0:T(8,128)}, f32[1,2048]{1,0:T(1,128)}, bf16[256,2048]{1,0:T(8,128)(2,1)}, bf16[2,4,256,256]{3,2,1,0:T(8,128)(2,1)}, bf16[4,80,1408]{2,1,0:T(8,128)(2,1)}) custom-call(bf16[2,4,256,2048]{3,2,1,0:T(8,128)(2,1)} %bitcast.77, bf16[2,4,4,4,128,256]{5,4,3,2,1,0:T(8,128)(2,1)} %get-tuple-element.88.weights, ...), custom_call_target="tpu_custom_call" | custom-call | tf_op jit(solution)/shard_map/pallas_call | solution.py:1297
  531.3 111.8 %shard_map.277 = (bf16[2048,1152]{1,0:T(8,128)(2,1)}, f32[4,8,128]{2,1,0:T(8,128)}, f32[4,8,384]{2,1,0:T(8,128)}, bf16[2,4,256,2048]{3,2,1,0:T(8,128)(2,1)}, bf1...) custom-call(s32[2]{0:T(128)} %add_subtract_fusion.limit_ref, ...), custom_call_target="tpu_custom_call" | custom-call | tf_op jit(solution)/shard_map/pallas_call | solution.py:1732
  643.2 7.0 convolution_convert_fusion.6
  650.2 15.5 %convolution_convert_fusion = bf16[2048,1152]{1,0:T(8,128)(2,1)} fusion(bf16[2048,2048]{1,0:T(8,128)(2,1)} %get-tuple-element.107, bf16[2048,1152]{1,0:T(8,128)(2,1)S(1)} %copy-done.7), kind=kOutput, calls=%fused_computation | convolution fusion | flops 9666035712 | bytes 17825792 | tf_op jit(solution)/shard_map/rd,rc->dc/dot_general | solution.py:71
  665.7 0.2 reshape.202
  666.0 0.1 copy.55
  666.1 0.1 copy.56
  666.1 0.8 slice_reduce_fusion.1
  666.9 0.1 reshape.201
  667.1 0.1 concatenate.21
  667.2 0.6 copy.63
  667.8 11.6 %convolution_convert_fusion.1 = bf16[2048,2048]{1,0:T(8,128)(2,1)} fusion(bf16[2048,704]{0,1:T(8,128)(2,1)} %copy-done.12, bf16[2048,704]{1,0:T(8,128)(2,1)} %bitcast.83), kind=kOutput, calls=%fused_computation.1 | convolution fusion | flops 5909774336 | bytes 14155776 | tf_op jit(solution)/shard_map/rf,df->rd/dot_general | solution.py:71
  679.4 15.7 %convolution_convert_fusion.2 = bf16[2048,2048]{1,0:T(8,128)(2,1)} fusion(bf16[2048,1152]{1,0:T(8,128)(2,1)} %get-tuple-element.102, bf16[2048,1152]{1,0:T(8,128)(2,1)S(1)} %bitcast.82), kind=kOutput, calls=%fused_computation.2 | convolution fusion | flops 9667870720 | bytes 17825792 | tf_op jit(solution)/shard_map/rc,dc->rd/dot_general | solution.py:71
  695.1 129.7 %shard_map.278 = (bf16[2,256,2048]{2,1,0:T(8,128)(2,1)}, bf16[2,256,2048]{2,1,0:T(8,128)(2,1)}, f32[1,2048]{1,0:T(1,128)}, bf16[4,16,128]{2,1,0:T(8,128)(2,1)}, ...) custom-call(bf16[2,4,256,2048]{3,2,1,0:T(8,128)(2,1)} %bitcast.76, bf16[2,4,256,2048]{3,2,1,0:T(8,128)(2,1)} %bitcast.75, ...), custom_call_target="tpu_custom_call" | custom-call | tf_op jit(solution)/shard_map/pallas_call | solution.py:1297
  824.8 5.6 shard_map.279
  830.4 1.5 copy.57
  831.9 0.7 convert_bitcast_fusion.2
  832.6 0.7 reshape.208
  833.4 0.5 fusion.4
  833.9 0.5 slice.50
  834.4 3.2 copy.77
  837.6 1.3 copy.78
  (55 shorter events, 0.3 us)
Async XLA Ops:
  0.6 10.1 %copy-start.4 = (f32[8,3,4,8]{3,2,1,0:T(4,128)S(1)}, f32[8,3,4,8]{3,2,1,0:T(4,128)}, u32[]{:S(2)}) copy-start(f32[8,3,4,8]{3,2,1,0:T(4,128)} %param.24) | copy-start | bytes 9220
  0.7 10.2 %copy-start.9 = (f32[128]{0:T(128)S(1)}, f32[128]{0:T(128)}, u32[]{:S(2)}) copy-start(f32[128]{0:T(128)} %param.18) | copy-start | bytes 1540
  0.7 10.2 %copy-start.10 = (f32[128]{0:T(128)S(1)}, f32[128]{0:T(128)}, u32[]{:S(2)}) copy-start(f32[128]{0:T(128)} %param.27) | copy-start | bytes 1540
  0.7 10.3 %copy-start.11 = (f32[8]{0:T(128)S(1)}, f32[8]{0:T(128)}, u32[]{:S(2)}) copy-start(f32[8]{0:T(128)} %param.25) | copy-start | bytes 100
  142.2 91.5 %copy-start = (bf16[2,256,2048]{2,1,0:T(8,128)(2,1)S(1)}, bf16[2,256,2048]{2,1,0:T(8,128)(2,1)}, u32[]{:S(2)}) copy-start(bf16[2,256,2048]{2,1,0:T(8,128)(2,1)} %grad_any.1) | copy-start | bytes 6291460
  142.2 91.5 %copy-start.1 = (bf16[2,256,2048]{2,1,0:T(8,128)(2,1)S(1)}, bf16[2,256,2048]{2,1,0:T(8,128)(2,1)}, u32[]{:S(2)}) copy-start(bf16[2,256,2048]{2,1,0:T(8,128)(2,1)} %input_ref.1) | copy-start | bytes 6291460
  334.7 18.9 %copy-start.2 = (bf16[4,4,128,704]{3,2,1,0:T(8,128)(2,1)S(1)}, bf16[4,4,128,704]{3,2,1,0:T(8,128)(2,1)}, u32[]{:S(2)}) copy-start(bf16[4,4,128,704]{3,2,1,0:T(8,128)(2,1)} %get-tuple-element.92) | copy-start | bytes 8650756
  368.3 1.6 copy-start.12
  380.8 24.4 %slice-start = ((s8[5767168]{0:T(1024)(128)(4,1)}), s8[1572864]{0:T(1024)(128)(4,1)S(1)}, s32[]{:S(2)}) async-start(s8[5767168]{0:T(1024)(128)(4,1)} %bitcast.68), calls=%async_computation | async-start | bytes 3145728
  385.6 19.6 %slice-start.1 = ((s8[5767168]{0:T(1024)(128)(4,1)}), s8[4194304]{0:T(1024)(128)(4,1)S(1)}, s32[]{:S(2)}) async-start(s8[5767168]{0:T(1024)(128)(4,1)} %bitcast.68), calls=%async_computation.1 | async-start | bytes 8388608
  385.6 19.6 %copy-start.13 = (bf16[2048,704]{0,1:T(8,128)(2,1)S(1)}, bf16[2048,704]{0,1:T(8,128)(2,1)}, u32[]{:S(2)}) copy-start(bf16[2048,704]{0,1:T(8,128)(2,1)} %get-tuple-element.172) | copy-start | bytes 8650756
  531.3 111.9 %copy-start.8 = (bf16[2048,256]{1,0:T(8,128)(2,1)S(1)}, bf16[2048,256]{1,0:T(8,128)(2,1)}, u32[]{:S(2)}) copy-start(bf16[2048,256]{1,0:T(8,128)(2,1)} %get-tuple-element.109) | copy-start | bytes 3145732
  643.2 7.0 copy-start.7
  650.2 15.5 %copy-start.5 = (f32[4,8,384]{2,1,0:T(8,128)S(1)}, f32[4,8,384]{2,1,0:T(8,128)}, u32[]{:S(2)}) copy-start(f32[4,8,384]{2,1,0:T(8,128)} %get-tuple-element.106) | copy-start | bytes 147460
  650.2 16.8 %copy-start.6 = (f32[1,2048]{1,0:T(1,128)S(1)}, f32[1,2048]{1,0:T(1,128)}, u32[]{:S(2)}) copy-start(f32[1,2048]{1,0:T(1,128)} %get-tuple-element.104) | copy-start | bytes 24580
  650.2 29.2 %slice-start.2 = ((s8[4718592]{0:T(1024)(128)(4,1)}), s8[524288]{0:T(1024)(128)(4,1)S(1)}, s32[]{:S(2)}) async-start(s8[4718592]{0:T(1024)(128)(4,1)} %bitcast.80), calls=%async_computation.2 | async-start | bytes 1048576
  667.8 11.6 %slice-start.3 = ((s8[4718592]{0:T(1024)(128)(4,1)}), s8[4194304]{0:T(1024)(128)(4,1)S(1)}, s32[]{:S(2)}) async-start(s8[4718592]{0:T(1024)(128)(4,1)} %bitcast.80), calls=%async_computation.3 | async-start | bytes 8388608
  824.8 12.8 %copy-start.3 = (bf16[2,256,2048]{2,1,0:T(8,128)(2,1)S(1)}, bf16[2,256,2048]{2,1,0:T(8,128)(2,1)}, u32[]{:S(2)}) copy-start(bf16[2,256,2048]{2,1,0:T(8,128)(2,1)} %get-tuple-element.199) | copy-start | bytes 6291460

commit v6 on v5

--- a/solution.py
+++ b/solution.py
@@ -10,6 +10,8 @@
 CONV = 4
 MATES = 4
 SMALL = 16
+CONV_ROW = 3
+BETA_ROW = 5
 
 
 epsilon = 1e-06
@@ -176,7 +178,7 @@
 
 def head_squash(logits, head):
     lanes = lax.broadcasted_iota(jnp.int32, logits.shape, 1)
-    column = jnp.sum(jnp.where(lanes == head, logits, 0.0), axis=1, keepdims=True)
+    column = jnp.sum(jnp.where(lanes == BETA_ROW + head, logits, 0.0), axis=1, keepdims=True)
     return jax.nn.sigmoid(jnp.broadcast_to(column, logits.shape))
 
 
@@ -604,7 +606,7 @@
             )
             lanes = lax.broadcasted_iota(jnp.int32, (CHUNK, head_size), 1)
             logit_grad = jnp.where(
-                lanes == head, beta_grad * (live * squash * (1.0 - squash)), 0.0
+                lanes == BETA_ROW + head, beta_grad * (live * squash * (1.0 - squash)), 0.0
             ).astype(low)
 
             there = pl.ds(pl.multiple_of(seq * span + start, CHUNK), CHUNK)
@@ -683,9 +685,12 @@
     def _():
         share.forward()
 
+    @pl.when(step == chains + 1)
+    def _():
+        share.forward_far()
+
     @pl.when(step == 2 * chains - 3)
     def _():
-        share.forward_far()
         for each in sums:
             each.round(3)
 
@@ -713,14 +718,18 @@
             each.finish()
 
 
-def project_kernel(input_ref, scale_ref, weight_ref, normed_ref, raw_ref, logit_ref):
+def project_kernel(input_ref, scale_ref, weight_ref, beta_ref, normed_ref, raw_ref, logit_ref):
     value = input_ref[...].astype(wide)
     normed = (value * inverse_rms(value) * scale_ref[...]).astype(low)
     normed_ref[...] = normed
-    out = dot(normed, weight_ref[...], NN)
-    width = raw_ref.shape[1]
-    raw_ref[...] = out[:, :width].astype(low)
-    logit_ref[...] = out[:, width:]
+    raw_ref[...] = dot(normed, weight_ref[...], NN).astype(low)
+    logit_ref[...] = dot(normed, beta_ref[...], NT)
+
+
+def back_project_kernel(grad_ref, weight_ref, beta_ref, out_ref):
+    width = weight_ref.shape[1]
+    total = dot(grad_ref[:, :width], weight_ref[...], NT)
+    out_ref[...] = (total + dot(grad_ref[:, width:], beta_ref[...], NN)).astype(low)
 
 
 MESH = pl.DeviceIdType.MESH
@@ -1133,7 +1142,9 @@
 
     def load(self, line):
         return pltpu.make_async_copy(
-            self.blocks.at[line, :, pl.ds(self.first, self.held.shape[2])],
+            self.blocks.at[
+                line, :, pl.ds(self.first, self.held.shape[2]), pl.ds(0, self.held.shape[3])
+            ],
             self.held.at[line],
             self.local_sems.at[line],
         )
@@ -1432,6 +1443,8 @@
     rows.send_relayed()
     for load in loads:
         load.wait()
+    for each in sums:
+        each.round(2)
     rows.wait_half(False)
     rows.wait_half(True)
 
@@ -1451,7 +1464,6 @@
             swap.begin(slot, index)
     rows.finish()
     for each in sums:
-        each.round(2)
         each.round(3)
     swap.finish()
     for each in sums:
@@ -1491,12 +1503,11 @@
     gain_ref[...] = jnp.zeros_like(gain_ref)
     rows.send_far()
     rows.send_near()
+    rows.send_relayed()
     outs.send_far()
-    rows.send_relayed()
     outs.send_near()
     for each in sums[1:]:
         each.round(2)
-    outs.send_relayed()
     rows.wait_half(False)
     rows.wait_half(True)
 
@@ -1520,8 +1531,11 @@
         swap = make(2, mine, theirs, place.sibling)
         swap.start()
         swap.wait_recv()
-        small.add_top(theirs, 3)
+        small.add_top(theirs, CONV_ROW)
         small.direct()
+    outs.send_relayed()
+    for each in sums[1:]:
+        each.round(3)
     outs.wait_half(False)
     outs.wait_half(True)
 
@@ -1533,7 +1547,7 @@
     second.start()
     second_local = pltpu.make_async_copy(low_output, block_output.at[place.core], local_sems.at[1])
     second_local.start()
-    for turn in range(3, lines):
+    for turn in range(4, lines):
         for each in sums[1:]:
             each.round(turn)
     for each in sums[:1]:
@@ -1552,51 +1566,139 @@
         each.finish(direct=each is sums[0])
 
 
-def first_rows_kernel(lines, whole, pieces, input_ref, *rest):
+def first_rows_kernel(input_ref, inputs, *scratch):
     place = Place()
-    ins, rest = rest[:pieces], rest[pieces:]
-    inputs, outs, scratch = rest[0], rest[1 : 1 + pieces], rest[1 + pieces :]
-    meet(place, far=bool(pieces), lines=lines if pieces else 0)
+    meet(place)
+    share = ShareRows(place, input_ref.at[place.core], inputs, scratch)
+    share.begin_half(False)
+    share.begin_half(True)
+    share.begin_rest()
+    share.forward()
+    share.forward_far()
+    share.finish()
+
+
+def first_rows(block_input):
+    seqs, rows, columns = block_input.shape
+    return remote_call(
+        first_rows_kernel,
+        0,
+        [(block_input, "any")],
+        [((seqs, MATES, rows, columns), low, "any")],
+        ShareRows.scratch(),
+    )[0]
+
+
+def first_kernel(lines, pieces, input_ref, *rest):
+    place = Place()
+    blocks, rest = rest[:pieces], rest[pieces:]
+    normed_out, raw_ref, logit_ref, small_ref, attn_out = rest[:5]
+    others, scratch = rest[5 : 3 + pieces], rest[3 + pieces :]
+    inputs, normed, small, attn, scale, out_sems = scratch[:6]
+    scratch = scratch[6:]
+    targets = (small, attn) + tuple(others)
+    meet(place, far=True, lines=lines)
     share = ShareRows(place, input_ref.at[place.core], inputs, scratch[:3])
     gathers = [
-        GatherLines(place, ins[index], outs[index], scratch[3 + 6 * index : 9 + 6 * index])
+        GatherLines(place, blocks[index], targets[index], scratch[3 + 6 * index : 9 + 6 * index])
         for index in range(pieces)
     ]
-    for gather in gathers[:whole]:
+    few, main = gathers[:2]
+    for gather in (few, main):
         gather.begin()
-    for gather in gathers[:whole]:
+    for gather in (few, main):
         gather.leave()
     share.begin_half(False)
     share.begin_half(True)
     share.begin_rest()
-    for gather in gathers[whole:]:
+    for gather in (few, main):
+        gather.onwards(1)
+    share.forward()
+    for gather in gathers[2:]:
         gather.begin()
-    share.forward()
-    for gather in gathers[:whole]:
-        gather.onwards(1)
+    few.onwards(2)
+    main.onwards(2)
+    for step in range(3, lines):
+        few.onwards(step)
     share.forward_far()
-    for step in range(2, lines):
-        for gather in gathers[:whole]:
-            gather.onwards(step)
     share.finish()
-    for gather in gathers[whole:]:
+    small_ref[...] = small[...]
+    _, _, tokens, model_width = inputs.shape
+    depth = small.shape[3]
+    parts = [(line, mate) for line in range(lines) for mate in range(MATES)]
+    for index, (line, mate) in enumerate(parts):
+        scale[:, index * depth : (index + 1) * depth] = small[line, mate, :1].astype(wide)
+    beta = jnp.concatenate([small[line, mate] for line, mate in parts], axis=1)
+    beta = over(beta, jnp.zeros((CHUNK - beta.shape[0], model_width), low))
+    outs = []
+    for slot in range(2):
+        for mate in range(MATES):
+            first = (slot * MATES + mate) * tokens
+
+            def body(here, slot=slot, mate=mate, first=first):
+                value = inputs[slot, mate, here].astype(wide)
+                there = pl.ds(pl.multiple_of(first + here.start, STEP), STEP)
+                normed[there] = (value * inverse_rms(value) * scale[...]).astype(low)
+
+            row_steps(0, tokens, body)
+            block = pl.ds(first, tokens)
+            logit_ref[block] = dot(normed[block], beta, NT)
+            outs.append(
+                pltpu.make_async_copy(
+                    normed.at[block], normed_out.at[block], out_sems.at[slot * MATES + mate]
+                )
+            )
+            outs[-1].start()
+    for step in range(3, lines):
+        main.onwards(step)
+    outs.append(pltpu.make_async_copy(attn, attn_out, out_sems.at[2 * MATES]))
+    outs[-1].start()
+    weight = attn[...].reshape(model_width, attn.shape[3])
+
+    def product(index, carry):
+        here = pl.ds(pl.multiple_of(index * tokens, STEP), tokens)
+        raw_ref[here] = dot(normed[here], weight, NN).astype(low)
+        return carry
+
+    lax.fori_loop(0, 2 * MATES, product, 0)
+    for gather in gathers[2:]:
         for slot in range(MATES):
             gather.arrive(slot)
+    for out in outs:
+        out.wait()
     for gather in gathers:
         gather.finish_plane()
-    for gather in gathers[:whole]:
+    for gather in (few, main):
         gather.finish_lines()
 
 
-def first_rows(block_input, blocks, whole, lines):
-    seqs, rows, columns = block_input.shape
-    shape = (seqs, MATES, rows, columns)
+def first_call(block_input, blocks, lines):
+    seqs, tokens, model_width = block_input.shape
+    rows = seqs * MATES * tokens
+    small, attn = ((lines,) + block.shape for block in blocks[:2])
+    shared = (seqs, MATES, tokens, model_width)
     return remote_call(
-        functools.partial(first_rows_kernel, lines, whole, len(blocks)),
+        functools.partial(first_kernel, lines, len(blocks)),
         0,
         [(array, "any") for array in (block_input, *blocks)],
-        [(shape, low, "any")] + [((lines,) + block.shape, low, "any") for block in blocks],
-        ShareRows.scratch() + GatherLines.scratch(lines) * len(blocks),
+        [
+            ((rows, model_width), low, "any"),
+            ((rows, attn[3]), low, "held"),
+            ((rows, CHUNK), wide, "held"),
+            (small, low, "held"),
+            (attn, low, "any"),
+        ]
+        + [((lines,) + block.shape, low, "any") for block in blocks[2:]],
+        [
+            pltpu.VMEM(shared, low),
+            pltpu.VMEM((rows, model_width), low),
+            pltpu.VMEM(small, low),
+            pltpu.VMEM(attn, low),
+            pltpu.VMEM((1, model_width), wide),
+            pltpu.SemaphoreType.DMA((2 * MATES + 1,)),
+        ]
+        + ShareRows.scratch()
+        + GatherLines.scratch(lines) * len(blocks),
     )
 
 
@@ -1661,22 +1763,22 @@
         + SumRows.scratch(rows, columns)
         + [pltpu.SemaphoreType.DMA((3,))] * 3
     )
-    for block in blocks:
-        scratch += SumLines.scratch(lines, block.shape[1:])
+    for block, kept in blocks:
+        scratch += SumLines.scratch(lines, block.shape[1:3] + (kept,))
     if blocks:
-        scratch += [pltpu.VMEM(blocks[0].shape, low)] * 2
+        scratch += [pltpu.VMEM(blocks[0][0].shape, low)] * 2
     return remote_call(
         functools.partial(last_rows_kernel, lines, len(blocks)),
         3,
         [(partial, "any"), (mlp_partial, "any")]
         + [(array, "held") for array in (mine, middle, middle_grad, scale)]
-        + [(block, "any") for block in blocks],
+        + [(block, "any") for block, _ in blocks],
         [
             ((seqs, rows, columns), low, "any"),
             ((seqs, rows, columns), low, "any"),
             ((1, columns), wide, "held"),
         ]
-        + [(block.shape[1:], low, "any") for block in blocks],
+        + [(block.shape[1:3] + (kept,), low, "any") for block, kept in blocks],
         scratch,
     )
 
@@ -1869,29 +1971,39 @@
     )
 
 
-def project(inputs, scale, weight, raw_width):
-    rows, model_width = inputs.shape
-    columns = weight.shape[1]
+def tiled_call(body, ins, wholes, outs):
     tile = 256
 
-    def tall(width):
-        return pl.BlockSpec((tile, width), lambda step: (step, 0))
+    def tall(shape):
+        return pl.BlockSpec((tile, shape[1]), lambda step: (step, 0))
 
     def whole(array):
         return pl.BlockSpec(array.shape, lambda step: (0, 0), pipeline_mode=pl.Buffered(1))
 
     return pl.pallas_call(
+        body,
+        grid=(ins[0].shape[0] // tile,),
+        in_specs=[tall(array.shape) for array in ins] + [whole(array) for array in wholes],
+        out_specs=[tall(shape) for shape, _ in outs],
+        out_shape=[jax.ShapeDtypeStruct(shape, dtype) for shape, dtype in outs],
+        compiler_params=pltpu.CompilerParams(vmem_limit_bytes=VMEM_BYTES),
+    )(*ins, *wholes)
+
+
+def project(inputs, scale, weight, beta):
+    rows, model_width = inputs.shape
+    return tiled_call(
         project_kernel,
-        grid=(rows // tile,),
-        in_specs=[tall(model_width), whole(scale), whole(weight)],
-        out_specs=[tall(model_width), tall(raw_width), tall(columns - raw_width)],
-        out_shape=[
-            jax.ShapeDtypeStruct((rows, model_width), low),
-            jax.ShapeDtypeStruct((rows, raw_width), low),
-            jax.ShapeDtypeStruct((rows, columns - raw_width), wide),
-        ],
-        compiler_params=pltpu.CompilerParams(vmem_limit_bytes=VMEM_BYTES),
-    )(inputs, scale, weight)
+        (inputs,),
+        (scale, weight, beta),
+        [((rows, model_width), low), ((rows, weight.shape[1]), low), ((rows, beta.shape[0]), wide)],
+    )
+
+
+def back_project(grads, weight, beta):
+    return tiled_call(
+        back_project_kernel, (grads,), (weight, beta), [((grads.shape[0], weight.shape[0]), low)]
+    )[0]
 
 
 def held_call(body, ins, outs):
@@ -1906,13 +2018,12 @@
 
 
 def pack_kernel(
-    heads, query, key, value, outgate, beta, output, swish, upward, downward,
+    heads, query, key, value, outgate, output, swish, upward, downward,
     attn_ref, output_ref, ups_ref, downs_ref,
 ):
     size = CHUNK
     width = heads * size
     units = downs_ref.shape[2]
-    beta_low = beta[...].astype(low)
     for mate in range(MATES):
         first = mate * width
         for head in range(heads):
@@ -1922,13 +2033,6 @@
                     :, first + head * size : first + (head + 1) * size
                 ].astype(low)
         attn_ref[mate, :, 3 * width : 4 * width] = outgate[:, first : first + width].astype(low)
-        shape = (beta.shape[1], size)
-        rows = lax.broadcasted_iota(jnp.int32, shape, 0)
-        columns = lax.broadcasted_iota(jnp.int32, shape, 1)
-        chosen = (rows == columns + mate * heads) & (columns < heads)
-        attn_ref[mate, :, 4 * width :] = dot(
-            beta_low, jnp.where(chosen, 1.0, 0.0).astype(low), NN
-        ).astype(low)
         output_ref[mate] = output[first : first + width, :].T.astype(low)
         here = mate * units
         ups_ref[mate, :, :units] = swish[:, here : here + units].astype(low)
@@ -1938,13 +2042,12 @@
 
 def unpack_kernel(
     heads, attn, outs, ups_low, ups_high, downs,
-    query, key, value, outgate, beta, output, swish, upward, downward,
+    query, key, value, outgate, output, swish, upward, downward,
 ):
     size = CHUNK
     width = heads * size
     units = downs.shape[2]
     split = ups_low.shape[1]
-    beta_all = None
     for mate in range(MATES):
         first = mate * width
         for head in range(heads):
@@ -1954,19 +2057,12 @@
                     mate, :, lanes : lanes + size
                 ].astype(wide)
         outgate[:, first : first + width] = attn[mate, :, 3 * width : 4 * width].astype(wide)
-        shape = (size, beta.shape[1])
-        rows = lax.broadcasted_iota(jnp.int32, shape, 0)
-        columns = lax.broadcasted_iota(jnp.int32, shape, 1)
-        chosen = (columns == rows + mate * heads) & (rows < heads)
-        part = dot(attn[mate, :, 4 * width :], jnp.where(chosen, 1.0, 0.0).astype(low), NN)
-        beta_all = part if beta_all is None else beta_all + part
         output[first : first + width, :] = outs[mate].astype(wide).T
         here = mate * units
         for rows_here, part in ((pl.ds(0, split), ups_low), (pl.ds(split, swish.shape[0] - split), ups_high)):
             swish[rows_here, here : here + units] = part[mate, :, :units].astype(wide)
             upward[rows_here, here : here + units] = part[mate, :, units:].astype(wide)
         downward[here : here + units, :] = downs[mate].astype(wide).T
-    beta[...] = beta_all
 
 
 def cut_columns(weight):
@@ -2015,41 +2111,44 @@
     width = heads * head_size
     units = swish_weight.shape[1] // MATES
 
-    near = lines <= 4 and depth % 128 == 0
+    conv_rows = -(-heads * 3 * CONV * gain_part // CHUNK)
+    near = 1 < lines <= 4 and depth == CHUNK and conv_rows == BETA_ROW - CONV_ROW
     rows = seq_count * MATES * tokens
     span = MATES * tokens
 
+    def in_rows(array):
+        return jnp.pad(array, ((0, 0), (0, -array.shape[1] % 128)))
+
+    def gains_of(attn, mlp, head):
+        return jnp.concatenate([attn, mlp, in_rows(head)], axis=1)
+
+    gains_cut = gains_of(attn_gain[None], mlp_gain[None], head_gain[None]).astype(low)
+    conv_cut = in_rows(conv_kernel.astype(low).reshape(MATES, -1))
+    beta_cut = beta_weight.astype(low).reshape(depth, MATES, heads).transpose(1, 2, 0)
     small_cut = jnp.concatenate(
-        [
-            jnp.broadcast_to(
-                jnp.concatenate([attn_gain, mlp_gain, head_gain]).astype(low)[None],
-                (MATES, 2 * depth + gain_part),
-            ),
-            jnp.zeros((MATES, -gain_part % 128), low),
-            conv_kernel.astype(low).reshape(MATES, -1),
-        ],
-        axis=1,
+        [jnp.broadcast_to(gains_cut, (MATES, gains_cut.shape[1])), conv_cut], axis=1
     )
-    sizes = (depth, depth, gain_part, -gain_part % 128, heads * 3 * CONV * gain_part)
-    starts = [sum(sizes[:index]) for index in range(len(sizes) + 1)]
-    small_cut = jnp.pad(small_cut, ((0, 0), (0, SMALL * 128 - starts[-1])))
+    conv_start, conv_size = gains_cut.shape[1], heads * 3 * CONV * gain_part
+    beta_start = small_cut.shape[1]
+    small_cut = jnp.concatenate([small_cut, beta_cut.reshape(MATES, -1)], axis=1)
+    small_size = small_cut.shape[1]
+    small_cut = jnp.pad(small_cut, ((0, 0), (0, SMALL * 128 - small_size)))
     small_cut = small_cut.reshape(MATES, SMALL, 128)
     streams_end, gates_end = 3 * width, 4 * width
-    attn_width = gates_end + head_size
     if near:
         cuts = held_call(
             functools.partial(pack_kernel, heads),
             (
-                query_weight, key_weight, value_weight, outgate_weight, beta_weight, output_weight,
+                query_weight, key_weight, value_weight, outgate_weight, output_weight,
                 swish_weight, upward_weight, downward_weight,
             ),
             [
                 ((MATES, depth, columns), low)
-                for columns in (attn_width, width, 2 * units, units)
+                for columns in (gates_end, width, 2 * units, units)
             ],
         )
-        input_rows, small, attn_full, output_full, ups_full, downward_full = first_rows(
-            block_input, (small_cut, *cuts), 2, lines
+        flat_normed, raw, logits, small, attn_full, output_full, ups_full, downward_full = first_call(
+            block_input, (small_cut, *cuts), lines
         )
         ups_split = depth // 128 * 80
         front_moves = ((output_full, (0, depth)), (ups_full, (0, ups_split)))
@@ -2062,34 +2161,35 @@
             axis=3,
         )
         streams_cut = streams_cut.transpose(1, 0, 2, 3, 4).reshape(MATES, depth, streams_end)
-        beta_cut = jnp.pad(
-            cut_columns(beta_weight.astype(low)), ((0, 0), (0, 0), (0, head_size - heads))
-        )
         cuts = (
             small_cut,
-            jnp.concatenate([streams_cut, cut_columns(outgate_weight.astype(low)), beta_cut], axis=2),
+            jnp.concatenate([streams_cut, cut_columns(outgate_weight.astype(low))], axis=2),
             cut_columns(output_weight.astype(low).T),
             jnp.concatenate([cut_columns(w.astype(low)) for w in (swish_weight, upward_weight)], axis=2),
             cut_columns(downward_weight.astype(low).T),
         )
-        input_rows, = first_rows(block_input, (), 0, lines)
+        input_rows = first_rows(block_input).reshape(rows, model_width)
         small, attn_full, output_full, ups_full, downward_full = (gather_weights(cut) for cut in cuts)
         front_moves = ((output_full, None),)
-    attn_full = attn_full.reshape(model_width, attn_width)
-    input_rows = input_rows.reshape(rows, model_width)
+    attn_full = attn_full.reshape(model_width, gates_end)
     small = small.reshape(count, SMALL * 128)
-    attn_small, mlp_small, head_small, _, conv_small = (
-        small[:, starts[index] : starts[index + 1]] for index in range(len(sizes))
-    )
+    attn_scale = small[:, :depth].reshape(1, model_width).astype(wide)
+    mlp_scale = small[:, depth : 2 * depth].reshape(1, model_width).astype(wide)
+    head_scale = small[:, 2 * depth : 2 * depth + gain_part].reshape(1, head_size).astype(wide)
     taps = (
-        conv_small.reshape(count, heads, 3, CONV, gain_part)
+        small[:, conv_start : conv_start + conv_size]
+        .reshape(count, heads, 3, CONV, gain_part)
         .transpose(1, 2, 3, 0, 4)
         .reshape(heads, 3 * CONV, head_size)
         .astype(wide)
     )
-    attn_scale = attn_small.reshape(1, model_width).astype(wide)
-    mlp_scale = mlp_small.reshape(1, model_width).astype(wide)
-    head_scale = head_small.reshape(1, head_size).astype(wide)
+    beta_rows = (
+        small[:, beta_start:small_size]
+        .reshape(count, heads, depth)
+        .transpose(1, 0, 2)
+        .reshape(heads, model_width)
+    )
+    beta_rows = jnp.pad(beta_rows, ((BETA_ROW, CHUNK - BETA_ROW - heads), (0, 0)))
 
     mine_low = pick(block_input, core)
     grad_mine = pick(out_grad, core)
@@ -2097,7 +2197,8 @@
     lengths_here = jnp.stack([pick(lengths, core), pick(lengths, 1 - core)])
     limit = lengths_here - line_of() * span
 
-    flat_normed, raw, logits = project(input_rows, attn_scale, attn_full, gates_end)
+    if not near:
+        flat_normed, raw, logits = project(input_rows, attn_scale, attn_full, beta_rows)
     sizes_of = (lines, seq_count, heads, span)
     (
         qkv, solved, wu, maps, total, tails, state, fresh, mixed, gated, gathered, output_all, *moved
@@ -2159,8 +2260,10 @@
     )
     attn_grad_rows = attn_grad_rows.reshape(rows, model_width)
     output_grad = cut_rows(matmul("rd,rc->dc", attn_grad_rows, gated).astype(low))
-    normed_part = matmul("rc,dc->rd", all_grads, attn_full).astype(low)
-    attn_grads = cut_rows(matmul("rd,rc->dc", flat_normed, all_grads).astype(low))
+    normed_part = back_project(all_grads, attn_full, beta_rows)
+    attn_grads = matmul("rd,rc->dc", flat_normed, all_grads).astype(low)
+    beta_grad = attn_grads[:, gates_end + BETA_ROW : gates_end + BETA_ROW + heads]
+    attn_grads = cut_rows(attn_grads)
 
     conv_grad = (
         taps_grad[:, :CONV]
@@ -2171,15 +2274,14 @@
     )
 
     def small_blocks(attn_gain_grad):
-        parts = [
+        gains = gains_of(
             attn_gain_grad.reshape(count, depth),
             mlp_gain_grad.reshape(count, depth),
             jnp.sum(head_gain_parts[:, 0], axis=0).reshape(count, gain_part),
-            jnp.zeros((count, -gain_part % 128), wide),
-            conv_grad,
-        ]
-        flat = jnp.concatenate(parts, axis=1).astype(low)
-        flat = jnp.pad(flat, ((0, 0), (0, SMALL * 128 - starts[-1])))
+        )
+        beta = beta_grad.reshape(count, depth, heads).transpose(0, 2, 1).reshape(count, -1)
+        flat = jnp.concatenate([gains.astype(low), in_rows(conv_grad.astype(low)), beta], axis=1)
+        flat = jnp.pad(flat, ((0, 0), (0, SMALL * 128 - small_size)))
         return flat.reshape(lines, MATES, SMALL, 128)
 
     last_ins = (
@@ -2192,7 +2294,11 @@
     )
     if near:
         ups_high, downward_sum = summed
-        blocks = (small_blocks(jnp.zeros((1, model_width), wide)), attn_grads, output_grad)
+        blocks = (
+            (small_blocks(jnp.zeros((1, model_width), wide)), 128),
+            (attn_grads, gates_end),
+            (output_grad, width),
+        )
         input_grad, block_output, _, small_sum, attn_sum, output_sum = last_rows(
             *last_ins, blocks, lines
         )
@@ -2202,23 +2308,23 @@
             [
                 (w.shape, wide)
                 for w in (
-                    query_weight, key_weight, value_weight, outgate_weight, beta_weight, output_weight,
+                    query_weight, key_weight, value_weight, outgate_weight, output_weight,
                     swish_weight, upward_weight, downward_weight,
                 )
             ],
         )
         small_sum = small_sum.reshape(MATES, SMALL * 128).astype(wide)
-        gains_sum = jnp.sum(small_sum[:, : starts[3]], axis=0)
+        gains_sum = jnp.sum(small_sum[:, :conv_start], axis=0)
     else:
         input_grad, block_output, attn_gain_grad = last_rows(*last_ins, (), lines)
         small_sum, attn_sum, output_sum, ups_sum, downward_sum = (
             scatter_grads(block)
             for block in (
-                small_blocks(attn_gain_grad), attn_grads, output_grad, ups_blocks, downward_blocks
+                small_blocks(attn_gain_grad), attn_grads[..., :gates_end], output_grad, ups_blocks, downward_blocks
             )
         )
         small_sum = small_sum.reshape(MATES, SMALL * 128)
-        gains_sum = jnp.sum(small_sum[:, : starts[3]], axis=0)
+        gains_sum = jnp.sum(small_sum[:, :conv_start], axis=0)
         gains_sum = gains_sum + other_core(gains_sum)
         streams_sum = (
             attn_sum[:, :, :streams_end]
@@ -2231,23 +2337,24 @@
             streams_sum[1],
             streams_sum[2],
             join_columns(attn_sum[:, :, streams_end:gates_end]),
-            join_columns(attn_sum[:, :, gates_end : gates_end + heads]),
             join_columns(output_sum).T,
             join_columns(ups_sum[:, :, :units]),
             join_columns(ups_sum[:, :, units:]),
             join_columns(downward_sum).T,
         )
-    conv_sum = small_sum[:, starts[4] : starts[5]]
+    conv_sum = small_sum[:, conv_start : conv_start + conv_size]
+    beta_sum = small_sum[:, beta_start:small_size].reshape(MATES * heads, depth).T
     return (
         block_output,
         input_grad,
         gains_sum[:depth],
-        *grads[:5],
+        *grads[:4],
+        beta_sum,
         conv_sum.reshape(MATES * heads, 3, CONV, gain_part),
-        gains_sum[2 * depth :],
-        grads[5],
+        gains_sum[2 * depth : 2 * depth + gain_part],
+        grads[4],
         gains_sum[depth : 2 * depth],
-        *grads[6:],
+        *grads[5:],
     )
 
 

time: 847 us -> 779 us (0.920)
  Pallas kernels: 680 us -> 619 us
  matrix products: 131 us -> 113 us
    pallas_call x4, Pallas kernels: 447 us -> 383 us  [remote_call(): pl.pallas_call(body, in_specs=[anywhere if kind == 'any' else held for _,...]
    dot_general x9 -> x8, matrix products: 131 us -> 113 us  [matmul(): return jnp.einsum(form, left, right, preferred_element_type=wide)]
where the time goes in v6:
time: 779 us; the launch traced here: 770 us
  Pallas kernels  619 us (79%)
  matrix products  113 us (15%)
  local copies, waits for them, and re-layouts  31.3 us (4%)
    pallas_call x4, Pallas kernels, remote_call(): pl.pallas_call(body, in_specs=[anywhere if kind == 'any' else held for _,...  383 us
    pallas_call x2, Pallas kernels, call(): pl.pallas_call(body, grid=(2 * self.chains,), in_specs=[spec for _, spec...  210 us
    dot_general x8, matrix products, matmul(): return jnp.einsum(form, left, right, preferred_element_type=wide)  113 us
    pallas_call x1, Pallas kernels, tiled_call(): pl.pallas_call(body, grid=(ins[0].shape[0] // tile,), in_specs=[tall(arra...  15.7 us

profile of v6, /device:TPU:0, one launch (start us, length us, event | category | flops | bytes accessed | tf_op | source)
XLA Modules:
  0.0 769.6 jit_solution(14661842832077629710)
XLA Ops:
  0.7 1.3 fusion.8
  2.0 1.9 add_subtract_fusion.limit_ref
  3.9 5.4 shard_map.271
  9.6 0.6 copy.79
  10.2 94.1 %shard_map.272 = (bf16[2048,2048]{1,0:T(8,128)(2,1)}, bf16[2048,1024]{1,0:T(8,128)(2,1)}, f32[2048,128]{1,0:T(8,128)}, bf16[4,4,16,128]{3,2,1,0:T(8,128)(2,1)}, ...) custom-call(bf16[2,256,2048]{2,1,0:T(8,128)(2,1)} %input_ref.1, ...), custom_call_target="tpu_custom_call" | custom-call | tf_op jit(solution)/shard_map/pallas_call | solution.py:1308
  104.3 0.9 copy.77
  105.4 0.7 reshape.245.taps_ref
  106.1 0.6 reshape.240.scale_ref
  106.7 94.9 %shard_map.273 = (bf16[2048,768]{1,0:T(8,128)(2,1)}, f32[4,8,128,128]{3,2,1,0:T(8,128)}, f32[4,8,128,256]{3,2,1,0:T(8,128)}, f32[4,8,128,128]{3,2,1,0:T(8,128)},...) custom-call(s32[2]{0:T(128)} %add_subtract_fusion.limit_ref, ...), custom_call_target="tpu_custom_call", output_to_operand_aliasing={{12}: (7, {}), {13}: (8, {})} | custom-call | tf_op jit(solution)/shard_map/pallas_call | solution.py:1834
  201.6 0.6 slice_convert_fusion
  202.2 1.6 dynamic-slice_bitcast_fusion
  203.8 99.1 %shard_map.274 = (f32[256,2048]{1,0:T(8,128)}, bf16[2,4,256,2048]{3,2,1,0:T(8,128)(2,1)}, bf16[2,4,256,2048]{3,2,1,0:T(8,128)(2,1)}, bf16[4,4,128,1408]{3,2,1,0:T(8,128)(2,1)}, bf16[4,4,128,704]{3,2,1,0:T(8,128)(2,1)}) custom-call(bf16[2,4,256,256]{3,2,1,0:T(8,128)(2,1)} %get-tuple-element.83.gathered, ...), custom_call_target="tpu_custom_call", output_to_operand_aliasing={{3}: (5, {}), {4}: (6, {})} | custom-call | tf_op jit(solution)/shard_map/pallas_call | solution.py:1308
  302.9 18.9 %fusion.9 = f32[2048,1408]{0,1:T(8,128)} fusion(bf16[2048,2048]{1,0:T(8,128)(2,1)} %bitcast.133, bf16[2048,1408]{1,0:T(8,128)(2,1)} %bitcast.95), kind=kOutput, calls=%fused_computation.52 | convolution fusion | flops 11811160064 | bytes 25690112 | tf_op jit(solution)/shard_map/rd,df->rf/dot_general | solution.py:73
  321.8 14.4 %multiply_convert_fusion.2 = (bf16[2048,704]{0,1:T(8,128)(2,1)}, bf16[2048,704]{0,1:T(8,128)(2,1)}, bf16[2048,704]{0,1:T(8,128)(2,1)S(1)}) fusion(f32[2048,1408]{0,1:T(8,128)} %fusion.9, bf16[2048,2048]{1,0:T(8,128)(2,1)} %bitcast.135, bf16[2048,704]{1,0:T(8,128)(2,1)S(1)} %bitcast.106), kind=kOutput, calls=%fused_computation.7 | convolution fusion | flops 5927206912 | bytes 31457280 | tf_op jit(solution)/shard_map/rd,df->rf/dot_general | solution.py:73
  336.3 1.6 copy-done.17
  337.9 10.8 %convolution_convert_fusion.4 = bf16[2048,704]{0,1:T(8,128)(2,1)} fusion(bf16[2048,704]{0,1:T(8,128)(2,1)S(1)} %get-tuple-element.125, bf16[2048,2048]{1,0:T(8,128)(2,1)} %bitcast.136), kind=kOutput, calls=%fused_computation.10 | convolution fusion | flops 5907021824 | bytes 14155776 | tf_op jit(solution)/shard_map/rd,rf->df/dot_general | solution.py:73
  348.8 4.8 copy.52
  353.6 19.3 %convolution_convert_fusion.3 = bf16[2048,1408]{1,0:T(8,128)(2,1)} fusion(bf16[2048,2048]{1,0:T(8,128)(2,1)} %bitcast.134, bf16[2048,704]{0,1:T(8,128)(2,1)} %get-tuple-element.124, bf16[2048,704]{0,1:T(8,128)(2,1)} %get-tuple-element.123), kind=kOutput, calls=%fused_computation.3 | convolution fusion | flops 11825577984 | bytes 19922944 | tf_op jit(solution)/shard_map/rd,rf->df/dot_general | solution.py:73
  372.8 17.4 %convolution_convert_fusion.2 = bf16[2048,2048]{1,0:T(8,128)(2,1)} fusion(bf16[2048,1408]{1,0:T(8,128)(2,1)S(1)} %bitcast.98, bf16[2048,704]{0,1:T(8,128)(2,1)} %get-tuple-element.124, bf16[2048,704]{0,1:T(8,128)(2,1)S(1)} %copy-done.18), kind=kOutput, calls=%fused_computation.2 | convolution fusion | flops 11826888704 | bytes 19922944 | tf_op jit(solution)/shard_map/rf,df->rd/dot_general | solution.py:73
  390.3 87.5 %shard_map.275 = (f32[256,2048]{1,0:T(8,128)}, f32[1,2048]{1,0:T(1,128)}, bf16[256,2048]{1,0:T(8,128)(2,1)}, bf16[2,4,256,256]{3,2,1,0:T(8,128)(2,1)}, bf16[4,80,1408]{2,1,0:T(8,128)(2,1)}) custom-call(bf16[2,4,256,2048]{3,2,1,0:T(8,128)(2,1)} %bitcast.103, bf16[2,4,4,4,128,256]{5,4,3,2,1,0:T(8,128)(2,1)} %get-tuple-element.84.weights, ...), custom_call_target="tpu_custom_call" | custom-call | tf_op jit(solution)/shard_map/pallas_call | solution.py:1308
  477.8 114.8 %shard_map.276 = (bf16[2048,1152]{1,0:T(8,128)(2,1)}, f32[4,8,128]{2,1,0:T(8,128)}, f32[4,8,384]{2,1,0:T(8,128)}, bf16[2,4,256,2048]{3,2,1,0:T(8,128)(2,1)}, bf1...) custom-call(s32[2]{0:T(128)} %add_subtract_fusion.limit_ref, ...), custom_call_target="tpu_custom_call" | custom-call | tf_op jit(solution)/shard_map/pallas_call | solution.py:1834
  592.6 7.0 convolution_convert_fusion.5
  599.7 14.3 %convolution_convert_fusion = bf16[2048,1152]{1,0:T(8,128)(2,1)S(1)} fusion(bf16[2048,2048]{1,0:T(8,128)(2,1)} %get-tuple-element.104, bf16[2048,1152]{1,0:T(8,128)(2,1)S(1)} %copy-done.3), kind=kOutput, calls=%fused_computation | convolution fusion | flops 9666035712 | bytes 17825792 | tf_op jit(solution)/shard_map/rd,rc->dc/dot_general | solution.py:73
  614.0 2.1 copy-done
  616.1 1.0 slice.71
  617.1 1.2 copy.56
  618.4 0.7 slice_reduce_fusion.1
  619.3 0.6 copy-done.9
  619.9 0.6 slice.56
  620.5 1.0 reshape.230
  621.5 0.7 reduce_sum.28
  622.2 1.0 copy.55
  623.2 0.6 constant_dynamic-update-slice_fusion.1
  623.8 0.6 constant_dynamic-update-slice_fusion
  624.4 0.8 pad_bitcast_fusion
  625.2 0.6 copy.68
  625.8 10.9 %convolution_convert_fusion.1 = bf16[2048,2048]{1,0:T(8,128)(2,1)} fusion(bf16[2048,704]{0,1:T(8,128)(2,1)} %copy-done.17, bf16[2048,704]{1,0:T(8,128)(2,1)S(1)} %bitcast.107), kind=kOutput, calls=%fused_computation.1 | convolution fusion | flops 5909774336 | bytes 14155776 | tf_op jit(solution)/shard_map/rf,df->rd/dot_general | solution.py:73
  636.8 0.7 bitcast_bitcast_fusion
  637.5 0.8 pad.33.beta_ref
  638.3 15.7 %shard_map.277 = bf16[2048,2048]{1,0:T(8,128)(2,1)} custom-call(bf16[2048,1152]{1,0:T(8,128)(2,1)} %get-tuple-element.98.grad_ref, bf16[2048,1024]{1,0:T(8,128)(2,1)} %bitcast.105, bf16[128,2048]{1,0:T(8,128)(2,1)} %pad.33.beta_ref), custom_call_target="tpu_custom_call" | custom-call | tf_op jit(solution)/shard_map/pallas_call | solution.py:1983
  654.0 102.0 %shard_map.278 = (bf16[2,256,2048]{2,1,0:T(8,128)(2,1)}, bf16[2,256,2048]{2,1,0:T(8,128)(2,1)}, f32[1,2048]{1,0:T(1,128)}, bf16[4,16,128]{2,1,0:T(8,128)(2,1)}, ...) custom-call(bf16[2,4,256,2048]{3,2,1,0:T(8,128)(2,1)} %bitcast.94, bf16[2,4,256,2048]{3,2,1,0:T(8,128)(2,1)} %bitcast.102, ...), custom_call_target="tpu_custom_call" | custom-call | tf_op jit(solution)/shard_map/pallas_call | solution.py:1308
  756.0 5.6 shard_map.279
  761.5 0.7 convert_bitcast_fusion.2
  762.3 0.7 reshape.238
  763.0 0.6 reshape.237
  763.6 0.5 fusion.7
  764.7 3.2 copy.92
  767.8 1.3 copy.93
  (68 shorter events, 1.3 us)
Async XLA Ops:
  0.6 8.6 %copy-start.8 = (f32[8,3,4,8]{3,2,1,0:T(4,128)S(1)}, f32[8,3,4,8]{3,2,1,0:T(4,128)}, u32[]{:S(2)}) copy-start(f32[8,3,4,8]{3,2,1,0:T(4,128)} %param.24) | copy-start | bytes 9220
  0.7 8.8 %copy-start.12 = (f32[128,8]{0,1:T(8,128)S(1)}, f32[128,8]{0,1:T(8,128)}, u32[]{:S(2)}) copy-start(f32[128,8]{0,1:T(8,128)} %param.23) | copy-start | bytes 12292
  0.7 8.8 %copy-start.14 = (f32[8]{0:T(128)S(1)}, f32[8]{0:T(128)}, u32[]{:S(2)}) copy-start(f32[8]{0:T(128)} %param.25) | copy-start | bytes 100
  0.7 8.8 %copy-start.15 = (f32[128]{0:T(128)S(1)}, f32[128]{0:T(128)}, u32[]{:S(2)}) copy-start(f32[128]{0:T(128)} %param.18) | copy-start | bytes 1540
  0.7 8.8 %copy-start.16 = (f32[128]{0:T(128)S(1)}, f32[128]{0:T(128)}, u32[]{:S(2)}) copy-start(f32[128]{0:T(128)} %param.27) | copy-start | bytes 1540
  105.1 96.5 %copy-start.7 = (bf16[2,8,16,128]{3,1,2,0:T(8,128)(2,1)}, bf16[2,8,16,128]{3,1,2,0:T(8,128)(2,1)S(1)}, u32[]{:S(2)}) copy-start(bf16[2,8,16,128]{3,1,2,0:T(8,128)(2,1)S(1)} %copy.77) | copy-start | bytes 196612
  106.7 95.5 %copy-start.1 = (bf16[2,256,2048]{2,1,0:T(8,128)(2,1)S(1)}, bf16[2,256,2048]{2,1,0:T(8,128)(2,1)}, u32[]{:S(2)}) copy-start(bf16[2,256,2048]{2,1,0:T(8,128)(2,1)} %grad_any.1) | copy-start | bytes 6291460
  106.7 95.5 %copy-start.2 = (bf16[2,256,2048]{2,1,0:T(8,128)(2,1)S(1)}, bf16[2,256,2048]{2,1,0:T(8,128)(2,1)}, u32[]{:S(2)}) copy-start(bf16[2,256,2048]{2,1,0:T(8,128)(2,1)} %input_ref.1) | copy-start | bytes 6291460
  302.9 18.9 %copy-start.4 = (bf16[4,4,128,704]{3,2,1,0:T(8,128)(2,1)S(1)}, bf16[4,4,128,704]{3,2,1,0:T(8,128)(2,1)}, u32[]{:S(2)}) copy-start(bf16[4,4,128,704]{3,2,1,0:T(8,128)(2,1)} %get-tuple-element.88) | copy-start | bytes 8650756
  336.3 1.6 copy-start.17
  348.8 24.1 %slice-start = ((s8[5767168]{0:T(1024)(128)(4,1)}), s8[1572864]{0:T(1024)(128)(4,1)S(1)}, s32[]{:S(2)}) async-start(s8[5767168]{0:T(1024)(128)(4,1)} %bitcast.96), calls=%async_computation | async-start | bytes 3145728
  353.6 19.3 %slice-start.1 = ((s8[5767168]{0:T(1024)(128)(4,1)}), s8[4194304]{0:T(1024)(128)(4,1)S(1)}, s32[]{:S(2)}) async-start(s8[5767168]{0:T(1024)(128)(4,1)} %bitcast.96), calls=%async_computation.1 | async-start | bytes 8388608
  353.6 19.3 %copy-start.18 = (bf16[2048,704]{0,1:T(8,128)(2,1)S(1)}, bf16[2048,704]{0,1:T(8,128)(2,1)}, u32[]{:S(2)}) copy-start(bf16[2048,704]{0,1:T(8,128)(2,1)} %get-tuple-element.123) | copy-start | bytes 8650756
  477.8 114.9 %copy-start.13 = (bf16[2048,256]{1,0:T(8,128)(2,1)S(1)}, bf16[2048,256]{1,0:T(8,128)(2,1)}, u32[]{:S(2)}) copy-start(bf16[2048,256]{1,0:T(8,128)(2,1)} %get-tuple-element.106) | copy-start | bytes 3145732
  592.6 7.0 copy-start.3
  599.7 19.5 %copy-start.11 = (f32[1,2048]{1,0:T(1,128)S(1)}, f32[1,2048]{1,0:T(1,128)}, u32[]{:S(2)}) copy-start(f32[1,2048]{1,0:T(1,128)} %get-tuple-element.101) | copy-start | bytes 24580
  599.7 20.2 %copy-start.10 = (f32[4,8,384]{2,1,0:T(8,128)S(1)}, f32[4,8,384]{2,1,0:T(8,128)}, u32[]{:S(2)}) copy-start(f32[4,8,384]{2,1,0:T(8,128)} %get-tuple-element.103) | copy-start | bytes 147460
  599.7 26.2 %copy-start.5 = (bf16[4,4,128,704]{3,2,1,0:T(8,128)(2,1)S(1)}, bf16[4,4,128,704]{3,2,1,0:T(8,128)(2,1)}, u32[]{:S(2)}) copy-start(bf16[4,4,128,704]{3,2,1,0:T(8,128)(2,1)} %get-tuple-element.88) | copy-start | bytes 8650756
  614.0 2.1 copy-start
  619.3 0.6 copy-start.9
  756.0 11.9 %copy-start.6 = (bf16[2,256,2048]{2,1,0:T(8,128)(2,1)S(1)}, bf16[2,256,2048]{2,1,0:T(8,128)(2,1)}, u32[]{:S(2)}) copy-start(bf16[2,256,2048]{2,1,0:T(8,128)(2,1)} %get-tuple-element.150) | copy-start | bytes 6291460

commit v7 on v6

--- a/solution.py
+++ b/solution.py
@@ -243,6 +243,9 @@
             pl.when(above)(tail(seq).start)
         for gather in gathers:
             gather.leave(False)
+        share.begin_half(False)
+        share.begin_half(True)
+        share.begin_rest()
         for seq in range(seqs):
 
             @pl.when(below)
@@ -300,29 +303,13 @@
 
         lax.fori_loop(0, chunks // TOGETHER, group, 0)
 
-    @pl.when((step == 1) & (step < chains))
-    def _():
-        for gather in gathers[:1]:
-            gather.onwards(1)
-
-    @pl.when((step == 2) & (step < chains))
-    def _():
-        for gather in gathers[:1]:
-            gather.onwards(2)
-
     @pl.when(step < chains)
     def _():
         form(step)
 
     @pl.when(step == chains - 2)
     def _():
-        for gather in gathers[:1]:
-            for number in range(3, lines):
-                gather.onwards(number)
-        share.begin_half(False)
-        share.begin_half(True)
-        share.begin_rest()
-        for gather in gathers[1:]:
+        for gather in gathers:
             gather.onwards(1)
 
     @pl.when(step == chains - 1)
@@ -356,6 +343,7 @@
             leaving = nn_low(pair(ends[index][:, :head_size]), enters[index])
             leaves[index] = (leaving + ends[index][:, head_size:]).astype(low)
         pl.when(above)(state_copy.start)
+        share.forward()
 
     def outputs(chain):
         enter = enters[chain]
@@ -394,18 +382,14 @@
     @pl.when(step == chains + heads - 1)
     def _():
         swap.begin(0)
-        share.forward()
-
-    @pl.when(step == 2 * chains - 2)
-    def _():
-        for gather in gathers[1:]:
+        share.forward_far()
+        for gather in gathers:
             gather.onwards(2)
 
     @pl.when(step == 2 * chains - 1)
     def _():
         swap.begin(1)
-        share.forward_far()
-        for gather in gathers[1:]:
+        for gather in gathers:
             for number in range(3, lines):
                 gather.onwards(number)
         for gather in gathers:
@@ -419,15 +403,18 @@
 
 def back_kernel(
     lines, heads, parts, limit_ref, raw_ref, tails_ref, taps_ref, logit_ref, gate_ref, scale_ref, qkv_ref,
-    wu_ref, map_ref, total_ref, grad_ref, mixed_ref, solved_ref, state_ref, fresh_in_ref, row_grad, *rest,
+    wu_ref, map_ref, total_ref, grad_ref, mixed_ref, solved_ref, state_ref, fresh_in_ref, row_grad, mlp_partial,
+    middle_ref, *rest,
 ):
     count = len(parts)
     blocks, rest = rest[:count], rest[count:]
-    all_ref, gain_ref, taps_grad_ref, row_grads = rest[:4]
-    results, scratch = rest[4 : 4 + count], rest[4 + count :]
+    all_ref, gain_ref, taps_grad_ref, row_grads, block_output = rest[:5]
+    results, scratch = rest[5 : 5 + count], rest[5 + count :]
     ext, pre_grads, maps, sources, out_grads, fresh_grads, leaving, leaves, enters = scratch[:9]
     halos, edges, returned, halo_sems, state_sems = scratch[9:14]
     share_scratch, scratch = scratch[14:17], scratch[17:]
+    low_output, out_sems = scratch[0], scratch[1:4]
+    outs_scratch, scratch = scratch[4:11], scratch[11:]
     step = pl.program_id(0)
     chains, chunks = maps.shape[0], maps.shape[1]
     span = chunks * CHUNK
@@ -439,6 +426,11 @@
         for index, (first, _) in enumerate(parts)
     ]
     share = ShareRows(place, row_grad, row_grads, share_scratch)
+    outs = SumRows(place, mlp_partial, outs_scratch)
+    to_sibling = sender(out_sems[:2])(
+        0, low_output, block_output.at[place.core], place.sibling
+    )
+    to_self = pltpu.make_async_copy(low_output, block_output.at[place.core], out_sems[2].at[0])
     below, above = place.line > 0, place.line < lines - 1
     rows, columns = grid_of_rows()
 
@@ -467,6 +459,7 @@
         share.begin_half(False)
         share.begin_half(True)
         share.begin_rest()
+        outs.begin()
         for each in sums:
             each.begin()
         for each in sums:
@@ -510,6 +503,14 @@
 
         gain = lax.fori_loop(0, chunks // TOGETHER, group, jnp.zeros((1, head_size), wide))
         gain_ref[0] = jnp.broadcast_to(gain, (8, head_size))
+
+    @pl.when(step == 1)
+    def _():
+        outs.send_far()
+
+    @pl.when(step == 2)
+    def _():
+        outs.send_near()
 
     @pl.when(step < chains)
     def _():
@@ -687,12 +688,25 @@
 
     @pl.when(step == chains + 1)
     def _():
+        outs.send_relayed()
+
+    @pl.when(step == chains + 2)
+    def _():
         share.forward_far()
-
-    @pl.when(step == 2 * chains - 3)
-    def _():
         for each in sums:
             each.round(3)
+
+    @pl.when(step == chains + 3)
+    def _():
+        outs.wait_half(False)
+        outs.wait_half(True)
+
+        def out_body(here):
+            low_output[here] = (middle_ref[here] + outs.total(here)).astype(low)
+
+        row_steps(0, low_output.shape[0], out_body)
+        to_sibling.start()
+        to_self.start()
 
     @pl.when(step == 2 * chains - 1)
     def _():
@@ -714,6 +728,9 @@
             pl.when(below)(halo(chain).wait_send)
         pl.when(below)(state_copy.wait_send)
         share.finish()
+        outs.finish()
+        to_self.wait()
+        to_sibling.wait()
         for each in sums:
             each.finish()
 
@@ -724,12 +741,6 @@
     normed_ref[...] = normed
     raw_ref[...] = dot(normed, weight_ref[...], NN).astype(low)
     logit_ref[...] = dot(normed, beta_ref[...], NT)
-
-
-def back_project_kernel(grad_ref, weight_ref, beta_ref, out_ref):
-    width = weight_ref.shape[1]
-    total = dot(grad_ref[:, :width], weight_ref[...], NT)
-    out_ref[...] = (total + dot(grad_ref[:, width:], beta_ref[...], NN)).astype(low)
 
 
 MESH = pl.DeviceIdType.MESH
@@ -821,10 +832,8 @@
 
 
 class SumRows:
-    SCRATCH = 4
-
     @staticmethod
-    def scratch(rows, columns):
+    def scratch(rows, columns, computed=False):
         return [
             pltpu.VMEM((MATES, rows, columns), low),
             pltpu.VMEM((MATES, rows, columns), low),
@@ -833,28 +842,46 @@
             pltpu.SemaphoreType.DMA((MATES,)),
             pltpu.SemaphoreType.DMA((10,)),
             pltpu.SemaphoreType.DMA((10,)),
-        ]
-
-    def __init__(self, place, partial, scratch):
-        self.place, self.partial = place, partial
-        self.own, self.swapped, self.relay, self.arrived, self.local_sems, send, receive = scratch
+        ] + [pltpu.VMEM((MATES, rows, columns), low)] * computed
+
+    def __init__(self, place, partial, scratch, compute=None):
+        self.place, self.partial, self.compute = place, partial, compute
+        self.own, self.swapped, self.relay, self.arrived, self.local_sems, send, receive = scratch[:7]
+        if compute:
+            self.other = scratch[7]
         self.make = sender((send, receive))
         self.rows = self.own.shape[1]
         self.order = [place.far, place.x, place.y, place.mate]
+        half, x, y = self.rows // 2, place.of(place.x), place.of(place.y)
+        own, relay, arrived = self.own, self.relay, self.arrived
+        self.far_low = self.make(4, own.at[0, :half], relay.at[0], y)
+        self.far_high = self.make(5, own.at[0, half:], relay.at[1], x)
+        self.x_high = self.make(6, own.at[1, half:], arrived.at[0, half:], x)
+        self.y_low = self.make(7, own.at[2, :half], arrived.at[1, :half], y)
+        self.x_low = self.make(8, own.at[1, :half], arrived.at[0, :half], x)
+        self.y_high = self.make(9, own.at[2, half:], arrived.at[1, half:], y)
+        self.swaps = [
+            self.make(
+                slot,
+                self.other.at[slot] if compute else partial.at[1, mate],
+                self.swapped.at[slot],
+                place.sibling,
+            )
+            for slot, mate in enumerate(self.order)
+        ]
+
+    def load(self, slot):
+        return pltpu.make_async_copy(
+            self.partial.at[0, self.order[slot]], self.own.at[slot], self.local_sems.at[slot]
+        )
 
     def begin(self):
-        self.swaps, self.loads = [], []
         for slot, mate in enumerate(self.order):
-            copy = self.make(
-                slot, self.partial.at[1, mate], self.swapped.at[slot], self.place.sibling
-            )
-            copy.start()
-            self.swaps.append(copy)
-            load = pltpu.make_async_copy(
-                self.partial.at[0, mate], self.own.at[slot], self.local_sems.at[slot]
-            )
-            load.start()
-            self.loads.append(load)
+            if self.compute:
+                self.compute(1, mate, self.other, slot)
+            else:
+                self.load(slot).start()
+            self.swaps[slot].start()
 
     def add(self, target, target_slot, source, source_slot, first, last, shift=0):
         def body(here):
@@ -866,48 +893,31 @@
         row_steps(first, last, body)
 
     def sum_cores(self, slot):
-        self.loads[slot].wait()
+        if self.compute:
+            self.compute(0, self.order[slot], self.own, slot)
+        else:
+            self.load(slot).wait()
         self.swaps[slot].wait_recv()
         self.add(self.own, slot, self.swapped, slot, 0, self.rows)
 
     def send_far(self):
-        half = self.rows // 2
         self.sum_cores(0)
-        self.far_low = self.make(
-            4, self.own.at[0, :half], self.relay.at[0], self.place.of(self.place.y)
-        )
-        self.far_high = self.make(
-            5, self.own.at[0, half:], self.relay.at[1], self.place.of(self.place.x)
-        )
         self.far_low.start()
         self.far_high.start()
 
     def send_near(self):
-        half, place = self.rows // 2, self.place
         self.sum_cores(1)
-        self.x_high = self.make(
-            6, self.own.at[1, half:], self.arrived.at[0, half:], place.of(place.x)
-        )
         self.x_high.start()
         self.sum_cores(2)
-        self.y_low = self.make(
-            7, self.own.at[2, :half], self.arrived.at[1, :half], place.of(place.y)
-        )
         self.y_low.start()
 
     def send_relayed(self):
-        half, place = self.rows // 2, self.place
+        half = self.rows // 2
         self.far_low.wait_recv()
         self.add(self.own, 1, self.relay, 0, 0, half)
-        self.x_low = self.make(
-            8, self.own.at[1, :half], self.arrived.at[0, :half], place.of(place.x)
-        )
         self.x_low.start()
         self.far_high.wait_recv()
         self.add(self.own, 2, self.relay, 1, half, self.rows, shift=half)
-        self.y_high = self.make(
-            9, self.own.at[2, half:], self.arrived.at[1, half:], place.of(place.y)
-        )
         self.y_high.start()
         self.sum_cores(3)
 
@@ -1341,27 +1351,40 @@
 def middle_kernel(lines, moves, gathered, weights, input_ref, scale_ref, grad_any, *rest):
     place = Place()
     count = len(moves)
-    middle_ref, shared, grads = rest[count : count + 3]
-    targets, scratch = rest[count + 3 : 2 * count + 3], rest[2 * count + 3 :]
-    normed, held, weight_sems = scratch[:3]
-    share = ShareRows(place, normed, shared, scratch[3:6])
-    other = ShareRows(place, grad_any.at[place.core], grads, scratch[6:9])
+    middle_ref, shared, grads, acts_out, hidden_out = rest[count : count + 5]
+    targets, scratch = rest[count + 5 : 2 * count + 5], rest[2 * count + 5 :]
+    normed, held, weight_sems, all_normed, ups, acts, hidden, out_sems, load_sems = scratch[:9]
+    scratch = scratch[9:]
+    share = ShareRows(place, normed, all_normed, scratch[:3])
+    other = ShareRows(place, grad_any.at[place.core], grads, scratch[3:6])
     gathers = [
-        GatherLines(place, None, target, scratch[9 + 6 * index : 15 + 6 * index], moves[index])
+        GatherLines(place, None, target, scratch[6 + 6 * index : 12 + 6 * index], moves[index])
         for index, target in enumerate(targets)
+        if moves[index]
     ]
-    meet(place, lines=lines if moves else 0)
+    meet(place, lines=lines if gathers else 0)
     loads = load_weights(weights, held, weight_sems)
     for load in loads:
         load.start()
-    for gather in gathers:
+    other.begin_half(False)
+    other.begin_half(True)
+    other.begin_rest()
+    for gather in gathers[:1]:
         gather.leave(False)
+    _, _, all_lines, _, depth, width = held.shape
+    early = moves[0][0] if gathers else depth
+
+    def load_ups(index):
+        part = (pl.ds(0, early), pl.ds(early, depth - early))[index]
+        return pltpu.make_async_copy(
+            targets[0].at[:, :, part], ups.at[:, :, part], load_sems.at[index]
+        )
+
+    load_ups(0).start()
     for load in loads:
         load.wait()
-    rows = normed.shape[0]
+    rows, model_width = normed.shape
     half = rows // 2
-    _, _, all_lines, _, depth, width = held.shape
-
     height = MATES * depth
     some = max(1, 512 // height)
 
@@ -1392,57 +1415,127 @@
     row_steps(half, rows, body)
     share.begin_half(True)
     share.begin_rest()
-    for gather in gathers:
+    for gather in gathers[:1]:
         gather.onwards(1)
+    for gather in gathers[1:]:
+        gather.leave(False)
+    for gather in gathers[:1]:
+        gather.onwards(2)
     share.forward()
-    other.begin_half(False)
-    other.begin_half(True)
-    other.begin_rest()
+    for gather in gathers[:1]:
+        for number in range(3, lines):
+            gather.onwards(number)
+    if early < depth:
+        load_ups(1).start()
+    for gather in gathers[1:]:
+        gather.onwards(1)
+    other.forward()
     share.forward_far()
-    for gather in gathers:
-        gather.onwards(2)
-    other.forward()
-    other.forward_far()
+    share.finish()
+    load_ups(0).wait()
+    if early < depth:
+        load_ups(1).wait()
+    weight = ups[...].reshape(model_width, ups.shape[3])
+    units = hidden.shape[2]
+    outs = []
+    for slot in range(2):
+        for mate in range(MATES):
+            index = slot * MATES + mate
+            values = dot(all_normed[slot, mate], weight, NN)
+            acts[index] = values.astype(low)
+            gate, up = values[:, :units], values[:, units:]
+            hidden[index] = (gate * jax.nn.sigmoid(gate) * up).astype(low)
+            here = pl.ds(index * rows, rows)
+            outs += [
+                pltpu.make_async_copy(acts.at[index], acts_out.at[here], out_sems.at[0, index]),
+                pltpu.make_async_copy(hidden.at[index], hidden_out.at[here], out_sems.at[1, index]),
+                pltpu.make_async_copy(
+                    all_normed.at[slot, mate], shared.at[slot, mate], out_sems.at[2, index]
+                ),
+            ]
+            for out in outs[-3:]:
+                out.start()
+        if slot == 0:
+            for gather in gathers[1:]:
+                gather.onwards(2)
+            other.forward_far()
     for number in range(3, lines):
-        for gather in gathers:
+        for gather in gathers[1:]:
             gather.onwards(number)
     for gather in gathers:
         gather.finish_lines()
-    share.finish()
     other.finish()
+    for out in outs:
+        out.wait()
+
+
+def columns_in_steps(lines, depth, body):
+    height = MATES * depth
+    some = max(1, 512 // height)
+
+    def one(step, carry):
+        body(
+            pl.ds(pl.multiple_of(step * some * height, 128), some * height),
+            pl.ds(step * some, some),
+            some * height,
+        )
+        return carry
+
+    lax.fori_loop(0, lines // some, one, 0)
 
 
 def turn_rows_kernel(
-    lines, parts, partial, weights, middle_ref, grad_ref, scale_ref, *rest
+    lines, parts, acts_grad, ups_any, weights, middle_ref, grad_ref, scale_ref, *rest
 ):
     place = Place()
     count = len(parts)
     blocks, rest = rest[:count], rest[count:]
     middle_grad_ref, gain_ref, low_grad, gated_grads = rest[:4]
     results, scratch = rest[4 : 4 + count], rest[4 + count :]
-    held, weight_sems, sent = scratch[:3]
-    rows = SumRows(place, partial, scratch[3:10])
-    swap = SwapBlocks(place, lambda slot, mate: sent.at[slot, mate], gated_grads, scratch[10:13])
+    held, load_sems, sent, acts, ups = scratch[:5]
+    all_lines, _, depth, units = ups.shape
+    tokens = low_grad.shape[0]
+
+    def compute(side_of, mate, target, slot):
+        first = pl.ds(pl.multiple_of((side_of * MATES + mate) * tokens, STEP), tokens)
+
+        def step(columns, part, size):
+            target[slot, :, columns] = dot(
+                acts[first], ups[part].reshape(size, units), NT
+            ).astype(low)
+
+        columns_in_steps(all_lines, depth, step)
+
+    rows = SumRows(place, None, scratch[5:13], compute)
+    swap = SwapBlocks(place, lambda slot, mate: sent.at[slot, mate], gated_grads, scratch[13:16])
     sums = [
-        SumLines(place, blocks[index], results[index], scratch[13 + 7 * index : 20 + 7 * index], first)
+        SumLines(place, blocks[index], results[index], scratch[16 + 7 * index : 23 + 7 * index], first)
         for index, (first, _) in enumerate(parts)
     ]
     meet(place, lines=lines if parts else 0, cores=True)
-    rows.begin()
+    loads = [
+        pltpu.make_async_copy(acts_grad, acts, load_sems.at[0]),
+        pltpu.make_async_copy(ups_any, ups, load_sems.at[1]),
+    ]
+    for load in loads:
+        load.start()
     for each in sums:
         each.begin()
-    loads = load_weights(weights, held, weight_sems)
-    for load in loads:
-        load.start()
+
+    def load_weight(slot):
+        return pltpu.make_async_copy(weights.at[slot], held, load_sems.at[2])
+
+    load_weight(0).start()
     gain_ref[...] = jnp.zeros_like(gain_ref)
-    rows.send_far()
     for each in sums:
         each.wait_loads()
         each.round(1)
+    for load in loads:
+        load.wait()
+    rows.begin()
+    rows.send_far()
     rows.send_near()
     rows.send_relayed()
-    for load in loads:
-        load.wait()
     for each in sums:
         each.round(2)
     rows.wait_half(False)
@@ -1455,13 +1548,16 @@
         low_grad[here] = total.astype(low)
         gain_ref[...] += jnp.sum(gains, axis=0, keepdims=True)
 
-    row_steps(0, low_grad.shape[0], body)
-    _, _, all_lines, _, depth, width = held.shape
+    row_steps(0, tokens, body)
+    width = held.shape[-1]
     for slot in range(2):
+        load_weight(slot).wait()
         for index, mate in enumerate(swap.order):
-            weight = held[slot, mate].reshape(all_lines * MATES * depth, width)
+            weight = held[mate].reshape(all_lines * MATES * depth, width)
             sent[slot, mate] = dot(low_grad[...], weight, NN).astype(low)
             swap.begin(slot, index)
+        if slot == 0:
+            load_weight(1).start()
     rows.finish()
     for each in sums:
         each.round(3)
@@ -1475,37 +1571,53 @@
 
 
 def last_rows_kernel(
-    lines, pieces, partial, mlp_partial, input_ref, middle_ref, middle_grad_ref, scale_ref, *rest
+    lines, pieces, all_grads, attn_any, beta_ref, input_ref, middle_grad_ref, scale_ref, *rest
 ):
     place = Place()
     blocks, rest = rest[:pieces], rest[pieces:]
-    input_grad, block_output, gain_ref = rest[:3]
-    results, scratch = rest[3 : 3 + pieces], rest[3 + pieces :]
-    low_grad, low_output = scratch[:2]
+    input_grad, gain_ref = rest[:2]
+    results, scratch = rest[2 : 2 + pieces], rest[2 + pieces :]
+    low_grad, grads, attn, load_sems = scratch[:4]
+    all_lines, _, depth, width = attn.shape
+    tokens = low_grad.shape[0]
+
+    def compute(side_of, mate, target, slot):
+        first = pl.ds(pl.multiple_of((side_of * MATES + mate) * tokens, STEP), tokens)
+
+        def step(columns, part, size):
+            total = dot(grads[first, :width], attn[part].reshape(size, width), NT)
+            total = total + dot(grads[first, width:], beta_ref[:, columns], NN)
+            target[slot, :, columns] = total.astype(low)
+
+        columns_in_steps(all_lines, depth, step)
+
     meet(place, far=bool(pieces), lines=lines if pieces else 0, straight=True)
-    rows = SumRows(place, partial, scratch[2:9])
-    outs = SumRows(place, mlp_partial, scratch[9:16])
-    make = sender(scratch[16:18])
-    local_sems = scratch[18]
+    rows = SumRows(place, None, scratch[4:12], compute)
+    make = sender(scratch[12:14])
+    scratch = scratch[14:]
     sums = [
-        SumLines(place, blocks[index], results[index], scratch[19 + 7 * index : 26 + 7 * index])
+        SumLines(place, blocks[index], results[index], scratch[7 * index : 7 * index + 7])
         for index in range(pieces)
     ]
-    whole = low_grad.shape[0]
+    loads = [
+        pltpu.make_async_copy(all_grads, grads, load_sems.at[0]),
+        pltpu.make_async_copy(attn_any, attn, load_sems.at[1]),
+    ]
     for each in sums:
         each.begin()
-    rows.begin()
-    outs.begin()
+    for load in loads:
+        load.start()
     for each in sums:
         each.wait_loads()
     for each in sums[1:]:
         each.round(1)
     gain_ref[...] = jnp.zeros_like(gain_ref)
+    for load in loads:
+        load.wait()
+    rows.begin()
     rows.send_far()
     rows.send_near()
     rows.send_relayed()
-    outs.send_far()
-    outs.send_near()
     for each in sums[1:]:
         each.round(2)
     rows.wait_half(False)
@@ -1518,48 +1630,33 @@
         low_grad[here] = (middle_grad_ref[here] + part).astype(low)
         gain_ref[...] += jnp.sum(gains, axis=0, keepdims=True)
 
-    row_steps(0, whole, body)
+    row_steps(0, tokens, body)
     first = make(0, low_grad, input_grad.at[place.core], place.sibling)
     first.start()
-    first_local = pltpu.make_async_copy(low_grad, input_grad.at[place.core], local_sems.at[0])
+    first_local = pltpu.make_async_copy(low_grad, input_grad.at[place.core], load_sems.at[2])
     first_local.start()
     if sums:
-        mine, theirs = scratch[19 + 7 * pieces :]
+        mine, theirs = scratch[7 * pieces :]
         small = sums[0]
         small.put_gains(gain_ref)
         mine[...] = small.held[...]
-        swap = make(2, mine, theirs, place.sibling)
+        swap = make(1, mine, theirs, place.sibling)
         swap.start()
         swap.wait_recv()
         small.add_top(theirs, CONV_ROW)
         small.direct()
-    outs.send_relayed()
     for each in sums[1:]:
         each.round(3)
-    outs.wait_half(False)
-    outs.wait_half(True)
-
-    def out_body(here):
-        low_output[here] = (middle_ref[here] + outs.total(here)).astype(low)
-
-    row_steps(0, whole, out_body)
-    second = make(1, low_output, block_output.at[place.core], place.sibling)
-    second.start()
-    second_local = pltpu.make_async_copy(low_output, block_output.at[place.core], local_sems.at[1])
-    second_local.start()
+    for each in sums[:1]:
+        each.exchange_direct()
     for turn in range(4, lines):
         for each in sums[1:]:
             each.round(turn)
-    for each in sums[:1]:
-        each.exchange_direct()
     for each in sums[1:]:
         each.exchange()
     rows.finish()
-    outs.finish()
     first_local.wait()
-    second_local.wait()
     first.wait()
-    second.wait()
     if sums:
         swap.wait_send()
     for each in sums:
@@ -1603,10 +1700,10 @@
         GatherLines(place, blocks[index], targets[index], scratch[3 + 6 * index : 9 + 6 * index])
         for index in range(pieces)
     ]
-    few, main = gathers[:2]
-    for gather in (few, main):
+    few, main, later = gathers[:3]
+    for gather in gathers[:3]:
         gather.begin()
-    for gather in (few, main):
+    for gather in gathers[:3]:
         gather.leave()
     share.begin_half(False)
     share.begin_half(True)
@@ -1614,13 +1711,15 @@
     for gather in (few, main):
         gather.onwards(1)
     share.forward()
-    for gather in gathers[2:]:
+    later.onwards(1)
+    for gather in gathers[3:]:
         gather.begin()
     few.onwards(2)
     main.onwards(2)
     for step in range(3, lines):
         few.onwards(step)
     share.forward_far()
+    later.onwards(2)
     share.finish()
     small_ref[...] = small[...]
     _, _, tokens, model_width = inputs.shape
@@ -1661,14 +1760,16 @@
         return carry
 
     lax.fori_loop(0, 2 * MATES, product, 0)
-    for gather in gathers[2:]:
+    for step in range(3, lines):
+        later.onwards(step)
+    for gather in gathers[3:]:
         for slot in range(MATES):
             gather.arrive(slot)
     for out in outs:
         out.wait()
     for gather in gathers:
         gather.finish_plane()
-    for gather in (few, main):
+    for gather in gathers[:3]:
         gather.finish_lines()
 
 
@@ -1706,34 +1807,50 @@
     rows, columns = mine.shape
     shared = (2, MATES, rows, columns)
     arrays = [array for array, _ in moving]
+    ups, downs = arrays
+    several = 2 * MATES
     return remote_call(
         functools.partial(middle_kernel, lines, tuple(part for _, part in moving)),
         1,
         [(gathered, "held"), (weights, "any"), (mine, "held"), (scale, "held"), (out_grad, "any")]
         + [(array, "any") for array in arrays],
-        [((rows, columns), wide, "held"), (shared, low, "any"), (shared, low, "any")]
+        [
+            ((rows, columns), wide, "held"),
+            (shared, low, "any"),
+            (shared, low, "any"),
+            ((several * rows, ups.shape[3]), low, "any"),
+            ((several * rows, downs.shape[3]), low, "any"),
+        ]
         + [(array.shape, low, "any") for array in arrays],
         [
             pltpu.VMEM((rows, columns), low),
             pltpu.VMEM(weights.shape, low),
             pltpu.SemaphoreType.DMA((2, MATES)),
+            pltpu.VMEM(shared, low),
+            pltpu.VMEM(ups.shape, low),
+            pltpu.VMEM((several, rows, ups.shape[3]), low),
+            pltpu.VMEM((several, rows, downs.shape[3]), low),
+            pltpu.SemaphoreType.DMA((3, several)),
+            pltpu.SemaphoreType.DMA((2,)),
         ]
         + ShareRows.scratch() * 2
         + GatherLines.scratch(lines) * len(arrays),
-        {5 + index: 3 + index for index in range(len(arrays))},
+        {5 + index: 5 + index for index in range(len(arrays))},
     )
 
 
-def turn_rows(partial, weights, middle, grad, scale, summing, lines):
-    seqs, _, rows, columns = partial.shape
+def turn_rows(acts_grad, ups, weights, middle, grad, scale, summing, lines):
+    rows, columns = middle.shape
     width = weights.shape[-1]
     blocks = (2, MATES, rows, width)
     scratch = [
-        pltpu.VMEM(weights.shape, low),
-        pltpu.SemaphoreType.DMA((2, MATES)),
+        pltpu.VMEM(weights.shape[1:], low),
+        pltpu.SemaphoreType.DMA((3,)),
         pltpu.VMEM(blocks, low),
+        pltpu.VMEM(acts_grad.shape, low),
+        pltpu.VMEM(ups.shape, low),
     ]
-    scratch += SumRows.scratch(rows, columns) + SwapBlocks.scratch()
+    scratch += SumRows.scratch(rows, columns, True) + SwapBlocks.scratch()
     outs = []
     for array, (_, height) in summing:
         shape = (MATES, height, array.shape[3])
@@ -1742,7 +1859,8 @@
     return remote_call(
         functools.partial(turn_rows_kernel, lines, tuple(part for _, part in summing)),
         2,
-        [(partial, "any"), (weights, "any"), (middle, "held"), (grad, "held"), (scale, "held")]
+        [(array, "any") for array in (acts_grad, ups, weights)]
+        + [(array, "held") for array in (middle, grad, scale)]
         + [(array, "any") for array, _ in summing],
         [
             ((rows, columns), wide, "held"),
@@ -1755,14 +1873,15 @@
     )
 
 
-def last_rows(partial, mlp_partial, mine, middle, middle_grad, scale, blocks, lines):
-    seqs, _, rows, columns = partial.shape
-    scratch = (
-        [pltpu.VMEM((rows, columns), low), pltpu.VMEM((rows, columns), low)]
-        + SumRows.scratch(rows, columns)
-        + SumRows.scratch(rows, columns)
-        + [pltpu.SemaphoreType.DMA((3,))] * 3
-    )
+def last_rows(all_grads, attn, beta, mine, middle_grad, scale, blocks, lines):
+    rows, columns = mine.shape
+    scratch = [
+        pltpu.VMEM((rows, columns), low),
+        pltpu.VMEM(all_grads.shape, low),
+        pltpu.VMEM(attn.shape, low),
+        pltpu.SemaphoreType.DMA((3,)),
+    ]
+    scratch += SumRows.scratch(rows, columns, True) + [pltpu.SemaphoreType.DMA((2,))] * 2
     for block, kept in blocks:
         scratch += SumLines.scratch(lines, block.shape[1:3] + (kept,))
     if blocks:
@@ -1770,14 +1889,10 @@
     return remote_call(
         functools.partial(last_rows_kernel, lines, len(blocks)),
         3,
-        [(partial, "any"), (mlp_partial, "any")]
-        + [(array, "held") for array in (mine, middle, middle_grad, scale)]
+        [(all_grads, "any"), (attn, "any")]
+        + [(array, "held") for array in (beta, mine, middle_grad, scale)]
         + [(block, "any") for block, _ in blocks],
-        [
-            ((seqs, rows, columns), low, "any"),
-            ((seqs, rows, columns), low, "any"),
-            ((1, columns), wide, "held"),
-        ]
+        [((2, rows, columns), low, "any"), ((1, columns), wide, "held")]
         + [(block.shape[1:3] + (kept,), low, "any") for block, kept in blocks],
         scratch,
     )
@@ -1909,7 +2024,7 @@
 
 def delta_back(
     limit, raw, tails, taps, logits, scale, qkv, wu, maps, total, grad, mixed, solved, state, fresh,
-    row_grad, summing, lines, seqs, heads, span,
+    row_grad, mlp_partial, middle, summing, lines, seqs, heads, span,
 ):
     steps = Steps(seqs, heads, span)
     chains, chunks, size = steps.chains, steps.chunks, CHUNK
@@ -1934,12 +2049,15 @@
         (state, steps.blocks("second")),
         (fresh, steps.blocks("second")),
         (row_grad, anywhere),
+        (mlp_partial, anywhere),
+        (middle, steps.whole(middle.shape)),
     ] + [(array, anywhere) for array, _ in summing]
     outs = [
         (all_shape, low, steps.whole(all_shape)),
         ((chains, 8, size), wide, steps.few("first", size)),
         ((chains, 8, 3 * size), wide, steps.few("second", 3 * size)),
         ((seqs, MATES) + row_grad.shape, low, anywhere),
+        ((seqs,) + row_grad.shape, low, anywhere),
     ]
     edges = (chains, 16, 3 * size)
     scratch = [
@@ -1958,6 +2076,8 @@
         pltpu.SemaphoreType.DMA((2, chains)),
         pltpu.SemaphoreType.DMA((2,)),
     ] + ShareRows.scratch()
+    scratch += [pltpu.VMEM(row_grad.shape, low)] + [pltpu.SemaphoreType.DMA((1,))] * 3
+    scratch += SumRows.scratch(*row_grad.shape)
     for array, (_, height) in summing:
         shape = (MATES, height, array.shape[3])
         scratch += SumLines.scratch(lines, shape)
@@ -1998,12 +2118,6 @@
         (scale, weight, beta),
         [((rows, model_width), low), ((rows, weight.shape[1]), low), ((rows, beta.shape[0]), wide)],
     )
-
-
-def back_project(grads, weight, beta):
-    return tiled_call(
-        back_project_kernel, (grads,), (weight, beta), [((grads.shape[0], weight.shape[0]), low)]
-    )[0]
 
 
 def held_call(body, ins, outs):
@@ -2150,8 +2264,8 @@
         flat_normed, raw, logits, small, attn_full, output_full, ups_full, downward_full = first_call(
             block_input, (small_cut, *cuts), lines
         )
-        ups_split = depth // 128 * 80
-        front_moves = ((output_full, (0, depth)), (ups_full, (0, ups_split)))
+        ups_split = depth // 128 * 96
+        front_moves = ((output_full, None), (ups_full, (0, ups_split)))
     else:
         streams_cut = jnp.stack(
             [
@@ -2171,6 +2285,7 @@
         input_rows = first_rows(block_input).reshape(rows, model_width)
         small, attn_full, output_full, ups_full, downward_full = (gather_weights(cut) for cut in cuts)
         front_moves = ((output_full, None),)
+    attn_blocks = attn_full
     attn_full = attn_full.reshape(model_width, gates_end)
     small = small.reshape(count, SMALL * 128)
     attn_scale = small[:, :depth].reshape(1, model_width).astype(wide)
@@ -2203,25 +2318,16 @@
     (
         qkv, solved, wu, maps, total, tails, state, fresh, mixed, gated, gathered, output_all, *moved
     ) = delta_front(limit, raw, taps, logits, head_scale, front_moves, *sizes_of)
-    middle_moves = ()
+    middle_moves = ((ups_full, None), (downward_full, None))
     if near:
-        ups_full = moved[1]
-        middle_moves = (
-            (ups_full, (ups_split, depth - ups_split)), (downward_full, (0, depth))
-        )
-    middle, mlp_normed, grad_rows, *moved = middle_rows(
+        middle_moves = ((moved[1], (ups_split, depth - ups_split)), (downward_full, (0, depth)))
+    middle, mlp_normed, grad_rows, acts, hidden, ups_full, downward_full = middle_rows(
         gathered, output_all, mine_low, mlp_scale, out_grad, middle_moves, lines
     )
     grad_rows = grad_rows.reshape(rows, model_width)
-    if near:
-        ups_full, downward_full = moved
-    ups_full = ups_full.reshape(model_width, 2 * units)
     downward_full = downward_full.reshape(model_width, units)
     mlp_normed = mlp_normed.reshape(rows, model_width)
-    acts = matmul("rd,df->rf", mlp_normed, ups_full)
-    gate_act, up_act = acts[:, :units], acts[:, units:]
-    silu_act = jax.nn.silu(gate_act)
-    hidden = (silu_act * up_act).astype(low)
+    gate_act, up_act = acts[:, :units].astype(wide), acts[:, units:].astype(wide)
     mlp_part = matmul("rf,df->rd", hidden, downward_full).astype(low)
 
     hidden_grad = matmul("rd,df->rf", grad_rows, downward_full)
@@ -2229,12 +2335,11 @@
     acts_grad = jnp.concatenate(
         [
             (hidden_grad * up_act * silu_slope(gate_act)).astype(low),
-            (hidden_grad * silu_act).astype(low),
+            (hidden_grad * jax.nn.silu(gate_act)).astype(low),
         ],
         axis=1,
     )
     ups_grad = matmul("rd,rf->df", mlp_normed, acts_grad).astype(low)
-    normed_two_part = matmul("rf,df->rd", acts_grad, ups_full).astype(low)
 
     def cut_rows(grad):
         return grad.reshape(lines, MATES, depth, grad.shape[1])
@@ -2242,25 +2347,21 @@
     ups_blocks, downward_blocks = cut_rows(ups_grad), cut_rows(downward_grad)
     turn_sums = back_sums = ()
     if near:
-        sums_split = depth // 128 * 80
-        turn_sums = ((ups_blocks, (0, sums_split)),)
+        sums_split = depth // 128 * 32
+        turn_sums = ((downward_blocks, (0, depth)), (ups_blocks, (0, sums_split)))
     middle_grad, mlp_gain_grad, attn_grad_mine, gated_grad, *summed = turn_rows(
-        normed_two_part.reshape(blocked), output_all, middle, grad_mine, mlp_scale, turn_sums, lines
+        acts_grad, ups_full, output_all, middle, grad_mine, mlp_scale, turn_sums, lines
     )
     if near:
-        ups_low, = summed
-        back_sums = (
-            (ups_blocks, (sums_split, depth - sums_split)),
-            (downward_blocks, (0, depth)),
-        )
-    all_grads, head_gain_parts, taps_grad, attn_grad_rows, *summed = delta_back(
+        downward_sum, ups_low = summed
+        back_sums = ((ups_blocks, (sums_split, depth - sums_split)),)
+    all_grads, head_gain_parts, taps_grad, attn_grad_rows, block_output, *summed = delta_back(
         limit, raw, tails, taps, logits, head_scale, qkv, wu, maps, total,
-        gated_grad.reshape(rows, width), mixed, solved, state, fresh, attn_grad_mine, back_sums,
-        *sizes_of,
+        gated_grad.reshape(rows, width), mixed, solved, state, fresh, attn_grad_mine, mlp_part.reshape(blocked), middle,
+        back_sums, *sizes_of,
     )
     attn_grad_rows = attn_grad_rows.reshape(rows, model_width)
     output_grad = cut_rows(matmul("rd,rc->dc", attn_grad_rows, gated).astype(low))
-    normed_part = back_project(all_grads, attn_full, beta_rows)
     attn_grads = matmul("rd,rc->dc", flat_normed, all_grads).astype(low)
     beta_grad = attn_grads[:, gates_end + BETA_ROW : gates_end + BETA_ROW + heads]
     attn_grads = cut_rows(attn_grads)
@@ -2284,24 +2385,15 @@
         flat = jnp.pad(flat, ((0, 0), (0, SMALL * 128 - small_size)))
         return flat.reshape(lines, MATES, SMALL, 128)
 
-    last_ins = (
-        normed_part.reshape(blocked),
-        mlp_part.reshape(blocked),
-        mine_low,
-        middle,
-        middle_grad,
-        attn_scale,
-    )
+    last_ins = (all_grads, attn_blocks, beta_rows, mine_low, middle_grad, attn_scale)
     if near:
-        ups_high, downward_sum = summed
+        ups_high, = summed
         blocks = (
             (small_blocks(jnp.zeros((1, model_width), wide)), 128),
             (attn_grads, gates_end),
             (output_grad, width),
         )
-        input_grad, block_output, _, small_sum, attn_sum, output_sum = last_rows(
-            *last_ins, blocks, lines
-        )
+        input_grad, _, small_sum, attn_sum, output_sum = last_rows(*last_ins, blocks, lines)
         grads = held_call(
             functools.partial(unpack_kernel, heads),
             (attn_sum, output_sum, ups_low, ups_high, downward_sum),
@@ -2316,7 +2408,7 @@
         small_sum = small_sum.reshape(MATES, SMALL * 128).astype(wide)
         gains_sum = jnp.sum(small_sum[:, :conv_start], axis=0)
     else:
-        input_grad, block_output, attn_gain_grad = last_rows(*last_ins, (), lines)
+        input_grad, attn_gain_grad = last_rows(*last_ins, (), lines)
         small_sum, attn_sum, output_sum, ups_sum, downward_sum = (
             scatter_grads(block)
             for block in (

time: 779 us -> 742 us (0.953)
  matrix products: 113 us -> 74.6 us
  local copies, waits for them, and re-layouts: 31.3 us -> 19.3 us
    dot_general x8 -> x6, matrix products: 113 us -> 74.6 us  [matmul(): return jnp.einsum(form, left, right, preferred_element_type=wide)]
    pallas_call x4, Pallas kernels: 383 us -> 415 us  [remote_call(): pl.pallas_call(body, in_specs=[anywhere if kind == 'any' else held for _,...]
    pallas_call x1 -> x0, Pallas kernels: 15.7 us -> none  [tiled_call(): pl.pallas_call(body, grid=(ins[0].shape[0] // tile,), in_specs=[tall(arra...]
    pallas_call x2, Pallas kernels: 210 us -> 198 us  [call(): pl.pallas_call(body, grid=(2 * self.chains,), in_specs=[spec for _, spec...]
where the time goes in v7:
time: 742 us; the launch traced here: 732 us
  Pallas kernels  624 us (84%)
  matrix products  74.6 us (10%)
  local copies, waits for them, and re-layouts  19.3 us (3%)
  other arithmetic  12.1 us (2%)
    pallas_call x4, Pallas kernels, remote_call(): pl.pallas_call(body, in_specs=[anywhere if kind == 'any' else held for _,...  415 us
    pallas_call x2, Pallas kernels, call(): pl.pallas_call(body, grid=(2 * self.chains,), in_specs=[spec for _, spec...  198 us
    dot_general x6, matrix products, matmul(): return jnp.einsum(form, left, right, preferred_element_type=wide)  74.6 us

profile of v7, /device:TPU:0, one launch (start us, length us, event | category | flops | bytes accessed | tf_op | source)
XLA Modules:
  0.0 731.5 jit_solution(10646257104357569755)
XLA Ops:
  0.7 1.3 fusion.14
  2.0 1.9 add_subtract_fusion.limit_ref
  3.9 0.8 convert_element_type.93
  4.7 0.1 reshape.197
  4.8 0.7 convert_element_type.94
  5.5 0.7 convert_bitcast_fusion.3
  6.1 0.7 convert.33
  6.8 0.7 convert.32
  7.5 0.6 copy.86
  8.1 5.4 shard_map.271
  13.5 105.5 %shard_map.272 = (bf16[2048,2048]{1,0:T(8,128)(2,1)}, bf16[2048,1024]{1,0:T(8,128)(2,1)}, f32[2048,128]{1,0:T(8,128)}, bf16[4,4,16,128]{3,2,1,0:T(8,128)(2,1)}, ...) custom-call(bf16[2,256,2048]{2,1,0:T(8,128)(2,1)} %input_ref.1, ...), custom_call_target="tpu_custom_call" | custom-call | tf_op jit(solution)/shard_map/pallas_call | solution.py:1318
  118.9 0.9 copy.84
  119.8 0.1 copy.67
  119.9 0.1 copy.65
  120.1 0.7 reshape.229.taps_ref
  120.8 0.6 reshape.224.scale_ref
  121.4 80.6 %shard_map.273 = (bf16[2048,768]{1,0:T(8,128)(2,1)}, f32[4,8,128,128]{3,2,1,0:T(8,128)}, f32[4,8,128,256]{3,2,1,0:T(8,128)}, f32[4,8,128,128]{3,2,1,0:T(8,128)},...) custom-call(s32[2]{0:T(128)} %add_subtract_fusion.limit_ref, ...), custom_call_target="tpu_custom_call", output_to_operand_aliasing={{12}: (7, {}), {13}: (8, {})} | custom-call | tf_op jit(solution)/shard_map/pallas_call | solution.py:1949
  202.0 1.5 dynamic-slice_bitcast_fusion
  203.5 0.6 slice_convert_fusion
  204.2 105.7 %shard_map.274 = (f32[256,2048]{1,0:T(8,128)}, bf16[2,4,256,2048]{3,2,1,0:T(8,128)(2,1)}, bf16[2,4,256,2048]{3,2,1,0:T(8,128)(2,1)}, bf16[2048,1408]{1,0:T(8,128...) custom-call(bf16[2,4,256,256]{3,2,1,0:T(8,128)(2,1)} %get-tuple-elem, ...), custom_call_target="tpu_custom_call", output_to_operand_aliasing={{5}: (5, {}), {6}: (6, {})} | custom-call | tf_op jit(solution)/shard_map/pallas_call | solution.py:1318
  309.9 13.7 %fusion.6 = (bf16[2048,704]{1,0:T(8,128)(2,1)S(1)}, bf16[2048,704]{1,0:T(8,128)(2,1)S(1)}) fusion(bf16[2048,1408]{1,0:T(8,128)(2,1)} %get-tuple-element.91, bf16[2048,2048]{1,0:T(8,128)(2,1)} %bitcast.121, bf16[2048,704]{1,0:T(8,128)(2,1)} %bitcast.93), kind=kOutput, calls=%fused_computation.12 | convolution fusion | flops 5927206912 | bytes 22806528 | tf_op jit(solution)/shard_map/rd,df->rf/dot_general | solution.py:73
  323.6 4.4 pad_maximum_fusion.acts_grad
  328.0 8.6 %convolution_convert_fusion.3 = bf16[2048,704]{0,1:T(8,128)(2,1)S(1)} fusion(bf16[2048,2048]{1,0:T(8,128)(2,1)} %bitcast.122, bf16[2048,704]{1,0:T(8,128)(2,1)S(1)} %copy-done.7), kind=kOutput, calls=%fused_computation.16 | convolution fusion | flops 5907021824 | bytes 14155776 | tf_op jit(solution)/shard_map/rd,rf->df/dot_general | solution.py:73
  336.6 2.8 copy.58
  339.4 19.3 %convolution_convert_fusion.2 = bf16[2048,1408]{1,0:T(8,128)(2,1)} fusion(bf16[2048,2048]{1,0:T(8,128)(2,1)} %bitcast.120, bf16[2048,1408]{1,0:T(8,128)(2,1)} %pad_maximum_fusion.acts_grad), kind=kOutput, calls=%fused_computation.5 | convolution fusion | flops 11814043648 | bytes 19922944 | tf_op jit(solution)/shard_map/rd,rf->df/dot_general | solution.py:73
  358.7 103.4 %shard_map.275 = (f32[256,2048]{1,0:T(8,128)}, f32[1,2048]{1,0:T(1,128)}, bf16[256,2048]{1,0:T(8,128)(2,1)}, bf16[2,4,256,256]{3,2,1,0:T(8,128)(2,1)}, bf16[4,12...) custom-call(bf16[2048,1408]{1,0:T(8,128)(2,1)} %pad_maximum_fusion.acts_grad, ...), custom_call_target="tpu_custom_call" | custom-call | tf_op jit(solution)/shard_map/pallas_call | solution.py:1318
  462.1 10.8 %convolution_convert_fusion.1 = bf16[2048,2048]{1,0:T(8,128)(2,1)} fusion(bf16[2048,704]{1,0:T(8,128)(2,1)} %get-tuple-element.94, bf16[2048,704]{1,0:T(8,128)(2,1)S(1)} %bitcast.94), kind=kOutput, calls=%fused_computation.4 | convolution fusion | flops 5909774336 | bytes 14155776 | tf_op jit(solution)/shard_map/rf,df->rd/dot_general | solution.py:73
  473.0 117.5 %shard_map.276 = (bf16[2048,1152]{1,0:T(8,128)(2,1)}, f32[4,8,128]{2,1,0:T(8,128)}, f32[4,8,384]{2,1,0:T(8,128)}, bf16[2,4,256,2048]{3,2,1,0:T(8,128)(2,1)}, bf1...) custom-call(s32[2]{0:T(128)} %add_subtract_fusion.limit_ref, ...), custom_call_target="tpu_custom_call" | custom-call | tf_op jit(solution)/shard_map/pallas_call | solution.py:1949
  590.5 0.8 pad.33.beta_ref
  591.4 0.7 slice_reduce_fusion.1
  592.2 0.8 slice.56
  593.0 0.2 reshape.214
  593.3 0.1 copy.61
  593.5 15.3 %convolution_convert_fusion = bf16[2048,1152]{1,0:T(8,128)(2,1)S(1)} fusion(bf16[2048,2048]{1,0:T(8,128)(2,1)} %get-tuple-element.109, bf16[2048,1152]{1,0:T(8,128)(2,1)} %get-tuple-element.103.all_grads), kind=kOutput, calls=%fused_computation.3 | convolution fusion | flops 9666035712 | bytes 17825792 | tf_op jit(solution)/shard_map/rd,rc->dc/dot_general | solution.py:73
  608.9 2.1 copy-done
  611.0 0.2 slice.69
  611.2 0.2 copy.62
  611.5 0.6 copy.75
  612.1 6.9 convolution_convert_fusion.4
  619.0 100.7 %shard_map.277 = (bf16[2,256,2048]{2,1,0:T(8,128)(2,1)}, f32[1,2048]{1,0:T(1,128)}, bf16[4,16,128]{2,1,0:T(8,128)(2,1)}, bf16[4,128,1024]{2,1,0:T(8,128)(2,1)}, bf16[4,128,256]{2,1,0:T(8,128)(2,1)}) custom-call(bf16[2048,1152]{1,0:T(8,128)(2,1)} %get-tuple-element.103.all_grads, bf16[4,4,128,1024]{3,2,1,0:T(8,128)(2,1)} %get-tuple-element.104.attn_any, ...), custom_call_target="tpu_custom_call" | custom-call | tf_op jit(solution)/shard_map/pallas_call | solution.py:1318
  719.7 0.9 convert_bitcast_fusion.2
  720.6 0.5 fusion.13
  721.2 5.4 shard_map.278
  726.6 0.6 reshape.221
  727.2 0.7 reshape.222
  727.9 0.5 slice.62
  728.4 1.3 copy.99
  729.7 1.3 copy.100
  (41 shorter events, 0.4 us)
Async XLA Ops:
  121.4 80.6 %copy-start.1 = (bf16[2,256,2048]{2,1,0:T(8,128)(2,1)S(1)}, bf16[2,256,2048]{2,1,0:T(8,128)(2,1)}, u32[]{:S(2)}) copy-start(bf16[2,256,2048]{2,1,0:T(8,128)(2,1)} %grad_any.1) | copy-start | bytes 6291460
  121.4 80.6 %copy-start.2 = (bf16[2,256,2048]{2,1,0:T(8,128)(2,1)S(1)}, bf16[2,256,2048]{2,1,0:T(8,128)(2,1)}, u32[]{:S(2)}) copy-start(bf16[2,256,2048]{2,1,0:T(8,128)(2,1)} %input_ref.1) | copy-start | bytes 6291460
  323.6 4.4 copy-start.7
  358.7 103.4 %copy-start.3 = (bf16[4,4,128,704]{3,2,1,0:T(8,128)(2,1)S(1)}, bf16[4,4,128,704]{3,2,1,0:T(8,128)(2,1)}, u32[]{:S(2)}) copy-start(bf16[4,4,128,704]{3,2,1,0:T(8,128)(2,1)} %get-tuple-element.90) | copy-start | bytes 8650756
  473.0 118.4 %copy-start.6 = (f32[1,2048]{1,0:T(1,128)S(1)}, f32[1,2048]{1,0:T(1,128)}, u32[]{:S(2)}) copy-start(f32[1,2048]{1,0:T(1,128)} %get-tuple-element.106) | copy-start | bytes 24580
  593.5 18.6 %copy-start.8 = (bf16[2048,256]{1,0:T(8,128)(2,1)S(1)}, bf16[2048,256]{1,0:T(8,128)(2,1)}, u32[]{:S(2)}) copy-start(bf16[2048,256]{1,0:T(8,128)(2,1)} %get-tuple-element.111) | copy-start | bytes 3145732
  608.9 2.1 copy-start
  719.7 8.7 %copy-start.4 = (bf16[2,256,2048]{2,1,0:T(8,128)(2,1)S(1)}, bf16[2,256,2048]{2,1,0:T(8,128)(2,1)}, u32[]{:S(2)}) copy-start(bf16[2,256,2048]{2,1,0:T(8,128)(2,1)} %get-tuple-element.152) | copy-start | bytes 6291460
  727.9 1.8 copy-start.5

commit v8 on v7

--- a/solution.py
+++ b/solution.py
@@ -73,14 +73,9 @@
     return jnp.einsum(form, left, right, preferred_element_type=wide)
 
 
-def silu_slope(value):
-    squash = jax.nn.sigmoid(value)
-    return squash * (1.0 + value * (1.0 - squash))
-
-
 CHUNK = 128
 TOGETHER = 4
-VMEM_BYTES = 58 * 1024 * 1024
+VMEM_BYTES = 60 * 1024 * 1024
 NN = (((1,), (0,)), ((), ()))
 NT = (((1,), (1,)), ((), ()))
 
@@ -1138,8 +1133,8 @@
             pltpu.VMEM((lines,) + shape, low),
             pltpu.VMEM((2, max(lines - 1, 1)) + shape, low),
             pltpu.SemaphoreType.DMA((lines + 1,)),
-            pltpu.SemaphoreType.DMA((2, lines)),
-            pltpu.SemaphoreType.DMA((2, lines)),
+            pltpu.SemaphoreType.DMA((2, lines, MATES)),
+            pltpu.SemaphoreType.DMA((2, lines, MATES)),
             pltpu.SemaphoreType.DMA((3,)),
             pltpu.SemaphoreType.DMA((3,)),
         ]
@@ -1149,6 +1144,7 @@
         self.held, self.came, self.local_sems, self.send, self.got, send, receive = scratch
         self.lines = self.held.shape[0]
         self.make = sender((send, receive))
+        self.order = [place.far, place.x, place.y, place.mate]
 
     def load(self, line):
         return pltpu.make_async_copy(
@@ -1187,25 +1183,25 @@
                 both = own + other[line, mate].astype(wide)
                 self.held[line, mate] = jnp.where(top, both, own).astype(low)
 
-    def copy(self, turn, way):
+    def copy(self, turn, way, mate):
         direction = 1 - 2 * way
         line = self.place.line + direction * (self.lines - turn)
         return line, pltpu.make_async_remote_copy(
-            src_ref=self.held.at[line],
-            dst_ref=self.came.at[way, turn - 1],
-            send_sem=self.send.at[way, turn],
-            recv_sem=self.got.at[way, turn],
+            src_ref=self.held.at[line, mate],
+            dst_ref=self.came.at[way, turn - 1, mate],
+            send_sem=self.send.at[way, turn, mate],
+            recv_sem=self.got.at[way, turn, mate],
             device_id=self.place.lines_away(direction),
             device_id_type=MESH,
         )
 
-    def arrival(self, turn, way):
-        slot = self.came.at[way, turn - 1]
+    def arrival(self, turn, way, mate):
+        slot = self.came.at[way, turn - 1, mate]
         return pltpu.make_async_remote_copy(
             src_ref=slot,
             dst_ref=slot,
-            send_sem=self.send.at[way, turn],
-            recv_sem=self.got.at[way, turn],
+            send_sem=self.send.at[way, turn, mate],
+            recv_sem=self.got.at[way, turn, mate],
             device_id=self.place.sibling,
             device_id_type=MESH,
         )
@@ -1217,39 +1213,35 @@
     def inner(self, way):
         return self.place.line >= 1 if way == 0 else self.place.line <= self.lines - 2
 
-    def add(self, line, way, turn):
-        def mates(mate, carry):
-            def body(here):
-                self.held[line, mate, here] = (
-                    self.held[line, mate, here].astype(wide)
-                    + self.came[way, turn - 1, mate, here].astype(wide)
-                ).astype(low)
-
-            row_steps(0, self.held.shape[2], body)
-            return carry
-
-        lax.fori_loop(0, self.held.shape[1], mates, 0)
+    def add(self, line, way, turn, mate):
+        def body(here):
+            self.held[line, mate, here] = (
+                self.held[line, mate, here].astype(wide)
+                + self.came[way, turn - 1, mate, here].astype(wide)
+            ).astype(low)
+
+        row_steps(0, self.held.shape[2], body)
 
     def round(self, turn):
         if turn >= self.lines:
             return
-        for way in (0, 1):
-            line, copy = self.copy(turn, way)
-
-            @pl.when(self.sends(turn, way))
-            def _(line=line, copy=copy, way=way):
-                if turn > 1:
-
-                    @pl.when(self.inner(way))
-                    def _():
-                        self.arrival(turn - 1, way).wait_recv()
-                        self.add(line, way, turn - 1)
-
-                copy.start()
+        for mate in self.order:
+            for way in (0, 1):
+                line, copy = self.copy(turn, way, mate)
+
+                @pl.when(self.sends(turn, way))
+                def _(line=line, copy=copy, way=way, mate=mate):
+                    if turn > 1:
+
+                        @pl.when(self.inner(way))
+                        def _():
+                            self.arrival(turn - 1, way, mate).wait_recv()
+                            self.add(line, way, turn - 1, mate)
+
+                    copy.start()
 
     def plane(self, index):
-        place = self.place
-        mate = (place.x, place.y, place.far)[index]
+        place, mate = self.place, self.order[index]
         return self.make(
             index, self.held.at[place.line, mate], self.result.at[place.mate], place.of(mate)
         )
@@ -1263,25 +1255,27 @@
         )
 
     def exchange(self):
-        for way in (0, 1):
-            if self.lines > 1:
-
-                @pl.when(self.inner(way))
-                def _(way=way):
-                    self.arrival(self.lines - 1, way).wait_recv()
-                    self.add(self.place.line, way, self.lines - 1)
-
-        for index in range(3):
-            self.plane(index).start()
-        self.local().start()
+        for index, mate in enumerate(self.order):
+            for way in (0, 1):
+                if self.lines > 1:
+
+                    @pl.when(self.inner(way))
+                    def _(way=way, mate=mate):
+                        self.arrival(self.lines - 1, way, mate).wait_recv()
+                        self.add(self.place.line, way, self.lines - 1, mate)
+
+            if index < 3:
+                self.plane(index).start()
+            else:
+                self.local().start()
 
     def straight(self, step):
         line = (self.place.line + step) % self.lines
         return pltpu.make_async_remote_copy(
             src_ref=self.held.at[line],
             dst_ref=self.came.at[0, step - 1],
-            send_sem=self.send.at[0, step],
-            recv_sem=self.got.at[0, step],
+            send_sem=self.send.at[0, step, 0],
+            recv_sem=self.got.at[0, step, 0],
             device_id=(line * MATES + self.place.mate, self.place.core),
             device_id_type=MESH,
         )
@@ -1293,7 +1287,8 @@
     def exchange_direct(self):
         for step in range(1, self.lines):
             self.straight(step).wait_recv()
-            self.add(self.place.line, 0, step)
+            for mate in range(MATES):
+                self.add(self.place.line, 0, step, mate)
         for index in range(3):
             self.plane(index).start()
         self.local().start()
@@ -1308,8 +1303,9 @@
             return
         for turn in range(1, self.lines):
             for way in (0, 1):
-                _, copy = self.copy(turn, way)
-                pl.when(self.sends(turn, way))(copy.wait_send)
+                for mate in self.order:
+                    _, copy = self.copy(turn, way, mate)
+                    pl.when(self.sends(turn, way))(copy.wait_send)
 
 
 def remote_call(body, identity, ins, outs, scratch, aliases=None):
@@ -1351,10 +1347,10 @@
 def middle_kernel(lines, moves, gathered, weights, input_ref, scale_ref, grad_any, *rest):
     place = Place()
     count = len(moves)
-    middle_ref, shared, grads, acts_out, hidden_out = rest[count : count + 5]
+    middle_ref, turned_out, grads, acts_out, hidden_out = rest[count : count + 5]
     targets, scratch = rest[count + 5 : 2 * count + 5], rest[2 * count + 5 :]
-    normed, held, weight_sems, all_normed, ups, acts, hidden, out_sems, load_sems = scratch[:9]
-    scratch = scratch[9:]
+    normed, held, weight_sems, all_normed, turned, ups, acts, hidden, out_sems, load_sems = scratch[:10]
+    scratch = scratch[10:]
     share = ShareRows(place, normed, all_normed, scratch[:3])
     other = ShareRows(place, grad_any.at[place.core], grads, scratch[3:6])
     gathers = [
@@ -1446,11 +1442,12 @@
             gate, up = values[:, :units], values[:, units:]
             hidden[index] = (gate * jax.nn.sigmoid(gate) * up).astype(low)
             here = pl.ds(index * rows, rows)
+            turned[:, here] = all_normed[slot, mate].T
             outs += [
                 pltpu.make_async_copy(acts.at[index], acts_out.at[here], out_sems.at[0, index]),
                 pltpu.make_async_copy(hidden.at[index], hidden_out.at[here], out_sems.at[1, index]),
                 pltpu.make_async_copy(
-                    all_normed.at[slot, mate], shared.at[slot, mate], out_sems.at[2, index]
+                    turned.at[:, here], turned_out.at[:, here], out_sems.at[2, index]
                 ),
             ]
             for out in outs[-3:]:
@@ -1484,15 +1481,57 @@
     lax.fori_loop(0, lines // some, one, 0)
 
 
+class Tiles:
+    def __init__(self, source, target, held_in, held_out, sems, body):
+        self.source, self.target, self.body = source, target, body
+        self.held_in, self.held_out, self.sems = held_in, held_out, sems
+        self.rows = held_in.shape[1]
+        self.count = source.shape[0] // self.rows
+
+    def load(self, tile):
+        return pltpu.make_async_copy(
+            self.source.at[pl.ds(tile * self.rows, self.rows)],
+            self.held_in.at[tile % 2],
+            self.sems.at[0, tile % 2],
+        )
+
+    def store(self, tile):
+        return pltpu.make_async_copy(
+            self.held_out.at[tile % 2],
+            self.target.at[pl.ds(tile * self.rows, self.rows)],
+            self.sems.at[1, tile % 2],
+        )
+
+    def begin(self):
+        self.load(0).start()
+
+    def run(self, first, last):
+        for tile in range(first, last):
+            self.load(tile).wait()
+            if tile + 1 < self.count:
+                self.load(tile + 1).start()
+            if tile >= 2:
+                self.store(tile - 2).wait()
+            self.body(self.held_in.at[tile % 2], self.held_out.at[tile % 2])
+            self.store(tile).start()
+
+    def finish(self):
+        for tile in range(max(self.count - 2, 0), self.count):
+            self.store(tile).wait()
+
+
 def turn_rows_kernel(
-    lines, parts, acts_grad, ups_any, weights, middle_ref, grad_ref, scale_ref, *rest
+    lines, parts, acts_grad, ups_any, weights, turned, hidden, downs_any, middle_ref, grad_ref,
+    scale_ref, *rest
 ):
     place = Place()
     count = len(parts)
     blocks, rest = rest[:count], rest[count:]
-    middle_grad_ref, gain_ref, low_grad, gated_grads = rest[:4]
-    results, scratch = rest[4 : 4 + count], rest[4 + count :]
-    held, load_sems, sent, acts, ups = scratch[:5]
+    middle_grad_ref, gain_ref, low_grad, gated_grads, ups_grad, mlp_part = rest[:6]
+    results, scratch = rest[6 : 6 + count], rest[6 + count :]
+    held, load_sems, sent, acts, ups, downs = scratch[:6]
+    turned_in, grad_out, grad_sems, hidden_in, part_out, part_sems = scratch[6:12]
+    scratch = scratch[12:]
     all_lines, _, depth, units = ups.shape
     tokens = low_grad.shape[0]
 
@@ -1506,38 +1545,60 @@
 
         columns_in_steps(all_lines, depth, step)
 
-    rows = SumRows(place, None, scratch[5:13], compute)
-    swap = SwapBlocks(place, lambda slot, mate: sent.at[slot, mate], gated_grads, scratch[13:16])
+    def weight_grad(tile_in, tile_out):
+        tile_out[...] = dot(tile_in[...], acts[...], NN).astype(low)
+
+    def back_down(tile_in, tile_out):
+        def step(columns, part, size):
+            tile_out[:, columns] = dot(
+                tile_in[...], downs[part].reshape(size, downs.shape[3]), NT
+            ).astype(low)
+
+        columns_in_steps(all_lines, depth, step)
+
+    grad_tiles = Tiles(turned, ups_grad, turned_in, grad_out, grad_sems, weight_grad)
+    part_tiles = Tiles(hidden, mlp_part, hidden_in, part_out, part_sems, back_down)
+    rows = SumRows(place, None, scratch[:8], compute)
+    swap = SwapBlocks(place, lambda slot, mate: sent.at[slot, mate], gated_grads, scratch[8:11])
     sums = [
-        SumLines(place, blocks[index], results[index], scratch[16 + 7 * index : 23 + 7 * index], first)
+        SumLines(place, blocks[index], results[index], scratch[11 + 7 * index : 18 + 7 * index], first)
         for index, (first, _) in enumerate(parts)
     ]
     meet(place, lines=lines if parts else 0, cores=True)
+    for each in sums:
+        each.begin()
     loads = [
         pltpu.make_async_copy(acts_grad, acts, load_sems.at[0]),
         pltpu.make_async_copy(ups_any, ups, load_sems.at[1]),
     ]
     for load in loads:
         load.start()
-    for each in sums:
-        each.begin()
 
     def load_weight(slot):
         return pltpu.make_async_copy(weights.at[slot], held, load_sems.at[2])
 
-    load_weight(0).start()
-    gain_ref[...] = jnp.zeros_like(gain_ref)
+    load_downs = pltpu.make_async_copy(downs_any, downs, load_sems.at[3])
     for each in sums:
         each.wait_loads()
         each.round(1)
+    load_weight(0).start()
+    load_downs.start()
+    grad_tiles.begin()
+    part_tiles.begin()
+    gain_ref[...] = jnp.zeros_like(gain_ref)
     for load in loads:
         load.wait()
     rows.begin()
     rows.send_far()
     rows.send_near()
-    rows.send_relayed()
+    some, all_tiles = grad_tiles.count // 4, grad_tiles.count
+    grad_tiles.run(0, some)
     for each in sums:
         each.round(2)
+    rows.send_relayed()
+    grad_tiles.run(some, 3 * some)
+    for each in sums:
+        each.round(3)
     rows.wait_half(False)
     rows.wait_half(True)
 
@@ -1559,24 +1620,28 @@
         if slot == 0:
             load_weight(1).start()
     rows.finish()
-    for each in sums:
-        each.round(3)
-    swap.finish()
+    grad_tiles.run(3 * some, all_tiles)
     for each in sums:
         for number in range(4, lines):
             each.round(number)
         each.exchange()
+    load_downs.wait()
+    part_tiles.run(0, part_tiles.count)
+    swap.finish()
+    for tiles in (grad_tiles, part_tiles):
+        tiles.finish()
     for each in sums:
         each.finish()
 
 
 def last_rows_kernel(
-    lines, pieces, all_grads, attn_any, beta_ref, input_ref, middle_grad_ref, scale_ref, *rest
+    lines, pieces, heads, all_grads, attn_any, turned, beta_ref, input_ref, middle_grad_ref, scale_ref, *rest
 ):
     place = Place()
     blocks, rest = rest[:pieces], rest[pieces:]
     input_grad, gain_ref = rest[:2]
-    results, scratch = rest[2 : 2 + pieces], rest[2 + pieces :]
+    count = pieces + 1 if pieces else 0
+    results, scratch = rest[2 : 2 + count], rest[2 + count :]
     low_grad, grads, attn, load_sems = scratch[:4]
     all_lines, _, depth, width = attn.shape
     tokens = low_grad.shape[0]
@@ -1596,30 +1661,80 @@
     make = sender(scratch[12:14])
     scratch = scratch[14:]
     sums = [
-        SumLines(place, blocks[index], results[index], scratch[7 * index : 7 * index + 7])
-        for index in range(pieces)
+        SumLines(
+            place,
+            blocks[index] if index < pieces else None,
+            results[index],
+            scratch[7 * index : 7 * index + 7],
+        )
+        for index in range(count)
     ]
     loads = [
         pltpu.make_async_copy(all_grads, grads, load_sems.at[0]),
         pltpu.make_async_copy(attn_any, attn, load_sems.at[1]),
     ]
-    for each in sums:
-        each.begin()
     for load in loads:
         load.start()
-    for each in sums:
-        each.wait_loads()
-    for each in sums[1:]:
-        each.round(1)
+    for each in sums[:pieces]:
+        each.begin()
     gain_ref[...] = jnp.zeros_like(gain_ref)
-    for load in loads:
+    if sums:
+        small, _, streams = sums
+        mine, theirs, turned_in, turned_sems = scratch[7 * count :]
+        lines_here = place.line * 2 < lines
+
+        def line_of_turn(turn):
+            return jnp.where(lines_here, lines - 1 - turn, turn)
+
+        height = turned_in.shape[1]
+        each_line = MATES * depth // height
+        mates_each = height // depth
+
+        def load_turned(index):
+            line = line_of_turn(index // each_line)
+            first = line * (MATES * depth) + index % each_line * height
+            return pltpu.make_async_copy(
+                turned.at[pl.ds(pl.multiple_of(first, 128), height)],
+                turned_in.at[index % 2],
+                turned_sems.at[index % 2],
+            )
+
+        kept = lax.broadcasted_iota(jnp.int32, (SMALL, CHUNK), 0)
+        kept = (kept >= BETA_ROW) & (kept < BETA_ROW + heads)
+
+        def weight_grads(first, last):
+            for index in range(first * each_line, last * each_line):
+                load_turned(index).wait()
+                if index + 1 < lines * each_line:
+                    load_turned(index + 1).start()
+                line = line_of_turn(index // each_line)
+                found = dot(turned_in[index % 2], grads[...], NN)
+                for number in range(mates_each):
+                    mate = index % each_line * mates_each + number
+                    part = found[number * depth : (number + 1) * depth]
+                    streams.held[line, mate] = part[:, :width].astype(low)
+                    small.held[line, mate] = jnp.where(
+                        kept, part[:, width:].T[:SMALL], small.held[line, mate].astype(wide)
+                    ).astype(low)
+
+        load_turned(0).start()
+        loads[0].wait()
+        small.wait_loads()
+        weight_grads(0, 1)
+        streams.round(1)
+        sums[1].wait_loads()
+        sums[1].round(1)
+        weight_grads(1, 2)
+    for load in loads[0 if not sums else 1 :]:
         load.wait()
     rows.begin()
     rows.send_far()
     rows.send_near()
-    rows.send_relayed()
+    if sums:
+        weight_grads(2, lines)
     for each in sums[1:]:
         each.round(2)
+    rows.send_relayed()
     rows.wait_half(False)
     rows.wait_half(True)
 
@@ -1636,8 +1751,6 @@
     first_local = pltpu.make_async_copy(low_grad, input_grad.at[place.core], load_sems.at[2])
     first_local.start()
     if sums:
-        mine, theirs = scratch[7 * pieces :]
-        small = sums[0]
         small.put_gains(gain_ref)
         mine[...] = small.held[...]
         swap = make(1, mine, theirs, place.sibling)
@@ -1689,10 +1802,10 @@
 def first_kernel(lines, pieces, input_ref, *rest):
     place = Place()
     blocks, rest = rest[:pieces], rest[pieces:]
-    normed_out, raw_ref, logit_ref, small_ref, attn_out = rest[:5]
+    turned_out, raw_ref, logit_ref, small_ref, attn_out = rest[:5]
     others, scratch = rest[5 : 3 + pieces], rest[3 + pieces :]
-    inputs, normed, small, attn, scale, out_sems = scratch[:6]
-    scratch = scratch[6:]
+    inputs, normed, turned, small, attn, scale, out_sems = scratch[:7]
+    scratch = scratch[7:]
     targets = (small, attn) + tuple(others)
     meet(place, far=True, lines=lines)
     share = ShareRows(place, input_ref.at[place.core], inputs, scratch[:3])
@@ -1701,15 +1814,17 @@
         for index in range(pieces)
     ]
     few, main, later = gathers[:3]
-    for gather in gathers[:3]:
+    for gather in (few, main):
         gather.begin()
-    for gather in gathers[:3]:
+    for gather in (few, main):
         gather.leave()
     share.begin_half(False)
     share.begin_half(True)
     share.begin_rest()
+    later.begin()
     for gather in (few, main):
         gather.onwards(1)
+    later.leave()
     share.forward()
     later.onwards(1)
     for gather in gathers[3:]:
@@ -1742,9 +1857,10 @@
             row_steps(0, tokens, body)
             block = pl.ds(first, tokens)
             logit_ref[block] = dot(normed[block], beta, NT)
+            turned[:, block] = normed[block].T
             outs.append(
                 pltpu.make_async_copy(
-                    normed.at[block], normed_out.at[block], out_sems.at[slot * MATES + mate]
+                    turned.at[:, block], turned_out.at[:, block], out_sems.at[slot * MATES + mate]
                 )
             )
             outs[-1].start()
@@ -1783,7 +1899,7 @@
         0,
         [(array, "any") for array in (block_input, *blocks)],
         [
-            ((rows, model_width), low, "any"),
+            ((model_width, rows), low, "any"),
             ((rows, attn[3]), low, "held"),
             ((rows, CHUNK), wide, "held"),
             (small, low, "held"),
@@ -1793,6 +1909,7 @@
         [
             pltpu.VMEM(shared, low),
             pltpu.VMEM((rows, model_width), low),
+            pltpu.VMEM((model_width, rows), low),
             pltpu.VMEM(small, low),
             pltpu.VMEM(attn, low),
             pltpu.VMEM((1, model_width), wide),
@@ -1816,7 +1933,7 @@
         + [(array, "any") for array in arrays],
         [
             ((rows, columns), wide, "held"),
-            (shared, low, "any"),
+            ((columns, several * rows), low, "any"),
             (shared, low, "any"),
             ((several * rows, ups.shape[3]), low, "any"),
             ((several * rows, downs.shape[3]), low, "any"),
@@ -1827,6 +1944,7 @@
             pltpu.VMEM(weights.shape, low),
             pltpu.SemaphoreType.DMA((2, MATES)),
             pltpu.VMEM(shared, low),
+            pltpu.VMEM((columns, several * rows), low),
             pltpu.VMEM(ups.shape, low),
             pltpu.VMEM((several, rows, ups.shape[3]), low),
             pltpu.VMEM((several, rows, downs.shape[3]), low),
@@ -1839,16 +1957,26 @@
     )
 
 
-def turn_rows(acts_grad, ups, weights, middle, grad, scale, summing, lines):
+def turn_rows(
+    acts_grad, ups, weights, turned, hidden, downs, middle, grad, scale, summing, lines
+):
     rows, columns = middle.shape
     width = weights.shape[-1]
     blocks = (2, MATES, rows, width)
+    all_rows, units = hidden.shape
     scratch = [
         pltpu.VMEM(weights.shape[1:], low),
-        pltpu.SemaphoreType.DMA((3,)),
+        pltpu.SemaphoreType.DMA((4,)),
         pltpu.VMEM(blocks, low),
         pltpu.VMEM(acts_grad.shape, low),
         pltpu.VMEM(ups.shape, low),
+        pltpu.VMEM(downs.shape, low),
+        pltpu.VMEM((2, rows, turned.shape[1]), low),
+        pltpu.VMEM((2, rows, acts_grad.shape[1]), low),
+        pltpu.SemaphoreType.DMA((2, 2)),
+        pltpu.VMEM((2, rows, units), low),
+        pltpu.VMEM((2, rows, columns), low),
+        pltpu.SemaphoreType.DMA((2, 2)),
     ]
     scratch += SumRows.scratch(rows, columns, True) + SwapBlocks.scratch()
     outs = []
@@ -1859,7 +1987,7 @@
     return remote_call(
         functools.partial(turn_rows_kernel, lines, tuple(part for _, part in summing)),
         2,
-        [(array, "any") for array in (acts_grad, ups, weights)]
+        [(array, "any") for array in (acts_grad, ups, weights, turned, hidden, downs)]
         + [(array, "held") for array in (middle, grad, scale)]
         + [(array, "any") for array, _ in summing],
         [
@@ -1867,13 +1995,15 @@
             ((1, columns), wide, "held"),
             ((rows, columns), low, "held"),
             (blocks, low, "any"),
+            ((turned.shape[0], acts_grad.shape[1]), low, "any"),
+            ((all_rows, columns), low, "any"),
         ]
         + outs,
         scratch,
     )
 
 
-def last_rows(all_grads, attn, beta, mine, middle_grad, scale, blocks, lines):
+def last_rows(all_grads, attn, turned, beta, mine, middle_grad, scale, blocks, lines, heads):
     rows, columns = mine.shape
     scratch = [
         pltpu.VMEM((rows, columns), low),
@@ -1882,18 +2012,20 @@
         pltpu.SemaphoreType.DMA((3,)),
     ]
     scratch += SumRows.scratch(rows, columns, True) + [pltpu.SemaphoreType.DMA((2,))] * 2
-    for block, kept in blocks:
-        scratch += SumLines.scratch(lines, block.shape[1:3] + (kept,))
+    results = [block.shape[1:] for block in blocks] + [attn.shape[1:]] * bool(blocks)
+    for shape in results:
+        scratch += SumLines.scratch(lines, shape)
     if blocks:
-        scratch += [pltpu.VMEM(blocks[0][0].shape, low)] * 2
+        scratch += [pltpu.VMEM(blocks[0].shape, low)] * 2
+        scratch += [pltpu.VMEM((2, 256, turned.shape[1]), low), pltpu.SemaphoreType.DMA((2,))]
     return remote_call(
-        functools.partial(last_rows_kernel, lines, len(blocks)),
+        functools.partial(last_rows_kernel, lines, len(blocks), heads),
         3,
-        [(all_grads, "any"), (attn, "any")]
+        [(array, "any") for array in (all_grads, attn, turned)]
         + [(array, "held") for array in (beta, mine, middle_grad, scale)]
-        + [(block, "any") for block, _ in blocks],
+        + [(block, "any") for block in blocks],
         [((2, rows, columns), low, "any"), ((1, columns), wide, "held")]
-        + [(block.shape[1:3] + (kept,), low, "any") for block, kept in blocks],
+        + [(shape, low, "any") for shape in results],
         scratch,
     )
 
@@ -2091,6 +2223,16 @@
     )
 
 
+def units_back_kernel(grad_ref, acts_ref, weight_ref, out_ref):
+    units = weight_ref.shape[1]
+    grad = dot(grad_ref[...], weight_ref[...], NN)
+    acts = acts_ref[...].astype(wide)
+    gate, up = acts[:, :units], acts[:, units:]
+    silu, slope = silu_parts(gate)
+    out_ref[:, :units] = (grad * up * slope).astype(low)
+    out_ref[:, units:] = (grad * silu).astype(low)
+
+
 def tiled_call(body, ins, wholes, outs):
     tile = 256
 
@@ -2155,13 +2297,12 @@
 
 
 def unpack_kernel(
-    heads, attn, outs, ups_low, ups_high, downs,
+    heads, attn, outs, ups, downs,
     query, key, value, outgate, output, swish, upward, downward,
 ):
     size = CHUNK
     width = heads * size
     units = downs.shape[2]
-    split = ups_low.shape[1]
     for mate in range(MATES):
         first = mate * width
         for head in range(heads):
@@ -2173,9 +2314,8 @@
         outgate[:, first : first + width] = attn[mate, :, 3 * width : 4 * width].astype(wide)
         output[first : first + width, :] = outs[mate].astype(wide).T
         here = mate * units
-        for rows_here, part in ((pl.ds(0, split), ups_low), (pl.ds(split, swish.shape[0] - split), ups_high)):
-            swish[rows_here, here : here + units] = part[mate, :, :units].astype(wide)
-            upward[rows_here, here : here + units] = part[mate, :, units:].astype(wide)
+        swish[:, here : here + units] = ups[mate, :, :units].astype(wide)
+        upward[:, here : here + units] = ups[mate, :, units:].astype(wide)
         downward[here : here + units, :] = downs[mate].astype(wide).T
 
 
@@ -2261,7 +2401,7 @@
                 for columns in (gates_end, width, 2 * units, units)
             ],
         )
-        flat_normed, raw, logits, small, attn_full, output_full, ups_full, downward_full = first_call(
+        normed_turned, raw, logits, small, attn_full, output_full, ups_full, downward_full = first_call(
             block_input, (small_cut, *cuts), lines
         )
         ups_split = depth // 128 * 96
@@ -2314,6 +2454,7 @@
 
     if not near:
         flat_normed, raw, logits = project(input_rows, attn_scale, attn_full, beta_rows)
+        normed_turned = flat_normed.T
     sizes_of = (lines, seq_count, heads, span)
     (
         qkv, solved, wu, maps, total, tails, state, fresh, mixed, gated, gathered, output_all, *moved
@@ -2321,40 +2462,29 @@
     middle_moves = ((ups_full, None), (downward_full, None))
     if near:
         middle_moves = ((moved[1], (ups_split, depth - ups_split)), (downward_full, (0, depth)))
-    middle, mlp_normed, grad_rows, acts, hidden, ups_full, downward_full = middle_rows(
+    middle, mlp_turned, grad_rows, acts, hidden, ups_full, downward_blocks = middle_rows(
         gathered, output_all, mine_low, mlp_scale, out_grad, middle_moves, lines
     )
     grad_rows = grad_rows.reshape(rows, model_width)
-    downward_full = downward_full.reshape(model_width, units)
-    mlp_normed = mlp_normed.reshape(rows, model_width)
-    gate_act, up_act = acts[:, :units].astype(wide), acts[:, units:].astype(wide)
-    mlp_part = matmul("rf,df->rd", hidden, downward_full).astype(low)
-
-    hidden_grad = matmul("rd,df->rf", grad_rows, downward_full)
+    downward_full = downward_blocks.reshape(model_width, units)
     downward_grad = matmul("rd,rf->df", grad_rows, hidden).astype(low)
-    acts_grad = jnp.concatenate(
-        [
-            (hidden_grad * up_act * silu_slope(gate_act)).astype(low),
-            (hidden_grad * jax.nn.silu(gate_act)).astype(low),
-        ],
-        axis=1,
+    (acts_grad,) = tiled_call(
+        units_back_kernel, (grad_rows, acts), (downward_full,), [(acts.shape, low)]
     )
-    ups_grad = matmul("rd,rf->df", mlp_normed, acts_grad).astype(low)
 
     def cut_rows(grad):
         return grad.reshape(lines, MATES, depth, grad.shape[1])
 
-    ups_blocks, downward_blocks = cut_rows(ups_grad), cut_rows(downward_grad)
-    turn_sums = back_sums = ()
+    downward_grad = cut_rows(downward_grad)
+    turn_sums = ((downward_grad, (0, depth)),) if near else ()
+    middle_grad, mlp_gain_grad, attn_grad_mine, gated_grad, ups_grad, mlp_part, *summed = turn_rows(
+        acts_grad, ups_full, output_all, mlp_turned, hidden, downward_blocks, middle, grad_mine,
+        mlp_scale, turn_sums, lines,
+    )
+    ups_grad = cut_rows(ups_grad)
+    back_sums = ((ups_grad, (0, depth)),) if near else ()
     if near:
-        sums_split = depth // 128 * 32
-        turn_sums = ((downward_blocks, (0, depth)), (ups_blocks, (0, sums_split)))
-    middle_grad, mlp_gain_grad, attn_grad_mine, gated_grad, *summed = turn_rows(
-        acts_grad, ups_full, output_all, middle, grad_mine, mlp_scale, turn_sums, lines
-    )
-    if near:
-        downward_sum, ups_low = summed
-        back_sums = ((ups_blocks, (sums_split, depth - sums_split)),)
+        downward_sum, = summed
     all_grads, head_gain_parts, taps_grad, attn_grad_rows, block_output, *summed = delta_back(
         limit, raw, tails, taps, logits, head_scale, qkv, wu, maps, total,
         gated_grad.reshape(rows, width), mixed, solved, state, fresh, attn_grad_mine, mlp_part.reshape(blocked), middle,
@@ -2362,9 +2492,11 @@
     )
     attn_grad_rows = attn_grad_rows.reshape(rows, model_width)
     output_grad = cut_rows(matmul("rd,rc->dc", attn_grad_rows, gated).astype(low))
-    attn_grads = matmul("rd,rc->dc", flat_normed, all_grads).astype(low)
-    beta_grad = attn_grads[:, gates_end + BETA_ROW : gates_end + BETA_ROW + heads]
-    attn_grads = cut_rows(attn_grads)
+    beta_grad = jnp.zeros((model_width, heads), low)
+    if not near:
+        attn_grads = matmul("dr,rc->dc", normed_turned, all_grads).astype(low)
+        beta_grad = attn_grads[:, gates_end + BETA_ROW : gates_end + BETA_ROW + heads]
+        attn_grads = cut_rows(attn_grads)
 
     conv_grad = (
         taps_grad[:, :CONV]
@@ -2385,18 +2517,14 @@
         flat = jnp.pad(flat, ((0, 0), (0, SMALL * 128 - small_size)))
         return flat.reshape(lines, MATES, SMALL, 128)
 
-    last_ins = (all_grads, attn_blocks, beta_rows, mine_low, middle_grad, attn_scale)
+    last_ins = (all_grads, attn_blocks, normed_turned, beta_rows, mine_low, middle_grad, attn_scale)
     if near:
-        ups_high, = summed
-        blocks = (
-            (small_blocks(jnp.zeros((1, model_width), wide)), 128),
-            (attn_grads, gates_end),
-            (output_grad, width),
-        )
-        input_grad, _, small_sum, attn_sum, output_sum = last_rows(*last_ins, blocks, lines)
+        ups_sum, = summed
+        blocks = (small_blocks(jnp.zeros((1, model_width), wide)), output_grad)
+        input_grad, _, small_sum, output_sum, attn_sum = last_rows(*last_ins, blocks, lines, heads)
         grads = held_call(
             functools.partial(unpack_kernel, heads),
-            (attn_sum, output_sum, ups_low, ups_high, downward_sum),
+            (attn_sum, output_sum, ups_sum, downward_sum),
             [
                 (w.shape, wide)
                 for w in (
@@ -2408,11 +2536,11 @@
         small_sum = small_sum.reshape(MATES, SMALL * 128).astype(wide)
         gains_sum = jnp.sum(small_sum[:, :conv_start], axis=0)
     else:
-        input_grad, attn_gain_grad = last_rows(*last_ins, (), lines)
+        input_grad, attn_gain_grad = last_rows(*last_ins, (), lines, heads)
         small_sum, attn_sum, output_sum, ups_sum, downward_sum = (
             scatter_grads(block)
             for block in (
-                small_blocks(attn_gain_grad), attn_grads[..., :gates_end], output_grad, ups_blocks, downward_blocks
+                small_blocks(attn_gain_grad), attn_grads[..., :gates_end], output_grad, ups_grad, downward_grad
             )
         )
         small_sum = small_sum.reshape(MATES, SMALL * 128)

time: 742 us -> 686 us (0.925)
  matrix products: 74.6 us -> 16.5 us
  Pallas kernels: 624 us -> 635 us
  other arithmetic: 12.1 us -> 3.37 us
    dot_general x6 -> x2, matrix products: 74.6 us -> 16.5 us  [matmul(): return jnp.einsum(form, left, right, preferred_element_type=wide)]
    pallas_call x4, Pallas kernels: 415 us -> 399 us  [remote_call(): pl.pallas_call(body, in_specs=[anywhere if kind == 'any' else held for _,...]
    pallas_call x0 -> x1, Pallas kernels: none -> 14.7 us  [tiled_call(): pl.pallas_call(body, grid=(ins[0].shape[0] // tile,), in_specs=[tall(arra...]
    pallas_call x2, Pallas kernels: 198 us -> 210 us  [call(): pl.pallas_call(body, grid=(2 * self.chains,), in_specs=[spec for _, spec...]
where the time goes in v8:
time: 686 us; the launch traced here: 673 us
  Pallas kernels  635 us (93%)
  local copies, waits for them, and re-layouts  17.1 us (2%)
  matrix products  16.5 us (2%)
    pallas_call x4, Pallas kernels, remote_call(): pl.pallas_call(body, in_specs=[anywhere if kind == 'any' else held for _,...  399 us
    pallas_call x2, Pallas kernels, call(): pl.pallas_call(body, grid=(2 * self.chains,), in_specs=[spec for _, spec...  210 us
    dot_general x2, matrix products, matmul(): return jnp.einsum(form, left, right, preferred_element_type=wide)  16.5 us
    pallas_call x1, Pallas kernels, tiled_call(): pl.pallas_call(body, grid=(ins[0].shape[0] // tile,), in_specs=[tall(arra...  14.7 us

profile of v8, /device:TPU:0, one launch (start us, length us, event | category | flops | bytes accessed | tf_op | source)
XLA Modules:
  0.0 672.7 jit_solution(4695097292287230916)
XLA Ops:
  0.7 1.3 fusion.5
  2.0 1.9 add_subtract_fusion.limit_ref
  3.9 0.0 copy-start.11
  3.9 5.4 shard_map.271
  9.3 0.0 copy-done.3
  9.3 0.1 reshape.188
  9.4 0.0 copy-done.7
  9.5 0.0 copy-done.9
  9.5 0.0 copy-done.10
  9.5 0.0 copy-done.11
  9.6 0.6 copy.74
  10.2 105.5 %shard_map.272 = (bf16[2048,2048]{1,0:T(8,128)(2,1)}, bf16[2048,1024]{1,0:T(8,128)(2,1)}, f32[2048,128]{1,0:T(8,128)}, bf16[4,4,16,128]{3,2,1,0:T(8,128)(2,1)}, ...) custom-call(bf16[2,256,2048]{2,1,0:T(8,128)(2,1)} %input_ref.1, ...), custom_call_target="tpu_custom_call" | custom-call | tf_op jit(solution)/shard_map/pallas_call | solution.py:1314
  115.7 0.9 copy.72
  116.6 0.1 copy.57
  116.7 0.1 copy.55
  116.9 0.7 reshape.217.taps_ref
  117.6 0.6 reshape.212.scale_ref
  118.2 81.6 %shard_map.273 = (bf16[2048,768]{1,0:T(8,128)(2,1)}, f32[4,8,128,128]{3,2,1,0:T(8,128)}, f32[4,8,128,256]{3,2,1,0:T(8,128)}, f32[4,8,128,128]{3,2,1,0:T(8,128)},...) custom-call(s32[2]{0:T(128)} %add_subtract_fusion.limit_ref, ...), custom_call_target="tpu_custom_call", output_to_operand_aliasing={{12}: (7, {}), {13}: (8, {})} | custom-call | tf_op jit(solution)/shard_map/pallas_call | solution.py:2081
  199.8 0.6 slice_convert_fusion
  200.4 0.0 copy-done
  200.4 2.7 dynamic-slice_bitcast_fusion
  203.1 106.8 %shard_map.274 = (f32[256,2048]{1,0:T(8,128)}, bf16[2048,2048]{1,0:T(8,128)(2,1)}, bf16[2,4,256,2048]{3,2,1,0:T(8,128)(2,1)}, bf16[2048,1408]{1,0:T(8,128)(2,1)}...) custom-call(bf16[2,4,256,256]{3,2,1,0:T(8,128)(2,1)} %get-tuple-elem, ...), custom_call_target="tpu_custom_call", output_to_operand_aliasing={{5}: (5, {}), {6}: (6, {})} | custom-call | tf_op jit(solution)/shard_map/pallas_call | solution.py:1314
  310.0 9.6 %convolution_convert_fusion = bf16[2048,704]{0,1:T(8,128)(2,1)S(1)} fusion(bf16[2048,2048]{1,0:T(8,128)(2,1)} %bitcast.75, bf16[2048,704]{1,0:T(8,128)(2,1)} %get-tuple-element.95.hidden), kind=kOutput, calls=%fused_computation | convolution fusion | flops 5907021824 | bytes 14155776 | tf_op jit(solution)/shard_map/rd,rf->df/dot_general | solution.py:73
  319.6 2.8 copy.50
  322.4 14.7 %shard_map.275.acts_grad = bf16[2048,1408]{1,0:T(8,128)(2,1)} custom-call(bf16[2048,2048]{1,0:T(8,128)(2,1)} %bitcast.76, bf16[2048,1408]{1,0:T(8,128)(2,1)} %get-tuple-element.91.acts_ref, bf16[2048,704]{1,0:T(8,128)(2,1)} %bitcast.72), custom_call_target="tpu_custom_call" | custom-call | tf_op jit(solution)/shard_map/pallas_call | solution.py:2245
  337.1 87.7 %shard_map.276 = (f32[256,2048]{1,0:T(8,128)}, f32[1,2048]{1,0:T(1,128)}, bf16[256,2048]{1,0:T(8,128)(2,1)}, bf16[2,4,256,256]{3,2,1,0:T(8,128)(2,1)}, bf16[2048...) custom-call(bf16[2048,1408]{1,0:T(8,128)(2,1)} %shard_map.275.acts_grad, ...), custom_call_target="tpu_custom_call" | custom-call | tf_op jit(solution)/shard_map/pallas_call | solution.py:1314
  424.8 0.0 copy-start.8
  424.9 128.6 %shard_map.277 = (bf16[2048,1152]{1,0:T(8,128)(2,1)}, f32[4,8,128]{2,1,0:T(8,128)}, f32[4,8,384]{2,1,0:T(8,128)}, bf16[2,4,256,2048]{3,2,1,0:T(8,128)(2,1)}, bf1...) custom-call(s32[2]{0:T(128)} %add_subtract_fusion.limit_ref, ...), custom_call_target="tpu_custom_call" | custom-call | tf_op jit(solution)/shard_map/pallas_call | solution.py:2081
  553.5 0.0 copy-done.8
  553.5 0.0 copy-start.6
  553.5 0.0 copy-start.5
  553.5 6.9 %convolution_convert_fusion.1 = bf16[2048,256]{1,0:T(8,128)(2,1)} fusion(bf16[2048,2048]{1,0:T(8,128)(2,1)} %bitcast.100, bf16[2048,256]{1,0:T(8,128)(2,1)S(1)} %copy-done.8), kind=kOutput, calls=%fused_computation.1 | convolution fusion | flops 2148007936 | bytes 10485760 | tf_op jit(solution)/shard_map/rd,rc->dc/dot_general | solution.py:73
  560.4 0.7 slice_reduce_fusion.1
  561.1 0.1 reshape.203
  561.3 0.2 reshape.204
  561.6 0.1 copy.53
  561.7 0.1 copy.58
  561.8 0.6 copy.64
  562.5 0.8 pad.33.beta_ref
  563.3 98.5 %shard_map.278 = (bf16[2,256,2048]{2,1,0:T(8,128)(2,1)}, f32[1,2048]{1,0:T(1,128)}, bf16[4,16,128]{2,1,0:T(8,128)(2,1)}, bf16[4,128,256]{2,1,0:T(8,128)(2,1)}, bf16[4,128,1024]{2,1,0:T(8,128)(2,1)}) custom-call(bf16[2048,1152]{1,0:T(8,128)(2,1)} %get-tuple-element.106.all_grads, bf16[4,4,128,1024]{3,2,1,0:T(8,128)(2,1)} %get-tuple-element.107.attn_any, ...), custom_call_target="tpu_custom_call" | custom-call | tf_op jit(solution)/shard_map/pallas_call | solution.py:1314
  661.9 5.6 shard_map.279
  667.5 0.7 reshape.210
  668.2 0.6 reshape.209
  668.8 0.5 fusion.4
  669.4 0.5 slice.50
  669.9 1.3 copy.87
  671.2 0.0 copy-done.2
  671.2 1.3 copy.88
  (41 shorter events, 0.3 us)
Async XLA Ops:
  3.9 5.4 copy-start.3
  3.9 5.6 copy-start.7
  3.9 5.6 copy-start.9
  3.9 5.6 copy-start.10
  3.9 5.6 copy-start.11
  118.2 82.2 %copy-start = (bf16[2,256,2048]{2,1,0:T(8,128)(2,1)S(1)}, bf16[2,256,2048]{2,1,0:T(8,128)(2,1)}, u32[]{:S(2)}) copy-start(bf16[2,256,2048]{2,1,0:T(8,128)(2,1)} %grad_any.1) | copy-start | bytes 6291460
  424.8 128.6 %copy-start.8 = (bf16[2048,256]{1,0:T(8,128)(2,1)S(1)}, bf16[2048,256]{1,0:T(8,128)(2,1)}, u32[]{:S(2)}) copy-start(bf16[2048,256]{1,0:T(8,128)(2,1)} %get-tuple-element.114) | copy-start | bytes 3145732
  553.5 7.7 %copy-start.6 = (f32[1,2048]{1,0:T(1,128)S(1)}, f32[1,2048]{1,0:T(1,128)}, u32[]{:S(2)}) copy-start(f32[1,2048]{1,0:T(1,128)} %get-tuple-element.110) | copy-start | bytes 24580
  553.5 7.8 %copy-start.5 = (f32[4,8,384]{2,1,0:T(8,128)S(1)}, f32[4,8,384]{2,1,0:T(8,128)}, u32[]{:S(2)}) copy-start(f32[4,8,384]{2,1,0:T(8,128)} %get-tuple-element.112) | copy-start | bytes 147460
  661.9 5.6 copy-start.4
  661.9 8.0 %copy-start.1 = (bf16[2,256,2048]{2,1,0:T(8,128)(2,1)S(1)}, bf16[2,256,2048]{2,1,0:T(8,128)(2,1)}, u32[]{:S(2)}) copy-start(bf16[2,256,2048]{2,1,0:T(8,128)(2,1)} %get-tuple-element.152) | copy-start | bytes 6291460
  668.8 2.4 copy-start.2

commit v9 on v8

--- a/solution.py
+++ b/solution.py
@@ -120,10 +120,6 @@
 
 def low_nn(left, right):
     return dot(side(left, left), over(*right), NN)
-
-
-def low_nt(left, right):
-    return dot(side(left, left), side(*right), NT)
 
 
 def grid_of_rows():
@@ -221,14 +217,16 @@
             device_id_type=MESH,
         )
 
-    state_copy = pltpu.make_async_remote_copy(
-        src_ref=leaves,
-        dst_ref=enters,
-        send_sem=state_sems.at[0],
-        recv_sem=state_sems.at[1],
-        device_id=place.lines_away(1),
-        device_id_type=MESH,
-    )
+    def state_copy(chain):
+        return pltpu.make_async_remote_copy(
+            src_ref=leaves.at[chain],
+            dst_ref=enters.at[chain],
+            send_sem=state_sems.at[0, chain],
+            recv_sem=state_sems.at[1, chain],
+            device_id=place.lines_away(1),
+            device_id_type=MESH,
+        )
+
     seqs = chains // heads
 
     @pl.when(step == 0)
@@ -325,19 +323,16 @@
 
         ends = lax.fori_loop(0, chunks, advance, (start,) * chains)
 
-        @pl.when(below)
-        def _():
-            state_copy.wait_recv()
-
         @pl.when(place.line == 0)
         def _():
             enters[...] = jnp.zeros_like(enters)
 
         for index in range(chains):
+            pl.when(below)(state_copy(index).wait_recv)
             total_ref[index] = ends[index][:, :head_size]
             leaving = nn_low(pair(ends[index][:, :head_size]), enters[index])
             leaves[index] = (leaving + ends[index][:, head_size:]).astype(low)
-        pl.when(above)(state_copy.start)
+            pl.when(above)(state_copy(index).start)
         share.forward()
 
     def outputs(chain):
@@ -393,7 +388,8 @@
         swap.finish()
         for seq in range(seqs):
             pl.when(above)(tail(seq).wait_send)
-        pl.when(above)(state_copy.wait_send)
+        for chain in range(chains):
+            pl.when(above)(state_copy(chain).wait_send)
 
 
 def back_kernel(
@@ -439,14 +435,15 @@
             device_id_type=MESH,
         )
 
-    state_copy = pltpu.make_async_remote_copy(
-        src_ref=enters,
-        dst_ref=leaves,
-        send_sem=state_sems.at[0],
-        recv_sem=state_sems.at[1],
-        device_id=place.lines_away(-1),
-        device_id_type=MESH,
-    )
+    def state_copy(chain):
+        return pltpu.make_async_remote_copy(
+            src_ref=enters.at[chain],
+            dst_ref=leaves.at[chain],
+            send_sem=state_sems.at[0, chain],
+            recv_sem=state_sems.at[1, chain],
+            device_id=place.lines_away(-1),
+            device_id_type=MESH,
+        )
 
     @pl.when(step == 0)
     def _():
@@ -487,12 +484,11 @@
                 query, key = qkv_ref[here, :head_size], qkv_ref[here, head_size : 2 * head_size]
                 scores = jnp.where(rows >= columns, dot(query, key, NT), 0.0)
                 turned = jnp.where(rows <= columns, dot(key, query, NT), 0.0)
-                grads = pair(mixed_grad)
-                fresh_grads[chain, chunk] = nn(pair(turned), grads)
-                reading = query.astype(wide) - nn(
-                    pair(scores), pair(wu_ref[0, chunk, :, :head_size])
+                fresh_grads[chain, chunk] = dot(turned.astype(low), mixed_grad.astype(low), NN)
+                reading = query.astype(wide) - dot(
+                    scores.astype(low), wu_ref[0, chunk, :, :head_size].astype(low), NN
                 )
-                sources[chain, chunk] = nn(pair(mixed_grad.T), pair(reading))
+                sources[chain, chunk] = dot(mixed_grad.T.astype(low), reading.astype(low), NN)
                 maps[chain, chunk] = map_ref[0, chunk]
             return gain
 
@@ -524,18 +520,15 @@
             0, chunks, advance, (jnp.zeros((head_size, head_size), wide),) * chains
         )
 
-        @pl.when(above)
-        def _():
-            state_copy.wait_recv()
-
         @pl.when(place.line == lines - 1)
         def _():
             leaves[...] = jnp.zeros_like(leaves)
 
         for index in range(chains):
+            pl.when(above)(state_copy(index).wait_recv)
             entering = low_nn(leaves[index], pair(total_ref[index]))
             enters[index] = (entering + ends[index]).astype(low)
-        pl.when(below)(state_copy.start)
+            pl.when(below)(state_copy(index).start)
 
         def again(number, states):
             chunk = chunks - 1 - number
@@ -571,27 +564,26 @@
             live = live_rows(limit, start)
             squash = head_squash(logit_ref[here], head)
             beta = squash * live
-            grads = pair(out_grads[chain, chunk])
-            fresh = pair(fresh_in_ref[0, chunk])
-            state = pair(state_ref[0, chunk])
-            leave = pair(leaving[chain, chunk])
-            both = wu_ref[0, chunk]
-            fresh_grad = fresh_grads[chain, chunk] + low_nt(key, leave)
-            fresh_pair = pair(fresh_grad)
-            score_grad = jnp.where(rows >= columns, nt(grads, fresh), 0.0)
-            turned_grad = jnp.where(rows <= columns, nt(fresh, grads), 0.0)
-            query_grad = nt(grads, state) + nn_low(pair(score_grad), key)
-            key_grad = nn_low(pair(turned_grad), query) + nn(fresh, leave)
-            wkey_grad = -nt(fresh_pair, state)
-            right_grad = nn_wide(pair(solved_ref[0, chunk].T), pair(side(wkey_grad, fresh_grad)))
-            right = pair(right_grad)
-            twos = pair(both)
-            found = dot(right[0], over(*twos), NT)
-            system_grad = found[:, :CHUNK] + found[:, CHUNK:] + dot(right[1], twos[0], NT)
+            grads = out_grads[chain, chunk].astype(low)
+            fresh = fresh_in_ref[0, chunk].astype(low)
+            state = state_ref[0, chunk].astype(low)
+            leave = leaving[chain, chunk].astype(low)
+            both = wu_ref[0, chunk].astype(low)
+            fresh_grad = fresh_grads[chain, chunk] + dot(key, leave, NT)
+            score_grad = jnp.where(rows >= columns, dot(grads, fresh, NT), 0.0)
+            turned_grad = jnp.where(rows <= columns, dot(fresh, grads, NT), 0.0)
+            query_grad = dot(
+                side(grads, score_grad.astype(low)), over(state.T, key), NN
+            )
+            key_grad = dot(side(turned_grad.astype(low), fresh), over(query, leave), NN)
+            wkey_grad = -dot(fresh_grad.astype(low), state, NT)
+            solved = solved_ref[0, chunk].T.astype(low)
+            right_grad = dot(solved, side(wkey_grad, fresh_grad).astype(low), NN)
+            system_grad = dot(right_grad.astype(low), both, NT)
             system_grad = jnp.where(rows > columns, -system_grad, 0.0)
             gram = dot(key, key, NT)
             gram_grad = beta * system_grad
-            key_grad = key_grad + nn_low(pair(gram_grad + gram_grad.T), key)
+            key_grad = key_grad + dot((gram_grad + gram_grad.T).astype(low), key, NN)
             key_right, value_right = right_grad[:, :head_size], right_grad[:, head_size:]
             key_grad = key_grad + beta * key_right
             value_grad = beta * value_right
@@ -630,11 +622,11 @@
             pre_grads[pl.ds(start + 16, CHUNK)] = jnp.concatenate(grads_pre, axis=1)
 
         def group(index, carry):
-            for number in range(2):
-                one(index * 2 + number)
+            for number in range(TOGETHER):
+                one(index * TOGETHER + number)
             return carry
 
-        lax.fori_loop(0, chunks // 2, group, 0)
+        lax.fori_loop(0, chunks // TOGETHER, group, 0)
 
         def back(block):
             parts = []
@@ -721,7 +713,8 @@
 
         for chain in range(chains):
             pl.when(below)(halo(chain).wait_send)
-        pl.when(below)(state_copy.wait_send)
+        for chain in range(chains):
+            pl.when(below)(state_copy(chain).wait_send)
         share.finish()
         outs.finish()
         to_self.wait()
@@ -1004,10 +997,11 @@
             self.copy(came).wait_recv()
             self.copy(then).start()
 
-    def finish(self):
-        self.local().wait()
-        for index in range(6, 11):
-            self.copy(index).wait_recv()
+    def finish(self, arrived=False):
+        if not arrived:
+            self.local().wait()
+            for index in range(6, 11):
+                self.copy(index).wait_recv()
         for index in range(11):
             self.copy(index).wait_send()
 
@@ -1512,7 +1506,7 @@
                 self.load(tile + 1).start()
             if tile >= 2:
                 self.store(tile - 2).wait()
-            self.body(self.held_in.at[tile % 2], self.held_out.at[tile % 2])
+            self.body(tile, self.held_in.at[tile % 2], self.held_out.at[tile % 2])
             self.store(tile).start()
 
     def finish(self):
@@ -1521,17 +1515,17 @@
 
 
 def turn_rows_kernel(
-    lines, parts, acts_grad, ups_any, weights, turned, hidden, downs_any, middle_ref, grad_ref,
-    scale_ref, *rest
+    lines, parts, acts_any, grads_any, ups_any, weights, turned, hidden, downs_any, middle_ref,
+    grad_ref, scale_ref, *rest
 ):
     place = Place()
+    blocks, rest = rest[: 1 if parts else 0], rest[1 if parts else 0 :]
     count = len(parts)
-    blocks, rest = rest[:count], rest[count:]
     middle_grad_ref, gain_ref, low_grad, gated_grads, ups_grad, mlp_part = rest[:6]
     results, scratch = rest[6 : 6 + count], rest[6 + count :]
     held, load_sems, sent, acts, ups, downs = scratch[:6]
-    turned_in, grad_out, grad_sems, hidden_in, part_out, part_sems = scratch[6:12]
-    scratch = scratch[12:]
+    turned_in, grad_out, grad_sems, hidden_in, part_out, part_sems, unit_sems = scratch[6:13]
+    scratch = scratch[13:]
     all_lines, _, depth, units = ups.shape
     tokens = low_grad.shape[0]
 
@@ -1545,10 +1539,44 @@
 
         columns_in_steps(all_lines, depth, step)
 
-    def weight_grad(tile_in, tile_out):
-        tile_out[...] = dot(tile_in[...], acts[...], NN).astype(low)
-
-    def back_down(tile_in, tile_out):
+    def weight_grad(tile, tile_in, tile_out):
+        found = dot(tile_in[...], acts[...], NN).astype(low)
+        tile_out[...] = found
+        if sums:
+            each_line = MATES * depth // tokens
+            for number in range(tokens // depth):
+                mate = tile % each_line * (tokens // depth) + number
+                sums[1].held[tile // each_line, mate] = found[
+                    number * depth : number * depth + parts[1][1]
+                ]
+
+    def load_units(tile):
+        here = pl.ds(tile * tokens, tokens)
+        half = tile % 2
+        return (
+            pltpu.make_async_copy(
+                grads_any.at[tile // MATES, tile % MATES], turned_in.at[half], unit_sems.at[0, half]
+            ),
+            pltpu.make_async_copy(acts_any.at[here], grad_out.at[half], unit_sems.at[1, half]),
+        )
+
+    def units_back():
+        inner = downs.shape[3]
+        for tile in range(2 * MATES):
+            for load in load_units(tile):
+                load.wait()
+            if tile + 1 < 2 * MATES:
+                for load in load_units(tile + 1):
+                    load.start()
+            grad = dot(turned_in[tile % 2], downs[...].reshape(-1, inner), NN)
+            values = grad_out[tile % 2].astype(wide)
+            gate, up = values[:, :inner], values[:, inner:]
+            silu, slope = silu_parts(gate)
+            here = pl.ds(tile * tokens, tokens)
+            acts[here, :inner] = (grad * up * slope).astype(low)
+            acts[here, inner:] = (grad * silu).astype(low)
+
+    def back_down(tile, tile_in, tile_out):
         def step(columns, part, size):
             tile_out[:, columns] = dot(
                 tile_in[...], downs[part].reshape(size, downs.shape[3]), NT
@@ -1561,44 +1589,52 @@
     rows = SumRows(place, None, scratch[:8], compute)
     swap = SwapBlocks(place, lambda slot, mate: sent.at[slot, mate], gated_grads, scratch[8:11])
     sums = [
-        SumLines(place, blocks[index], results[index], scratch[11 + 7 * index : 18 + 7 * index], first)
-        for index, (first, _) in enumerate(parts)
+        SumLines(
+            place,
+            None if index else blocks[0],
+            results[index],
+            scratch[11 + 7 * index : 18 + 7 * index],
+        )
+        for index in range(count)
     ]
     meet(place, lines=lines if parts else 0, cores=True)
-    for each in sums:
+    load_downs = pltpu.make_async_copy(downs_any, downs, load_sems.at[3])
+    load_downs.start()
+    for load in load_units(0):
+        load.start()
+    for each in sums[:1]:
         each.begin()
-    loads = [
-        pltpu.make_async_copy(acts_grad, acts, load_sems.at[0]),
-        pltpu.make_async_copy(ups_any, ups, load_sems.at[1]),
-    ]
-    for load in loads:
-        load.start()
+    load_ups = pltpu.make_async_copy(ups_any, ups, load_sems.at[1])
+    load_ups.start()
 
     def load_weight(slot):
         return pltpu.make_async_copy(weights.at[slot], held, load_sems.at[2])
 
-    load_downs = pltpu.make_async_copy(downs_any, downs, load_sems.at[3])
-    for each in sums:
+    for each in sums[:1]:
         each.wait_loads()
         each.round(1)
     load_weight(0).start()
-    load_downs.start()
-    grad_tiles.begin()
     part_tiles.begin()
     gain_ref[...] = jnp.zeros_like(gain_ref)
-    for load in loads:
-        load.wait()
+    load_downs.wait()
+    units_back()
+    grad_tiles.begin()
+    load_ups.wait()
+    for each in sums[:1]:
+        each.round(2)
     rows.begin()
     rows.send_far()
     rows.send_near()
-    some, all_tiles = grad_tiles.count // 4, grad_tiles.count
-    grad_tiles.run(0, some)
-    for each in sums:
+    all_tiles = grad_tiles.count
+    grad_tiles.run(0, all_tiles)
+    for each in sums[1:]:
+        each.round(1)
+    rows.send_relayed()
+    for each in sums[:1]:
+        each.round(3)
+    part_tiles.run(0, part_tiles.count // 2)
+    for each in sums[1:]:
         each.round(2)
-    rows.send_relayed()
-    grad_tiles.run(some, 3 * some)
-    for each in sums:
-        each.round(3)
     rows.wait_half(False)
     rows.wait_half(True)
 
@@ -1620,13 +1656,13 @@
         if slot == 0:
             load_weight(1).start()
     rows.finish()
-    grad_tiles.run(3 * some, all_tiles)
-    for each in sums:
-        for number in range(4, lines):
-            each.round(number)
+    for each in sums[1:]:
+        each.round(3)
+    for each in sums[:1]:
         each.exchange()
-    load_downs.wait()
-    part_tiles.run(0, part_tiles.count)
+    part_tiles.run(part_tiles.count // 2, part_tiles.count)
+    for each in sums[1:]:
+        each.exchange()
     swap.finish()
     for tiles in (grad_tiles, part_tiles):
         tiles.finish()
@@ -1673,10 +1709,10 @@
         pltpu.make_async_copy(all_grads, grads, load_sems.at[0]),
         pltpu.make_async_copy(attn_any, attn, load_sems.at[1]),
     ]
+    for each in sums[:pieces]:
+        each.begin()
     for load in loads:
         load.start()
-    for each in sums[:pieces]:
-        each.begin()
     gain_ref[...] = jnp.zeros_like(gain_ref)
     if sums:
         small, _, streams = sums
@@ -1718,12 +1754,12 @@
                     ).astype(low)
 
         load_turned(0).start()
+        sums[1].wait_loads()
+        sums[1].round(1)
         loads[0].wait()
         small.wait_loads()
         weight_grads(0, 1)
         streams.round(1)
-        sums[1].wait_loads()
-        sums[1].round(1)
         weight_grads(1, 2)
     for load in loads[0 if not sums else 1 :]:
         load.wait()
@@ -1804,8 +1840,8 @@
     blocks, rest = rest[:pieces], rest[pieces:]
     turned_out, raw_ref, logit_ref, small_ref, attn_out = rest[:5]
     others, scratch = rest[5 : 3 + pieces], rest[3 + pieces :]
-    inputs, normed, turned, small, attn, scale, out_sems = scratch[:7]
-    scratch = scratch[7:]
+    inputs, normed, turned, small, attn, scale, totals, out_sems = scratch[:8]
+    scratch = scratch[8:]
     targets = (small, attn) + tuple(others)
     meet(place, far=True, lines=lines)
     share = ShareRows(place, input_ref.at[place.core], inputs, scratch[:3])
@@ -1825,17 +1861,10 @@
     for gather in (few, main):
         gather.onwards(1)
     later.leave()
+    for step in range(2, lines):
+        few.onwards(step)
     share.forward()
     later.onwards(1)
-    for gather in gathers[3:]:
-        gather.begin()
-    few.onwards(2)
-    main.onwards(2)
-    for step in range(3, lines):
-        few.onwards(step)
-    share.forward_far()
-    later.onwards(2)
-    share.finish()
     small_ref[...] = small[...]
     _, _, tokens, model_width = inputs.shape
     depth = small.shape[3]
@@ -1845,39 +1874,73 @@
     beta = jnp.concatenate([small[line, mate] for line, mate in parts], axis=1)
     beta = over(beta, jnp.zeros((CHUNK - beta.shape[0], model_width), low))
     outs = []
-    for slot in range(2):
-        for mate in range(MATES):
-            first = (slot * MATES + mate) * tokens
-
-            def body(here, slot=slot, mate=mate, first=first):
-                value = inputs[slot, mate, here].astype(wide)
-                there = pl.ds(pl.multiple_of(first + here.start, STEP), STEP)
-                normed[there] = (value * inverse_rms(value) * scale[...]).astype(low)
-
-            row_steps(0, tokens, body)
-            block = pl.ds(first, tokens)
-            logit_ref[block] = dot(normed[block], beta, NT)
-            turned[:, block] = normed[block].T
-            outs.append(
-                pltpu.make_async_copy(
-                    turned.at[:, block], turned_out.at[:, block], out_sems.at[slot * MATES + mate]
-                )
+
+    def norm(slot, mate):
+        first = pl.multiple_of((slot * MATES + mate) * tokens, CHUNK)
+
+        def body(here):
+            value = inputs[slot, mate, here].astype(wide)
+            there = pl.ds(pl.multiple_of(first + here.start, STEP), STEP)
+            normed[there] = (value * inverse_rms(value) * scale[...]).astype(low)
+
+        row_steps(0, tokens, body)
+        block = pl.ds(first, tokens)
+        logit_ref[block] = dot(normed[block], beta, NT)
+        turned[:, block] = normed[block].T
+        outs.append(
+            pltpu.make_async_copy(
+                turned.at[:, block], turned_out.at[:, block], out_sems.at[len(outs)]
             )
-            outs[-1].start()
+        )
+        outs[-1].start()
+
+    share.local().wait()
+    for mate in (place.mate, place.x, place.y):
+        norm(0, mate)
+    main.onwards(2)
+    share.forward_far()
+    for gather in gathers[3:]:
+        gather.begin()
+    norm(0, place.far)
+    later.onwards(2)
+    for index, mate in ((6, place.mate), (7, place.x), (8, place.y)):
+        share.copy(index).wait_recv()
+        norm(1, mate)
+    for index in (9, 10):
+        share.copy(index).wait_recv()
+    norm(1, place.far)
+    height = MATES * depth
+    lower = place.line * 2 < lines
+    first_line = jnp.where(lower, 0, 1)
+    last_line = jnp.where(lower, lines - 1, 0)
+    width = attn.shape[3]
+
+    def tile(index):
+        return pl.ds(pl.multiple_of(index * tokens, STEP), tokens)
+
+    def most(index, carry):
+        here = tile(index)
+        columns = pl.ds(pl.multiple_of(first_line * height, CHUNK), (lines - 1) * height)
+        weight = attn[pl.ds(first_line, lines - 1)].reshape((lines - 1) * height, width)
+        totals[here] = dot(normed[here, columns], weight, NN)
+        return carry
+
+    def rest_of(index, carry):
+        here = tile(index)
+        columns = pl.ds(pl.multiple_of(last_line * height, CHUNK), height)
+        weight = attn[last_line].reshape(height, width)
+        raw_ref[here] = (totals[here] + dot(normed[here, columns], weight, NN)).astype(low)
+        return carry
+
+    lax.fori_loop(0, 2 * MATES, most, 0)
     for step in range(3, lines):
         main.onwards(step)
     outs.append(pltpu.make_async_copy(attn, attn_out, out_sems.at[2 * MATES]))
     outs[-1].start()
-    weight = attn[...].reshape(model_width, attn.shape[3])
-
-    def product(index, carry):
-        here = pl.ds(pl.multiple_of(index * tokens, STEP), tokens)
-        raw_ref[here] = dot(normed[here], weight, NN).astype(low)
-        return carry
-
-    lax.fori_loop(0, 2 * MATES, product, 0)
+    lax.fori_loop(0, 2 * MATES, rest_of, 0)
     for step in range(3, lines):
         later.onwards(step)
+    share.finish(arrived=True)
     for gather in gathers[3:]:
         for slot in range(MATES):
             gather.arrive(slot)
@@ -1913,6 +1976,7 @@
             pltpu.VMEM(small, low),
             pltpu.VMEM(attn, low),
             pltpu.VMEM((1, model_width), wide),
+            pltpu.VMEM((rows, attn[3]), wide),
             pltpu.SemaphoreType.DMA((2 * MATES + 1,)),
         ]
         + ShareRows.scratch()
@@ -1958,7 +2022,7 @@
 
 
 def turn_rows(
-    acts_grad, ups, weights, turned, hidden, downs, middle, grad, scale, summing, lines
+    acts, grads, ups, weights, turned, hidden, downs, middle, grad, scale, downward_grad, ups_rows, lines
 ):
     rows, columns = middle.shape
     width = weights.shape[-1]
@@ -1968,34 +2032,37 @@
         pltpu.VMEM(weights.shape[1:], low),
         pltpu.SemaphoreType.DMA((4,)),
         pltpu.VMEM(blocks, low),
-        pltpu.VMEM(acts_grad.shape, low),
+        pltpu.VMEM(acts.shape, low),
         pltpu.VMEM(ups.shape, low),
         pltpu.VMEM(downs.shape, low),
-        pltpu.VMEM((2, rows, turned.shape[1]), low),
-        pltpu.VMEM((2, rows, acts_grad.shape[1]), low),
+        pltpu.VMEM((2, rows, columns), low),
+        pltpu.VMEM((2, rows, acts.shape[1]), low),
         pltpu.SemaphoreType.DMA((2, 2)),
         pltpu.VMEM((2, rows, units), low),
         pltpu.VMEM((2, rows, columns), low),
         pltpu.SemaphoreType.DMA((2, 2)),
+        pltpu.SemaphoreType.DMA((2, 2)),
     ]
     scratch += SumRows.scratch(rows, columns, True) + SwapBlocks.scratch()
-    outs = []
-    for array, (_, height) in summing:
-        shape = (MATES, height, array.shape[3])
-        scratch += SumLines.scratch(lines, shape)
-        outs.append((shape, low, "any"))
+    outs, parts = [], ()
+    if downward_grad is not None:
+        _, _, depth, _ = downward_grad.shape
+        parts = ((0, depth), (0, ups_rows))
+        for shape in ((MATES, depth, units), (MATES, ups_rows, acts.shape[1])):
+            scratch += SumLines.scratch(lines, shape)
+            outs.append((shape, low, "any"))
     return remote_call(
-        functools.partial(turn_rows_kernel, lines, tuple(part for _, part in summing)),
+        functools.partial(turn_rows_kernel, lines, parts),
         2,
-        [(array, "any") for array in (acts_grad, ups, weights, turned, hidden, downs)]
+        [(array, "any") for array in (acts, grads, ups, weights, turned, hidden, downs)]
         + [(array, "held") for array in (middle, grad, scale)]
-        + [(array, "any") for array, _ in summing],
+        + [(downward_grad, "any")] * bool(parts),
         [
             ((rows, columns), wide, "held"),
             ((1, columns), wide, "held"),
             ((rows, columns), low, "held"),
             (blocks, low, "any"),
-            ((turned.shape[0], acts_grad.shape[1]), low, "any"),
+            ((turned.shape[0], acts.shape[1]), low, "any"),
             ((all_rows, columns), low, "any"),
         ]
         + outs,
@@ -2138,7 +2205,7 @@
         pltpu.VMEM(states, low),
         pltpu.VMEM(tails, low),
         pltpu.SemaphoreType.DMA((2, seqs)),
-        pltpu.SemaphoreType.DMA((2,)),
+        pltpu.SemaphoreType.DMA((2, chains)),
         pltpu.VMEM((seqs, span, heads * size), low),
     ]
     scratch += ShareRows.scratch() + SwapBlocks.scratch()
@@ -2206,7 +2273,7 @@
         pltpu.VMEM(edges, wide),
         pltpu.VMEM(edges, low),
         pltpu.SemaphoreType.DMA((2, chains)),
-        pltpu.SemaphoreType.DMA((2,)),
+        pltpu.SemaphoreType.DMA((2, chains)),
     ] + ShareRows.scratch()
     scratch += [pltpu.VMEM(row_grad.shape, low)] + [pltpu.SemaphoreType.DMA((1,))] * 3
     scratch += SumRows.scratch(*row_grad.shape)
@@ -2221,16 +2288,6 @@
         outs,
         scratch,
     )
-
-
-def units_back_kernel(grad_ref, acts_ref, weight_ref, out_ref):
-    units = weight_ref.shape[1]
-    grad = dot(grad_ref[...], weight_ref[...], NN)
-    acts = acts_ref[...].astype(wide)
-    gate, up = acts[:, :units], acts[:, units:]
-    silu, slope = silu_parts(gate)
-    out_ref[:, :units] = (grad * up * slope).astype(low)
-    out_ref[:, units:] = (grad * silu).astype(low)
 
 
 def tiled_call(body, ins, wholes, outs):
@@ -2297,7 +2354,7 @@
 
 
 def unpack_kernel(
-    heads, attn, outs, ups, downs,
+    heads, attn, outs, ups_low, ups_high, downs,
     query, key, value, outgate, output, swish, upward, downward,
 ):
     size = CHUNK
@@ -2314,8 +2371,9 @@
         outgate[:, first : first + width] = attn[mate, :, 3 * width : 4 * width].astype(wide)
         output[first : first + width, :] = outs[mate].astype(wide).T
         here = mate * units
-        swish[:, here : here + units] = ups[mate, :, :units].astype(wide)
-        upward[:, here : here + units] = ups[mate, :, units:].astype(wide)
+        ups = over(ups_low[mate], ups_high[mate]).astype(wide)
+        swish[:, here : here + units] = ups[:, :units]
+        upward[:, here : here + units] = ups[:, units:]
         downward[here : here + units, :] = downs[mate].astype(wide).T
 
 
@@ -2465,26 +2523,23 @@
     middle, mlp_turned, grad_rows, acts, hidden, ups_full, downward_blocks = middle_rows(
         gathered, output_all, mine_low, mlp_scale, out_grad, middle_moves, lines
     )
-    grad_rows = grad_rows.reshape(rows, model_width)
-    downward_full = downward_blocks.reshape(model_width, units)
-    downward_grad = matmul("rd,rf->df", grad_rows, hidden).astype(low)
-    (acts_grad,) = tiled_call(
-        units_back_kernel, (grad_rows, acts), (downward_full,), [(acts.shape, low)]
-    )
+    downward_grad = matmul(
+        "rd,rf->df", grad_rows.reshape(rows, model_width), hidden
+    ).astype(low)
 
     def cut_rows(grad):
         return grad.reshape(lines, MATES, depth, grad.shape[1])
 
     downward_grad = cut_rows(downward_grad)
-    turn_sums = ((downward_grad, (0, depth)),) if near else ()
+    ups_rows = depth // 4
     middle_grad, mlp_gain_grad, attn_grad_mine, gated_grad, ups_grad, mlp_part, *summed = turn_rows(
-        acts_grad, ups_full, output_all, mlp_turned, hidden, downward_blocks, middle, grad_mine,
-        mlp_scale, turn_sums, lines,
+        acts, grad_rows, ups_full, output_all, mlp_turned, hidden, downward_blocks, middle, grad_mine,
+        mlp_scale, downward_grad if near else None, ups_rows, lines,
     )
     ups_grad = cut_rows(ups_grad)
-    back_sums = ((ups_grad, (0, depth)),) if near else ()
+    back_sums = ((ups_grad, (ups_rows, depth - ups_rows)),) if near else ()
     if near:
-        downward_sum, = summed
+        downward_sum, ups_low = summed
     all_grads, head_gain_parts, taps_grad, attn_grad_rows, block_output, *summed = delta_back(
         limit, raw, tails, taps, logits, head_scale, qkv, wu, maps, total,
         gated_grad.reshape(rows, width), mixed, solved, state, fresh, attn_grad_mine, mlp_part.reshape(blocked), middle,
@@ -2519,12 +2574,12 @@
 
     last_ins = (all_grads, attn_blocks, normed_turned, beta_rows, mine_low, middle_grad, attn_scale)
     if near:
-        ups_sum, = summed
+        ups_high, = summed
         blocks = (small_blocks(jnp.zeros((1, model_width), wide)), output_grad)
         input_grad, _, small_sum, output_sum, attn_sum = last_rows(*last_ins, blocks, lines, heads)
         grads = held_call(
             functools.partial(unpack_kernel, heads),
-            (attn_sum, output_sum, ups_sum, downward_sum),
+            (attn_sum, output_sum, ups_low, ups_high, downward_sum),
             [
                 (w.shape, wide)
                 for w in (

time: 686 us -> 658 us (0.959)
  Pallas kernels: 635 us -> 610 us
    pallas_call x2, Pallas kernels: 210 us -> 191 us  [call(): pl.pallas_call(body, grid=(2 * self.chains,), in_specs=[spec for _, spec...]
    pallas_call x1 -> x0, Pallas kernels: 14.7 us -> none  [tiled_call(): pl.pallas_call(body, grid=(ins[0].shape[0] // tile,), in_specs=[tall(arra...]
    pallas_call x4, Pallas kernels: 399 us -> 407 us  [remote_call(): pl.pallas_call(body, in_specs=[anywhere if kind == 'any' else held for _,...]
where the time goes in v9:
time: 658 us; the launch traced here: 648 us
  Pallas kernels  610 us (93%)
  local copies, waits for them, and re-layouts  17.1 us (3%)
  matrix products  16.5 us (3%)
    pallas_call x4, Pallas kernels, remote_call(): pl.pallas_call(body, in_specs=[anywhere if kind == 'any' else held for _,...  407 us
    pallas_call x2, Pallas kernels, call(): pl.pallas_call(body, grid=(2 * self.chains,), in_specs=[spec for _, spec...  191 us
    dot_general x2, matrix products, matmul(): return jnp.einsum(form, left, right, preferred_element_type=wide)  16.5 us

profile of v9, /device:TPU:0, one launch (start us, length us, event | category | flops | bytes accessed | tf_op | source)
XLA Modules:
  0.0 648.0 jit_solution(13611081693142810683)
XLA Ops:
  0.7 1.3 fusion.5
  2.0 1.9 add_subtract_fusion.limit_ref
  3.9 0.0 copy-start.11
  3.9 5.4 shard_map.271
  9.3 0.0 copy-done.3
  9.3 0.1 reshape.185
  9.4 0.0 copy-done.7
  9.5 0.0 copy-done.9
  9.5 0.0 copy-done.10
  9.5 0.0 copy-done.11
  9.6 0.6 copy.74
  10.2 102.0 %shard_map.272 = (bf16[2048,2048]{1,0:T(8,128)(2,1)}, bf16[2048,1024]{1,0:T(8,128)(2,1)}, f32[2048,128]{1,0:T(8,128)}, bf16[4,4,16,128]{3,2,1,0:T(8,128)(2,1)}, ...) custom-call(bf16[2,256,2048]{2,1,0:T(8,128)(2,1)} %input_ref.1, ...), custom_call_target="tpu_custom_call" | custom-call | tf_op jit(solution)/shard_map/pallas_call | solution.py:1308
  112.2 0.9 copy.72
  113.0 0.1 copy.57
  113.2 0.1 copy.55
  113.3 0.7 reshape.213.taps_ref
  114.0 0.6 reshape.208.scale_ref
  114.6 82.1 %shard_map.273 = (bf16[2048,768]{1,0:T(8,128)(2,1)}, f32[4,8,128,128]{3,2,1,0:T(8,128)}, f32[4,8,128,256]{3,2,1,0:T(8,128)}, f32[4,8,128,128]{3,2,1,0:T(8,128)},...) custom-call(s32[2]{0:T(128)} %add_subtract_fusion.limit_ref, ...), custom_call_target="tpu_custom_call", output_to_operand_aliasing={{12}: (7, {}), {13}: (8, {})} | custom-call | tf_op jit(solution)/shard_map/pallas_call | solution.py:2148
  196.7 0.6 slice_convert_fusion
  197.3 0.0 copy-done
  197.3 2.7 dynamic-slice_bitcast_fusion
  200.1 103.5 %shard_map.274 = (f32[256,2048]{1,0:T(8,128)}, bf16[2048,2048]{1,0:T(8,128)(2,1)}, bf16[2,4,256,2048]{3,2,1,0:T(8,128)(2,1)}, bf16[2048,1408]{1,0:T(8,128)(2,1)}...) custom-call(bf16[2,4,256,256]{3,2,1,0:T(8,128)(2,1)} %get-tuple-elem, ...), custom_call_target="tpu_custom_call", output_to_operand_aliasing={{5}: (5, {}), {6}: (6, {})} | custom-call | tf_op jit(solution)/shard_map/pallas_call | solution.py:1308
  303.6 9.6 %convolution_convert_fusion = bf16[2048,704]{0,1:T(8,128)(2,1)S(1)} fusion(bf16[2048,2048]{1,0:T(8,128)(2,1)} %bitcast.73, bf16[2048,704]{1,0:T(8,128)(2,1)} %get-tuple-element.95.hidden), kind=kOutput, calls=%fused_computation | convolution fusion | flops 5907021824 | bytes 14155776 | tf_op jit(solution)/shard_map/rd,rf->df/dot_general | solution.py:73
  313.2 2.8 copy.50
  316.0 103.6 %shard_map.275 = (f32[256,2048]{1,0:T(8,128)}, f32[1,2048]{1,0:T(1,128)}, bf16[256,2048]{1,0:T(8,128)(2,1)}, bf16[2,4,256,256]{3,2,1,0:T(8,128)(2,1)}, bf16[2048...) custom-call(bf16[2048,1408]{1,0:T(8,128)(2,1)} %get-tuple-element.91, ...), custom_call_target="tpu_custom_call" | custom-call | tf_op jit(solution)/shard_map/pallas_call | solution.py:1308
  419.5 0.0 copy-start.8
  419.6 109.0 %shard_map.276 = (bf16[2048,1152]{1,0:T(8,128)(2,1)}, f32[4,8,128]{2,1,0:T(8,128)}, f32[4,8,384]{2,1,0:T(8,128)}, bf16[2,4,256,2048]{3,2,1,0:T(8,128)(2,1)}, bf1...) custom-call(s32[2]{0:T(128)} %add_subtract_fusion.limit_ref, ...), custom_call_target="tpu_custom_call" | custom-call | tf_op jit(solution)/shard_map/pallas_call | solution.py:2148
  528.6 0.0 copy-done.8
  528.6 0.0 copy-start.6
  528.6 0.0 copy-start.5
  528.6 6.9 %convolution_convert_fusion.1 = bf16[2048,256]{1,0:T(8,128)(2,1)} fusion(bf16[2048,2048]{1,0:T(8,128)(2,1)} %bitcast.97, bf16[2048,256]{1,0:T(8,128)(2,1)S(1)} %copy-done.8), kind=kOutput, calls=%fused_computation.1 | convolution fusion | flops 2148007936 | bytes 10485760 | tf_op jit(solution)/shard_map/rd,rc->dc/dot_general | solution.py:73
  535.5 0.7 slice_reduce_fusion.1
  536.2 0.1 reshape.199
  536.4 0.0 copy-done.5
  536.4 0.2 reshape.200
  536.7 0.1 copy.53
  536.8 0.1 copy.58
  536.9 0.6 copy.64
  537.6 0.8 pad.33.beta_ref
  538.4 98.5 %shard_map.277 = (bf16[2,256,2048]{2,1,0:T(8,128)(2,1)}, f32[1,2048]{1,0:T(1,128)}, bf16[4,16,128]{2,1,0:T(8,128)(2,1)}, bf16[4,128,256]{2,1,0:T(8,128)(2,1)}, bf16[4,128,1024]{2,1,0:T(8,128)(2,1)}) custom-call(bf16[2048,1152]{1,0:T(8,128)(2,1)} %get-tuple-element.107.all_grads, bf16[4,4,128,1024]{3,2,1,0:T(8,128)(2,1)} %get-tuple-element.108.attn_any, ...), custom_call_target="tpu_custom_call" | custom-call | tf_op jit(solution)/shard_map/pallas_call | solution.py:1308
  636.9 5.6 shard_map.278
  642.5 0.7 reshape.206
  643.3 0.6 reshape.205
  643.9 0.5 fusion.4
  644.4 0.5 slice.50
  644.9 1.3 copy.87
  646.2 0.0 copy-done.2
  646.2 1.3 copy.88
  (40 shorter events, 0.3 us)
Async XLA Ops:
  3.9 5.4 copy-start.3
  3.9 5.6 copy-start.7
  3.9 5.6 copy-start.9
  3.9 5.6 copy-start.10
  3.9 5.6 copy-start.11
  114.6 82.7 %copy-start = (bf16[2,256,2048]{2,1,0:T(8,128)(2,1)S(1)}, bf16[2,256,2048]{2,1,0:T(8,128)(2,1)}, u32[]{:S(2)}) copy-start(bf16[2,256,2048]{2,1,0:T(8,128)(2,1)} %grad_any.1) | copy-start | bytes 6291460
  419.5 109.0 %copy-start.8 = (bf16[2048,256]{1,0:T(8,128)(2,1)S(1)}, bf16[2048,256]{1,0:T(8,128)(2,1)}, u32[]{:S(2)}) copy-start(bf16[2048,256]{1,0:T(8,128)(2,1)} %get-tuple-element.115) | copy-start | bytes 3145732
  528.6 7.7 %copy-start.6 = (f32[1,2048]{1,0:T(1,128)S(1)}, f32[1,2048]{1,0:T(1,128)}, u32[]{:S(2)}) copy-start(f32[1,2048]{1,0:T(1,128)} %get-tuple-element.111) | copy-start | bytes 24580
  528.6 7.8 %copy-start.5 = (f32[4,8,384]{2,1,0:T(8,128)S(1)}, f32[4,8,384]{2,1,0:T(8,128)}, u32[]{:S(2)}) copy-start(f32[4,8,384]{2,1,0:T(8,128)} %get-tuple-element.113) | copy-start | bytes 147460
  636.9 5.6 copy-start.4
  636.9 8.0 %copy-start.1 = (bf16[2,256,2048]{2,1,0:T(8,128)(2,1)S(1)}, bf16[2,256,2048]{2,1,0:T(8,128)(2,1)}, u32[]{:S(2)}) copy-start(bf16[2,256,2048]{2,1,0:T(8,128)(2,1)} %get-tuple-element.154) | copy-start | bytes 6291460
  643.9 2.4 copy-start.2

commit v10 on v9

--- a/solution.py
+++ b/solution.py
@@ -162,6 +162,10 @@
     return value * squash, squash * (1.0 + value * (1.0 - squash))
 
 
+def live_here(lengths, place, seq, span):
+    return lengths[(place.core + seq) % 2] - place.line * span
+
+
 def live_rows(limit, start):
     rows = lax.broadcasted_iota(jnp.int32, (CHUNK, CHUNK), 0)
     return jnp.where(rows + start < limit, 1.0, 0.0).astype(wide)
@@ -174,7 +178,7 @@
 
 
 def front_kernel(
-    lines, heads, moves, limit_ref, raw_any, raw_ref, taps_ref, logit_ref, gate_ref, scale_ref, *rest,
+    lines, heads, moves, lengths_ref, raw_any, raw_ref, taps_ref, logit_ref, gate_ref, scale_ref, *rest,
 ):
     count = len(moves)
     outs = rest[count:]
@@ -256,7 +260,7 @@
         ext[:16] = tails[seq, :, pl.ds(pl.multiple_of(head * 3 * head_size, 128), 3 * head_size)].astype(wide)
         ext[16:] = raw_ref[...].astype(wide)
         taps = taps_ref[0]
-        limit = limit_ref[seq]
+        limit = live_here(lengths_ref, place, seq, span)
 
         def group(index, carry):
             first = index * TOGETHER
@@ -393,7 +397,7 @@
 
 
 def back_kernel(
-    lines, heads, parts, limit_ref, raw_ref, tails_ref, taps_ref, logit_ref, gate_ref, scale_ref, qkv_ref,
+    lines, heads, parts, lengths_ref, raw_ref, tails_ref, taps_ref, logit_ref, gate_ref, scale_ref, qkv_ref,
     wu_ref, map_ref, total_ref, grad_ref, mixed_ref, solved_ref, state_ref, fresh_in_ref, row_grad, mlp_partial,
     middle_ref, *rest,
 ):
@@ -551,7 +555,7 @@
         ext[:16] = tails_ref[seq, :, pl.ds(pl.multiple_of(head * 3 * head_size, 128), 3 * head_size)].astype(wide)
         ext[16:] = raw_ref[...].astype(wide)
         taps = taps_ref[0]
-        limit = limit_ref[seq]
+        limit = live_here(lengths_ref, place, seq, span)
         pre_grads[:16] = jnp.zeros((16, 3 * head_size), wide)
         pre_grads[span + 16 :] = jnp.zeros((16, 3 * head_size), wide)
 
@@ -1126,7 +1130,7 @@
         return [
             pltpu.VMEM((lines,) + shape, low),
             pltpu.VMEM((2, max(lines - 1, 1)) + shape, low),
-            pltpu.SemaphoreType.DMA((lines + 1,)),
+            pltpu.SemaphoreType.DMA((lines * MATES + 1,)),
             pltpu.SemaphoreType.DMA((2, lines, MATES)),
             pltpu.SemaphoreType.DMA((2, lines, MATES)),
             pltpu.SemaphoreType.DMA((3,)),
@@ -1140,22 +1144,34 @@
         self.make = sender((send, receive))
         self.order = [place.far, place.x, place.y, place.mate]
 
-    def load(self, line):
-        return pltpu.make_async_copy(
-            self.blocks.at[
-                line, :, pl.ds(self.first, self.held.shape[2]), pl.ds(0, self.held.shape[3])
-            ],
-            self.held.at[line],
-            self.local_sems.at[line],
-        )
+    def loads(self):
+        lines, mates, height, width = self.held.shape
+        if len(self.blocks.shape) == 4:
+            return [
+                pltpu.make_async_copy(
+                    self.blocks.at[line, :, pl.ds(self.first, height)],
+                    self.held.at[line],
+                    self.local_sems.at[line],
+                )
+                for line in range(lines)
+            ]
+        return [
+            pltpu.make_async_copy(
+                self.blocks.at[:, pl.ds((line * mates + mate) * width, width)],
+                self.held.at[line, mate],
+                self.local_sems.at[line * mates + mate],
+            )
+            for line in range(lines)
+            for mate in range(mates)
+        ]
 
     def begin(self):
-        for line in range(self.lines):
-            self.load(line).start()
+        for load in self.loads():
+            load.start()
 
     def wait_loads(self):
-        for line in range(self.lines):
-            self.load(line).wait()
+        for load in self.loads():
+            load.wait()
 
     def put_gains(self, gains):
         lines, mates, height, lanes = self.held.shape
@@ -1245,7 +1261,7 @@
         return pltpu.make_async_copy(
             self.held.at[place.line, place.mate],
             self.result.at[place.mate],
-            self.local_sems.at[self.lines],
+            self.local_sems.at[self.lines * MATES],
         )
 
     def exchange(self):
@@ -1338,13 +1354,13 @@
     ]
 
 
-def middle_kernel(lines, moves, gathered, weights, input_ref, scale_ref, grad_any, *rest):
+def middle_kernel(lines, moves, gathered, weights, input_any, scale_ref, grad_any, *rest):
     place = Place()
     count = len(moves)
     middle_ref, turned_out, grads, acts_out, hidden_out = rest[count : count + 5]
     targets, scratch = rest[count + 5 : 2 * count + 5], rest[2 * count + 5 :]
     normed, held, weight_sems, all_normed, turned, ups, acts, hidden, out_sems, load_sems = scratch[:10]
-    scratch = scratch[10:]
+    input_ref, scratch = scratch[10], scratch[11:]
     share = ShareRows(place, normed, all_normed, scratch[:3])
     other = ShareRows(place, grad_any.at[place.core], grads, scratch[3:6])
     gathers = [
@@ -1354,6 +1370,7 @@
     ]
     meet(place, lines=lines if gathers else 0)
     loads = load_weights(weights, held, weight_sems)
+    loads.append(pltpu.make_async_copy(input_any.at[place.core], input_ref, load_sems.at[2]))
     for load in loads:
         load.start()
     other.begin_half(False)
@@ -1515,8 +1532,8 @@
 
 
 def turn_rows_kernel(
-    lines, parts, acts_any, grads_any, ups_any, weights, turned, hidden, downs_any, middle_ref,
-    grad_ref, scale_ref, *rest
+    lines, parts, acts_any, grads_any, ups_any, weights, turned, hidden, downs_any, out_grad_any,
+    middle_ref, scale_ref, *rest
 ):
     place = Place()
     blocks, rest = rest[: 1 if parts else 0], rest[1 if parts else 0 :]
@@ -1525,7 +1542,7 @@
     results, scratch = rest[6 : 6 + count], rest[6 + count :]
     held, load_sems, sent, acts, ups, downs = scratch[:6]
     turned_in, grad_out, grad_sems, hidden_in, part_out, part_sems, unit_sems = scratch[6:13]
-    scratch = scratch[13:]
+    grad_ref, scratch = scratch[13], scratch[14:]
     all_lines, _, depth, units = ups.shape
     tokens = low_grad.shape[0]
 
@@ -1561,14 +1578,14 @@
         )
 
     def units_back():
-        inner = downs.shape[3]
+        inner = downs.shape[0]
         for tile in range(2 * MATES):
             for load in load_units(tile):
                 load.wait()
             if tile + 1 < 2 * MATES:
                 for load in load_units(tile + 1):
                     load.start()
-            grad = dot(turned_in[tile % 2], downs[...].reshape(-1, inner), NN)
+            grad = dot(turned_in[tile % 2], downs[...], NT)
             values = grad_out[tile % 2].astype(wide)
             gate, up = values[:, :inner], values[:, inner:]
             silu, slope = silu_parts(gate)
@@ -1578,9 +1595,7 @@
 
     def back_down(tile, tile_in, tile_out):
         def step(columns, part, size):
-            tile_out[:, columns] = dot(
-                tile_in[...], downs[part].reshape(size, downs.shape[3]), NT
-            ).astype(low)
+            tile_out[:, columns] = dot(tile_in[...], downs[:, columns], NN).astype(low)
 
         columns_in_steps(all_lines, depth, step)
 
@@ -1598,14 +1613,28 @@
         for index in range(count)
     ]
     meet(place, lines=lines if parts else 0, cores=True)
-    load_downs = pltpu.make_async_copy(downs_any, downs, load_sems.at[3])
-    load_downs.start()
+    if len(downs_any.shape) == 2:
+        load_downs = [pltpu.make_async_copy(downs_any, downs, load_sems.at[3])]
+    else:
+        load_downs = [
+            pltpu.make_async_copy(
+                downs_any.at[line, mate],
+                downs.at[:, pl.ds((line * MATES + mate) * depth, depth)],
+                load_sems.at[3 + line * MATES + mate],
+            )
+            for line in range(lines)
+            for mate in range(MATES)
+        ]
+    for load in load_downs:
+        load.start()
     for load in load_units(0):
         load.start()
     for each in sums[:1]:
         each.begin()
     load_ups = pltpu.make_async_copy(ups_any, ups, load_sems.at[1])
     load_ups.start()
+    load_grad = pltpu.make_async_copy(out_grad_any.at[place.core], grad_ref, load_sems.at[0])
+    load_grad.start()
 
     def load_weight(slot):
         return pltpu.make_async_copy(weights.at[slot], held, load_sems.at[2])
@@ -1616,10 +1645,12 @@
     load_weight(0).start()
     part_tiles.begin()
     gain_ref[...] = jnp.zeros_like(gain_ref)
-    load_downs.wait()
+    for load in load_downs:
+        load.wait()
     units_back()
     grad_tiles.begin()
     load_ups.wait()
+    load_grad.wait()
     for each in sums[:1]:
         each.round(2)
     rows.begin()
@@ -1671,14 +1702,15 @@
 
 
 def last_rows_kernel(
-    lines, pieces, heads, all_grads, attn_any, turned, beta_ref, input_ref, middle_grad_ref, scale_ref, *rest
+    lines, pieces, heads, all_grads, attn_any, turned, input_any, beta_ref, middle_grad_ref, scale_ref, *rest
 ):
     place = Place()
     blocks, rest = rest[:pieces], rest[pieces:]
     input_grad, gain_ref = rest[:2]
     count = pieces + 1 if pieces else 0
     results, scratch = rest[2 : 2 + count], rest[2 + count :]
-    low_grad, grads, attn, load_sems = scratch[:4]
+    low_grad, grads, attn, load_sems, input_ref = scratch[:5]
+    scratch = scratch[1:]
     all_lines, _, depth, width = attn.shape
     tokens = low_grad.shape[0]
 
@@ -1708,6 +1740,7 @@
     loads = [
         pltpu.make_async_copy(all_grads, grads, load_sems.at[0]),
         pltpu.make_async_copy(attn_any, attn, load_sems.at[1]),
+        pltpu.make_async_copy(input_any.at[place.core], input_ref, load_sems.at[3]),
     ]
     for each in sums[:pieces]:
         each.begin()
@@ -1984,8 +2017,8 @@
     )
 
 
-def middle_rows(gathered, weights, mine, scale, out_grad, moving, lines):
-    rows, columns = mine.shape
+def middle_rows(gathered, weights, block_input, scale, out_grad, moving, lines):
+    _, rows, columns = block_input.shape
     shared = (2, MATES, rows, columns)
     arrays = [array for array, _ in moving]
     ups, downs = arrays
@@ -1993,14 +2026,14 @@
     return remote_call(
         functools.partial(middle_kernel, lines, tuple(part for _, part in moving)),
         1,
-        [(gathered, "held"), (weights, "any"), (mine, "held"), (scale, "held"), (out_grad, "any")]
+        [(gathered, "held"), (weights, "any"), (block_input, "any"), (scale, "held"), (out_grad, "any")]
         + [(array, "any") for array in arrays],
         [
             ((rows, columns), wide, "held"),
             ((columns, several * rows), low, "any"),
             (shared, low, "any"),
             ((several * rows, ups.shape[3]), low, "any"),
-            ((several * rows, downs.shape[3]), low, "any"),
+            ((several * rows, downs.shape[2]), low, "any"),
         ]
         + [(array.shape, low, "any") for array in arrays],
         [
@@ -2011,9 +2044,10 @@
             pltpu.VMEM((columns, several * rows), low),
             pltpu.VMEM(ups.shape, low),
             pltpu.VMEM((several, rows, ups.shape[3]), low),
-            pltpu.VMEM((several, rows, downs.shape[3]), low),
+            pltpu.VMEM((several, rows, downs.shape[2]), low),
             pltpu.SemaphoreType.DMA((3, several)),
-            pltpu.SemaphoreType.DMA((2,)),
+            pltpu.SemaphoreType.DMA((3,)),
+            pltpu.VMEM((rows, columns), low),
         ]
         + ShareRows.scratch() * 2
         + GatherLines.scratch(lines) * len(arrays),
@@ -2022,7 +2056,8 @@
 
 
 def turn_rows(
-    acts, grads, ups, weights, turned, hidden, downs, middle, grad, scale, downward_grad, ups_rows, lines
+    acts, grads, ups, weights, turned, hidden, downs, out_grad, middle, scale, downward_grad, ups_rows,
+    lines,
 ):
     rows, columns = middle.shape
     width = weights.shape[-1]
@@ -2030,11 +2065,11 @@
     all_rows, units = hidden.shape
     scratch = [
         pltpu.VMEM(weights.shape[1:], low),
-        pltpu.SemaphoreType.DMA((4,)),
+        pltpu.SemaphoreType.DMA((3 + lines * MATES,)),
         pltpu.VMEM(blocks, low),
         pltpu.VMEM(acts.shape, low),
         pltpu.VMEM(ups.shape, low),
-        pltpu.VMEM(downs.shape, low),
+        pltpu.VMEM((units, columns), low),
         pltpu.VMEM((2, rows, columns), low),
         pltpu.VMEM((2, rows, acts.shape[1]), low),
         pltpu.SemaphoreType.DMA((2, 2)),
@@ -2042,20 +2077,21 @@
         pltpu.VMEM((2, rows, columns), low),
         pltpu.SemaphoreType.DMA((2, 2)),
         pltpu.SemaphoreType.DMA((2, 2)),
+        pltpu.VMEM((rows, columns), low),
     ]
     scratch += SumRows.scratch(rows, columns, True) + SwapBlocks.scratch()
     outs, parts = [], ()
     if downward_grad is not None:
-        _, _, depth, _ = downward_grad.shape
-        parts = ((0, depth), (0, ups_rows))
-        for shape in ((MATES, depth, units), (MATES, ups_rows, acts.shape[1])):
+        depth = ups.shape[2]
+        parts = ((0, units), (0, ups_rows))
+        for shape in ((MATES, units, depth), (MATES, ups_rows, acts.shape[1])):
             scratch += SumLines.scratch(lines, shape)
             outs.append((shape, low, "any"))
     return remote_call(
         functools.partial(turn_rows_kernel, lines, parts),
         2,
-        [(array, "any") for array in (acts, grads, ups, weights, turned, hidden, downs)]
-        + [(array, "held") for array in (middle, grad, scale)]
+        [(array, "any") for array in (acts, grads, ups, weights, turned, hidden, downs, out_grad)]
+        + [(array, "held") for array in (middle, scale)]
         + [(downward_grad, "any")] * bool(parts),
         [
             ((rows, columns), wide, "held"),
@@ -2070,13 +2106,16 @@
     )
 
 
-def last_rows(all_grads, attn, turned, beta, mine, middle_grad, scale, blocks, lines, heads):
-    rows, columns = mine.shape
+def last_rows(
+    all_grads, attn, turned, block_input, beta, middle_grad, scale, blocks, lines, heads
+):
+    _, rows, columns = block_input.shape
     scratch = [
         pltpu.VMEM((rows, columns), low),
         pltpu.VMEM(all_grads.shape, low),
         pltpu.VMEM(attn.shape, low),
-        pltpu.SemaphoreType.DMA((3,)),
+        pltpu.SemaphoreType.DMA((4,)),
+        pltpu.VMEM((rows, columns), low),
     ]
     scratch += SumRows.scratch(rows, columns, True) + [pltpu.SemaphoreType.DMA((2,))] * 2
     results = [block.shape[1:] for block in blocks] + [attn.shape[1:]] * bool(blocks)
@@ -2088,8 +2127,8 @@
     return remote_call(
         functools.partial(last_rows_kernel, lines, len(blocks), heads),
         3,
-        [(array, "any") for array in (all_grads, attn, turned)]
-        + [(array, "held") for array in (beta, mine, middle_grad, scale)]
+        [(array, "any") for array in (all_grads, attn, turned, block_input)]
+        + [(array, "held") for array in (beta, middle_grad, scale)]
         + [(block, "any") for block in blocks],
         [((2, rows, columns), low, "any"), ((1, columns), wide, "held")]
         + [(shape, low, "any") for shape in results],
@@ -2162,7 +2201,7 @@
         )(*[array for array, _ in ins])
 
 
-def delta_front(limit, raw, taps, logits, scale, moving, lines, seqs, heads, span):
+def delta_front(lengths, raw, taps, logits, scale, moving, lines, seqs, heads, span):
     steps = Steps(seqs, heads, span)
     chains, chunks, size = steps.chains, steps.chunks, CHUNK
     squares, doubles = (chains, chunks, CHUNK, size), (chains, chunks, CHUNK, 2 * size)
@@ -2171,7 +2210,7 @@
     anywhere = pl.BlockSpec(memory_space=pl.ANY)
     arrays = [array for array, _ in moving]
     ins = [
-        (limit, pl.BlockSpec(memory_space=pltpu.SMEM)),
+        (lengths, pl.BlockSpec(memory_space=pltpu.SMEM)),
         (raw, anywhere),
         (raw, steps.streams("first")),
         (taps, steps.taps("first")),
@@ -2222,7 +2261,7 @@
 
 
 def delta_back(
-    limit, raw, tails, taps, logits, scale, qkv, wu, maps, total, grad, mixed, solved, state, fresh,
+    lengths, raw, tails, taps, logits, scale, qkv, wu, maps, total, grad, mixed, solved, state, fresh,
     row_grad, mlp_partial, middle, summing, lines, seqs, heads, span,
 ):
     steps = Steps(seqs, heads, span)
@@ -2231,7 +2270,7 @@
     all_shape = (seqs * span, (4 * heads + 1) * size)
     anywhere = pl.BlockSpec(memory_space=pl.ANY)
     ins = [
-        (limit, pl.BlockSpec(memory_space=pltpu.SMEM)),
+        (lengths, pl.BlockSpec(memory_space=pltpu.SMEM)),
         (raw, steps.streams("second")),
         (tails, steps.whole(tails.shape)),
         (taps, steps.taps("second")),
@@ -2336,7 +2375,7 @@
 ):
     size = CHUNK
     width = heads * size
-    units = downs_ref.shape[2]
+    units = downs_ref.shape[1]
     for mate in range(MATES):
         first = mate * width
         for head in range(heads):
@@ -2350,7 +2389,7 @@
         here = mate * units
         ups_ref[mate, :, :units] = swish[:, here : here + units].astype(low)
         ups_ref[mate, :, units:] = upward[:, here : here + units].astype(low)
-        downs_ref[mate] = downward[here : here + units, :].T.astype(low)
+        downs_ref[mate] = downward[here : here + units, :].astype(low)
 
 
 def unpack_kernel(
@@ -2359,7 +2398,7 @@
 ):
     size = CHUNK
     width = heads * size
-    units = downs.shape[2]
+    units = downs.shape[1]
     for mate in range(MATES):
         first = mate * width
         for head in range(heads):
@@ -2374,7 +2413,7 @@
         ups = over(ups_low[mate], ups_high[mate]).astype(wide)
         swish[:, here : here + units] = ups[:, :units]
         upward[:, here : here + units] = ups[:, units:]
-        downward[here : here + units, :] = downs[mate].astype(wide).T
+        downward[here : here + units, :] = downs[mate].astype(wide)
 
 
 def cut_columns(weight):
@@ -2456,8 +2495,9 @@
             ),
             [
                 ((MATES, depth, columns), low)
-                for columns in (gates_end, width, 2 * units, units)
-            ],
+                for columns in (gates_end, width, 2 * units)
+            ]
+            + [((MATES, units, depth), low)],
         )
         normed_turned, raw, logits, small, attn_full, output_full, ups_full, downward_full = first_call(
             block_input, (small_cut, *cuts), lines
@@ -2478,7 +2518,7 @@
             jnp.concatenate([streams_cut, cut_columns(outgate_weight.astype(low))], axis=2),
             cut_columns(output_weight.astype(low).T),
             jnp.concatenate([cut_columns(w.astype(low)) for w in (swish_weight, upward_weight)], axis=2),
-            cut_columns(downward_weight.astype(low).T),
+            downward_weight.astype(low).reshape(MATES, units, depth),
         )
         input_rows = first_rows(block_input).reshape(rows, model_width)
         small, attn_full, output_full, ups_full, downward_full = (gather_weights(cut) for cut in cuts)
@@ -2504,11 +2544,7 @@
     )
     beta_rows = jnp.pad(beta_rows, ((BETA_ROW, CHUNK - BETA_ROW - heads), (0, 0)))
 
-    mine_low = pick(block_input, core)
-    grad_mine = pick(out_grad, core)
     blocked = (seq_count, MATES, tokens, model_width)
-    lengths_here = jnp.stack([pick(lengths, core), pick(lengths, 1 - core)])
-    limit = lengths_here - line_of() * span
 
     if not near:
         flat_normed, raw, logits = project(input_rows, attn_scale, attn_full, beta_rows)
@@ -2516,24 +2552,25 @@
     sizes_of = (lines, seq_count, heads, span)
     (
         qkv, solved, wu, maps, total, tails, state, fresh, mixed, gated, gathered, output_all, *moved
-    ) = delta_front(limit, raw, taps, logits, head_scale, front_moves, *sizes_of)
+    ) = delta_front(lengths, raw, taps, logits, head_scale, front_moves, *sizes_of)
     middle_moves = ((ups_full, None), (downward_full, None))
     if near:
-        middle_moves = ((moved[1], (ups_split, depth - ups_split)), (downward_full, (0, depth)))
+        middle_moves = ((moved[1], (ups_split, depth - ups_split)), (downward_full, (0, units)))
     middle, mlp_turned, grad_rows, acts, hidden, ups_full, downward_blocks = middle_rows(
-        gathered, output_all, mine_low, mlp_scale, out_grad, middle_moves, lines
+        gathered, output_all, block_input, mlp_scale, out_grad, middle_moves, lines
     )
     downward_grad = matmul(
-        "rd,rf->df", grad_rows.reshape(rows, model_width), hidden
+        "rf,rd->fd", hidden, grad_rows.reshape(rows, model_width)
     ).astype(low)
 
     def cut_rows(grad):
         return grad.reshape(lines, MATES, depth, grad.shape[1])
 
-    downward_grad = cut_rows(downward_grad)
     ups_rows = depth // 4
+    if not near:
+        downward_blocks = downward_blocks.transpose(2, 0, 1, 3).reshape(units, model_width)
     middle_grad, mlp_gain_grad, attn_grad_mine, gated_grad, ups_grad, mlp_part, *summed = turn_rows(
-        acts, grad_rows, ups_full, output_all, mlp_turned, hidden, downward_blocks, middle, grad_mine,
+        acts, grad_rows, ups_full, output_all, mlp_turned, hidden, downward_blocks, out_grad, middle,
         mlp_scale, downward_grad if near else None, ups_rows, lines,
     )
     ups_grad = cut_rows(ups_grad)
@@ -2541,7 +2578,7 @@
     if near:
         downward_sum, ups_low = summed
     all_grads, head_gain_parts, taps_grad, attn_grad_rows, block_output, *summed = delta_back(
-        limit, raw, tails, taps, logits, head_scale, qkv, wu, maps, total,
+        lengths, raw, tails, taps, logits, head_scale, qkv, wu, maps, total,
         gated_grad.reshape(rows, width), mixed, solved, state, fresh, attn_grad_mine, mlp_part.reshape(blocked), middle,
         back_sums, *sizes_of,
     )
@@ -2572,7 +2609,7 @@
         flat = jnp.pad(flat, ((0, 0), (0, SMALL * 128 - small_size)))
         return flat.reshape(lines, MATES, SMALL, 128)
 
-    last_ins = (all_grads, attn_blocks, normed_turned, beta_rows, mine_low, middle_grad, attn_scale)
+    last_ins = (all_grads, attn_blocks, normed_turned, block_input, beta_rows, middle_grad, attn_scale)
     if near:
         ups_high, = summed
         blocks = (small_blocks(jnp.zeros((1, model_width), wide)), output_grad)
@@ -2592,10 +2629,11 @@
         gains_sum = jnp.sum(small_sum[:, :conv_start], axis=0)
     else:
         input_grad, attn_gain_grad = last_rows(*last_ins, (), lines, heads)
+        downward_cut = downward_grad.reshape(units, lines, MATES, depth).transpose(1, 2, 0, 3)
         small_sum, attn_sum, output_sum, ups_sum, downward_sum = (
             scatter_grads(block)
             for block in (
-                small_blocks(attn_gain_grad), attn_grads[..., :gates_end], output_grad, ups_grad, downward_grad
+                small_blocks(attn_gain_grad), attn_grads[..., :gates_end], output_grad, ups_grad, downward_cut
             )
         )
         small_sum = small_sum.reshape(MATES, SMALL * 128)
@@ -2615,7 +2653,7 @@
             join_columns(output_sum).T,
             join_columns(ups_sum[:, :, :units]),
             join_columns(ups_sum[:, :, units:]),
-            join_columns(downward_sum).T,
+            downward_sum.reshape(MATES * units, depth),
         )
     conv_sum = small_sum[:, conv_start : conv_start + conv_size]
     beta_sum = small_sum[:, beta_start:small_size].reshape(MATES * heads, depth).T

time: 658 us -> 648 us (0.985)
  local copies, waits for them, and re-layouts: 17.1 us -> 10.3 us
where the time goes in v10:
time: 648 us; the launch traced here: 638 us
  Pallas kernels  607 us (94%)
  matrix products  17.6 us (3%)
  local copies, waits for them, and re-layouts  10.3 us (2%)
    pallas_call x4, Pallas kernels, remote_call(): pl.pallas_call(body, in_specs=[anywhere if kind == 'any' else held for _,...  407 us
    pallas_call x2, Pallas kernels, call(): pl.pallas_call(body, grid=(2 * self.chains,), in_specs=[spec for _, spec...  190 us
    dot_general x2, matrix products, matmul(): return jnp.einsum(form, left, right, preferred_element_type=wide)  17.6 us

profile of v10, /device:TPU:0, one launch (start us, length us, event | category | flops | bytes accessed | tf_op | source)
XLA Modules:
  0.0 637.8 jit_solution(10523059891908941823)
XLA Ops:
  0.7 0.0 copy-start.2
  0.7 0.0 copy-start.6
  0.7 0.0 copy-start.8
  0.7 0.0 copy-start.9
  0.7 0.0 copy-start.10
  0.7 5.2 shard_map.271
  5.9 0.0 copy-done.2
  6.0 0.1 reshape.182
  6.1 0.0 copy-done.6
  6.1 0.0 copy-done.8
  6.1 0.0 copy-done.9
  6.1 0.0 copy-done.10
  6.2 0.6 copy.71
  6.8 102.0 %shard_map.272 = (bf16[2048,2048]{1,0:T(8,128)(2,1)}, bf16[2048,1024]{1,0:T(8,128)(2,1)}, f32[2048,128]{1,0:T(8,128)}, bf16[4,4,16,128]{3,2,1,0:T(8,128)(2,1)}, ...) custom-call(bf16[2,256,2048]{2,1,0:T(8,128)(2,1)} %input_any.3, ...), custom_call_target="tpu_custom_call" | custom-call | tf_op jit(solution)/shard_map/pallas_call | solution.py:1324
  108.8 0.9 copy.69
  109.7 0.1 copy.54
  109.8 0.1 copy.52
  109.9 0.7 reshape.209.taps_ref
  110.7 0.6 reshape.204.scale_ref
  111.3 81.9 %shard_map.273 = (bf16[2048,768]{1,0:T(8,128)(2,1)}, f32[4,8,128,128]{3,2,1,0:T(8,128)}, f32[4,8,128,256]{3,2,1,0:T(8,128)}, f32[4,8,128,128]{3,2,1,0:T(8,128)},...) custom-call(s32[2]{0:T(128)} %lengths_ref.3, ...), custom_call_target="tpu_custom_call", output_to_operand_aliasing={{12}: (7, {}), {13}: (8, {})} | custom-call | tf_op jit(solution)/shard_map/pallas_call | solution.py:2187
  193.1 0.6 slice_convert_fusion
  193.8 101.8 %shard_map.274 = (f32[256,2048]{1,0:T(8,128)}, bf16[2048,2048]{1,0:T(8,128)(2,1)}, bf16[2,4,256,2048]{3,2,1,0:T(8,128)(2,1)}, bf16[2048,1408]{1,0:T(8,128)(2,1)}...) custom-call(bf16[2,4,256,256]{3,2,1,0:T(8,128)(2,1)} %get-tuple-elem, ...), custom_call_target="tpu_custom_call", output_to_operand_aliasing={{5}: (5, {}), {6}: (6, {})} | custom-call | tf_op jit(solution)/shard_map/pallas_call | solution.py:1324
  295.6 10.7 %convolution_convert_fusion.rest_0_ = bf16[704,2048]{1,0:T(8,128)(2,1)} fusion(bf16[2048,704]{1,0:T(8,128)(2,1)} %get-tuple-element.95.hidden, bf16[2048,2048]{1,0:T(8,128)(2,1)} %bitcast.67), kind=kOutput, calls=%fused_computation | convolution fusion | flops 5907021824 | bytes 14155776 | tf_op jit(solution)/shard_map/rf,rd->fd/dot_general | solution.py:73
  306.3 104.2 %shard_map.275 = (f32[256,2048]{1,0:T(8,128)}, f32[1,2048]{1,0:T(1,128)}, bf16[256,2048]{1,0:T(8,128)(2,1)}, bf16[2,4,256,256]{3,2,1,0:T(8,128)(2,1)}, bf16[2048...) custom-call(bf16[2048,1408]{1,0:T(8,128)(2,1)} %get-tuple-element.91, ...), custom_call_target="tpu_custom_call" | custom-call | tf_op jit(solution)/shard_map/pallas_call | solution.py:1324
  410.5 0.0 copy-start.7
  410.5 107.7 %shard_map.276 = (bf16[2048,1152]{1,0:T(8,128)(2,1)}, f32[4,8,128]{2,1,0:T(8,128)}, f32[4,8,384]{2,1,0:T(8,128)}, bf16[2,4,256,2048]{3,2,1,0:T(8,128)(2,1)}, bf1...) custom-call(s32[2]{0:T(128)} %lengths_ref.3, bf16[2048,1024]{1,0:T(8,128)(2,1)} %get-tuple-element.77.raw_any.raw_ref.gate_ref, ...), custom_call_target="tpu_custom_call" | custom-call | tf_op jit(solution)/shard_map/pallas_call | solution.py:2187
  518.3 0.0 copy-done.7
  518.3 0.0 copy-start.5
  518.3 0.0 copy-start.4
  518.3 6.9 %convolution_convert_fusion.1 = bf16[2048,256]{1,0:T(8,128)(2,1)} fusion(bf16[2048,2048]{1,0:T(8,128)(2,1)} %bitcast.91, bf16[2048,256]{1,0:T(8,128)(2,1)S(1)} %copy-done.7), kind=kOutput, calls=%fused_computation.1 | convolution fusion | flops 2148007936 | bytes 10485760 | tf_op jit(solution)/shard_map/rd,rc->dc/dot_general | solution.py:73
  525.2 0.7 slice_reduce_fusion.1
  525.9 0.1 reshape.195
  526.0 0.0 copy-done.5
  526.1 0.0 copy-done.4
  526.1 0.2 reshape.196
  526.4 0.1 copy.50
  526.5 0.1 copy.55
  526.6 0.6 copy.61
  527.3 0.8 pad.33.beta_ref
  528.1 98.8 %shard_map.277 = (bf16[2,256,2048]{2,1,0:T(8,128)(2,1)}, f32[1,2048]{1,0:T(1,128)}, bf16[4,16,128]{2,1,0:T(8,128)(2,1)}, bf16[4,128,256]{2,1,0:T(8,128)(2,1)}, bf16[4,128,1024]{2,1,0:T(8,128)(2,1)}) custom-call(bf16[2048,1152]{1,0:T(8,128)(2,1)} %get-tuple-element.107.all_grads, bf16[4,4,128,1024]{3,2,1,0:T(8,128)(2,1)} %get-tuple-element.108.attn_any, ...), custom_call_target="tpu_custom_call" | custom-call | tf_op jit(solution)/shard_map/pallas_call | solution.py:1324
  626.9 0.0 copy-start.3
  626.9 5.4 shard_map.278
  632.4 0.7 reshape.202
  633.1 0.6 reshape.201
  633.7 0.5 fusion.4
  634.2 0.5 slice.50
  634.7 1.3 copy.84
  636.1 1.3 copy.85
  (34 shorter events, 0.3 us)
Async XLA Ops:
  0.7 5.3 copy-start.2
  0.7 5.4 copy-start.6
  0.7 5.4 copy-start.8
  0.7 5.4 copy-start.9
  0.7 5.5 copy-start.10
  410.5 107.7 %copy-start.7 = (bf16[2048,256]{1,0:T(8,128)(2,1)S(1)}, bf16[2048,256]{1,0:T(8,128)(2,1)}, u32[]{:S(2)}) copy-start(bf16[2048,256]{1,0:T(8,128)(2,1)} %get-tuple-element.115) | copy-start | bytes 3145732
  518.3 7.7 %copy-start.5 = (f32[1,2048]{1,0:T(1,128)S(1)}, f32[1,2048]{1,0:T(1,128)}, u32[]{:S(2)}) copy-start(f32[1,2048]{1,0:T(1,128)} %get-tuple-element.111) | copy-start | bytes 24580
  518.3 7.8 %copy-start.4 = (f32[4,8,384]{2,1,0:T(8,128)S(1)}, f32[4,8,384]{2,1,0:T(8,128)}, u32[]{:S(2)}) copy-start(f32[4,8,384]{2,1,0:T(8,128)} %get-tuple-element.113) | copy-start | bytes 147460
  626.9 5.4 copy-start.3
  626.9 7.8 %copy-start = (bf16[2,256,2048]{2,1,0:T(8,128)(2,1)S(1)}, bf16[2,256,2048]{2,1,0:T(8,128)(2,1)}, u32[]{:S(2)}) copy-start(bf16[2,256,2048]{2,1,0:T(8,128)(2,1)} %get-tuple-element.150) | copy-start | bytes 6291460
  633.7 2.4 copy-start.1
